TPU v7x, 32 devices: a whole 2x2x4 slice. The times are simulated.
32 devices in a mesh: member: 2 (over x), tx: 8 (over z, y), ty: 2 (over core).
Axes of the slice: x: 2, y: 2, z: 4, core: 2. Of those that a mesh axis runs over, the one named last changes fastest.
Arguments:
- state: float32 [12, 3, 4, 48, 48], P('member', None, None, 'tx', 'ty'), parts along dimension 0, may hold values from -6 to 6
- coriolis: float32 [6, 48, 48], P(None, 'tx', 'ty'), may hold values from -0.3 to 0.3
- wave_speed: float32 [4], replicated, may hold values from 0.1 to 0.4
- edges: int32 [6, 4, 3], replicated, may hold values from 0 to 5, as said below
Outputs:
- state_out: float32 [12, 3, 4, 48, 48], P('member', None, None, 'tx', 'ty'), parts along dimension 0
There are 2 independent parts, one for each index of `member`. A program takes and returns all parts, laid end to end along the dimension named above; an argument that names none is the same for every part. Nothing has to cross between parts.
Inputs may be any that keep to these rules, and one draw needn't show every extreme that they name: edges[f, s] = (g, t, r): side s of face f meets side t of face g, r = 1 where the along-edge directions are opposite. The table is the connectivity of a cube whose faces carry arbitrary labels and frame rotations; the relation is symmetric.
All inputs are finite; a program needn't handle non-finite values.
Results may differ from a plain program's by a relative error of at most 0.00002.
Values sent between devices are 32-bit elements; how exact they have to be, the bound alone decides.
No kernel may reach another device: no remote copies, remote signals or barrier semaphores. Data moves between devices by JAX's collectives and lax.ppermute only.
A program may use at most 128 MiB of HBM per device.

v0:
```python
import jax
import jax.numpy as jnp
from jax import lax
from jax.sharding import PartitionSpec as P

SUBSTEPS = 2


def padded_2(block, sides, width):
    for axis, dim in sides:
        count = lax.axis_size(axis)
        forward = [(i, i + 1) for i in range(count - 1)]
        backward = [(target, source) for source, target in forward]
        low = lax.ppermute(
            lax.slice_in_dim(block, block.shape[dim] - width, None, axis=dim), axis, forward
        )
        high = lax.ppermute(lax.slice_in_dim(block, 0, width, axis=dim), axis, backward)
        block = jnp.concatenate([low, block, high], axis=dim)
    return block


def spread(block, axis, owner):
    block = jnp.where(lax.axis_index(axis) == owner, block, jnp.zeros_like(block))
    return lax.psum(block, axis)


def rotate_strip(strip_data, side_index, far_side, flipped):
    normal_part = jnp.where(far_side < 2, strip_data[1], strip_data[2])
    along_part = jnp.where(far_side < 2, strip_data[2], strip_data[1])
    sign_here = 2.0 * (side_index % 2) - 1.0
    sign_there = (2 * (far_side % 2) - 1).astype(jnp.float32)
    normal_part = -sign_here * sign_there * normal_part
    along_part = (1 - 2 * flipped).astype(jnp.float32) * along_part
    if side_index < 2:
        return jnp.stack([strip_data[0], normal_part, along_part])
    return jnp.stack([strip_data[0], along_part, normal_part])


def window_strip(store, side_pick, neighbour, flipped, start, width):
    full_length = store.shape[5]
    begin = jnp.where(flipped == 1, full_length - start - width, start)
    zero = jnp.zeros((), jnp.int32)
    sizes_here = (1, 1, store.shape[2], store.shape[3], store.shape[4], width)
    piece = lax.dynamic_slice(store, (side_pick, neighbour, zero, zero, zero, begin), sizes_here)[
        0, 0
    ]
    return jnp.where(flipped == 1, jnp.flip(piece, 3), piece)


def side_halo(edge_store, edges, face_index, side_index, start, width):
    neighbour = edges[face_index, side_index, 0]
    far_side = edges[face_index, side_index, 1]
    flipped = edges[face_index, side_index, 2]
    strip_data = window_strip(edge_store, far_side, neighbour, flipped, start, width)
    return rotate_strip(strip_data, side_index, far_side, flipped)


def advance(padded, wave_speed, coriolis_part, cells_x, cells_y):
    height = padded[..., 0, :, :, :]
    wind_east = padded[..., 1, :, :, :]
    wind_north = padded[..., 2, :, :, :]
    speed = wave_speed[:, None, None]
    east_pred = wind_east[..., 1 : cells_x + 5, 3 : cells_y + 3] - speed * (
        0.5
        * (
            height[..., 2 : cells_x + 6, 3 : cells_y + 3]
            - height[..., 0 : cells_x + 4, 3 : cells_y + 3]
        )
    )
    north_pred = wind_north[..., 3 : cells_x + 3, 1 : cells_y + 5] - speed * (
        0.5
        * (
            height[..., 3 : cells_x + 3, 2 : cells_y + 6]
            - height[..., 3 : cells_x + 3, 0 : cells_y + 4]
        )
    )
    flux_east = (
        8.0 * (east_pred[..., 3 : cells_x + 3, :] - east_pred[..., 1 : cells_x + 1, :])
        - (east_pred[..., 4 : cells_x + 4, :] - east_pred[..., 0:cells_x, :])
    ) / 12.0
    flux_north = (
        8.0 * (north_pred[..., 3 : cells_y + 3] - north_pred[..., 1 : cells_y + 1])
        - (north_pred[..., 4 : cells_y + 4] - north_pred[..., 0:cells_y])
    ) / 12.0
    height_new = height[..., 3 : cells_x + 3, 3 : cells_y + 3] - speed * (flux_east + flux_north)
    east_inner = east_pred[..., 2 : cells_x + 2, :]
    north_inner = north_pred[..., 2 : cells_y + 2]
    turning = coriolis_part[..., None, :, :]
    return jnp.stack(
        [height_new, east_inner + turning * north_inner, north_inner - turning * east_inner],
        axis=-4,
    )


def one_substep(state, coriolis, wave_speed, edges, count_x, count_y, index_x, index_y):
    faces = state.shape[0]
    cells_x = state.shape[3]
    cells_y = state.shape[4]
    padded = padded_2(state, (("tx", 3), ("ty", 4)), 3)
    west_rim = state[:, :, :, 0:3, :]
    east_rim = jnp.flip(state[:, :, :, cells_x - 3 :, :], 3)
    south_rim = jnp.swapaxes(state[:, :, :, :, 0:3], 3, 4)
    north_rim = jnp.swapaxes(jnp.flip(state[:, :, :, :, cells_y - 3 :], 4), 3, 4)
    west_part = spread(west_rim, "tx", 0)
    east_part = spread(east_rim, "tx", count_x - 1)
    west_full, east_full = (
        lax.all_gather(west_part, "ty", axis=4, tiled=True),
        lax.all_gather(east_part, "ty", axis=4, tiled=True),
    )
    south_row, north_row = (
        lax.all_gather(south_rim, "tx", axis=4, tiled=True),
        lax.all_gather(north_rim, "tx", axis=4, tiled=True),
    )
    south_all, north_all = (
        lax.all_gather(south_row, "ty", axis=0, tiled=True),
        lax.all_gather(north_row, "ty", axis=0, tiled=True),
    )
    south_full = south_all[0:faces]
    north_full = north_all[(count_y - 1) * faces : count_y * faces]
    edge_store = jnp.stack([west_full, east_full, south_full, north_full])
    halos = []
    for side_index in range(4):
        if side_index < 2:
            slabs = jnp.stack(
                [
                    side_halo(edge_store, edges, face_index, side_index, index_y * cells_y, cells_y)
                    for face_index in range(faces)
                ]
            )
        else:
            slabs = jnp.stack(
                [
                    side_halo(edge_store, edges, face_index, side_index, index_x * cells_x, cells_x)
                    for face_index in range(faces)
                ]
            )
        halos.append(slabs)
    west_region = padded[:, :, :, 0:3, 3 : cells_y + 3]
    padded = padded.at[:, :, :, 0:3, 3 : cells_y + 3].set(
        jnp.where(index_x == 0, jnp.flip(halos[0], 3), west_region)
    )
    east_region = padded[:, :, :, cells_x + 3 : cells_x + 6, 3 : cells_y + 3]
    padded = padded.at[:, :, :, cells_x + 3 : cells_x + 6, 3 : cells_y + 3].set(
        jnp.where(index_x == count_x - 1, halos[1], east_region)
    )
    south_region = padded[:, :, :, 3 : cells_x + 3, 0:3]
    padded = padded.at[:, :, :, 3 : cells_x + 3, 0:3].set(
        jnp.where(index_y == 0, jnp.swapaxes(jnp.flip(halos[2], 3), 3, 4), south_region)
    )
    north_region = padded[:, :, :, 3 : cells_x + 3, cells_y + 3 : cells_y + 6]
    padded = padded.at[:, :, :, 3 : cells_x + 3, cells_y + 3 : cells_y + 6].set(
        jnp.where(index_y == count_y - 1, jnp.swapaxes(halos[3], 3, 4), north_region)
    )
    return advance(padded, wave_speed, coriolis, cells_x, cells_y)


def on_device(state, coriolis, wave_speed, edges):
    count_x = lax.axis_size("tx")
    count_y = lax.axis_size("ty")
    index_x = lax.axis_index("tx")
    index_y = lax.axis_index("ty")
    for substep_index in range(SUBSTEPS):
        state = one_substep(state, coriolis, wave_speed, edges, count_x, count_y, index_x, index_y)
    return state


def solution(mesh):
    in_specs = (P("member", None, None, "tx", "ty"), P(None, "tx", "ty"), P(), P())
    out_specs = P("member", None, None, "tx", "ty")
    return jax.shard_map(
        on_device, mesh=mesh, in_specs=in_specs, out_specs=out_specs, check_vma=False
    )
```

profile of v0, /device:TPU:0, one launch (start us, length us, event | category | flops | bytes accessed | tf_op | source)
XLA Modules:
  0.0 791.6 jit_solution(7254401410040592155)
XLA Ops:
  3.0 6.1 collective-permute-start
  168.9 33.1 %all_gather.40 = f32[6,3,4,3,48]{0,2,3,1,4:T(4,128)S(1)} all-gather(f32[6,3,4,3,6]{0,2,3,1,4:T(4,128)S(1)} %reverse_bitcast_fusion.1), channel_id=1, replica_groups=mesh['member'=2,'tx'=8,'ty'=2] {'tx'}, dimensions={4}, use_global_device_ids=true | all-gather | bytes 46656 | tf_op jit(solution)/shard_map/all_gather | solution.py:112
  202.4 2.0 all_gather.41
  204.4 32.4 %all_gather.38 = f32[6,3,4,3,48]{0,2,3,1,4:T(4,128)S(1)} all-gather(f32[6,3,4,3,6]{0,2,3,1,4:T(4,128)S(1)} %bitcast.455), channel_id=1, replica_groups=mesh['member'=2,'tx'=8,'ty'=2] {'tx'}, dimensions={4}, use_global_device_ids=true | all-gather | bytes 46656 | tf_op jit(solution)/shard_map/all_gather | solution.py:111
  241.5 82.7 %all-reduce.1 = (f32[6,3,4,3,24]{3,2,4,0,1:T(4,128)}, f32[6,3,4,3,24]{3,2,4,0,1:T(4,128)S(1)}) all-reduce(f32[6,3,4,3,24]{3,2,4,0,1:T(4,128)S(1)} %broadcast_select_fusion.1, f32[6,3,4,3,24]{3,2,4,0,1:T(4,128)S(1)} %copy.373), channel_id=1, replica_groups=mesh['member'=2,'tx'=8,'ty'=2] {'tx'}, use_global_device_ids=true, to_apply=%region_2.3 | all-reduce | flops 10368 | bytes 82944 | tf_op jit(solution)/shard_map/psum | solution.py:24
  324.2 3.0 copy.375
  327.2 2.4 all_gather.37
  331.9 2.4 all_gather.36
  358.1 2.1 collective-permute-start.2
  365.9 2.3 copy.383
  370.3 2.5 dynamic-slice_select_fusion.1
  372.8 14.5 %scatter.26 = f32[6,3,4,12,30]{3,2,4,0,1:T(4,128)S(1)} dynamic-update-slice(f32[6,3,4,12,30]{3,2,4,0,1:T(4,128)S(1)} %copy.385, f32[6,3,4,3,24]{3,2,4,0,1:T(4,128)S(1)} %dynamic-slice_select_fusion.1, s32[]{:T(128)} %constant.473.clone.1, s32[]{:T(128)} %constant.473.clone.1, s32[]{:T(128)} %constant.473.clone.1, s32[]{:T(128)} %bitcast.42, s32[]{:T(128)} %bitcast.43) | dynamic-update-slice | bytes 41476 | tf_op jit(solution)/shard_map/scatter | solution.py:139
  389.1 71.2 %scatter.29 = f32[6,3,4,12,30]{3,2,4,1,0:T(4,128)S(1)} dynamic-update-slice(f32[6,3,4,12,30]{3,2,4,1,0:T(4,128)S(1)} %copy.387, f32[6,3,4,3,24]{3,2,4,1,0:T(4,128)S(1)} %copy.388, s32[]{:T(128)} %constant.473.clone.1, s32[]{:T(128)} %constant.473.clone.1, s32[]{:T(128)} %constant.473.clone.1, s32[]{:T(128)} %constant.492.clone.1, s32[]{:T(128)} %constant.475.clone.1) | dynamic-update-slice | bytes 41476 | tf_op jit(solution)/shard_map/scatter | solution.py:143
  460.5 8.1 %scatter.30 = f32[6,3,4,12,30]{3,2,4,1,0:T(4,128)S(1)} dynamic-update-slice(f32[6,3,4,12,30]{3,2,4,1,0:T(4,128)S(1)} %scatter.29, f32[6,3,4,6,3]{3,2,4,1,0:T(4,128)S(1)} %slice_select_fusion.5, s32[]{:T(128)} %constant.473.clone.1, s32[]{:T(128)} %constant.473.clone.1, s32[]{:T(128)} %constant.473.clone.1, s32[]{:T(128)} %constant.475.clone.1, s32[]{:T(128)} %constant.473.clone.1) | dynamic-update-slice | bytes 10372 | tf_op jit(solution)/shard_map/scatter | solution.py:147
  468.7 8.1 %scatter.31 = f32[6,3,4,12,30]{3,2,4,1,0:T(4,128)S(1)} dynamic-update-slice(f32[6,3,4,12,30]{3,2,4,1,0:T(4,128)S(1)} %scatter.30, f32[6,3,4,6,3]{3,2,4,1,0:T(4,128)S(1)} %slice_select_fusion.4, s32[]{:T(128)} %constant.473.clone.1, s32[]{:T(128)} %constant.473.clone.1, s32[]{:T(128)} %constant.473.clone.1, s32[]{:T(128)} %constant.475.clone.1, s32[]{:T(128)} %constant.494.clone.1) | dynamic-update-slice | bytes 10372 | tf_op jit(solution)/shard_map/scatter | solution.py:151
  481.8 2.4 rev.201
  488.0 32.8 %all_gather.46 = f32[6,3,4,3,48]{0,2,3,1,4:T(4,128)S(1)} all-gather(f32[6,3,4,3,6]{0,2,3,1,4:T(4,128)} %copy.401), channel_id=1, replica_groups=mesh['member'=2,'tx'=8,'ty'=2] {'tx'}, dimensions={4}, use_global_device_ids=true | all-gather | bytes 46656 | tf_op jit(solution)/shard_map/all_gather | solution.py:112
  521.7 2.2 all_gather.47
  524.5 34.7 %all_gather.44 = f32[6,3,4,3,48]{0,2,3,1,4:T(4,128)} all-gather(f32[6,3,4,3,6]{0,2,3,1,4:T(4,128)} %copy.399), channel_id=1, replica_groups=mesh['member'=2,'tx'=8,'ty'=2] {'tx'}, dimensions={4}, use_global_device_ids=true | all-gather | bytes 46656 | tf_op jit(solution)/shard_map/all_gather | solution.py:111
  559.2 2.1 copy.400
  561.4 2.2 all_gather.45
  565.3 85.3 %all-reduce = (f32[6,3,4,3,24]{3,2,4,0,1:T(4,128)S(1)}, f32[6,3,4,3,24]{3,2,4,0,1:T(4,128)}) all-reduce(f32[6,3,4,3,24]{3,2,4,0,1:T(4,128)} %broadcast_select_fusion.2, f32[6,3,4,3,24]{3,2,4,0,1:T(4,128)S(1)} %get-tuple-element.113), channel_id=1, replica_groups=mesh['member'=2,'tx'=8,'ty'=2] {'tx'}, use_global_device_ids=true, to_apply=%region_4.5 | all-reduce | flops 10368 | bytes 82944 | tf_op jit(solution)/shard_map/psum | solution.py:24
  652.5 2.4 all_gather.43
  655.3 3.0 copy.397
  658.4 2.6 all_gather.42
  676.5 2.4 rev.209
  680.3 2.1 pad_maximum_fusion
  682.4 2.5 dynamic-slice_select_fusion
  684.9 14.5 %scatter.34 = f32[6,3,4,12,30]{3,2,4,0,1:T(4,128)S(1)} dynamic-update-slice(f32[6,3,4,12,30]{3,2,4,0,1:T(4,128)S(1)} %pad_maximum_fusion, f32[6,3,4,3,24]{3,2,4,0,1:T(4,128)S(1)} %dynamic-slice_select_fusion, s32[]{:T(128)} %constant.473.clone.1, s32[]{:T(128)} %constant.473.clone.1, s32[]{:T(128)} %constant.473.clone.1, s32[]{:T(128)} %bitcast.42, s32[]{:T(128)} %bitcast.43) | dynamic-update-slice | bytes 41476 | tf_op jit(solution)/shard_map/scatter | solution.py:139
  700.0 71.3 %scatter.35 = f32[6,3,4,12,30]{3,2,4,0,1:T(4,128)S(1)} dynamic-update-slice(f32[6,3,4,12,30]{3,2,4,0,1:T(4,128)S(1)} %scatter.34, f32[6,3,4,3,24]{3,2,4,0,1:T(4,128)S(1)} %slice_select_fusion, s32[]{:T(128)} %constant.473.clone.1, s32[]{:T(128)} %constant.473.clone.1, s32[]{:T(128)} %constant.473.clone.1, s32[]{:T(128)} %constant.492.clone.1, s32[]{:T(128)} %constant.475.clone.1) | dynamic-update-slice | bytes 41476 | tf_op jit(solution)/shard_map/scatter | solution.py:143
  771.4 8.1 %scatter.36 = f32[6,3,4,12,30]{3,2,4,0,1:T(4,128)S(1)} dynamic-update-slice(f32[6,3,4,12,30]{3,2,4,0,1:T(4,128)S(1)} %scatter.35, f32[6,3,4,6,3]{3,2,4,0,1:T(4,128)S(1)} %slice_select_fusion.3, s32[]{:T(128)} %constant.473.clone.1, s32[]{:T(128)} %constant.473.clone.1, s32[]{:T(128)} %constant.473.clone.1, s32[]{:T(128)} %constant.475.clone.1, s32[]{:T(128)} %constant.473.clone.1) | dynamic-update-slice | bytes 10372 | tf_op jit(solution)/shard_map/scatter | solution.py:147
  779.7 8.1 %scatter.39 = f32[6,3,4,12,30]{3,2,4,0,1:T(4,128)S(1)} dynamic-update-slice(f32[6,3,4,12,30]{3,2,4,0,1:T(4,128)S(1)} %scatter.36, f32[6,3,4,6,3]{3,2,4,0,1:T(4,128)S(1)} %slice_select_fusion.2, s32[]{:T(128)} %constant.473.clone.1, s32[]{:T(128)} %constant.473.clone.1, s32[]{:T(128)} %constant.473.clone.1, s32[]{:T(128)} %constant.475.clone.1, s32[]{:T(128)} %constant.494.clone.1) | dynamic-update-slice | bytes 10372 | tf_op jit(solution)/shard_map/scatter | solution.py:151
  (319 shorter events, 70.4 us)
Async XLA Ops:
  0.0 150.5 %copy-start.2 = (f32[6,3,4,6,24]{4,2,3,1,0:T(4,128)S(1)}, f32[6,3,4,6,24]{4,2,3,1,0:T(4,128)}, u32[]{:S(2)}) copy-start(f32[6,3,4,6,24]{4,2,3,1,0:T(4,128)} %param.20) | copy-start | bytes 124420
  0.0 76.8 %copy-start.9 = (s32[6,4,3]{0,1,2:T(4,128)S(1)}, s32[6,4,3]{0,1,2:T(4,128)}, u32[]{:S(2)}) copy-start(s32[6,4,3]{0,1,2:T(4,128)} %param.23) | copy-start | bytes 868
  1.7 354.4 %collective-permute-start.1 = (f32[6,3,4,3,24]{4,2,3,1,0:T(4,128)}, f32[6,3,4,3,24]{4,2,3,1,0:T(4,128)}, u32[]{:S(2)}, u32[]{:S(2)}) collective-permute-start(f32[6,3,4,3,24]{4,2,3,1,0:T(4,128)} %get-tuple-element.176), channel_id=1, source_target_pairs={{2,0},{4,2},{6,4},{8,6},{10,8},{12,10},{14,12},{3,1},{5,3},{7,5},{... | collective-permute-start | bytes 62216 | tf_op jit(solution)/shard_map/ppermute | solution.py:17
  3.0 352.1 %collective-permute-start = (f32[6,3,4,3,24]{4,2,3,1,0:T(4,128)}, f32[6,3,4,3,24]{4,2,3,1,0:T(4,128)}, u32[]{:S(2)}, u32[]{:S(2)}) collective-permute-start(f32[6,3,4,3,24]{4,2,3,1,0:T(4,128)} %get-tuple-element.175), channel_id=1, source_target_pairs={{0,2},{2,4},{4,6},{6,8},{8,10},{10,12},{12,14},{1,3},{3,5},{5,7},{... | collective-permute-start | bytes 62216 | tf_op jit(solution)/shard_map/ppermute | solution.py:14
  111.1 41.1 %copy-start.19 = (f32[4]{0:T(128)S(1)}, f32[4]{0:T(128)}, u32[]{:S(2)}) copy-start(f32[4]{0:T(128)} %param.22) | copy-start | bytes 52
  353.4 1.0 copy-start.18
  353.7 4.3 copy-start.10
  356.1 6.2 copy-start.17
  358.1 10.1 %collective-permute-start.2 = (f32[6,3,4,12,3]{4,2,3,1,0:T(4,128)}, f32[6,3,4,12,3]{4,2,3,1,0:T(4,128)S(1)}, u32[]{:S(2)}, u32[]{:S(2)}) collective-permute-start(f32[6,3,4,12,3]{4,2,3,1,0:T(4,128)} %get-tuple-element.172), channel_id=1, source_target_pairs={{0,1},{2,3},{4,5},{6,7},{8,9},{10,11},{12,13},{14,15},{16,17},{18,... | collective-permute-start | bytes 31112 | tf_op jit(solution)/shard_map/ppermute | solution.py:14
  360.1 8.0 %collective-permute-start.3 = (f32[6,3,4,12,3]{4,2,3,1,0:T(4,128)S(1)}, f32[6,3,4,12,3]{4,2,3,1,0:T(4,128)}, u32[]{:S(2)}, u32[]{:S(2)}) collective-permute-start(f32[6,3,4,12,3]{4,2,3,1,0:T(4,128)S(1)} %get-tuple-element.173), channel_id=1, source_target_pairs={{1,0},{3,2},{5,4},{7,6},{9,8},{11,10},{13,12},{15,14},{17,16},{19,... | collective-permute-start | bytes 31112 | tf_op jit(solution)/shard_map/ppermute | solution.py:17
  362.3 115.5 %copy-start.5 = (f32[6,6,24]{1,2,0:T(8,128)}, f32[6,6,24]{1,2,0:T(8,128)S(1)}, u32[]{:S(2)}) copy-start(f32[6,6,24]{1,2,0:T(8,128)S(1)} %copy.392) | copy-start | bytes 10372
  387.3 1.2 copy-start.3
  389.1 71.3 %copy-start.11 = (f32[6,3,4,3,6]{4,2,3,1,0:T(4,128)S(1)}, f32[6,3,4,3,6]{4,2,3,1,0:T(4,128)}, u32[]{:S(2)}) copy-start(f32[6,3,4,3,6]{4,2,3,1,0:T(4,128)} %copy-done.10) | copy-start | bytes 15556
  478.7 192.8 %copy-start = (f32[6,1,4,6,24]{3,2,4,0,1:T(4,128)}, f32[6,1,4,6,24]{3,2,4,0,1:T(4,128)S(1)}, u32[]{:S(2)}) copy-start(f32[6,1,4,6,24]{3,2,4,0,1:T(4,128)S(1)} %get-tuple-element.123) | copy-start | bytes 41476
  524.5 39.7 %copy-start.4 = (f32[6,3,4,3,24]{3,2,4,0,1:T(4,128)S(1)}, f32[6,3,4,3,24]{3,2,4,0,1:T(4,128)}, u32[]{:S(2)}) copy-start(f32[6,3,4,3,24]{3,2,4,0,1:T(4,128)} %rev.201) | copy-start | bytes 62212
  658.4 2.9 copy-start.7
  658.4 3.0 copy-start.8
  661.5 1.2 copy-start.16
  662.7 6.9 collective-permute-start.4
  664.0 7.0 collective-permute-start.5
  668.8 0.6 copy-start.14
  668.9 0.6 copy-start.12
  672.5 7.8 collective-permute-start.6
  674.4 5.9 collective-permute-start.7
  680.3 2.1 copy-start.1
  700.0 71.3 %copy-start.15 = (f32[6,3,4,3,6]{4,2,3,0,1:T(4,128)S(1)}, f32[6,3,4,3,6]{4,2,3,0,1:T(4,128)}, u32[]{:S(2)}) copy-start(f32[6,3,4,3,6]{4,2,3,0,1:T(4,128)} %copy-done.14) | copy-start | bytes 15556
  700.0 79.6 %copy-start.13 = (f32[6,3,4,3,6]{4,2,3,0,1:T(4,128)S(1)}, f32[6,3,4,3,6]{4,2,3,0,1:T(4,128)}, u32[]{:S(2)}) copy-start(f32[6,3,4,3,6]{4,2,3,0,1:T(4,128)} %copy-done.12) | copy-start | bytes 15556
  787.9 1.0 copy-start.6
where the time goes:
time: 805 us; the launch traced here: 792 us
  blocking collectives  319 us (40%)
  local copies, waits for them, and re-layouts  262 us (33%)
  between operations  169 us (21%)
  other arithmetic  23.1 us (3%)
  starting transfers between devices  17 us (2%)
    psum x2, blocking collectives, spread(): return lax.psum(block, axis)  168 us
    scatter x2, local copies, waits for them, and re-layouts, one_substep(): padded.at[:, :, :, cells_x + 3:cells_x + 6, 3:cells_y + 3]  143 us
    all_gather x2, blocking collectives, one_substep(): lax.all_gather(south_rim, 'tx', axis=4, tiled=True)  67.1 us
    all_gather x2, blocking collectives, one_substep(): lax.all_gather(north_rim, 'tx', axis=4, tiled=True)  65.9 us
    scatter x3, local copies, waits for them, and re-layouts, one_substep(): padded.at[:, :, :, 0:3, 3:cells_y + 3]  29 us
    scatter x2, local copies, waits for them, and re-layouts, one_substep(): padded.at[:, :, :, 3:cells_x + 3, 0:3]  16.2 us
    scatter x2, local copies, waits for them, and re-layouts, one_substep(): padded.at[:, :, :, 3:cells_x + 3, cells_y + 3:cells_y + 6]  16.2 us
  transfers between devices with their start and end apart: 8, of which 1 were waited for; matrix products, arithmetic and copies ran while one was open for 5% of the time, Pallas kernels for 0%

commit v1 on v0

--- a/solution.py
+++ b/solution.py
@@ -1,9 +1,306 @@
+import functools
+
 import jax
 import jax.numpy as jnp
 from jax import lax
+from jax.experimental import pallas as pl
+from jax.experimental.pallas import tpu as pltpu
 from jax.sharding import PartitionSpec as P
 
 SUBSTEPS = 2
+LANES = 128
+WINDOW = 64
+MARGIN = 8
+VMEM_LIMIT = 32 * 1024 * 1024
+
+
+def pack_kernel(cx, cy, state_ref, coriolis_ref, out_ref):
+    faces, fields = state_ref.shape[:2]
+    levels = state_ref.shape[3]
+    pairs = faces // 2
+    group = pairs * levels
+    half = cx // 2
+    base = fields * half * group
+    out_ref[0] = jnp.zeros(out_ref.shape[1:], jnp.float32)
+    for face in range(faces):
+        for parity in range(2):
+            lane = (face % 2) * WINDOW + MARGIN + parity * cy
+            for xp in range(half):
+                for field in range(fields):
+                    row = field * half * group + xp * group + (face // 2) * levels
+                    out_ref[0, row : row + levels, lane : lane + cy] = state_ref[
+                        face, field, 2 * xp + parity
+                    ]
+                row = base + xp * pairs + face // 2
+                out_ref[0, row : row + 1, lane : lane + cy] = coriolis_ref[
+                    face, 2 * xp + parity : 2 * xp + parity + 1
+                ]
+    for copy in range(1, out_ref.shape[0]):
+        out_ref[copy] = out_ref[0]
+
+
+def step_kernel(
+    cx, cy, count_x, parts_ref, speed_ref, edges_ref, out_ref,
+    z_ref, cor_ref, pred_ref, store_ref, tile_ref, flip_ref,
+):
+    fields = z_ref.shape[0]
+    levels = 4
+    cells = cx * count_x
+    faces = store_ref.shape[0] // 4
+    pairs = faces // 2
+    group = pairs * levels
+    half = cx // 2
+    index_x = lax.axis_index("tx")
+    index_y = lax.axis_index("ty")
+
+    def row_of(x):
+        return (x + 4) * group
+
+    def lanes_of(rows):
+        return lax.broadcasted_iota(jnp.int32, (rows, LANES), 1)
+
+    def unpack(source, carry):
+        low = lanes_of(group) % WINDOW < MARGIN + cy
+        for field in range(fields):
+            for xp in range(half):
+                row = field * half * group + xp * group
+                south = parts_ref[0, source, row : row + group]
+                north = parts_ref[1, source, row : row + group]
+                even = jnp.where(low, south, pltpu.roll(north, cy, 1))
+                odd = jnp.where(low, pltpu.roll(south, LANES - cy, 1), north)
+                at = source * (cx * group) + row_of(2 * xp)
+                z_ref[field, pl.ds(at, group)] = even
+                z_ref[field, pl.ds(at + group, group)] = odd
+        base = fields * half * group
+        rows = half * pairs
+        low = lanes_of(rows) % WINDOW < MARGIN + cy
+        south = parts_ref[0, source, base : base + rows]
+        north = parts_ref[1, source, base : base + rows]
+        even = jnp.where(low, south, pltpu.roll(north, cy, 1))
+        odd = jnp.where(low, pltpu.roll(south, LANES - cy, 1), north)
+        for parity, values in enumerate((even, odd)):
+            for xp in range(half):
+                for pair in range(pairs):
+                    at = source * (cx * group) + (2 * xp + parity) * group + pair * levels
+                    line = values[xp * pairs + pair : xp * pairs + pair + 1]
+                    cor_ref[pl.ds(at, levels)] = jnp.broadcast_to(line, (levels, LANES))
+        return carry
+
+    lax.fori_loop(0, count_x, unpack, 0)
+
+    def speed_rows(rows):
+        level = lax.broadcasted_iota(jnp.int32, (rows, LANES), 0) % levels
+        values = jnp.full((rows, LANES), speed_ref[0], jnp.float32)
+        for index in range(1, levels):
+            values = jnp.where(level == index, speed_ref[index], values)
+        return values
+
+    def collect():
+        lane = lanes_of(cells)
+        place = lane % WINDOW
+
+        def body(pair, carry):
+            for slot, field in ((0, 0), (1, 2)):
+                merged = jnp.zeros((cells, LANES), jnp.float32)
+                for level in range(levels):
+                    lines = z_ref[field, pl.ds(row_of(0) + pair * levels + level, cells, group)]
+                    shift = (3 * level - (MARGIN + cells - 3)) % LANES
+                    gap = WINDOW - cells + 3
+                    here = place - 3 * level
+                    wanted = ((here >= 0) & (here < 3)) | ((here >= gap) & (here < gap + 3))
+                    merged = jnp.where(wanted, pltpu.roll(lines, shift, 1), merged)
+                merged = jnp.concatenate(
+                    [merged, jnp.zeros((LANES - cells, LANES), jnp.float32)], axis=0
+                )
+                flip_ref[...] = merged.T
+                for side in (2, 3):
+                    for odd in range(2):
+                        for depth in range(3):
+                            if side == 3:
+                                base = odd * WINDOW + 2 - depth
+                            else:
+                                base = ((odd + 1) % 2) * WINDOW + gap + depth
+                            at = slot * 3 * levels + depth * levels
+                            store_ref[(2 * pair + odd) * 4 + side, at : at + levels] = flip_ref[
+                                pl.ds(base, levels, 3)
+                            ]
+            for slot, field in ((0, 0), (1, 1)):
+                for side in (0, 1):
+                    for depth in range(3):
+                        x = depth if side == 0 else cells - 1 - depth
+                        lines = z_ref[field, pl.ds(row_of(x) + pair * levels, levels)]
+                        at = slot * 3 * levels + depth * levels
+                        for odd in range(2):
+                            store_ref[(2 * pair + odd) * 4 + side, at : at + levels] = pltpu.roll(
+                                lines, LANES - MARGIN - odd * WINDOW, 1
+                            )
+            return carry
+
+        lax.fori_loop(0, pairs, body, 0)
+
+    def fetch(face, side):
+        at = (face * 4 + side) * 3
+        neighbour = edges_ref[at]
+        far_side = edges_ref[at + 1]
+        flipped = edges_ref[at + 2]
+        block = store_ref[neighbour * 4 + far_side]
+        lane = lanes_of(block.shape[0])
+        order = jnp.where((flipped == 1) & (lane < cells), cells - 1 - lane, lane)
+        block = jnp.take_along_axis(block, order, axis=1)
+        sign_here = 2 * (side % 2) - 1
+        sign_there = 2 * (far_side % 2) - 1
+        sign = (-sign_here * sign_there).astype(jnp.float32)
+        normal = lax.broadcasted_iota(jnp.int32, block.shape, 0) >= 3 * levels
+        return jnp.where(normal, sign * block, block)
+
+    def rim_rows(side):
+        def body(pair, carry):
+            first = pltpu.roll(fetch(2 * pair, side), MARGIN, 1)
+            second = pltpu.roll(fetch(2 * pair + 1, side), MARGIN + WINDOW, 1)
+            both = jnp.where(lanes_of(first.shape[0]) < WINDOW, first, second)
+            for slot, field in ((0, 0), (1, 1)):
+                for depth in range(3):
+                    x = -1 - depth if side == 0 else cells + depth
+                    at = slot * 3 * levels + depth * levels
+                    z_ref[field, pl.ds(row_of(x) + pair * levels, levels)] = both[at : at + levels]
+            return carry
+
+        lax.fori_loop(0, pairs, body, 0)
+
+    def rim_columns(start, count):
+        def body(pair, carry):
+            for odd in range(2):
+                for side in (2, 3):
+                    block = fetch(2 * pair + odd, side)
+                    for slot in range(2):
+                        for depth in range(3):
+                            at = slot * 3 * levels + depth * levels
+                            if side == 3:
+                                base = odd * WINDOW + depth
+                            else:
+                                base = ((odd + 1) % 2) * WINDOW + 15 - depth
+                            tile_ref[slot, pl.ds(base, levels, 16)] = block[at : at + levels]
+            place = lanes_of(count) % WINDOW
+            rim = ((place >= MARGIN - 3) & (place < MARGIN)) | (
+                (place >= MARGIN + cells) & (place < MARGIN + cells + 3)
+            )
+            for slot, field in ((0, 0), (1, 2)):
+                flip_ref[...] = tile_ref[slot].T
+                lines = flip_ref[pl.ds(start, count)]
+                for level in range(levels):
+                    rolled = pltpu.roll(lines, (MARGIN + cells - 16 * level) % LANES, 1)
+                    at = pl.ds(row_of(start) + pair * levels + level, count, group)
+                    z_ref[field, at] = jnp.where(rim, rolled, z_ref[field, at])
+            return carry
+
+        lax.fori_loop(0, pairs, body, 0)
+
+    def predict(at, rows):
+        speed = speed_rows(rows)
+        ahead = z_ref[0, pl.ds(at + group, rows)]
+        behind = z_ref[0, pl.ds(at - group, rows)]
+        pred_ref[pl.ds(at, rows)] = z_ref[1, pl.ds(at, rows)] - speed * (0.5 * (ahead - behind))
+
+    def update(at, rows):
+        speed = speed_rows(rows)
+        height = z_ref[0, pl.ds(at, rows)]
+        north_pred = z_ref[2, pl.ds(at, rows)] - speed * (
+            0.5 * (pltpu.roll(height, LANES - 1, 1) - pltpu.roll(height, 1, 1))
+        )
+        east_pred = pred_ref[pl.ds(at, rows)]
+        flux_east = 8.0 * (
+            pred_ref[pl.ds(at + group, rows)] - pred_ref[pl.ds(at - group, rows)]
+        ) - (pred_ref[pl.ds(at + 2 * group, rows)] - pred_ref[pl.ds(at - 2 * group, rows)])
+        flux_north = 8.0 * (
+            pltpu.roll(north_pred, LANES - 1, 1) - pltpu.roll(north_pred, 1, 1)
+        ) - (pltpu.roll(north_pred, LANES - 2, 1) - pltpu.roll(north_pred, 2, 1))
+        height = height - speed * ((flux_east + flux_north) * (1.0 / 12.0))
+        turning = cor_ref[pl.ds(at - row_of(0), rows)]
+        return height, east_pred + turning * north_pred, north_pred - turning * east_pred
+
+    collect()
+    rim_rows(0)
+    rim_rows(1)
+    rim_columns(0, cells)
+    chunk = cx * group
+
+    def predict_all(index, carry):
+        predict(row_of(-2) + index * (4 * group), 4 * group)
+        return carry
+
+    lax.fori_loop(0, (cells + 4) // 4, predict_all, 0)
+
+    def update_all(index, carry):
+        at = row_of(0) + index * chunk
+        for field, values in enumerate(update(at, chunk)):
+            z_ref[field, pl.ds(at, chunk)] = values
+        return carry
+
+    lax.fori_loop(0, count_x, update_all, 0)
+
+    collect()
+
+    @pl.when(index_x == 0)
+    def _():
+        rim_rows(0)
+
+    @pl.when(index_x == count_x - 1)
+    def _():
+        rim_rows(1)
+
+    rim_columns(index_x * cx, cx)
+    at = row_of(0) + index_x * chunk
+    predict(at - 2 * group, chunk + 4 * group)
+    for field, values in enumerate(update(at, chunk)):
+        for odd in range(2):
+            shift = LANES - (MARGIN + odd * WINDOW) - index_y * cy
+            rolled = pltpu.roll(values, shift, 1)
+            for x in range(cx):
+                for pair in range(pairs):
+                    row = x * group + pair * levels
+                    out_ref[2 * pair + odd, field, x] = rolled[row : row + levels, :cy]
+
+
+def fast_on_device(state, coriolis, wave_speed, edges):
+    count_x = lax.axis_size("tx")
+    faces, fields, levels, cx, cy = state.shape
+    pairs = faces // 2
+    group = pairs * levels
+    rows = fields * (cx // 2) * group + (cx // 2) * pairs
+    rows = -(-rows // 8) * 8
+    cells = cx * count_x
+    packed = pl.pallas_call(
+        functools.partial(pack_kernel, cx, cy),
+        out_shape=jax.ShapeDtypeStruct((count_x, rows, LANES), jnp.float32),
+        in_specs=[pl.BlockSpec(memory_space=pltpu.VMEM)] * 2,
+        out_specs=pl.BlockSpec(memory_space=pltpu.VMEM),
+        compiler_params=pltpu.CompilerParams(vmem_limit_bytes=VMEM_LIMIT),
+        name="pack",
+    )(jnp.swapaxes(state, 2, 3), coriolis)
+    column = lax.all_to_all(packed, "tx", 0, 0)
+    parts = lax.all_gather(column, "ty")
+    z_rows = (cells + 8) * group
+    out = pl.pallas_call(
+        functools.partial(step_kernel, cx, cy, count_x),
+        out_shape=jax.ShapeDtypeStruct((faces, fields, cx, levels, cy), jnp.float32),
+        in_specs=[
+            pl.BlockSpec(memory_space=pltpu.VMEM),
+            pl.BlockSpec(memory_space=pltpu.SMEM),
+            pl.BlockSpec(memory_space=pltpu.SMEM),
+        ],
+        out_specs=pl.BlockSpec(memory_space=pltpu.VMEM),
+        scratch_shapes=[
+            pltpu.VMEM((fields, z_rows, LANES), jnp.float32),
+            pltpu.VMEM((cells * group, LANES), jnp.float32),
+            pltpu.VMEM((z_rows, LANES), jnp.float32),
+            pltpu.VMEM((faces * 4, 6 * levels, LANES), jnp.float32),
+            pltpu.VMEM((2, LANES, LANES), jnp.float32),
+            pltpu.VMEM((LANES, LANES), jnp.float32),
+        ],
+        compiler_params=pltpu.CompilerParams(vmem_limit_bytes=VMEM_LIMIT),
+        name="substeps",
+    )(parts, wave_speed, edges.reshape(-1))
+    return jnp.swapaxes(out, 2, 3)
 
 
 def padded_2(block, sides, width):
@@ -164,9 +461,28 @@
     return state
 
 
+def fits(state):
+    count_x = lax.axis_size("tx")
+    faces, fields, levels, cells_x, cells_y = state.shape
+    return (
+        lax.axis_size("ty") == 2
+        and faces % 2 == 0
+        and levels == 4
+        and cells_x == 6
+        and cells_x * count_x == 2 * cells_y
+        and 2 * cells_y + 2 * MARGIN <= WINDOW
+    )
+
+
+def either(state, coriolis, wave_speed, edges):
+    if fits(state):
+        return fast_on_device(state, coriolis, wave_speed, edges)
+    return on_device(state, coriolis, wave_speed, edges)
+
+
 def solution(mesh):
     in_specs = (P("member", None, None, "tx", "ty"), P(None, "tx", "ty"), P(), P())
     out_specs = P("member", None, None, "tx", "ty")
     return jax.shard_map(
-        on_device, mesh=mesh, in_specs=in_specs, out_specs=out_specs, check_vma=False
-    )
+        either, mesh=mesh, in_specs=in_specs, out_specs=out_specs, check_vma=False
+    )

time: 805 us -> 36.6 us (0.05); the launches traced: 792 us -> 36.2 us
  blocking collectives: 319 us -> 2.5 us
  local copies, waits for them, and re-layouts: 262 us -> 2.54 us
  between operations: 169 us -> 0.01 us
  other arithmetic: 23.1 us -> 0 us
  waiting for transfers between devices: 0.93 us -> 13.6 us
  Pallas kernels: 0 us -> 10.2 us
  starting transfers between devices: 17 us -> 7.41 us
    scatter x9 -> x0, local copies, waits for them, and re-layouts: 204 us -> none  [the longest x2 143 us: one_substep(): padded.at[:, :, :, cells_x + 3:cells_x + 6, 3:cells_y + 3]]
    psum x2 -> x0, blocking collectives: 168 us -> none  [spread(): return lax.psum(block, axis)]
    all_gather x12 -> x1, blocking collectives: 151 us -> 2.5 us  [fast_on_device(): parts = lax.all_gather(column, 'ty')]
    ppermute x8 -> x0, starting transfers between devices: 17 us -> none  [the longest x4 11.4 us: padded_2(): lax.ppermute(lax.slice_in_dim(block, block.shape[dim] - width, None, axis...]
    all_to_all x0 -> x1, waiting for transfers between devices: none -> 13.6 us  [fast_on_device(): column = lax.all_to_all(packed, 'tx', 0, 0)]
    rev x52 -> x0, local copies, waits for them, and re-layouts: 12.9 us -> none  [the longest x48 4.93 us: window_strip(): return jnp.where(flipped == 1, jnp.flip(piece, 3), piece)]
    pallas_call x0 -> x2, Pallas kernels: none -> 10.2 us  [the longest x1 9.2 us: fast_on_device(): pl.pallas_call(functools.partial(step_kernel, cx, cy, count_x), out_shape...]
    psum x4 -> x0, local copies, waits for them, and re-layouts: 9.8 us -> none  [spread(): return lax.psum(block, axis)]
  transfers between devices with their start and end apart: 8 -> 1, of which waited for: 1 -> 1; matrix products, arithmetic and copies ran while one was open for 5% -> 1% of each run, Pallas kernels for 0% -> 0%
where the time goes in v1:
time: 36.6 us; the launch traced here: 36.2 us
  waiting for transfers between devices  13.6 us (37%)
  Pallas kernels  10.2 us (28%)
  starting transfers between devices  7.41 us (20%)
  local copies, waits for them, and re-layouts  2.54 us (7%)
  blocking collectives  2.5 us (7%)
    all_to_all x1, waiting for transfers between devices, fast_on_device(): column = lax.all_to_all(packed, 'tx', 0, 0)  13.6 us
    pallas_call x1, Pallas kernels, fast_on_device(): pl.pallas_call(functools.partial(step_kernel, cx, cy, count_x), out_shape...  9.2 us
    all_to_all x1, starting transfers between devices, fast_on_device(): column = lax.all_to_all(packed, 'tx', 0, 0)  7.41 us
    all_gather x1, blocking collectives, fast_on_device(): parts = lax.all_gather(column, 'ty')  2.5 us
    unnamed x9, local copies, waits for them, and re-layouts  2.44 us
    pallas_call x1, Pallas kernels, fast_on_device(): pl.pallas_call(functools.partial(pack_kernel, cx, cy), out_shape=jax.Shap...  1.02 us
  transfers between devices with their start and end apart: 1, of which 1 were waited for; matrix products, arithmetic and copies ran while one was open for 1% of the time, Pallas kernels for 0%

profile of v1, /device:TPU:0, one launch (start us, length us, event | category | flops | bytes accessed | tf_op | source)
XLA Modules:
  0.0 36.2 jit_solution(15738023136933081363)
XLA Ops:
  0.0 0.0 copy-start
  0.0 0.9 %copy-done = f32[6,3,4,6,24]{4,2,3,1,0:T(4,128)S(1)} copy-done((f32[6,3,4,6,24]{4,2,3,1,0:T(4,128)S(1)}, f32[6,3,4,6,24]{4,2,3,1,0:T(4,128)}, u32[]{:S(2)}) %copy-start) | copy-done | bytes 41496
  0.9 0.0 copy-start.1
  0.9 0.7 %copy-done.1 = f32[6,6,24]{2,1,0:T(8,128)S(1)} copy-done((f32[6,6,24]{2,1,0:T(8,128)S(1)}, f32[6,6,24]{2,1,0:T(8,128)}, u32[]{:S(2)}) %copy-start.1) | copy-done | bytes 3480
  1.7 1.0 %pack.1 = f32[8,120,128]{2,1,0:T(8,128)} custom-call(f32[6,3,6,4,24]{4,3,2,1,0:T(4,128)S(1)} %bitcast.4, f32[6,6,24]{2,1,0:T(8,128)S(1)} %copy-done.1), custom_call_target="tpu_custom_call" | custom-call | tf_op jit(solution)/shard_map/pack/pallas_call | solution.py:272
  2.7 0.0 copy-start.3
  2.7 7.4 %all-to-all-start = ((f32[8,120,128]{2,1,0:T(8,128)}), f32[8,120,128]{2,1,0:T(8,128)S(1)}, u32[]{:S(2)}, u32[]{:S(2)}) async-start(f32[8,120,128]{2,1,0:T(8,128)} %pack.1), calls=%async_computation | async-start | bytes 983040 | tf_op jit(solution)/shard_map/all_to_all | solution.py:280
  10.1 0.0 copy-done.3
  10.1 0.1 copy.7
  10.2 0.1 reshape.3.edges_ref
  10.3 13.6 %all-to-all-done = f32[8,120,128]{2,1,0:T(8,128)S(1)} async-done(((f32[8,120,128]{2,1,0:T(8,128)}), f32[8,120,128]{2,1,0:T(8,128)S(1)}, u32[]{:S(2)}, u32[]{:S(2)}) %all-to-all-start) | async-done | bytes 491552 | tf_op jit(solution)/shard_map/all_to_all | solution.py:280
  23.9 2.5 %all-gather = f32[16,120,128]{2,1,0:T(8,128)S(1)} all-gather(f32[8,120,128]{2,1,0:T(8,128)S(1)} %all-to-all-done), channel_id=2, replica_groups=mesh['member'=2,'tx'=8,'ty'=2] {'ty'}, dimensions={0}, use_global_device_ids=true | all-gather | bytes 1474560 | tf_op jit(solution)/shard_map/all_gather | solution.py:281
  26.4 0.0 copy-start.2
  26.4 0.7 %copy-done.2 = f32[4]{0:T(128)S(1)} copy-done((f32[4]{0:T(128)S(1)}, f32[4]{0:T(128)}, u32[]{:S(2)}) %copy-start.2) | copy-done | bytes 40
  27.1 9.2 %substeps.1 = f32[6,3,6,4,24]{4,3,2,1,0:T(4,128)} custom-call(f32[2,8,120,128]{3,2,1,0:T(8,128)S(1)} %bitcast.3, f32[4]{0:T(128)S(1)} %copy-done.2, s32[72]{0:T(128)S(1)} %reshape.3.edges_ref), custom_call_target="tpu_custom_call" | custom-call | tf_op jit(solution)/shard_map/substeps/pallas_call | solution.py:283
Async XLA Ops:
  0.0 0.9 %copy-start = (f32[6,3,4,6,24]{4,2,3,1,0:T(4,128)S(1)}, f32[6,3,4,6,24]{4,2,3,1,0:T(4,128)}, u32[]{:S(2)}) copy-start(f32[6,3,4,6,24]{4,2,3,1,0:T(4,128)} %param.4) | copy-start | bytes 124420
  0.9 0.7 %copy-start.1 = (f32[6,6,24]{2,1,0:T(8,128)S(1)}, f32[6,6,24]{2,1,0:T(8,128)}, u32[]{:S(2)}) copy-start(f32[6,6,24]{2,1,0:T(8,128)} %coriolis_ref.1) | copy-start | bytes 10372
  2.7 7.4 %copy-start.3 = (s32[6,4,3]{0,1,2:T(4,128)S(1)}, s32[6,4,3]{0,1,2:T(4,128)}, u32[]{:S(2)}) copy-start(s32[6,4,3]{0,1,2:T(4,128)} %param.7) | copy-start | bytes 868
  2.7 21.2 %all-to-all-start = ((f32[8,120,128]{2,1,0:T(8,128)}), f32[8,120,128]{2,1,0:T(8,128)S(1)}, u32[]{:S(2)}, u32[]{:S(2)}) async-start(f32[8,120,128]{2,1,0:T(8,128)} %pack.1), calls=%async_computation | async-start | bytes 983040 | tf_op jit(solution)/shard_map/all_to_all | solution.py:280
  26.4 0.7 %copy-start.2 = (f32[4]{0:T(128)S(1)}, f32[4]{0:T(128)}, u32[]{:S(2)}) copy-start(f32[4]{0:T(128)} %speed_ref.1) | copy-start | bytes 52

commit v2 on v1

--- a/solution.py
+++ b/solution.py
@@ -64,8 +64,8 @@
         for field in range(fields):
             for xp in range(half):
                 row = field * half * group + xp * group
-                south = parts_ref[0, source, row : row + group]
-                north = parts_ref[1, source, row : row + group]
+                south = parts_ref[0, source ^ index_x, row : row + group]
+                north = parts_ref[1, source ^ index_x, row : row + group]
                 even = jnp.where(low, south, pltpu.roll(north, cy, 1))
                 odd = jnp.where(low, pltpu.roll(south, LANES - cy, 1), north)
                 at = source * (cx * group) + row_of(2 * xp)
@@ -74,8 +74,8 @@
         base = fields * half * group
         rows = half * pairs
         low = lanes_of(rows) % WINDOW < MARGIN + cy
-        south = parts_ref[0, source, base : base + rows]
-        north = parts_ref[1, source, base : base + rows]
+        south = parts_ref[0, source ^ index_x, base : base + rows]
+        north = parts_ref[1, source ^ index_x, base : base + rows]
         even = jnp.where(low, south, pltpu.roll(north, cy, 1))
         odd = jnp.where(low, pltpu.roll(south, LANES - cy, 1), north)
         for parity, values in enumerate((even, odd)):
@@ -271,13 +271,17 @@
     cells = cx * count_x
     packed = pl.pallas_call(
         functools.partial(pack_kernel, cx, cy),
-        out_shape=jax.ShapeDtypeStruct((count_x, rows, LANES), jnp.float32),
+        out_shape=jax.ShapeDtypeStruct((1, rows, LANES), jnp.float32),
         in_specs=[pl.BlockSpec(memory_space=pltpu.VMEM)] * 2,
         out_specs=pl.BlockSpec(memory_space=pltpu.VMEM),
         compiler_params=pltpu.CompilerParams(vmem_limit_bytes=VMEM_LIMIT),
         name="pack",
     )(jnp.swapaxes(state, 2, 3), coriolis)
-    column = lax.all_to_all(packed, "tx", 0, 0)
+    chunks = [packed[0]]
+    for other in range(1, count_x):
+        pairs_of = [(index, index ^ other) for index in range(count_x)]
+        chunks.append(lax.ppermute(packed[0], "tx", pairs_of))
+    column = jnp.stack(chunks)
     parts = lax.all_gather(column, "ty")
     z_rows = (cells + 8) * group
     out = pl.pallas_call(

time: 36.6 us -> 34.4 us (0.940)
  waiting for transfers between devices: 13.6 us -> 6.93 us
  starting transfers between devices: 7.41 us -> 12.6 us
  Pallas kernels: 10.2 us -> 9.42 us
    all_to_all x1 -> x0, waiting for transfers between devices: 13.6 us -> none  [fast_on_device(): column = lax.all_to_all(packed, 'tx', 0, 0)]
    ppermute x0 -> x7, starting transfers between devices: none -> 12.6 us  [fast_on_device(): chunks.append(lax.ppermute(packed[0], 'tx', pairs_of))]
    all_to_all x1 -> x0, starting transfers between devices: 7.41 us -> none  [fast_on_device(): column = lax.all_to_all(packed, 'tx', 0, 0)]
    ppermute x0 -> x7, waiting for transfers between devices: none -> 6.93 us  [fast_on_device(): chunks.append(lax.ppermute(packed[0], 'tx', pairs_of))]
    pallas_call x1, Pallas kernels: 1.02 us -> 0.21 us  [fast_on_device(): pl.pallas_call(functools.partial(pack_kernel, cx, cy), out_shape=jax.Shap...]
    unnamed x9 -> x16, local copies, waits for them, and re-layouts: 2.44 us -> 2.49 us
  transfers between devices with their start and end apart: 1 -> 7, of which waited for: 1 -> 2; matrix products, arithmetic and copies ran while one was open for 1% -> 1% of each run, Pallas kernels for 0% -> 0%
where the time goes in v2:
time: 34.4 us; the launch traced here: 34.1 us
  starting transfers between devices  12.6 us (37%)
  Pallas kernels  9.42 us (27%)
  waiting for transfers between devices  6.93 us (20%)
  local copies, waits for them, and re-layouts  2.59 us (8%)
  blocking collectives  2.5 us (7%)
    ppermute x7, starting transfers between devices, fast_on_device(): chunks.append(lax.ppermute(packed[0], 'tx', pairs_of))  12.6 us
    pallas_call x1, Pallas kernels, fast_on_device(): pl.pallas_call(functools.partial(step_kernel, cx, cy, count_x), out_shape...  9.2 us
    ppermute x7, waiting for transfers between devices, fast_on_device(): chunks.append(lax.ppermute(packed[0], 'tx', pairs_of))  6.93 us
    all_gather x1, blocking collectives, fast_on_device(): parts = lax.all_gather(column, 'ty')  2.5 us
    unnamed x16, local copies, waits for them, and re-layouts  2.49 us
  transfers between devices with their start and end apart: 7, of which 2 were waited for; matrix products, arithmetic and copies ran while one was open for 1% of the time, Pallas kernels for 0%

profile of v2, /device:TPU:0, one launch (start us, length us, event | category | flops | bytes accessed | tf_op | source)
XLA Modules:
  0.0 34.1 jit_solution(16972477817915654722)
XLA Ops:
  0.0 0.0 copy-start
  0.0 0.9 %copy-done = f32[6,3,4,6,24]{4,2,3,1,0:T(4,128)S(1)} copy-done((f32[6,3,4,6,24]{4,2,3,1,0:T(4,128)S(1)}, f32[6,3,4,6,24]{4,2,3,1,0:T(4,128)}, u32[]{:S(2)}) %copy-start) | copy-done | bytes 41496
  0.9 0.0 copy-start.1
  0.9 0.7 %copy-done.1 = f32[6,6,24]{2,1,0:T(8,128)S(1)} copy-done((f32[6,6,24]{2,1,0:T(8,128)S(1)}, f32[6,6,24]{2,1,0:T(8,128)}, u32[]{:S(2)}) %copy-start.1) | copy-done | bytes 3480
  1.7 0.0 copy-start.3
  1.7 0.2 pack.1
  1.9 3.0 %collective-permute-start = (f32[120,128]{1,0:T(8,128)S(1)}, f32[120,128]{1,0:T(8,128)S(1)}, u32[]{:S(2)}, u32[]{:S(2)}) collective-permute-start(f32[120,128]{1,0:T(8,128)S(1)} %bitcast.19), channel_id=1, source_target_pairs={{0,2},{2,0},{4,6},{6,4},{8,10},{10,8},{12,14},{14,12},{1,3},{3,1},... | collective-permute-start | bytes 184328 | tf_op jit(solution)/shard_map/ppermute | solution.py:283
  4.9 1.6 %collective-permute-start.1 = (f32[120,128]{1,0:T(8,128)S(1)}, f32[120,128]{1,0:T(8,128)S(1)}, u32[]{:S(2)}, u32[]{:S(2)}) collective-permute-start(f32[120,128]{1,0:T(8,128)S(1)} %bitcast.20), channel_id=1, source_target_pairs={{0,4},{2,6},{4,0},{6,2},{8,12},{10,14},{12,8},{14,10},{1,5},{3,7},... | collective-permute-start | bytes 184328 | tf_op jit(solution)/shard_map/ppermute | solution.py:283
  6.5 0.0 collective-permute-start.2
  6.5 3.0 %collective-permute-start.3 = (f32[120,128]{1,0:T(8,128)S(1)}, f32[120,128]{1,0:T(8,128)S(1)}, u32[]{:S(2)}, u32[]{:S(2)}) collective-permute-start(f32[120,128]{1,0:T(8,128)S(1)} %bitcast.22), channel_id=1, source_target_pairs={{0,8},{2,10},{4,12},{6,14},{8,0},{10,2},{12,4},{14,6},{1,9},{3,11}... | collective-permute-start | bytes 184328 | tf_op jit(solution)/shard_map/ppermute | solution.py:283
  9.5 1.3 %collective-permute-start.4 = (f32[120,128]{1,0:T(8,128)S(1)}, f32[120,128]{1,0:T(8,128)S(1)}, u32[]{:S(2)}, u32[]{:S(2)}) collective-permute-start(f32[120,128]{1,0:T(8,128)S(1)} %bitcast.23), channel_id=1, source_target_pairs={{0,10},{2,8},{4,14},{6,12},{8,2},{10,0},{12,6},{14,4},{1,11},{3,9}... | collective-permute-start | bytes 184328 | tf_op jit(solution)/shard_map/ppermute | solution.py:283
  10.8 0.0 copy-done.3
  10.8 0.1 copy.7
  10.9 0.1 reshape.3.edges_ref
  11.0 0.0 collective-permute-done
  11.0 3.7 %collective-permute-start.5 = (f32[120,128]{1,0:T(8,128)S(1)}, f32[120,128]{1,0:T(8,128)S(1)}, u32[]{:S(2)}, u32[]{:S(2)}) collective-permute-start(f32[120,128]{1,0:T(8,128)S(1)} %bitcast.24), channel_id=1, source_target_pairs={{0,12},{2,14},{4,8},{6,10},{8,4},{10,6},{12,0},{14,2},{1,13},{3,15... | collective-permute-start | bytes 184328 | tf_op jit(solution)/shard_map/ppermute | solution.py:283
  14.7 0.0 collective-permute-done.1
  14.7 0.1 collective-permute-start.6
  14.8 0.0 collective-permute-done.2
  14.8 0.0 collective-permute-done.3
  14.8 4.3 %collective-permute-done.4 = f32[120,128]{1,0:T(8,128)S(1)} collective-permute-done((f32[120,128]{1,0:T(8,128)S(1)}, f32[120,128]{1,0:T(8,128)S(1)}, u32[]{:S(2)}, u32[]{:S(2)}) %collective-permute-start.4) | collective-permute-done | bytes 61472 | tf_op jit(solution)/shard_map/ppermute | solution.py:283
  19.2 0.0 collective-permute-done.5
  19.2 2.6 %collective-permute-done.6 = f32[120,128]{1,0:T(8,128)S(1)} collective-permute-done((f32[120,128]{1,0:T(8,128)S(1)}, f32[120,128]{1,0:T(8,128)S(1)}, u32[]{:S(2)}, u32[]{:S(2)}) %collective-permute-start.6) | collective-permute-done | bytes 61472 | tf_op jit(solution)/shard_map/ppermute | solution.py:283
  21.8 2.5 %all-gather = f32[16,120,128]{2,1,0:T(8,128)S(1)} all-gather(f32[8,120,128]{2,1,0:T(8,128)S(1)} %bitcast_dynamic-update-slice_fusion), channel_id=2, replica_groups=mesh['member'=2,'tx'=8,'ty'=2] {'ty'}, dimensions={0}, use_global_device_ids=true | all-gather | bytes 1474560 | tf_op jit(solution)/shard_map/all_gather | solution.py:285
  24.3 0.0 copy-start.2
  24.3 0.7 %copy-done.2 = f32[4]{0:T(128)S(1)} copy-done((f32[4]{0:T(128)S(1)}, f32[4]{0:T(128)}, u32[]{:S(2)}) %copy-start.2) | copy-done | bytes 40
  24.9 9.2 %substeps.1 = f32[6,3,6,4,24]{4,3,2,1,0:T(4,128)} custom-call(f32[2,8,120,128]{3,2,1,0:T(8,128)S(1)} %bitcast.18, f32[4]{0:T(128)S(1)} %copy-done.2, s32[72]{0:T(128)S(1)} %reshape.3.edges_ref), custom_call_target="tpu_custom_call" | custom-call | tf_op jit(solution)/shard_map/substeps/pallas_call | solution.py:287
  (8 shorter events, 0.0 us)
Async XLA Ops:
  0.0 0.9 %copy-start = (f32[6,3,4,6,24]{4,2,3,1,0:T(4,128)S(1)}, f32[6,3,4,6,24]{4,2,3,1,0:T(4,128)}, u32[]{:S(2)}) copy-start(f32[6,3,4,6,24]{4,2,3,1,0:T(4,128)} %param.4) | copy-start | bytes 124420
  0.9 0.7 %copy-start.1 = (f32[6,6,24]{2,1,0:T(8,128)S(1)}, f32[6,6,24]{2,1,0:T(8,128)}, u32[]{:S(2)}) copy-start(f32[6,6,24]{2,1,0:T(8,128)} %coriolis_ref.1) | copy-start | bytes 10372
  1.7 9.1 %copy-start.3 = (s32[6,4,3]{0,1,2:T(4,128)S(1)}, s32[6,4,3]{0,1,2:T(4,128)}, u32[]{:S(2)}) copy-start(s32[6,4,3]{0,1,2:T(4,128)} %param.7) | copy-start | bytes 868
  1.9 9.1 %collective-permute-start = (f32[120,128]{1,0:T(8,128)S(1)}, f32[120,128]{1,0:T(8,128)S(1)}, u32[]{:S(2)}, u32[]{:S(2)}) collective-permute-start(f32[120,128]{1,0:T(8,128)S(1)} %bitcast.19), channel_id=1, source_target_pairs={{0,2},{2,0},{4,6},{6,4},{8,10},{10,8},{12,14},{14,12},{1,3},{3,1},... | collective-permute-start | bytes 184328 | tf_op jit(solution)/shard_map/ppermute | solution.py:283
  4.9 9.8 %collective-permute-start.1 = (f32[120,128]{1,0:T(8,128)S(1)}, f32[120,128]{1,0:T(8,128)S(1)}, u32[]{:S(2)}, u32[]{:S(2)}) collective-permute-start(f32[120,128]{1,0:T(8,128)S(1)} %bitcast.20), channel_id=1, source_target_pairs={{0,4},{2,6},{4,0},{6,2},{8,12},{10,14},{12,8},{14,10},{1,5},{3,7},... | collective-permute-start | bytes 184328 | tf_op jit(solution)/shard_map/ppermute | solution.py:283
  6.5 8.3 %collective-permute-start.2 = (f32[120,128]{1,0:T(8,128)S(1)}, f32[120,128]{1,0:T(8,128)S(1)}, u32[]{:S(2)}, u32[]{:S(2)}) collective-permute-start(f32[120,128]{1,0:T(8,128)S(1)} %bitcast.21), channel_id=1, source_target_pairs={{0,6},{2,4},{4,2},{6,0},{8,14},{10,12},{12,10},{14,8},{1,7},{3,5},... | collective-permute-start | bytes 184328 | tf_op jit(solution)/shard_map/ppermute | solution.py:283
  6.5 8.3 %collective-permute-start.3 = (f32[120,128]{1,0:T(8,128)S(1)}, f32[120,128]{1,0:T(8,128)S(1)}, u32[]{:S(2)}, u32[]{:S(2)}) collective-permute-start(f32[120,128]{1,0:T(8,128)S(1)} %bitcast.22), channel_id=1, source_target_pairs={{0,8},{2,10},{4,12},{6,14},{8,0},{10,2},{12,4},{14,6},{1,9},{3,11}... | collective-permute-start | bytes 184328 | tf_op jit(solution)/shard_map/ppermute | solution.py:283
  9.5 9.7 %collective-permute-start.4 = (f32[120,128]{1,0:T(8,128)S(1)}, f32[120,128]{1,0:T(8,128)S(1)}, u32[]{:S(2)}, u32[]{:S(2)}) collective-permute-start(f32[120,128]{1,0:T(8,128)S(1)} %bitcast.23), channel_id=1, source_target_pairs={{0,10},{2,8},{4,14},{6,12},{8,2},{10,0},{12,6},{14,4},{1,11},{3,9}... | collective-permute-start | bytes 184328 | tf_op jit(solution)/shard_map/ppermute | solution.py:283
  11.0 8.2 %collective-permute-start.5 = (f32[120,128]{1,0:T(8,128)S(1)}, f32[120,128]{1,0:T(8,128)S(1)}, u32[]{:S(2)}, u32[]{:S(2)}) collective-permute-start(f32[120,128]{1,0:T(8,128)S(1)} %bitcast.24), channel_id=1, source_target_pairs={{0,12},{2,14},{4,8},{6,10},{8,4},{10,6},{12,0},{14,2},{1,13},{3,15... | collective-permute-start | bytes 184328 | tf_op jit(solution)/shard_map/ppermute | solution.py:283
  14.7 7.1 %collective-permute-start.6 = (f32[120,128]{1,0:T(8,128)S(1)}, f32[120,128]{1,0:T(8,128)S(1)}, u32[]{:S(2)}, u32[]{:S(2)}) collective-permute-start(f32[120,128]{1,0:T(8,128)S(1)} %bitcast.25), channel_id=1, source_target_pairs={{0,14},{2,12},{4,10},{6,8},{8,6},{10,4},{12,2},{14,0},{1,15},{3,13... | collective-permute-start | bytes 184328 | tf_op jit(solution)/shard_map/ppermute | solution.py:283
  24.3 0.7 %copy-start.2 = (f32[4]{0:T(128)S(1)}, f32[4]{0:T(128)}, u32[]{:S(2)}) copy-start(f32[4]{0:T(128)} %speed_ref.1) | copy-start | bytes 52

commit v3 on v1

--- a/solution.py
+++ b/solution.py
@@ -14,44 +14,54 @@
 VMEM_LIMIT = 32 * 1024 * 1024
 
 
-def pack_kernel(cx, cy, state_ref, coriolis_ref, out_ref):
+def pack_kernel(cx, cy, state_hbm, coriolis_hbm, out_ref, state_ref, coriolis_ref, sems):
+    copies = [
+        pltpu.make_async_copy(state_hbm, state_ref, sems.at[0]),
+        pltpu.make_async_copy(coriolis_hbm, coriolis_ref, sems.at[1]),
+    ]
+    for copy in copies:
+        copy.start()
     faces, fields = state_ref.shape[:2]
     levels = state_ref.shape[3]
     pairs = faces // 2
     group = pairs * levels
     half = cx // 2
     base = fields * half * group
-    out_ref[0] = jnp.zeros(out_ref.shape[1:], jnp.float32)
+    out_ref[...] = jnp.zeros(out_ref.shape, jnp.float32)
+    for copy in copies:
+        copy.wait()
     for face in range(faces):
         for parity in range(2):
             lane = (face % 2) * WINDOW + MARGIN + parity * cy
             for xp in range(half):
                 for field in range(fields):
                     row = field * half * group + xp * group + (face // 2) * levels
-                    out_ref[0, row : row + levels, lane : lane + cy] = state_ref[
+                    out_ref[row : row + levels, lane : lane + cy] = state_ref[
                         face, field, 2 * xp + parity
                     ]
                 row = base + xp * pairs + face // 2
-                out_ref[0, row : row + 1, lane : lane + cy] = coriolis_ref[
+                out_ref[row : row + 1, lane : lane + cy] = coriolis_ref[
                     face, 2 * xp + parity : 2 * xp + parity + 1
                 ]
-    for copy in range(1, out_ref.shape[0]):
-        out_ref[copy] = out_ref[0]
 
 
 def step_kernel(
-    cx, cy, count_x, parts_ref, speed_ref, edges_ref, out_ref,
-    z_ref, cor_ref, pred_ref, store_ref, tile_ref, flip_ref,
+    cx, cy, count_x, parts_ref, speed_hbm, edges_ref, out_ref,
+    z_ref, cor_ref, pred_ref, store_ref, tile_ref, flip_ref, speed_ref, speed_smem, sem,
 ):
     fields = z_ref.shape[0]
     levels = 4
+    slots = 16
     cells = cx * count_x
     faces = store_ref.shape[0] // 4
     pairs = faces // 2
     group = pairs * levels
     half = cx // 2
+    chunk = cx * group
     index_x = lax.axis_index("tx")
     index_y = lax.axis_index("ty")
+    speed_copy = pltpu.make_async_copy(speed_hbm, speed_smem, sem)
+    speed_copy.start()
 
     def row_of(x):
         return (x + 4) * group
@@ -59,150 +69,169 @@
     def lanes_of(rows):
         return lax.broadcasted_iota(jnp.int32, (rows, LANES), 1)
 
-    def unpack(source, carry):
+    for place in range(count_x):
+        source = place ^ index_x
+        start = pl.multiple_of(source * chunk, 8)
         low = lanes_of(group) % WINDOW < MARGIN + cy
         for field in range(fields):
             for xp in range(half):
                 row = field * half * group + xp * group
-                south = parts_ref[0, source, row : row + group]
-                north = parts_ref[1, source, row : row + group]
+                south = parts_ref[0, place, row : row + group]
+                north = parts_ref[1, place, row : row + group]
                 even = jnp.where(low, south, pltpu.roll(north, cy, 1))
                 odd = jnp.where(low, pltpu.roll(south, LANES - cy, 1), north)
-                at = source * (cx * group) + row_of(2 * xp)
-                z_ref[field, pl.ds(at, group)] = even
-                z_ref[field, pl.ds(at + group, group)] = odd
+                z_ref[field, pl.ds(start + row_of(2 * xp), group)] = even
+                z_ref[field, pl.ds(start + row_of(2 * xp + 1), group)] = odd
         base = fields * half * group
         rows = half * pairs
         low = lanes_of(rows) % WINDOW < MARGIN + cy
-        south = parts_ref[0, source, base : base + rows]
-        north = parts_ref[1, source, base : base + rows]
+        south = parts_ref[0, place, base : base + rows]
+        north = parts_ref[1, place, base : base + rows]
         even = jnp.where(low, south, pltpu.roll(north, cy, 1))
         odd = jnp.where(low, pltpu.roll(south, LANES - cy, 1), north)
         for parity, values in enumerate((even, odd)):
             for xp in range(half):
                 for pair in range(pairs):
-                    at = source * (cx * group) + (2 * xp + parity) * group + pair * levels
+                    at = start + (2 * xp + parity) * group + pair * levels
                     line = values[xp * pairs + pair : xp * pairs + pair + 1]
                     cor_ref[pl.ds(at, levels)] = jnp.broadcast_to(line, (levels, LANES))
-        return carry
-
-    lax.fori_loop(0, count_x, unpack, 0)
-
-    def speed_rows(rows):
-        level = lax.broadcasted_iota(jnp.int32, (rows, LANES), 0) % levels
-        values = jnp.full((rows, LANES), speed_ref[0], jnp.float32)
-        for index in range(1, levels):
-            values = jnp.where(level == index, speed_ref[index], values)
-        return values
+
+    speed_copy.wait()
+    level_of = lax.broadcasted_iota(jnp.int32, speed_ref.shape, 0) % levels
+    speeds = jnp.full(speed_ref.shape, speed_smem[0], jnp.float32)
+    for index in range(1, levels):
+        speeds = jnp.where(level_of == index, speed_smem[index], speeds)
+    speed_ref[...] = speeds
 
     def collect():
-        lane = lanes_of(cells)
-        place = lane % WINDOW
-
-        def body(pair, carry):
+        position = lanes_of(cells) % WINDOW
+        gap = WINDOW - cells + 3
+        wide = gap + 3 * levels
+        for pair in range(pairs):
+            merged = jnp.zeros((cells, LANES), jnp.float32)
             for slot, field in ((0, 0), (1, 2)):
-                merged = jnp.zeros((cells, LANES), jnp.float32)
                 for level in range(levels):
                     lines = z_ref[field, pl.ds(row_of(0) + pair * levels + level, cells, group)]
-                    shift = (3 * level - (MARGIN + cells - 3)) % LANES
-                    gap = WINDOW - cells + 3
-                    here = place - 3 * level
+                    offset = slot * wide + 3 * level
+                    here = position - offset
                     wanted = ((here >= 0) & (here < 3)) | ((here >= gap) & (here < gap + 3))
+                    shift = (offset - (MARGIN + cells - 3)) % LANES
                     merged = jnp.where(wanted, pltpu.roll(lines, shift, 1), merged)
-                merged = jnp.concatenate(
-                    [merged, jnp.zeros((LANES - cells, LANES), jnp.float32)], axis=0
-                )
-                flip_ref[...] = merged.T
+            merged = jnp.concatenate(
+                [merged, jnp.zeros((LANES - cells, LANES), jnp.float32)], axis=0
+            )
+            flip_ref[pair] = merged.T
+            for slot in range(2):
                 for side in (2, 3):
                     for odd in range(2):
                         for depth in range(3):
+                            base = slot * wide
                             if side == 3:
-                                base = odd * WINDOW + 2 - depth
+                                base += odd * WINDOW + 2 - depth
                             else:
-                                base = ((odd + 1) % 2) * WINDOW + gap + depth
-                            at = slot * 3 * levels + depth * levels
+                                base += ((odd + 1) % 2) * WINDOW + gap + depth
+                            at = slot * slots + depth * levels
                             store_ref[(2 * pair + odd) * 4 + side, at : at + levels] = flip_ref[
-                                pl.ds(base, levels, 3)
+                                pair, pl.ds(base, levels, 3)
                             ]
-            for slot, field in ((0, 0), (1, 1)):
+            for slot in range(2):
                 for side in (0, 1):
                     for depth in range(3):
                         x = depth if side == 0 else cells - 1 - depth
-                        lines = z_ref[field, pl.ds(row_of(x) + pair * levels, levels)]
-                        at = slot * 3 * levels + depth * levels
+                        row = row_of(x) + pair * levels
+                        lines = z_ref[slot, row : row + levels]
+                        at = slot * slots + depth * levels
                         for odd in range(2):
                             store_ref[(2 * pair + odd) * 4 + side, at : at + levels] = pltpu.roll(
                                 lines, LANES - MARGIN - odd * WINDOW, 1
                             )
-            return carry
-
-        lax.fori_loop(0, pairs, body, 0)
-
-    def fetch(face, side):
+
+    def fetch(face, side, position):
         at = (face * 4 + side) * 3
         neighbour = edges_ref[at]
         far_side = edges_ref[at + 1]
         flipped = edges_ref[at + 2]
         block = store_ref[neighbour * 4 + far_side]
-        lane = lanes_of(block.shape[0])
-        order = jnp.where((flipped == 1) & (lane < cells), cells - 1 - lane, lane)
+        order = jnp.where(flipped == 1, cells - 1 - position, position)
+        order = jnp.where((position >= 0) & (position < cells), order, 0)
         block = jnp.take_along_axis(block, order, axis=1)
         sign_here = 2 * (side % 2) - 1
         sign_there = 2 * (far_side % 2) - 1
         sign = (-sign_here * sign_there).astype(jnp.float32)
-        normal = lax.broadcasted_iota(jnp.int32, block.shape, 0) >= 3 * levels
+        normal = lax.broadcasted_iota(jnp.int32, block.shape, 0) >= slots
         return jnp.where(normal, sign * block, block)
 
     def rim_rows(side):
-        def body(pair, carry):
-            first = pltpu.roll(fetch(2 * pair, side), MARGIN, 1)
-            second = pltpu.roll(fetch(2 * pair + 1, side), MARGIN + WINDOW, 1)
-            both = jnp.where(lanes_of(first.shape[0]) < WINDOW, first, second)
-            for slot, field in ((0, 0), (1, 1)):
+        lane = lanes_of(2 * slots)
+        for pair in range(pairs):
+            first = fetch(2 * pair, side, lane - MARGIN)
+            second = fetch(2 * pair + 1, side, lane - (MARGIN + WINDOW))
+            both = jnp.where(lane < WINDOW, first, second)
+            for slot in range(2):
                 for depth in range(3):
                     x = -1 - depth if side == 0 else cells + depth
-                    at = slot * 3 * levels + depth * levels
-                    z_ref[field, pl.ds(row_of(x) + pair * levels, levels)] = both[at : at + levels]
-            return carry
-
-        lax.fori_loop(0, pairs, body, 0)
-
-    def rim_columns(start, count):
-        def body(pair, carry):
+                    at = slot * slots + depth * levels
+                    row = row_of(x) + pair * levels
+                    z_ref[slot, row : row + levels] = both[at : at + levels]
+
+    def tile_rows(odd, side, depth):
+        if side == 3:
+            return pl.ds(odd * WINDOW + depth, levels, 16)
+        return pl.ds(((odd + 1) % 2) * WINDOW + 15 - depth, levels, 16)
+
+    def put_columns(lines, field, start, pair):
+        count = lines.shape[0]
+        position = lanes_of(count) % WINDOW
+        rim = ((position >= MARGIN - 3) & (position < MARGIN)) | (
+            (position >= MARGIN + cells) & (position < MARGIN + cells + 3)
+        )
+        for level in range(levels):
+            rolled = pltpu.roll(lines, (MARGIN + cells - 16 * level) % LANES, 1)
+            at = pl.ds(row_of(start) + pair * levels + level, count, group)
+            z_ref[field, at] = jnp.where(rim, rolled, z_ref[field, at])
+
+    def rim_columns_all():
+        for pair in range(pairs):
             for odd in range(2):
                 for side in (2, 3):
-                    block = fetch(2 * pair + odd, side)
+                    block = fetch(2 * pair + odd, side, lanes_of(2 * slots))
                     for slot in range(2):
                         for depth in range(3):
-                            at = slot * 3 * levels + depth * levels
-                            if side == 3:
-                                base = odd * WINDOW + depth
-                            else:
-                                base = ((odd + 1) % 2) * WINDOW + 15 - depth
-                            tile_ref[slot, pl.ds(base, levels, 16)] = block[at : at + levels]
-            place = lanes_of(count) % WINDOW
-            rim = ((place >= MARGIN - 3) & (place < MARGIN)) | (
-                (place >= MARGIN + cells) & (place < MARGIN + cells + 3)
-            )
+                            at = slot * slots + depth * levels
+                            tile_ref[2 * pair + slot, tile_rows(odd, side, depth)] = block[
+                                at : at + levels
+                            ]
             for slot, field in ((0, 0), (1, 2)):
-                flip_ref[...] = tile_ref[slot].T
-                lines = flip_ref[pl.ds(start, count)]
-                for level in range(levels):
-                    rolled = pltpu.roll(lines, (MARGIN + cells - 16 * level) % LANES, 1)
-                    at = pl.ds(row_of(start) + pair * levels + level, count, group)
-                    z_ref[field, at] = jnp.where(rim, rolled, z_ref[field, at])
-            return carry
-
-        lax.fori_loop(0, pairs, body, 0)
+                put_columns(tile_ref[2 * pair + slot].T[:cells], field, 0, pair)
+
+    def rim_columns_own():
+        lane = lanes_of(2 * slots)
+        second = lax.broadcasted_iota(jnp.int32, lane.shape, 0) >= slots
+        for odd in range(2):
+            for side in (2, 3):
+                total = jnp.zeros((slots, LANES), jnp.float32)
+                for pair in range(pairs):
+                    local = lane - jnp.where(second, 8 * (pairs + pair), 8 * pair)
+                    block = fetch(2 * pair + odd, side, index_x * cx + local)
+                    block = jnp.where((local >= 0) & (local < 8), block, 0.0)
+                    total = total + block[:slots] + block[slots:]
+                for depth in range(3):
+                    at = depth * levels
+                    tile_ref[0, tile_rows(odd, side, depth)] = total[at : at + levels]
+        turned = tile_ref[0].T
+        for slot, field in ((0, 0), (1, 2)):
+            for pair in range(pairs):
+                at = 8 * (slot * pairs + pair)
+                put_columns(turned[at : at + cx], field, index_x * cx, pair)
 
     def predict(at, rows):
-        speed = speed_rows(rows)
+        speed = speed_ref[:rows]
         ahead = z_ref[0, pl.ds(at + group, rows)]
         behind = z_ref[0, pl.ds(at - group, rows)]
         pred_ref[pl.ds(at, rows)] = z_ref[1, pl.ds(at, rows)] - speed * (0.5 * (ahead - behind))
 
     def update(at, rows):
-        speed = speed_rows(rows)
+        speed = speed_ref[:rows]
         height = z_ref[0, pl.ds(at, rows)]
         north_pred = z_ref[2, pl.ds(at, rows)] - speed * (
             0.5 * (pltpu.roll(height, LANES - 1, 1) - pltpu.roll(height, 1, 1))
@@ -221,22 +250,13 @@
     collect()
     rim_rows(0)
     rim_rows(1)
-    rim_columns(0, cells)
-    chunk = cx * group
-
-    def predict_all(index, carry):
-        predict(row_of(-2) + index * (4 * group), 4 * group)
-        return carry
-
-    lax.fori_loop(0, (cells + 4) // 4, predict_all, 0)
-
-    def update_all(index, carry):
+    rim_columns_all()
+    for first in range(-2, cells + 2, 4):
+        predict(row_of(first), 4 * group)
+    for index in range(count_x):
         at = row_of(0) + index * chunk
         for field, values in enumerate(update(at, chunk)):
-            z_ref[field, pl.ds(at, chunk)] = values
-        return carry
-
-    lax.fori_loop(0, count_x, update_all, 0)
+            z_ref[field, at : at + chunk] = values
 
     collect()
 
@@ -248,8 +268,8 @@
     def _():
         rim_rows(1)
 
-    rim_columns(index_x * cx, cx)
-    at = row_of(0) + index_x * chunk
+    rim_columns_own()
+    at = pl.multiple_of(row_of(0) + index_x * chunk, 8)
     predict(at - 2 * group, chunk + 4 * group)
     for field, values in enumerate(update(at, chunk)):
         for odd in range(2):
@@ -271,36 +291,50 @@
     cells = cx * count_x
     packed = pl.pallas_call(
         functools.partial(pack_kernel, cx, cy),
-        out_shape=jax.ShapeDtypeStruct((count_x, rows, LANES), jnp.float32),
-        in_specs=[pl.BlockSpec(memory_space=pltpu.VMEM)] * 2,
+        out_shape=jax.ShapeDtypeStruct((rows, LANES), jnp.float32),
+        in_specs=[pl.BlockSpec(memory_space=pltpu.HBM)] * 2,
         out_specs=pl.BlockSpec(memory_space=pltpu.VMEM),
+        scratch_shapes=[
+            pltpu.VMEM((faces, fields, cx, levels, cy), jnp.float32),
+            pltpu.VMEM((faces, cx, cy), jnp.float32),
+            pltpu.SemaphoreType.DMA((2,)),
+        ],
         compiler_params=pltpu.CompilerParams(vmem_limit_bytes=VMEM_LIMIT),
         name="pack",
     )(jnp.swapaxes(state, 2, 3), coriolis)
-    column = lax.all_to_all(packed, "tx", 0, 0)
-    parts = lax.all_gather(column, "ty")
+    chunks = [packed] * count_x
+    for other in reversed(range(1, count_x)):
+        partners = [(index, index ^ other) for index in range(count_x)]
+        chunks[other] = lax.ppermute(packed, "tx", partners)
+    parts = lax.all_gather(jnp.stack(chunks), "ty")
     z_rows = (cells + 8) * group
-    out = pl.pallas_call(
-        functools.partial(step_kernel, cx, cy, count_x),
-        out_shape=jax.ShapeDtypeStruct((faces, fields, cx, levels, cy), jnp.float32),
-        in_specs=[
-            pl.BlockSpec(memory_space=pltpu.VMEM),
-            pl.BlockSpec(memory_space=pltpu.SMEM),
-            pl.BlockSpec(memory_space=pltpu.SMEM),
-        ],
-        out_specs=pl.BlockSpec(memory_space=pltpu.VMEM),
-        scratch_shapes=[
-            pltpu.VMEM((fields, z_rows, LANES), jnp.float32),
-            pltpu.VMEM((cells * group, LANES), jnp.float32),
-            pltpu.VMEM((z_rows, LANES), jnp.float32),
-            pltpu.VMEM((faces * 4, 6 * levels, LANES), jnp.float32),
-            pltpu.VMEM((2, LANES, LANES), jnp.float32),
-            pltpu.VMEM((LANES, LANES), jnp.float32),
-        ],
-        compiler_params=pltpu.CompilerParams(vmem_limit_bytes=VMEM_LIMIT),
-        name="substeps",
-    )(parts, wave_speed, edges.reshape(-1))
-    return jnp.swapaxes(out, 2, 3)
+    return jnp.swapaxes(
+        pl.pallas_call(
+            functools.partial(step_kernel, cx, cy, count_x),
+            out_shape=jax.ShapeDtypeStruct((faces, fields, cx, levels, cy), jnp.float32),
+            in_specs=[
+                pl.BlockSpec(memory_space=pltpu.VMEM),
+                pl.BlockSpec(memory_space=pltpu.HBM),
+                pl.BlockSpec(memory_space=pltpu.SMEM),
+            ],
+            out_specs=pl.BlockSpec(memory_space=pltpu.VMEM),
+            scratch_shapes=[
+                pltpu.VMEM((fields, z_rows, LANES), jnp.float32),
+                pltpu.VMEM((cells * group, LANES), jnp.float32),
+                pltpu.VMEM((z_rows, LANES), jnp.float32),
+                pltpu.VMEM((faces * 4, 32, LANES), jnp.float32),
+                pltpu.VMEM((faces, LANES, LANES), jnp.float32),
+                pltpu.VMEM((pairs, LANES, LANES), jnp.float32),
+                pltpu.VMEM(((cx + 4) * group, LANES), jnp.float32),
+                pltpu.SMEM((levels,), jnp.float32),
+                pltpu.SemaphoreType.DMA,
+            ],
+            compiler_params=pltpu.CompilerParams(vmem_limit_bytes=VMEM_LIMIT),
+            name="substeps",
+        )(parts, wave_speed, edges.reshape(-1)),
+        2,
+        3,
+    )
 
 
 def padded_2(block, sides, width):

time: 36.6 us -> 31.1 us (0.85)
  waiting for transfers between devices: 13.6 us -> 6.93 us
  starting transfers between devices: 7.41 us -> 12.6 us
  Pallas kernels: 10.2 us -> 6.16 us
    all_to_all x1 -> x0, waiting for transfers between devices: 13.6 us -> none  [fast_on_device(): column = lax.all_to_all(packed, 'tx', 0, 0)]
    ppermute x0 -> x7, starting transfers between devices: none -> 12.6 us  [fast_on_device(): chunks[other] = lax.ppermute(packed, 'tx', partners)]
    all_to_all x1 -> x0, starting transfers between devices: 7.41 us -> none  [fast_on_device(): column = lax.all_to_all(packed, 'tx', 0, 0)]
    ppermute x0 -> x7, waiting for transfers between devices: none -> 6.93 us  [fast_on_device(): chunks[other] = lax.ppermute(packed, 'tx', partners)]
    pallas_call x1, Pallas kernels: 9.2 us -> 5.66 us  [fast_on_device(): pl.pallas_call(functools.partial(step_kernel, cx, cy, count_x), out_shape...]
    pallas_call x1, Pallas kernels: 1.02 us -> 0.5 us  [fast_on_device(): pl.pallas_call(functools.partial(pack_kernel, cx, cy), out_shape=jax.Shap...]
    unnamed x9 -> x16, local copies, waits for them, and re-layouts: 2.44 us -> 2.49 us
  transfers between devices with their start and end apart: 1 -> 7, of which waited for: 1 -> 2; matrix products, arithmetic and copies ran while one was open for 1% -> 1% of each run, Pallas kernels for 0% -> 0%
where the time goes in v3:
time: 31.1 us; the launch traced here: 30.9 us
  starting transfers between devices  12.6 us (41%)
  waiting for transfers between devices  6.93 us (22%)
  Pallas kernels  6.16 us (20%)
  local copies, waits for them, and re-layouts  2.59 us (8%)
  blocking collectives  2.5 us (8%)
    ppermute x7, starting transfers between devices, fast_on_device(): chunks[other] = lax.ppermute(packed, 'tx', partners)  12.6 us
    ppermute x7, waiting for transfers between devices, fast_on_device(): chunks[other] = lax.ppermute(packed, 'tx', partners)  6.93 us
    pallas_call x1, Pallas kernels, fast_on_device(): pl.pallas_call(functools.partial(step_kernel, cx, cy, count_x), out_shape...  5.66 us
    all_gather x1, blocking collectives, fast_on_device(): parts = lax.all_gather(jnp.stack(chunks), 'ty')  2.5 us
    unnamed x16, local copies, waits for them, and re-layouts  2.49 us
  transfers between devices with their start and end apart: 7, of which 2 were waited for; matrix products, arithmetic and copies ran while one was open for 1% of the time, Pallas kernels for 0%

profile of v3, /device:TPU:0, one launch (start us, length us, event | category | flops | bytes accessed | tf_op | source)
XLA Modules:
  0.0 30.9 jit_solution(16642122155723685238)
XLA Ops:
  0.0 0.0 copy-start
  0.0 0.9 %copy-done = f32[6,3,4,6,24]{4,2,3,1,0:T(4,128)S(1)} copy-done((f32[6,3,4,6,24]{4,2,3,1,0:T(4,128)S(1)}, f32[6,3,4,6,24]{4,2,3,1,0:T(4,128)}, u32[]{:S(2)}) %copy-start) | copy-done | bytes 41496
  0.9 0.0 copy-start.1
  0.9 0.7 %copy-done.1 = f32[6,6,24]{2,1,0:T(8,128)S(1)} copy-done((f32[6,6,24]{2,1,0:T(8,128)S(1)}, f32[6,6,24]{2,1,0:T(8,128)}, u32[]{:S(2)}) %copy-start.1) | copy-done | bytes 3480
  1.7 0.5 %pack.1 = f32[120,128]{1,0:T(8,128)S(1)} custom-call(f32[6,3,6,4,24]{4,3,2,1,0:T(4,128)S(1)} %bitcast.20, f32[6,6,24]{2,1,0:T(8,128)S(1)} %copy-done.1), custom_call_target="tpu_custom_call" | custom-call | tf_op jit(solution)/shard_map/pack/pallas_call | solution.py:292
  2.2 0.0 copy-start.3
  2.2 3.0 %collective-permute-start = (f32[120,128]{1,0:T(8,128)S(1)}, f32[120,128]{1,0:T(8,128)S(1)}, u32[]{:S(2)}, u32[]{:S(2)}) collective-permute-start(f32[120,128]{1,0:T(8,128)S(1)} %pack.1), channel_id=1, source_target_pairs={{0,2},{2,0},{4,6},{6,4},{8,10},{10,8},{12,14},{14,12},{1,3},{3,1},... | collective-permute-start | bytes 184328 | tf_op jit(solution)/shard_map/ppermute | solution.py:308
  5.2 1.6 %collective-permute-start.1 = (f32[120,128]{1,0:T(8,128)S(1)}, f32[120,128]{1,0:T(8,128)S(1)}, u32[]{:S(2)}, u32[]{:S(2)}) collective-permute-start(f32[120,128]{1,0:T(8,128)S(1)} %pack.1), channel_id=1, source_target_pairs={{0,4},{2,6},{4,0},{6,2},{8,12},{10,14},{12,8},{14,10},{1,5},{3,7},... | collective-permute-start | bytes 184328 | tf_op jit(solution)/shard_map/ppermute | solution.py:308
  6.8 0.0 collective-permute-start.2
  6.8 3.0 %collective-permute-start.3 = (f32[120,128]{1,0:T(8,128)S(1)}, f32[120,128]{1,0:T(8,128)S(1)}, u32[]{:S(2)}, u32[]{:S(2)}) collective-permute-start(f32[120,128]{1,0:T(8,128)S(1)} %pack.1), channel_id=1, source_target_pairs={{0,8},{2,10},{4,12},{6,14},{8,0},{10,2},{12,4},{14,6},{1,9},{3,11}... | collective-permute-start | bytes 184328 | tf_op jit(solution)/shard_map/ppermute | solution.py:308
  9.8 1.3 %collective-permute-start.4 = (f32[120,128]{1,0:T(8,128)S(1)}, f32[120,128]{1,0:T(8,128)S(1)}, u32[]{:S(2)}, u32[]{:S(2)}) collective-permute-start(f32[120,128]{1,0:T(8,128)S(1)} %pack.1), channel_id=1, source_target_pairs={{0,10},{2,8},{4,14},{6,12},{8,2},{10,0},{12,6},{14,4},{1,11},{3,9}... | collective-permute-start | bytes 184328 | tf_op jit(solution)/shard_map/ppermute | solution.py:308
  11.1 0.0 copy-done.3
  11.1 0.1 copy.7
  11.2 0.1 reshape.3.edges_ref
  11.3 0.0 collective-permute-done
  11.3 3.7 %collective-permute-start.5 = (f32[120,128]{1,0:T(8,128)S(1)}, f32[120,128]{1,0:T(8,128)S(1)}, u32[]{:S(2)}, u32[]{:S(2)}) collective-permute-start(f32[120,128]{1,0:T(8,128)S(1)} %pack.1), channel_id=1, source_target_pairs={{0,12},{2,14},{4,8},{6,10},{8,4},{10,6},{12,0},{14,2},{1,13},{3,15... | collective-permute-start | bytes 184328 | tf_op jit(solution)/shard_map/ppermute | solution.py:308
  15.0 0.0 collective-permute-done.1
  15.0 0.1 collective-permute-start.6
  15.1 0.0 collective-permute-done.2
  15.1 0.0 collective-permute-done.3
  15.1 4.3 %collective-permute-done.4 = f32[120,128]{1,0:T(8,128)S(1)} collective-permute-done((f32[120,128]{1,0:T(8,128)S(1)}, f32[120,128]{1,0:T(8,128)S(1)}, u32[]{:S(2)}, u32[]{:S(2)}) %collective-permute-start.4) | collective-permute-done | bytes 61472 | tf_op jit(solution)/shard_map/ppermute | solution.py:308
  19.5 0.0 collective-permute-done.5
  19.5 2.6 %collective-permute-done.6 = f32[120,128]{1,0:T(8,128)S(1)} collective-permute-done((f32[120,128]{1,0:T(8,128)S(1)}, f32[120,128]{1,0:T(8,128)S(1)}, u32[]{:S(2)}, u32[]{:S(2)}) %collective-permute-start.6) | collective-permute-done | bytes 61472 | tf_op jit(solution)/shard_map/ppermute | solution.py:308
  22.1 2.5 %all-gather = f32[16,120,128]{2,1,0:T(8,128)S(1)} all-gather(f32[8,120,128]{2,1,0:T(8,128)S(1)} %bitcast_dynamic-update-slice_fusion), channel_id=2, replica_groups=mesh['member'=2,'tx'=8,'ty'=2] {'ty'}, dimensions={0}, use_global_device_ids=true | all-gather | bytes 1474560 | tf_op jit(solution)/shard_map/all_gather | solution.py:309
  24.6 0.0 copy-start.2
  24.6 0.7 %copy-done.2 = f32[4]{0:T(128)S(1)} copy-done((f32[4]{0:T(128)S(1)}, f32[4]{0:T(128)}, u32[]{:S(2)}) %copy-start.2) | copy-done | bytes 40
  25.2 5.7 %substeps.1 = f32[6,3,6,4,24]{4,3,2,1,0:T(4,128)} custom-call(f32[2,8,120,128]{3,2,1,0:T(8,128)S(1)} %bitcast.19, f32[4]{0:T(128)S(1)} %copy-done.2, s32[72]{0:T(128)S(1)} %reshape.3.edges_ref), custom_call_target="tpu_custom_call" | custom-call | tf_op jit(solution)/shard_map/substeps/pallas_call | solution.py:312
  (8 shorter events, 0.0 us)
Async XLA Ops:
  0.0 0.9 %copy-start = (f32[6,3,4,6,24]{4,2,3,1,0:T(4,128)S(1)}, f32[6,3,4,6,24]{4,2,3,1,0:T(4,128)}, u32[]{:S(2)}) copy-start(f32[6,3,4,6,24]{4,2,3,1,0:T(4,128)} %param.4) | copy-start | bytes 124420
  0.9 0.7 %copy-start.1 = (f32[6,6,24]{2,1,0:T(8,128)S(1)}, f32[6,6,24]{2,1,0:T(8,128)}, u32[]{:S(2)}) copy-start(f32[6,6,24]{2,1,0:T(8,128)} %coriolis_hbm.1) | copy-start | bytes 10372
  2.2 8.9 %copy-start.3 = (s32[6,4,3]{0,1,2:T(4,128)S(1)}, s32[6,4,3]{0,1,2:T(4,128)}, u32[]{:S(2)}) copy-start(s32[6,4,3]{0,1,2:T(4,128)} %param.7) | copy-start | bytes 868
  2.2 9.1 %collective-permute-start = (f32[120,128]{1,0:T(8,128)S(1)}, f32[120,128]{1,0:T(8,128)S(1)}, u32[]{:S(2)}, u32[]{:S(2)}) collective-permute-start(f32[120,128]{1,0:T(8,128)S(1)} %pack.1), channel_id=1, source_target_pairs={{0,2},{2,0},{4,6},{6,4},{8,10},{10,8},{12,14},{14,12},{1,3},{3,1},... | collective-permute-start | bytes 184328 | tf_op jit(solution)/shard_map/ppermute | solution.py:308
  5.2 9.8 %collective-permute-start.1 = (f32[120,128]{1,0:T(8,128)S(1)}, f32[120,128]{1,0:T(8,128)S(1)}, u32[]{:S(2)}, u32[]{:S(2)}) collective-permute-start(f32[120,128]{1,0:T(8,128)S(1)} %pack.1), channel_id=1, source_target_pairs={{0,4},{2,6},{4,0},{6,2},{8,12},{10,14},{12,8},{14,10},{1,5},{3,7},... | collective-permute-start | bytes 184328 | tf_op jit(solution)/shard_map/ppermute | solution.py:308
  6.8 8.3 %collective-permute-start.2 = (f32[120,128]{1,0:T(8,128)S(1)}, f32[120,128]{1,0:T(8,128)S(1)}, u32[]{:S(2)}, u32[]{:S(2)}) collective-permute-start(f32[120,128]{1,0:T(8,128)S(1)} %pack.1), channel_id=1, source_target_pairs={{0,6},{2,4},{4,2},{6,0},{8,14},{10,12},{12,10},{14,8},{1,7},{3,5},... | collective-permute-start | bytes 184328 | tf_op jit(solution)/shard_map/ppermute | solution.py:308
  6.8 8.3 %collective-permute-start.3 = (f32[120,128]{1,0:T(8,128)S(1)}, f32[120,128]{1,0:T(8,128)S(1)}, u32[]{:S(2)}, u32[]{:S(2)}) collective-permute-start(f32[120,128]{1,0:T(8,128)S(1)} %pack.1), channel_id=1, source_target_pairs={{0,8},{2,10},{4,12},{6,14},{8,0},{10,2},{12,4},{14,6},{1,9},{3,11}... | collective-permute-start | bytes 184328 | tf_op jit(solution)/shard_map/ppermute | solution.py:308
  9.8 9.7 %collective-permute-start.4 = (f32[120,128]{1,0:T(8,128)S(1)}, f32[120,128]{1,0:T(8,128)S(1)}, u32[]{:S(2)}, u32[]{:S(2)}) collective-permute-start(f32[120,128]{1,0:T(8,128)S(1)} %pack.1), channel_id=1, source_target_pairs={{0,10},{2,8},{4,14},{6,12},{8,2},{10,0},{12,6},{14,4},{1,11},{3,9}... | collective-permute-start | bytes 184328 | tf_op jit(solution)/shard_map/ppermute | solution.py:308
  11.3 8.2 %collective-permute-start.5 = (f32[120,128]{1,0:T(8,128)S(1)}, f32[120,128]{1,0:T(8,128)S(1)}, u32[]{:S(2)}, u32[]{:S(2)}) collective-permute-start(f32[120,128]{1,0:T(8,128)S(1)} %pack.1), channel_id=1, source_target_pairs={{0,12},{2,14},{4,8},{6,10},{8,4},{10,6},{12,0},{14,2},{1,13},{3,15... | collective-permute-start | bytes 184328 | tf_op jit(solution)/shard_map/ppermute | solution.py:308
  15.0 7.1 %collective-permute-start.6 = (f32[120,128]{1,0:T(8,128)S(1)}, f32[120,128]{1,0:T(8,128)S(1)}, u32[]{:S(2)}, u32[]{:S(2)}) collective-permute-start(f32[120,128]{1,0:T(8,128)S(1)} %pack.1), channel_id=1, source_target_pairs={{0,14},{2,12},{4,10},{6,8},{8,6},{10,4},{12,2},{14,0},{1,15},{3,13... | collective-permute-start | bytes 184328 | tf_op jit(solution)/shard_map/ppermute | solution.py:308
  24.6 0.7 %copy-start.2 = (f32[4]{0:T(128)S(1)}, f32[4]{0:T(128)}, u32[]{:S(2)}) copy-start(f32[4]{0:T(128)} %speed_hbm.1) | copy-start | bytes 52

commit v4 on v3

--- a/solution.py
+++ b/solution.py
@@ -14,7 +14,33 @@
 VMEM_LIMIT = 32 * 1024 * 1024
 
 
-def pack_kernel(cx, cy, state_hbm, coriolis_hbm, out_ref, state_ref, coriolis_ref, sems):
+def window_start(source, target, count_x, index_y, cx, cy, far):
+    width = 2 * cx
+    near = jnp.minimum(target, count_x - 1 - target)
+    inward = jnp.minimum(cx * near - jnp.where(far, cx, cx // 2), cy - width)
+    rim = (source == 0) | (source == count_x - 1)
+    start = jnp.where(rim, jnp.maximum(inward, 0), 0)
+    return jnp.where(index_y == 0, start, cy - width - start)
+
+
+def windows(source, target, count_x, index_y, cx, cy):
+    low_far = source == count_x - 1
+    lower = window_start(source, target, count_x, index_y, cx, cy, low_far)
+    upper = window_start(source, target, count_x, index_y, cx, cy, ~low_far)
+    return lower, upper
+
+
+def unit_place(field, x, cx, group, width):
+    per_row = 60 // width
+    index = field * cx + x
+    return (index // per_row) * group, (index % per_row) * width
+
+
+def pack_kernel(
+    cx, cy, count_x, distant, state_hbm, coriolis_hbm, full_ref, *rest
+):
+    small_refs = rest[: len(distant)]
+    state_ref, coriolis_ref, sems = rest[len(distant) :]
     copies = [
         pltpu.make_async_copy(state_hbm, state_ref, sems.at[0]),
         pltpu.make_async_copy(coriolis_hbm, coriolis_ref, sems.at[1]),
@@ -26,8 +52,11 @@
     pairs = faces // 2
     group = pairs * levels
     half = cx // 2
+    width = 2 * cx
     base = fields * half * group
-    out_ref[...] = jnp.zeros(out_ref.shape, jnp.float32)
+    index_x = lax.axis_index("tx")
+    index_y = lax.axis_index("ty")
+    full_ref[...] = jnp.zeros(full_ref.shape, jnp.float32)
     for copy in copies:
         copy.wait()
     for face in range(faces):
@@ -36,18 +65,43 @@
             for xp in range(half):
                 for field in range(fields):
                     row = field * half * group + xp * group + (face // 2) * levels
-                    out_ref[row : row + levels, lane : lane + cy] = state_ref[
+                    full_ref[row : row + levels, lane : lane + cy] = state_ref[
                         face, field, 2 * xp + parity
                     ]
-                row = base + xp * pairs + face // 2
-                out_ref[row : row + 1, lane : lane + cy] = coriolis_ref[
+                row = base + (2 * xp + parity) * pairs + face // 2
+                lane_at = (face % 2) * WINDOW + MARGIN
+                full_ref[row : row + 1, lane_at : lane_at + cy] = coriolis_ref[
                     face, 2 * xp + parity : 2 * xp + parity + 1
                 ]
+    for small_ref, offset in zip(small_refs, distant):
+        target = (index_x + offset + count_x) % count_x
+        starts = windows(index_x, target, count_x, index_y, cx, cy)
+        blocks = {}
+
+        def put(row, lane, lines):
+            position = lax.broadcasted_iota(jnp.int32, lines.shape, 1) % WINDOW
+            here = (position >= lane) & (position < lane + width)
+            blocks[row] = jnp.where(here, lines, blocks.get(row, jnp.zeros_like(lines)))
+
+        for field in range(fields):
+            for x in range(cx):
+                row = field * half * group + (x // 2) * group
+                at, lane = unit_place(field, x, cx, group, width)
+                shift = lane - MARGIN - (x % 2) * cy - starts[x // half] + 2 * LANES
+                put(at, lane, pltpu.roll(full_ref[row : row + group], shift % LANES, 1))
+        for part in range(2):
+            row = base + part * half * pairs
+            at, lane = unit_place(fields, part, cx, group, width)
+            shift = lane - MARGIN - starts[part] + 2 * LANES
+            lines = full_ref[row : row + group]
+            put(at, lane, pltpu.roll(lines, shift % LANES, 1))
+        for row, lines in blocks.items():
+            small_ref[row : row + group] = lines
 
 
 def step_kernel(
-    cx, cy, count_x, parts_ref, speed_hbm, edges_ref, out_ref,
-    z_ref, cor_ref, pred_ref, store_ref, tile_ref, flip_ref, speed_ref, speed_smem, sem,
+    cx, cy, count_x, near, distant, full_rows, small_rows, parts_ref, table_ref, out_ref,
+    z_ref, cor_ref, pred_ref, store_ref, tile_ref, flip_ref, speed_ref,
 ):
     fields = z_ref.shape[0]
     levels = 4
@@ -58,10 +112,9 @@
     group = pairs * levels
     half = cx // 2
     chunk = cx * group
+    width = 2 * cx
     index_x = lax.axis_index("tx")
     index_y = lax.axis_index("ty")
-    speed_copy = pltpu.make_async_copy(speed_hbm, speed_smem, sem)
-    speed_copy.start()
 
     def row_of(x):
         return (x + 4) * group
@@ -69,38 +122,68 @@
     def lanes_of(rows):
         return lax.broadcasted_iota(jnp.int32, (rows, LANES), 1)
 
-    for place in range(count_x):
-        source = place ^ index_x
+    south_half = lanes_of(group) % WINDOW < MARGIN + cy
+
+    def put_coriolis(start, x, values, at):
+        for pair in range(pairs):
+            line = values[at + pair : at + pair + 1]
+            rows = pl.ds(start + x * group + pair * levels, levels)
+            cor_ref[rows] = jnp.broadcast_to(line, (levels, LANES))
+
+    for place, offset in enumerate(near):
+        source = (index_x - offset + count_x) % count_x
         start = pl.multiple_of(source * chunk, 8)
-        low = lanes_of(group) % WINDOW < MARGIN + cy
+        top = place * full_rows
         for field in range(fields):
             for xp in range(half):
-                row = field * half * group + xp * group
-                south = parts_ref[0, place, row : row + group]
-                north = parts_ref[1, place, row : row + group]
-                even = jnp.where(low, south, pltpu.roll(north, cy, 1))
-                odd = jnp.where(low, pltpu.roll(south, LANES - cy, 1), north)
+                row = top + field * half * group + xp * group
+                south = parts_ref[0, row : row + group]
+                north = parts_ref[1, row : row + group]
+                even = jnp.where(south_half, south, pltpu.roll(north, cy, 1))
+                odd = jnp.where(south_half, pltpu.roll(south, LANES - cy, 1), north)
                 z_ref[field, pl.ds(start + row_of(2 * xp), group)] = even
                 z_ref[field, pl.ds(start + row_of(2 * xp + 1), group)] = odd
-        base = fields * half * group
-        rows = half * pairs
-        low = lanes_of(rows) % WINDOW < MARGIN + cy
-        south = parts_ref[0, place, base : base + rows]
-        north = parts_ref[1, place, base : base + rows]
-        even = jnp.where(low, south, pltpu.roll(north, cy, 1))
-        odd = jnp.where(low, pltpu.roll(south, LANES - cy, 1), north)
-        for parity, values in enumerate((even, odd)):
-            for xp in range(half):
-                for pair in range(pairs):
-                    at = start + (2 * xp + parity) * group + pair * levels
-                    line = values[xp * pairs + pair : xp * pairs + pair + 1]
-                    cor_ref[pl.ds(at, levels)] = jnp.broadcast_to(line, (levels, LANES))
-
-    speed_copy.wait()
+        for part in range(2):
+            row = top + fields * half * group + part * half * pairs
+            south = parts_ref[0, row : row + group]
+            north = parts_ref[1, row : row + group]
+            values = jnp.where(south_half, south, pltpu.roll(north, cy, 1))
+            for x in range(half):
+                put_coriolis(start, part * half + x, values, x * pairs)
+
+    for place, offset in enumerate(distant):
+        source = (index_x - offset + count_x) % count_x
+        start = pl.multiple_of(source * chunk, 8)
+        top = len(near) * full_rows + place * small_rows
+        from_south = windows(source, index_x, count_x, 0, cx, cy)
+        from_north = windows(source, index_x, count_x, 1, cx, cy)
+
+        def lines_at(at, lane, part):
+            row = top + at
+            south = parts_ref[0, row : row + group]
+            north = parts_ref[1, row : row + group]
+            south_shift = MARGIN + from_south[part] - lane + LANES
+            north_shift = MARGIN + cy + from_north[part] - lane + LANES
+            return jnp.where(
+                south_half,
+                pltpu.roll(south, south_shift % LANES, 1),
+                pltpu.roll(north, north_shift % LANES, 1),
+            )
+
+        for field in range(fields):
+            for x in range(cx):
+                at, lane = unit_place(field, x, cx, group, width)
+                z_ref[field, pl.ds(start + row_of(x), group)] = lines_at(at, lane, x // half)
+        for part in range(2):
+            at, lane = unit_place(fields, part, cx, group, width)
+            values = lines_at(at, lane, part)
+            for x in range(half):
+                put_coriolis(start, part * half + x, values, x * pairs)
+
     level_of = lax.broadcasted_iota(jnp.int32, speed_ref.shape, 0) % levels
-    speeds = jnp.full(speed_ref.shape, speed_smem[0], jnp.float32)
+    speeds = jnp.full(speed_ref.shape, table_ref[0], jnp.float32)
     for index in range(1, levels):
-        speeds = jnp.where(level_of == index, speed_smem[index], speeds)
+        speeds = jnp.where(level_of == index, table_ref[index], speeds)
     speed_ref[...] = speeds
 
     def collect():
@@ -147,10 +230,10 @@
                             )
 
     def fetch(face, side, position):
-        at = (face * 4 + side) * 3
-        neighbour = edges_ref[at]
-        far_side = edges_ref[at + 1]
-        flipped = edges_ref[at + 2]
+        at = levels + (face * 4 + side) * 3
+        neighbour = table_ref[at].astype(jnp.int32)
+        far_side = table_ref[at + 1].astype(jnp.int32)
+        flipped = table_ref[at + 2].astype(jnp.int32)
         block = store_ref[neighbour * 4 + far_side]
         order = jnp.where(flipped == 1, cells - 1 - position, position)
         order = jnp.where((position >= 0) & (position < cells), order, 0)
@@ -286,14 +369,18 @@
     faces, fields, levels, cx, cy = state.shape
     pairs = faces // 2
     group = pairs * levels
-    rows = fields * (cx // 2) * group + (cx // 2) * pairs
-    rows = -(-rows // 8) * 8
     cells = cx * count_x
+    near = (0, 1, -1)
+    distant = (4, 3, -3, 2, -2)
+    full_rows = fields * (cx // 2) * group + (cx // 2) * pairs + group
+    full_rows = -(-full_rows // 8) * 8
+    small_rows = unit_place(fields, 1, cx, group, 2 * cx)[0] + group
     packed = pl.pallas_call(
-        functools.partial(pack_kernel, cx, cy),
-        out_shape=jax.ShapeDtypeStruct((rows, LANES), jnp.float32),
+        functools.partial(pack_kernel, cx, cy, count_x, distant),
+        out_shape=[jax.ShapeDtypeStruct((full_rows, LANES), jnp.float32)]
+        + [jax.ShapeDtypeStruct((small_rows, LANES), jnp.float32)] * len(distant),
         in_specs=[pl.BlockSpec(memory_space=pltpu.HBM)] * 2,
-        out_specs=pl.BlockSpec(memory_space=pltpu.VMEM),
+        out_specs=[pl.BlockSpec(memory_space=pltpu.VMEM)] * (1 + len(distant)),
         scratch_shapes=[
             pltpu.VMEM((faces, fields, cx, levels, cy), jnp.float32),
             pltpu.VMEM((faces, cx, cy), jnp.float32),
@@ -302,39 +389,40 @@
         compiler_params=pltpu.CompilerParams(vmem_limit_bytes=VMEM_LIMIT),
         name="pack",
     )(jnp.swapaxes(state, 2, 3), coriolis)
-    chunks = [packed] * count_x
-    for other in reversed(range(1, count_x)):
-        partners = [(index, index ^ other) for index in range(count_x)]
-        chunks[other] = lax.ppermute(packed, "tx", partners)
-    parts = lax.all_gather(jnp.stack(chunks), "ty")
+
+    def moved(block, offset):
+        return lax.ppermute(
+            block, "tx", [(index, (index + offset) % count_x) for index in range(count_x)]
+        )
+
+    chunks = [packed[0]] + [moved(packed[0], offset) for offset in near[1:]]
+    chunks += [moved(block, offset) for block, offset in zip(packed[1:], distant)]
+    parts = lax.all_gather(jnp.concatenate(chunks), "ty")
+    table = jnp.concatenate([wave_speed, edges.reshape(-1).astype(jnp.float32)])
     z_rows = (cells + 8) * group
-    return jnp.swapaxes(
-        pl.pallas_call(
-            functools.partial(step_kernel, cx, cy, count_x),
-            out_shape=jax.ShapeDtypeStruct((faces, fields, cx, levels, cy), jnp.float32),
-            in_specs=[
-                pl.BlockSpec(memory_space=pltpu.VMEM),
-                pl.BlockSpec(memory_space=pltpu.HBM),
-                pl.BlockSpec(memory_space=pltpu.SMEM),
-            ],
-            out_specs=pl.BlockSpec(memory_space=pltpu.VMEM),
-            scratch_shapes=[
-                pltpu.VMEM((fields, z_rows, LANES), jnp.float32),
-                pltpu.VMEM((cells * group, LANES), jnp.float32),
-                pltpu.VMEM((z_rows, LANES), jnp.float32),
-                pltpu.VMEM((faces * 4, 32, LANES), jnp.float32),
-                pltpu.VMEM((faces, LANES, LANES), jnp.float32),
-                pltpu.VMEM((pairs, LANES, LANES), jnp.float32),
-                pltpu.VMEM(((cx + 4) * group, LANES), jnp.float32),
-                pltpu.SMEM((levels,), jnp.float32),
-                pltpu.SemaphoreType.DMA,
-            ],
-            compiler_params=pltpu.CompilerParams(vmem_limit_bytes=VMEM_LIMIT),
-            name="substeps",
-        )(parts, wave_speed, edges.reshape(-1)),
-        2,
-        3,
-    )
+    out = pl.pallas_call(
+        functools.partial(
+            step_kernel, cx, cy, count_x, near, distant, full_rows, small_rows
+        ),
+        out_shape=jax.ShapeDtypeStruct((faces, fields, cx, levels, cy), jnp.float32),
+        in_specs=[
+            pl.BlockSpec(memory_space=pltpu.VMEM),
+            pl.BlockSpec(memory_space=pltpu.SMEM),
+        ],
+        out_specs=pl.BlockSpec(memory_space=pltpu.VMEM),
+        scratch_shapes=[
+            pltpu.VMEM((fields, z_rows, LANES), jnp.float32),
+            pltpu.VMEM((cells * group, LANES), jnp.float32),
+            pltpu.VMEM((z_rows, LANES), jnp.float32),
+            pltpu.VMEM((faces * 4, 32, LANES), jnp.float32),
+            pltpu.VMEM((faces, LANES, LANES), jnp.float32),
+            pltpu.VMEM((pairs, LANES, LANES), jnp.float32),
+            pltpu.VMEM(((cx + 4) * group, LANES), jnp.float32),
+        ],
+        compiler_params=pltpu.CompilerParams(vmem_limit_bytes=VMEM_LIMIT),
+        name="substeps",
+    )(parts, table)
+    return jnp.swapaxes(out, 2, 3)
 
 
 def padded_2(block, sides, width):
@@ -503,6 +591,8 @@
         and faces % 2 == 0
         and levels == 4
         and cells_x == 6
+        and cells_y == 24
+        and count_x == 8
         and cells_x * count_x == 2 * cells_y
         and 2 * cells_y + 2 * MARGIN <= WINDOW
     )

time: 31.1 us -> 27.8 us (0.89)
  waiting for transfers between devices: 6.93 us -> 1.79 us
  starting transfers between devices: 12.6 us -> 14.7 us
    ppermute x7, waiting for transfers between devices: 6.93 us -> 1.79 us  [moved(): lax.ppermute(block, 'tx', [(index, (index + offset) % count_x) for index...]
    ppermute x7, starting transfers between devices: 12.6 us -> 14.7 us  [moved(): lax.ppermute(block, 'tx', [(index, (index + offset) % count_x) for index...]
    unnamed x16 -> x15, local copies, waits for them, and re-layouts: 2.49 us -> 2.26 us
  transfers between devices with their start and end apart: 7 -> 7, of which waited for: 2 -> 1; matrix products, arithmetic and copies ran while one was open for 1% -> 1% of each run, Pallas kernels for 0% -> 0%
where the time goes in v4:
time: 27.8 us; the launch traced here: 27.6 us
  starting transfers between devices  14.7 us (53%)
  Pallas kernels  6.17 us (22%)
  local copies, waits for them, and re-layouts  2.48 us (9%)
  blocking collectives  2.28 us (8%)
  waiting for transfers between devices  1.79 us (6%)
    ppermute x7, starting transfers between devices, moved(): lax.ppermute(block, 'tx', [(index, (index + offset) % count_x) for index...  14.7 us
    pallas_call x1, Pallas kernels, fast_on_device(): pl.pallas_call(functools.partial(step_kernel, cx, cy, count_x, near, dist...  5.39 us
    all_gather x1, blocking collectives, fast_on_device(): parts = lax.all_gather(jnp.concatenate(chunks), 'ty')  2.28 us
    unnamed x15, local copies, waits for them, and re-layouts  2.26 us
    ppermute x7, waiting for transfers between devices, moved(): lax.ppermute(block, 'tx', [(index, (index + offset) % count_x) for index...  1.79 us
    pallas_call x1, Pallas kernels, fast_on_device(): pl.pallas_call(functools.partial(pack_kernel, cx, cy, count_x, distant),...  0.78 us
  transfers between devices with their start and end apart: 7, of which 1 were waited for; matrix products, arithmetic and copies ran while one was open for 1% of the time, Pallas kernels for 0%

profile of v4, /device:TPU:0, one launch (start us, length us, event | category | flops | bytes accessed | tf_op | source)
XLA Modules:
  0.0 27.6 jit_solution(11869650537773904190)
XLA Ops:
  0.0 0.0 copy-start
  0.0 0.9 %copy-done = f32[6,3,4,6,24]{4,2,3,1,0:T(4,128)S(1)} copy-done((f32[6,3,4,6,24]{4,2,3,1,0:T(4,128)S(1)}, f32[6,3,4,6,24]{4,2,3,1,0:T(4,128)}, u32[]{:S(2)}) %copy-start) | copy-done | bytes 41496
  0.9 0.0 copy-start.1
  0.9 0.7 %copy-done.1 = f32[6,6,24]{2,1,0:T(8,128)S(1)} copy-done((f32[6,6,24]{2,1,0:T(8,128)S(1)}, f32[6,6,24]{2,1,0:T(8,128)}, u32[]{:S(2)}) %copy-start.1) | copy-done | bytes 3480
  1.7 0.8 %pack.1 = (f32[136,128]{1,0:T(8,128)S(1)}, f32[48,128]{1,0:T(8,128)S(1)}, f32[48,128]{1,0:T(8,128)S(1)}, f32[48,128]{1,0:T(8,128)S(1)}, f32[48,128]{1,0:T(8,128)S(1)}, /*index=5*/f32[48,128]{1,0:T(8,128)S(1)}) custom-call(f32[6,3,6,4,24]{4,3,2,1,0:T(4,128)S(1)} %bitcast.4, f32[6,6,24]{2,1,0:T(8,128)S(1)} %copy-done.1), custom_call_target="tpu_custom_call" | custom-call | tf_op jit(solution)/shard_map/pack/pallas_call | solution.py:378
  2.5 3.0 %collective-permute-start = (f32[136,128]{1,0:T(8,128)S(1)}, f32[136,128]{1,0:T(8,128)S(1)}, u32[]{:S(2)}, u32[]{:S(2)}) collective-permute-start(f32[136,128]{1,0:T(8,128)S(1)} %get-tuple-element.11), channel_id=1, source_target_pairs={{0,2},{2,4},{4,6},{6,8},{8,10},{10,12},{12,14},{14,0},{1,3},{3,5},... | collective-permute-start | bytes 208904 | tf_op jit(solution)/shard_map/ppermute | solution.py:394
  5.5 3.1 %collective-permute-start.1 = (f32[136,128]{1,0:T(8,128)S(1)}, f32[136,128]{1,0:T(8,128)S(1)}, u32[]{:S(2)}, u32[]{:S(2)}) collective-permute-start(f32[136,128]{1,0:T(8,128)S(1)} %get-tuple-element.11), channel_id=1, source_target_pairs={{0,14},{2,0},{4,2},{6,4},{8,6},{10,8},{12,10},{14,12},{1,15},{3,1}... | collective-permute-start | bytes 208904 | tf_op jit(solution)/shard_map/ppermute | solution.py:394
  8.6 0.9 %collective-permute-start.2 = (f32[48,128]{1,0:T(8,128)S(1)}, f32[48,128]{1,0:T(8,128)S(1)}, u32[]{:S(2)}, u32[]{:S(2)}) collective-permute-start(f32[48,128]{1,0:T(8,128)S(1)} %get-tuple-element.12), channel_id=1, source_target_pairs={{0,8},{2,10},{4,12},{6,14},{8,0},{10,2},{12,4},{14,6},{1,9},{3,11}... | collective-permute-start | bytes 73736 | tf_op jit(solution)/shard_map/ppermute | solution.py:394
  9.5 1.6 %collective-permute-start.3 = (f32[48,128]{1,0:T(8,128)S(1)}, f32[48,128]{1,0:T(8,128)S(1)}, u32[]{:S(2)}, u32[]{:S(2)}) collective-permute-start(f32[48,128]{1,0:T(8,128)S(1)} %get-tuple-element.13), channel_id=1, source_target_pairs={{0,6},{2,8},{4,10},{6,12},{8,14},{10,0},{12,2},{14,4},{1,7},{3,9},... | collective-permute-start | bytes 73736 | tf_op jit(solution)/shard_map/ppermute | solution.py:394
  11.1 0.0 copy-start.2
  11.1 2.2 %collective-permute-start.4 = (f32[48,128]{1,0:T(8,128)S(1)}, f32[48,128]{1,0:T(8,128)S(1)}, u32[]{:S(2)}, u32[]{:S(2)}) collective-permute-start(f32[48,128]{1,0:T(8,128)S(1)} %get-tuple-element.14), channel_id=1, source_target_pairs={{0,10},{2,12},{4,14},{6,0},{8,2},{10,4},{12,6},{14,8},{1,11},{3,13... | collective-permute-start | bytes 73736 | tf_op jit(solution)/shard_map/ppermute | solution.py:394
  13.3 0.0 copy-done.2
  13.3 0.1 copy.6
  13.4 0.0 copy-start.3
  13.4 0.1 convert_element_type.7
  13.5 0.6 %copy-done.3 = f32[4]{0:T(128)S(1)} copy-done((f32[4]{0:T(128)S(1)}, f32[4]{0:T(128)}, u32[]{:S(2)}) %copy-start.3) | copy-done | bytes 40
  14.1 0.1 pad_maximum_fusion.table_ref
  14.2 0.0 collective-permute-done
  14.2 1.6 %collective-permute-start.5 = (f32[48,128]{1,0:T(8,128)S(1)}, f32[48,128]{1,0:T(8,128)S(1)}, u32[]{:S(2)}, u32[]{:S(2)}) collective-permute-start(f32[48,128]{1,0:T(8,128)S(1)} %get-tuple-element.15), channel_id=1, source_target_pairs={{0,4},{2,6},{4,8},{6,10},{8,12},{10,14},{12,0},{14,2},{1,5},{3,7},... | collective-permute-start | bytes 73736 | tf_op jit(solution)/shard_map/ppermute | solution.py:394
  15.8 0.0 collective-permute-done.1
  15.8 2.3 %collective-permute-start.6 = (f32[48,128]{1,0:T(8,128)S(1)}, f32[48,128]{1,0:T(8,128)S(1)}, u32[]{:S(2)}, u32[]{:S(2)}) collective-permute-start(f32[48,128]{1,0:T(8,128)S(1)} %get-tuple-element.16), channel_id=1, source_target_pairs={{0,12},{2,14},{4,0},{6,2},{8,4},{10,6},{12,8},{14,10},{1,13},{3,15... | collective-permute-start | bytes 73736 | tf_op jit(solution)/shard_map/ppermute | solution.py:394
  18.1 0.0 collective-permute-done.2
  18.1 0.0 collective-permute-done.3
  18.1 0.0 collective-permute-done.4
  18.1 1.8 %collective-permute-done.5 = f32[48,128]{1,0:T(8,128)S(1)} collective-permute-done((f32[48,128]{1,0:T(8,128)S(1)}, f32[48,128]{1,0:T(8,128)S(1)}, u32[]{:S(2)}, u32[]{:S(2)}) %collective-permute-start.5) | collective-permute-done | bytes 24608 | tf_op jit(solution)/shard_map/ppermute | solution.py:394
  19.9 0.0 collective-permute-done.6
  19.9 2.3 %all-gather = f32[1296,128]{1,0:T(8,128)S(1)} all-gather(f32[648,128]{1,0:T(8,128)S(1)} %constant_dynamic-update-slice_fusion), channel_id=2, replica_groups=mesh['member'=2,'tx'=8,'ty'=2] {'ty'}, dimensions={0}, use_global_device_ids=true | all-gather | bytes 995328 | tf_op jit(solution)/shard_map/all_gather | solution.py:400
  22.2 5.4 %substeps.1 = f32[6,3,6,4,24]{4,3,2,1,0:T(4,128)} custom-call(f32[2,648,128]{2,1,0:T(8,128)S(1)} %bitcast.3, f32[76]{0:T(128)S(1)} %pad_maximum_fusion.table_ref), custom_call_target="tpu_custom_call" | custom-call | tf_op jit(solution)/shard_map/substeps/pallas_call | solution.py:403
  (9 shorter events, 0.0 us)
Async XLA Ops:
  0.0 0.9 %copy-start = (f32[6,3,4,6,24]{4,2,3,1,0:T(4,128)S(1)}, f32[6,3,4,6,24]{4,2,3,1,0:T(4,128)}, u32[]{:S(2)}) copy-start(f32[6,3,4,6,24]{4,2,3,1,0:T(4,128)} %param.4) | copy-start | bytes 124420
  0.9 0.7 %copy-start.1 = (f32[6,6,24]{2,1,0:T(8,128)S(1)}, f32[6,6,24]{2,1,0:T(8,128)}, u32[]{:S(2)}) copy-start(f32[6,6,24]{2,1,0:T(8,128)} %coriolis_hbm.1) | copy-start | bytes 10372
  2.5 11.7 %collective-permute-start = (f32[136,128]{1,0:T(8,128)S(1)}, f32[136,128]{1,0:T(8,128)S(1)}, u32[]{:S(2)}, u32[]{:S(2)}) collective-permute-start(f32[136,128]{1,0:T(8,128)S(1)} %get-tuple-element.11), channel_id=1, source_target_pairs={{0,2},{2,4},{4,6},{6,8},{8,10},{10,12},{12,14},{14,0},{1,3},{3,5},... | collective-permute-start | bytes 208904 | tf_op jit(solution)/shard_map/ppermute | solution.py:394
  5.5 10.3 %collective-permute-start.1 = (f32[136,128]{1,0:T(8,128)S(1)}, f32[136,128]{1,0:T(8,128)S(1)}, u32[]{:S(2)}, u32[]{:S(2)}) collective-permute-start(f32[136,128]{1,0:T(8,128)S(1)} %get-tuple-element.11), channel_id=1, source_target_pairs={{0,14},{2,0},{4,2},{6,4},{8,6},{10,8},{12,10},{14,12},{1,15},{3,1}... | collective-permute-start | bytes 208904 | tf_op jit(solution)/shard_map/ppermute | solution.py:394
  8.6 9.5 %collective-permute-start.2 = (f32[48,128]{1,0:T(8,128)S(1)}, f32[48,128]{1,0:T(8,128)S(1)}, u32[]{:S(2)}, u32[]{:S(2)}) collective-permute-start(f32[48,128]{1,0:T(8,128)S(1)} %get-tuple-element.12), channel_id=1, source_target_pairs={{0,8},{2,10},{4,12},{6,14},{8,0},{10,2},{12,4},{14,6},{1,9},{3,11}... | collective-permute-start | bytes 73736 | tf_op jit(solution)/shard_map/ppermute | solution.py:394
  9.5 8.6 %collective-permute-start.3 = (f32[48,128]{1,0:T(8,128)S(1)}, f32[48,128]{1,0:T(8,128)S(1)}, u32[]{:S(2)}, u32[]{:S(2)}) collective-permute-start(f32[48,128]{1,0:T(8,128)S(1)} %get-tuple-element.13), channel_id=1, source_target_pairs={{0,6},{2,8},{4,10},{6,12},{8,14},{10,0},{12,2},{14,4},{1,7},{3,9},... | collective-permute-start | bytes 73736 | tf_op jit(solution)/shard_map/ppermute | solution.py:394
  11.1 2.2 %copy-start.2 = (s32[6,4,3]{0,1,2:T(4,128)S(1)}, s32[6,4,3]{0,1,2:T(4,128)}, u32[]{:S(2)}) copy-start(s32[6,4,3]{0,1,2:T(4,128)} %param.7) | copy-start | bytes 868
  11.1 7.0 %collective-permute-start.4 = (f32[48,128]{1,0:T(8,128)S(1)}, f32[48,128]{1,0:T(8,128)S(1)}, u32[]{:S(2)}, u32[]{:S(2)}) collective-permute-start(f32[48,128]{1,0:T(8,128)S(1)} %get-tuple-element.14), channel_id=1, source_target_pairs={{0,10},{2,12},{4,14},{6,0},{8,2},{10,4},{12,6},{14,8},{1,11},{3,13... | collective-permute-start | bytes 73736 | tf_op jit(solution)/shard_map/ppermute | solution.py:394
  13.4 0.7 %copy-start.3 = (f32[4]{0:T(128)S(1)}, f32[4]{0:T(128)}, u32[]{:S(2)}) copy-start(f32[4]{0:T(128)} %param.6) | copy-start | bytes 52
  14.2 5.7 %collective-permute-start.5 = (f32[48,128]{1,0:T(8,128)S(1)}, f32[48,128]{1,0:T(8,128)S(1)}, u32[]{:S(2)}, u32[]{:S(2)}) collective-permute-start(f32[48,128]{1,0:T(8,128)S(1)} %get-tuple-element.15), channel_id=1, source_target_pairs={{0,4},{2,6},{4,8},{6,10},{8,12},{10,14},{12,0},{14,2},{1,5},{3,7},... | collective-permute-start | bytes 73736 | tf_op jit(solution)/shard_map/ppermute | solution.py:394
  15.8 4.1 %collective-permute-start.6 = (f32[48,128]{1,0:T(8,128)S(1)}, f32[48,128]{1,0:T(8,128)S(1)}, u32[]{:S(2)}, u32[]{:S(2)}) collective-permute-start(f32[48,128]{1,0:T(8,128)S(1)} %get-tuple-element.16), channel_id=1, source_target_pairs={{0,12},{2,14},{4,0},{6,2},{8,4},{10,6},{12,8},{14,10},{1,13},{3,15... | collective-permute-start | bytes 73736 | tf_op jit(solution)/shard_map/ppermute | solution.py:394

commit v5 on v4

--- a/solution.py
+++ b/solution.py
@@ -37,10 +37,10 @@
 
 
 def pack_kernel(
-    cx, cy, count_x, distant, state_hbm, coriolis_hbm, full_ref, *rest
+    cx, cy, count_x, full_rows, small_rows, state_hbm, coriolis_hbm,
+    swap_ref, keep_ref, middle_ref, state_ref, coriolis_ref, sems,
 ):
-    small_refs = rest[: len(distant)]
-    state_ref, coriolis_ref, sems = rest[len(distant) :]
+    full_ref = swap_ref.at[pl.ds(0, full_rows)]
     copies = [
         pltpu.make_async_copy(state_hbm, state_ref, sems.at[0]),
         pltpu.make_async_copy(coriolis_hbm, coriolis_ref, sems.at[1]),
@@ -73,7 +73,12 @@
                 full_ref[row : row + 1, lane_at : lane_at + cy] = coriolis_ref[
                     face, 2 * xp + parity : 2 * xp + parity + 1
                 ]
-    for small_ref, offset in zip(small_refs, distant):
+    sense = 1 - 2 * index_y
+    wanted = [(middle_ref, 0, count_x // 2)]
+    for place, distance in enumerate((2, 3)):
+        wanted.append((keep_ref, place * small_rows, sense * distance))
+        wanted.append((swap_ref, full_rows + place * small_rows, -sense * distance))
+    for small_ref, top, offset in wanted:
         target = (index_x + offset + count_x) % count_x
         starts = windows(index_x, target, count_x, index_y, cx, cy)
         blocks = {}
@@ -96,11 +101,11 @@
             lines = full_ref[row : row + group]
             put(at, lane, pltpu.roll(lines, shift % LANES, 1))
         for row, lines in blocks.items():
-            small_ref[row : row + group] = lines
+            small_ref[top + row : top + row + group] = lines
 
 
 def step_kernel(
-    cx, cy, count_x, near, distant, full_rows, small_rows, parts_ref, table_ref, out_ref,
+    cx, cy, count_x, full_rows, small_rows, parts_ref, table_ref, out_ref,
     z_ref, cor_ref, pred_ref, store_ref, tile_ref, flip_ref, speed_ref,
 ):
     fields = z_ref.shape[0]
@@ -130,38 +135,48 @@
             rows = pl.ds(start + x * group + pair * levels, levels)
             cor_ref[rows] = jnp.broadcast_to(line, (levels, LANES))
 
-    for place, offset in enumerate(near):
+    near = [(0, (0, 0), (1, 0))]
+    distant = []
+    for core in range(2):
+        sense = 1 - 2 * core
+        places = [(core, full_rows), (core, 2 * full_rows)]
+        near.append((sense, places[core], places[1 - core]))
+        for place, distance in enumerate((2, 3)):
+            top = 3 * full_rows + 2 * place * small_rows
+            places = [(core, top), (core, top + small_rows)]
+            distant.append((sense * distance, places[core], places[1 - core]))
+    top = 3 * full_rows + 4 * small_rows
+    distant.append((count_x // 2, (0, top), (1, top)))
+
+    for offset, (south_core, south_top), (north_core, north_top) in near:
         source = (index_x - offset + count_x) % count_x
         start = pl.multiple_of(source * chunk, 8)
-        top = place * full_rows
         for field in range(fields):
             for xp in range(half):
-                row = top + field * half * group + xp * group
-                south = parts_ref[0, row : row + group]
-                north = parts_ref[1, row : row + group]
+                row = field * half * group + xp * group
+                south = parts_ref[south_core, south_top + row : south_top + row + group]
+                north = parts_ref[north_core, north_top + row : north_top + row + group]
                 even = jnp.where(south_half, south, pltpu.roll(north, cy, 1))
                 odd = jnp.where(south_half, pltpu.roll(south, LANES - cy, 1), north)
                 z_ref[field, pl.ds(start + row_of(2 * xp), group)] = even
                 z_ref[field, pl.ds(start + row_of(2 * xp + 1), group)] = odd
         for part in range(2):
-            row = top + fields * half * group + part * half * pairs
-            south = parts_ref[0, row : row + group]
-            north = parts_ref[1, row : row + group]
+            row = fields * half * group + part * half * pairs
+            south = parts_ref[south_core, south_top + row : south_top + row + group]
+            north = parts_ref[north_core, north_top + row : north_top + row + group]
             values = jnp.where(south_half, south, pltpu.roll(north, cy, 1))
             for x in range(half):
                 put_coriolis(start, part * half + x, values, x * pairs)
 
-    for place, offset in enumerate(distant):
+    for offset, south_place, north_place in distant:
         source = (index_x - offset + count_x) % count_x
         start = pl.multiple_of(source * chunk, 8)
-        top = len(near) * full_rows + place * small_rows
         from_south = windows(source, index_x, count_x, 0, cx, cy)
         from_north = windows(source, index_x, count_x, 1, cx, cy)
 
         def lines_at(at, lane, part):
-            row = top + at
-            south = parts_ref[0, row : row + group]
-            north = parts_ref[1, row : row + group]
+            south = parts_ref[south_place[0], south_place[1] + at : south_place[1] + at + group]
+            north = parts_ref[north_place[0], north_place[1] + at : north_place[1] + at + group]
             south_shift = MARGIN + from_south[part] - lane + LANES
             north_shift = MARGIN + cy + from_north[part] - lane + LANES
             return jnp.where(
@@ -370,17 +385,18 @@
     pairs = faces // 2
     group = pairs * levels
     cells = cx * count_x
-    near = (0, 1, -1)
-    distant = (4, 3, -3, 2, -2)
     full_rows = fields * (cx // 2) * group + (cx // 2) * pairs + group
     full_rows = -(-full_rows // 8) * 8
     small_rows = unit_place(fields, 1, cx, group, 2 * cx)[0] + group
-    packed = pl.pallas_call(
-        functools.partial(pack_kernel, cx, cy, count_x, distant),
-        out_shape=[jax.ShapeDtypeStruct((full_rows, LANES), jnp.float32)]
-        + [jax.ShapeDtypeStruct((small_rows, LANES), jnp.float32)] * len(distant),
+    swap, keep, middle = pl.pallas_call(
+        functools.partial(pack_kernel, cx, cy, count_x, full_rows, small_rows),
+        out_shape=[
+            jax.ShapeDtypeStruct((full_rows + 2 * small_rows, LANES), jnp.float32),
+            jax.ShapeDtypeStruct((2 * small_rows, LANES), jnp.float32),
+            jax.ShapeDtypeStruct((small_rows, LANES), jnp.float32),
+        ],
         in_specs=[pl.BlockSpec(memory_space=pltpu.HBM)] * 2,
-        out_specs=[pl.BlockSpec(memory_space=pltpu.VMEM)] * (1 + len(distant)),
+        out_specs=[pl.BlockSpec(memory_space=pltpu.VMEM)] * 3,
         scratch_shapes=[
             pltpu.VMEM((faces, fields, cx, levels, cy), jnp.float32),
             pltpu.VMEM((faces, cx, cy), jnp.float32),
@@ -390,19 +406,36 @@
         name="pack",
     )(jnp.swapaxes(state, 2, 3), coriolis)
 
-    def moved(block, offset):
-        return lax.ppermute(
-            block, "tx", [(index, (index + offset) % count_x) for index in range(count_x)]
+    def moved(block, distance):
+        pairs_of = []
+        for index in range(count_x):
+            for core in range(2):
+                target = (index + distance * (1 - 2 * core)) % count_x
+                pairs_of.append((2 * index + core, 2 * target + core))
+        return lax.ppermute(block, ("tx", "ty"), pairs_of)
+
+    own = swap[:full_rows]
+    other = lax.ppermute(swap, "ty", [(0, 1), (1, 0)])
+    first = moved(jnp.concatenate([own, other[:full_rows]]), 1)
+    seconds = [
+        moved(
+            jnp.concatenate(
+                [
+                    keep[place * small_rows : (place + 1) * small_rows],
+                    other[full_rows + place * small_rows : full_rows + (place + 1) * small_rows],
+                ]
+            ),
+            distance,
         )
-
-    chunks = [packed[0]] + [moved(packed[0], offset) for offset in near[1:]]
-    chunks += [moved(block, offset) for block, offset in zip(packed[1:], distant)]
-    parts = lax.all_gather(jnp.concatenate(chunks), "ty")
+        for place, distance in enumerate((2, 3))
+    ]
+    last = moved(middle, count_x // 2)
+    parts = lax.all_gather(jnp.concatenate([own, first, *seconds, last]), "ty")
     table = jnp.concatenate([wave_speed, edges.reshape(-1).astype(jnp.float32)])
     z_rows = (cells + 8) * group
     out = pl.pallas_call(
         functools.partial(
-            step_kernel, cx, cy, count_x, near, distant, full_rows, small_rows
+            step_kernel, cx, cy, count_x, full_rows, small_rows
         ),
         out_shape=jax.ShapeDtypeStruct((faces, fields, cx, levels, cy), jnp.float32),
         in_specs=[

time: 27.8 us -> 26.1 us (0.939)
  starting transfers between devices: 14.7 us -> 7.66 us
  waiting for transfers between devices: 1.79 us -> 6.38 us
  local copies, waits for them, and re-layouts: 2.48 us -> 3.16 us
    ppermute x7 -> x5, starting transfers between devices: 14.7 us -> 7.66 us  [the longest x4 7.14 us: moved(): return lax.ppermute(block, ('tx', 'ty'), pairs_of)]
    ppermute x7 -> x5, waiting for transfers between devices: 1.79 us -> 6.38 us  [the longest x4 6.38 us: moved(): return lax.ppermute(block, ('tx', 'ty'), pairs_of)]
    unnamed x15 -> x11, local copies, waits for them, and re-layouts: 2.26 us -> 2.92 us
  transfers between devices with their start and end apart: 7 -> 5, of which waited for: 1 -> 2; matrix products, arithmetic and copies ran while one was open for 1% -> 1% of each run, Pallas kernels for 0% -> 0%
where the time goes in v5:
time: 26.1 us; the launch traced here: 25.8 us
  starting transfers between devices  7.66 us (29%)
  waiting for transfers between devices  6.38 us (24%)
  Pallas kernels  6.17 us (24%)
  local copies, waits for them, and re-layouts  3.16 us (12%)
  blocking collectives  2.28 us (9%)
    ppermute x4, starting transfers between devices, moved(): return lax.ppermute(block, ('tx', 'ty'), pairs_of)  7.14 us
    ppermute x4, waiting for transfers between devices, moved(): return lax.ppermute(block, ('tx', 'ty'), pairs_of)  6.38 us
    pallas_call x1, Pallas kernels, fast_on_device(): pl.pallas_call(functools.partial(step_kernel, cx, cy, count_x, full_rows,...  5.39 us
    unnamed x11, local copies, waits for them, and re-layouts  2.92 us
    all_gather x1, blocking collectives, fast_on_device(): parts = lax.all_gather(jnp.concatenate([own, first, *seconds, last]), 'ty')  2.28 us
    pallas_call x1, Pallas kernels, fast_on_device(): pl.pallas_call(functools.partial(pack_kernel, cx, cy, count_x, full_rows,...  0.78 us
  transfers between devices with their start and end apart: 5, of which 2 were waited for; matrix products, arithmetic and copies ran while one was open for 1% of the time, Pallas kernels for 0%

profile of v5, /device:TPU:0, one launch (start us, length us, event | category | flops | bytes accessed | tf_op | source)
XLA Modules:
  0.0 25.8 jit_solution(9434064522264242416)
XLA Ops:
  0.0 0.0 copy-start
  0.0 0.9 %copy-done = f32[6,3,4,6,24]{4,2,3,1,0:T(4,128)S(1)} copy-done((f32[6,3,4,6,24]{4,2,3,1,0:T(4,128)S(1)}, f32[6,3,4,6,24]{4,2,3,1,0:T(4,128)}, u32[]{:S(2)}) %copy-start) | copy-done | bytes 41496
  0.9 0.0 copy-start.1
  0.9 0.7 %copy-done.1 = f32[6,6,24]{2,1,0:T(8,128)S(1)} copy-done((f32[6,6,24]{2,1,0:T(8,128)S(1)}, f32[6,6,24]{2,1,0:T(8,128)}, u32[]{:S(2)}) %copy-start.1) | copy-done | bytes 3480
  1.7 0.8 %pack.1 = (f32[232,128]{1,0:T(8,128)S(1)}, f32[96,128]{1,0:T(8,128)S(1)}, f32[48,128]{1,0:T(8,128)S(1)}) custom-call(f32[6,3,6,4,24]{4,3,2,1,0:T(4,128)S(1)} %bitcast.4, f32[6,6,24]{2,1,0:T(8,128)S(1)} %copy-done.1), custom_call_target="tpu_custom_call" | custom-call | tf_op jit(solution)/shard_map/pack/pallas_call | solution.py:391
  2.5 0.5 %collective-permute-start = (f32[232,128]{1,0:T(8,128)S(1)}, f32[232,128]{1,0:T(8,128)S(1)}, u32[]{:S(2)}, u32[]{:S(2)}) collective-permute-start(f32[232,128]{1,0:T(8,128)S(1)} %get-tuple-element.8), channel_id=1, source_target_pairs={{0,1},{1,0},{2,3},{3,2},{4,5},{5,4},{6,7},{7,6},{8,9},{9,8},{10,11... | collective-permute-start | bytes 356360 | tf_op jit(solution)/shard_map/ppermute | solution.py:418
  3.0 3.7 %collective-permute-start.4 = (f32[48,128]{1,0:T(8,128)S(1)}, f32[48,128]{1,0:T(8,128)S(1)}, u32[]{:S(2)}, u32[]{:S(2)}) collective-permute-start(f32[48,128]{1,0:T(8,128)S(1)} %get-tuple-element.10), channel_id=1, source_target_pairs={{0,8},{1,9},{2,10},{3,11},{4,12},{5,13},{6,14},{7,15},{8,0},{9,1},... | collective-permute-start | bytes 73736 | tf_op jit(solution)/shard_map/ppermute | solution.py:415
  6.7 0.0 copy-start.2
  6.7 0.7 %copy-done.2 = s32[6,4,3]{0,1,2:T(4,128)S(1)} copy-done((s32[6,4,3]{0,1,2:T(4,128)S(1)}, s32[6,4,3]{0,1,2:T(4,128)}, u32[]{:S(2)}) %copy-start.2) | copy-done | bytes 312
  7.4 0.1 copy.6
  7.5 0.0 copy-start.3
  7.5 0.1 convert_element_type.7
  7.6 0.6 %copy-done.3 = f32[4]{0:T(128)S(1)} copy-done((f32[4]{0:T(128)S(1)}, f32[4]{0:T(128)}, u32[]{:S(2)}) %copy-start.3) | copy-done | bytes 40
  8.1 0.1 pad_maximum_fusion.3.table_ref
  8.2 0.0 collective-permute-done
  8.2 1.6 %collective-permute-start.1 = (f32[272,128]{1,0:T(8,128)S(1)}, f32[272,128]{1,0:T(8,128)S(1)}, u32[]{:S(2)}, u32[]{:S(2)}) collective-permute-start(f32[272,128]{1,0:T(8,128)S(1)} %pad_maximum_fusion), channel_id=1, source_target_pairs={{0,2},{1,15},{2,4},{3,1},{4,6},{5,3},{6,8},{7,5},{8,10},{9,7},{10,... | collective-permute-start | bytes 417800 | tf_op jit(solution)/shard_map/ppermute | solution.py:415
  9.8 1.6 %collective-permute-start.2 = (f32[96,128]{1,0:T(8,128)S(1)}, f32[96,128]{1,0:T(8,128)S(1)}, u32[]{:S(2)}, u32[]{:S(2)}) collective-permute-start(f32[96,128]{1,0:T(8,128)S(1)} %pad_maximum_fusion.1), channel_id=1, source_target_pairs={{0,4},{1,13},{2,6},{3,15},{4,8},{5,1},{6,10},{7,3},{8,12},{9,5},{1... | collective-permute-start | bytes 147464 | tf_op jit(solution)/shard_map/ppermute | solution.py:415
  11.5 0.3 %collective-permute-start.3 = (f32[96,128]{1,0:T(8,128)S(1)}, f32[96,128]{1,0:T(8,128)S(1)}, u32[]{:S(2)}, u32[]{:S(2)}) collective-permute-start(f32[96,128]{1,0:T(8,128)S(1)} %pad_maximum_fusion.2), channel_id=1, source_target_pairs={{0,6},{1,11},{2,8},{3,13},{4,10},{5,15},{6,12},{7,1},{8,14},{9,3},... | collective-permute-start | bytes 147464 | tf_op jit(solution)/shard_map/ppermute | solution.py:415
  11.7 4.8 %collective-permute-done.1 = f32[272,128]{1,0:T(8,128)S(1)} collective-permute-done((f32[272,128]{1,0:T(8,128)S(1)}, f32[272,128]{1,0:T(8,128)S(1)}, u32[]{:S(2)}, u32[]{:S(2)}) %collective-permute-start.1) | collective-permute-done | bytes 139296 | tf_op jit(solution)/shard_map/ppermute | solution.py:415
  16.6 0.0 collective-permute-done.2
  16.6 1.5 %collective-permute-done.3 = f32[96,128]{1,0:T(8,128)S(1)} collective-permute-done((f32[96,128]{1,0:T(8,128)S(1)}, f32[96,128]{1,0:T(8,128)S(1)}, u32[]{:S(2)}, u32[]{:S(2)}) %collective-permute-start.3) | collective-permute-done | bytes 49184 | tf_op jit(solution)/shard_map/ppermute | solution.py:415
  18.2 0.0 collective-permute-done.4
  18.2 2.3 %all-gather = f32[1296,128]{1,0:T(8,128)S(1)} all-gather(f32[648,128]{1,0:T(8,128)S(1)} %constant_dynamic-update-slice_fusion), channel_id=2, replica_groups=mesh['member'=2,'tx'=8,'ty'=2] {'ty'}, dimensions={0}, use_global_device_ids=true | all-gather | bytes 995328 | tf_op jit(solution)/shard_map/all_gather | solution.py:433
  20.5 5.4 %substeps.1 = f32[6,3,6,4,24]{4,3,2,1,0:T(4,128)} custom-call(f32[2,648,128]{2,1,0:T(8,128)S(1)} %bitcast.3, f32[76]{0:T(128)S(1)} %pad_maximum_fusion.3.table_ref), custom_call_target="tpu_custom_call" | custom-call | tf_op jit(solution)/shard_map/substeps/pallas_call | solution.py:436
  (12 shorter events, 0.1 us)
Async XLA Ops:
  0.0 0.9 %copy-start = (f32[6,3,4,6,24]{4,2,3,1,0:T(4,128)S(1)}, f32[6,3,4,6,24]{4,2,3,1,0:T(4,128)}, u32[]{:S(2)}) copy-start(f32[6,3,4,6,24]{4,2,3,1,0:T(4,128)} %param.4) | copy-start | bytes 124420
  0.9 0.7 %copy-start.1 = (f32[6,6,24]{2,1,0:T(8,128)S(1)}, f32[6,6,24]{2,1,0:T(8,128)}, u32[]{:S(2)}) copy-start(f32[6,6,24]{2,1,0:T(8,128)} %coriolis_hbm.1) | copy-start | bytes 10372
  2.5 5.7 %collective-permute-start = (f32[232,128]{1,0:T(8,128)S(1)}, f32[232,128]{1,0:T(8,128)S(1)}, u32[]{:S(2)}, u32[]{:S(2)}) collective-permute-start(f32[232,128]{1,0:T(8,128)S(1)} %get-tuple-element.8), channel_id=1, source_target_pairs={{0,1},{1,0},{2,3},{3,2},{4,5},{5,4},{6,7},{7,6},{8,9},{9,8},{10,11... | collective-permute-start | bytes 356360 | tf_op jit(solution)/shard_map/ppermute | solution.py:418
  3.0 15.2 %collective-permute-start.4 = (f32[48,128]{1,0:T(8,128)S(1)}, f32[48,128]{1,0:T(8,128)S(1)}, u32[]{:S(2)}, u32[]{:S(2)}) collective-permute-start(f32[48,128]{1,0:T(8,128)S(1)} %get-tuple-element.10), channel_id=1, source_target_pairs={{0,8},{1,9},{2,10},{3,11},{4,12},{5,13},{6,14},{7,15},{8,0},{9,1},... | collective-permute-start | bytes 73736 | tf_op jit(solution)/shard_map/ppermute | solution.py:415
  6.7 0.7 %copy-start.2 = (s32[6,4,3]{0,1,2:T(4,128)S(1)}, s32[6,4,3]{0,1,2:T(4,128)}, u32[]{:S(2)}) copy-start(s32[6,4,3]{0,1,2:T(4,128)} %param.7) | copy-start | bytes 868
  7.5 0.7 %copy-start.3 = (f32[4]{0:T(128)S(1)}, f32[4]{0:T(128)}, u32[]{:S(2)}) copy-start(f32[4]{0:T(128)} %param.6) | copy-start | bytes 52
  8.2 8.3 %collective-permute-start.1 = (f32[272,128]{1,0:T(8,128)S(1)}, f32[272,128]{1,0:T(8,128)S(1)}, u32[]{:S(2)}, u32[]{:S(2)}) collective-permute-start(f32[272,128]{1,0:T(8,128)S(1)} %pad_maximum_fusion), channel_id=1, source_target_pairs={{0,2},{1,15},{2,4},{3,1},{4,6},{5,3},{6,8},{7,5},{8,10},{9,7},{10,... | collective-permute-start | bytes 417800 | tf_op jit(solution)/shard_map/ppermute | solution.py:415
  9.8 6.8 %collective-permute-start.2 = (f32[96,128]{1,0:T(8,128)S(1)}, f32[96,128]{1,0:T(8,128)S(1)}, u32[]{:S(2)}, u32[]{:S(2)}) collective-permute-start(f32[96,128]{1,0:T(8,128)S(1)} %pad_maximum_fusion.1), channel_id=1, source_target_pairs={{0,4},{1,13},{2,6},{3,15},{4,8},{5,1},{6,10},{7,3},{8,12},{9,5},{1... | collective-permute-start | bytes 147464 | tf_op jit(solution)/shard_map/ppermute | solution.py:415
  11.5 6.7 %collective-permute-start.3 = (f32[96,128]{1,0:T(8,128)S(1)}, f32[96,128]{1,0:T(8,128)S(1)}, u32[]{:S(2)}, u32[]{:S(2)}) collective-permute-start(f32[96,128]{1,0:T(8,128)S(1)} %pad_maximum_fusion.2), channel_id=1, source_target_pairs={{0,6},{1,11},{2,8},{3,13},{4,10},{5,15},{6,12},{7,1},{8,14},{9,3},... | collective-permute-start | bytes 147464 | tf_op jit(solution)/shard_map/ppermute | solution.py:415

commit v6 on v5

--- a/solution.py
+++ b/solution.py
@@ -38,7 +38,7 @@
 
 def pack_kernel(
     cx, cy, count_x, full_rows, small_rows, state_hbm, coriolis_hbm,
-    swap_ref, keep_ref, middle_ref, state_ref, coriolis_ref, sems,
+    swap_ref, keep_ref, middle_ref, state_ref, coriolis_ref, line_ref, sems,
 ):
     full_ref = swap_ref.at[pl.ds(0, full_rows)]
     copies = [
@@ -57,6 +57,7 @@
     index_x = lax.axis_index("tx")
     index_y = lax.axis_index("ty")
     full_ref[...] = jnp.zeros(full_ref.shape, jnp.float32)
+    line_ref[...] = jnp.zeros(line_ref.shape, jnp.float32)
     for copy in copies:
         copy.wait()
     for face in range(faces):
@@ -68,11 +69,12 @@
                     full_ref[row : row + levels, lane : lane + cy] = state_ref[
                         face, field, 2 * xp + parity
                     ]
-                row = base + (2 * xp + parity) * pairs + face // 2
+                x = 2 * xp + parity
+                row = base + xp * pairs + face // 2
+                full_ref[row : row + 1, lane : lane + cy] = coriolis_ref[face, x : x + 1]
+                row = (x // half) * 16 + (x % half) * pairs + face // 2
                 lane_at = (face % 2) * WINDOW + MARGIN
-                full_ref[row : row + 1, lane_at : lane_at + cy] = coriolis_ref[
-                    face, 2 * xp + parity : 2 * xp + parity + 1
-                ]
+                line_ref[row : row + 1, lane_at : lane_at + cy] = coriolis_ref[face, x : x + 1]
     sense = 1 - 2 * index_y
     wanted = [(middle_ref, 0, count_x // 2)]
     for place, distance in enumerate((2, 3)):
@@ -95,18 +97,17 @@
                 shift = lane - MARGIN - (x % 2) * cy - starts[x // half] + 2 * LANES
                 put(at, lane, pltpu.roll(full_ref[row : row + group], shift % LANES, 1))
         for part in range(2):
-            row = base + part * half * pairs
             at, lane = unit_place(fields, part, cx, group, width)
             shift = lane - MARGIN - starts[part] + 2 * LANES
-            lines = full_ref[row : row + group]
+            lines = line_ref[16 * part : 16 * part + group]
             put(at, lane, pltpu.roll(lines, shift % LANES, 1))
         for row, lines in blocks.items():
             small_ref[top + row : top + row + group] = lines
 
 
 def step_kernel(
-    cx, cy, count_x, full_rows, small_rows, parts_ref, table_ref, out_ref,
-    z_ref, cor_ref, pred_ref, store_ref, tile_ref, flip_ref, speed_ref,
+    cx, cy, count_x, full_rows, small_rows, own_ref, other_ref, near_ref, near_other_ref,
+    far_ref, far_other_ref, table_ref, out_ref, z_ref, cor_ref, pred_ref, store_ref, tile_ref, flip_ref, speed_ref,
 ):
     fields = z_ref.shape[0]
     levels = 4
@@ -128,6 +129,12 @@
         return lax.broadcasted_iota(jnp.int32, (rows, LANES), 1)
 
     south_half = lanes_of(group) % WINDOW < MARGIN + cy
+    south_is_own = index_y == 0
+    own_half = south_half == south_is_own
+
+    def from_owner(offset):
+        source = (index_x - offset + 2 * count_x) % count_x
+        return source, pl.multiple_of(source * chunk, 8)
 
     def put_coriolis(start, x, values, at):
         for pair in range(pairs):
@@ -135,65 +142,86 @@
             rows = pl.ds(start + x * group + pair * levels, levels)
             cor_ref[rows] = jnp.broadcast_to(line, (levels, LANES))
 
-    near = [(0, (0, 0), (1, 0))]
-    distant = []
-    for core in range(2):
-        sense = 1 - 2 * core
-        places = [(core, full_rows), (core, 2 * full_rows)]
-        near.append((sense, places[core], places[1 - core]))
-        for place, distance in enumerate((2, 3)):
-            top = 3 * full_rows + 2 * place * small_rows
-            places = [(core, top), (core, top + small_rows)]
-            distant.append((sense * distance, places[core], places[1 - core]))
-    top = 3 * full_rows + 4 * small_rows
-    distant.append((count_x // 2, (0, top), (1, top)))
-
-    for offset, (south_core, south_top), (north_core, north_top) in near:
-        source = (index_x - offset + count_x) % count_x
-        start = pl.multiple_of(source * chunk, 8)
+    def put_block(start, lines_of):
+        base = fields * half * group
         for field in range(fields):
             for xp in range(half):
-                row = field * half * group + xp * group
-                south = parts_ref[south_core, south_top + row : south_top + row + group]
-                north = parts_ref[north_core, north_top + row : north_top + row + group]
-                even = jnp.where(south_half, south, pltpu.roll(north, cy, 1))
-                odd = jnp.where(south_half, pltpu.roll(south, LANES - cy, 1), north)
+                even, odd = lines_of(field * half * group + xp * group, group)
                 z_ref[field, pl.ds(start + row_of(2 * xp), group)] = even
                 z_ref[field, pl.ds(start + row_of(2 * xp + 1), group)] = odd
+        for parity, values in enumerate(lines_of(base, half * pairs)):
+            for xp in range(half):
+                put_coriolis(start, 2 * xp + parity, values, xp * pairs)
+
+    def put_distant(source, start, lines_of):
+        starts_south = windows(source, index_x, count_x, 0, cx, cy)
+        starts_north = windows(source, index_x, count_x, 1, cx, cy)
+
+        def lines_at(field, x, part):
+            at, lane = unit_place(field, x, cx, group, width)
+            south_shift = (MARGIN + starts_south[part] - lane + LANES) % LANES
+            north_shift = (MARGIN + cy + starts_north[part] - lane + LANES) % LANES
+            return lines_of(at, south_shift, north_shift)
+
+        for field in range(fields):
+            for x in range(cx):
+                z_ref[field, pl.ds(start + row_of(x), group)] = lines_at(field, x, x // half)
         for part in range(2):
-            row = fields * half * group + part * half * pairs
-            south = parts_ref[south_core, south_top + row : south_top + row + group]
-            north = parts_ref[north_core, north_top + row : north_top + row + group]
-            values = jnp.where(south_half, south, pltpu.roll(north, cy, 1))
+            values = lines_at(fields, part, part)
             for x in range(half):
                 put_coriolis(start, part * half + x, values, x * pairs)
 
-    for offset, south_place, north_place in distant:
-        source = (index_x - offset + count_x) % count_x
-        start = pl.multiple_of(source * chunk, 8)
-        from_south = windows(source, index_x, count_x, 0, cx, cy)
-        from_north = windows(source, index_x, count_x, 1, cx, cy)
-
-        def lines_at(at, lane, part):
-            south = parts_ref[south_place[0], south_place[1] + at : south_place[1] + at + group]
-            north = parts_ref[north_place[0], north_place[1] + at : north_place[1] + at + group]
-            south_shift = MARGIN + from_south[part] - lane + LANES
-            north_shift = MARGIN + cy + from_north[part] - lane + LANES
-            return jnp.where(
-                south_half,
-                pltpu.roll(south, south_shift % LANES, 1),
-                pltpu.roll(north, north_shift % LANES, 1),
-            )
-
-        for field in range(fields):
-            for x in range(cx):
-                at, lane = unit_place(field, x, cx, group, width)
-                z_ref[field, pl.ds(start + row_of(x), group)] = lines_at(at, lane, x // half)
-        for part in range(2):
-            at, lane = unit_place(fields, part, cx, group, width)
-            values = lines_at(at, lane, part)
-            for x in range(half):
-                put_coriolis(start, part * half + x, values, x * pairs)
+    def own_lines(row, rows):
+        mine = own_ref[row : row + rows]
+        theirs = other_ref[row : row + rows]
+        up, down = index_y * cy, (1 - index_y) * cy
+        even = jnp.where(own_half[:rows], pltpu.roll(mine, up, 1), pltpu.roll(theirs, down, 1))
+        mine = pltpu.roll(mine, (LANES - down) % LANES, 1)
+        theirs = pltpu.roll(theirs, (LANES - up) % LANES, 1)
+        return even, jnp.where(own_half[:rows], mine, theirs)
+
+    put_block(from_owner(0)[1], own_lines)
+
+    sense = 1 - 2 * index_y
+    for block_ref, far_block_ref, toward, south_first in (
+        (near_ref, far_ref, sense, index_y),
+        (near_other_ref, far_other_ref, -sense, 1 - index_y),
+    ):
+        south_top = pl.multiple_of(south_first * full_rows, 8)
+        north_top = pl.multiple_of((1 - south_first) * full_rows, 8)
+
+        def near_lines(row, rows, block_ref=block_ref, south_top=south_top, north_top=north_top):
+            south = block_ref[pl.ds(south_top + row, rows)]
+            north = block_ref[pl.ds(north_top + row, rows)]
+            low = south_half[:rows]
+            even = jnp.where(low, south, pltpu.roll(north, cy, 1))
+            return even, jnp.where(low, pltpu.roll(south, LANES - cy, 1), north)
+
+        put_block(from_owner(toward)[1], near_lines)
+        for place, distance in enumerate((2, 3)):
+            top = 2 * place * small_rows
+            south_top = pl.multiple_of(top + south_first * small_rows, 8)
+            north_top = pl.multiple_of(top + (1 - south_first) * small_rows, 8)
+
+            def far_lines(
+                at, south_shift, north_shift,
+                block_ref=far_block_ref, south_top=south_top, north_top=north_top,
+            ):
+                south = block_ref[pl.ds(south_top + at, group)]
+                north = block_ref[pl.ds(north_top + at, group)]
+                south = pltpu.roll(south, south_shift, 1)
+                return jnp.where(south_half, south, pltpu.roll(north, north_shift, 1))
+
+            put_distant(*from_owner(toward * distance), far_lines)
+
+    def middle_lines(at, south_shift, north_shift):
+        row = 4 * small_rows + at
+        mine_shift = jnp.where(south_is_own, south_shift, north_shift)
+        other_shift = jnp.where(south_is_own, north_shift, south_shift)
+        mine = pltpu.roll(far_ref[row : row + group], mine_shift, 1)
+        return jnp.where(own_half, mine, pltpu.roll(far_other_ref[row : row + group], other_shift, 1))
+
+    put_distant(*from_owner(count_x // 2), middle_lines)
 
     level_of = lax.broadcasted_iota(jnp.int32, speed_ref.shape, 0) % levels
     speeds = jnp.full(speed_ref.shape, table_ref[0], jnp.float32)
@@ -385,7 +413,7 @@
     pairs = faces // 2
     group = pairs * levels
     cells = cx * count_x
-    full_rows = fields * (cx // 2) * group + (cx // 2) * pairs + group
+    full_rows = fields * (cx // 2) * group + (cx // 2) * pairs
     full_rows = -(-full_rows // 8) * 8
     small_rows = unit_place(fields, 1, cx, group, 2 * cx)[0] + group
     swap, keep, middle = pl.pallas_call(
@@ -400,6 +428,7 @@
         scratch_shapes=[
             pltpu.VMEM((faces, fields, cx, levels, cy), jnp.float32),
             pltpu.VMEM((faces, cx, cy), jnp.float32),
+            pltpu.VMEM((32, LANES), jnp.float32),
             pltpu.SemaphoreType.DMA((2,)),
         ],
         compiler_params=pltpu.CompilerParams(vmem_limit_bytes=VMEM_LIMIT),
@@ -414,8 +443,12 @@
                 pairs_of.append((2 * index + core, 2 * target + core))
         return lax.ppermute(block, ("tx", "ty"), pairs_of)
 
+    def across(block):
+        return lax.ppermute(block, "ty", [(0, 1), (1, 0)])
+
     own = swap[:full_rows]
-    other = lax.ppermute(swap, "ty", [(0, 1), (1, 0)])
+    other = across(swap)
+    wave_speed, edges, other = lax.optimization_barrier((wave_speed, edges, other))
     first = moved(jnp.concatenate([own, other[:full_rows]]), 1)
     seconds = [
         moved(
@@ -429,8 +462,8 @@
         )
         for place, distance in enumerate((2, 3))
     ]
-    last = moved(middle, count_x // 2)
-    parts = lax.all_gather(jnp.concatenate([own, first, *seconds, last]), "ty")
+    far = jnp.concatenate([*seconds, moved(middle, count_x // 2)])
+    pieces = (own, other, first, across(first), far, across(far))
     table = jnp.concatenate([wave_speed, edges.reshape(-1).astype(jnp.float32)])
     z_rows = (cells + 8) * group
     out = pl.pallas_call(
@@ -438,10 +471,8 @@
             step_kernel, cx, cy, count_x, full_rows, small_rows
         ),
         out_shape=jax.ShapeDtypeStruct((faces, fields, cx, levels, cy), jnp.float32),
-        in_specs=[
-            pl.BlockSpec(memory_space=pltpu.VMEM),
-            pl.BlockSpec(memory_space=pltpu.SMEM),
-        ],
+        in_specs=[pl.BlockSpec(memory_space=pltpu.VMEM)] * 6
+        + [pl.BlockSpec(memory_space=pltpu.SMEM)],
         out_specs=pl.BlockSpec(memory_space=pltpu.VMEM),
         scratch_shapes=[
             pltpu.VMEM((fields, z_rows, LANES), jnp.float32),
@@ -454,7 +485,7 @@
         ],
         compiler_params=pltpu.CompilerParams(vmem_limit_bytes=VMEM_LIMIT),
         name="substeps",
-    )(parts, table)
+    )(*pieces, table)
     return jnp.swapaxes(out, 2, 3)
 
 

time: 26.1 us -> 25.8 us (0.989)
  blocking collectives: 2.28 us -> 0 us
  waiting for transfers between devices: 6.38 us -> 8.47 us
    all_gather x1 -> x0, blocking collectives: 2.28 us -> none  [fast_on_device(): parts = lax.all_gather(jnp.concatenate([own, first, *seconds, last]), 'ty')]
    ppermute x1 -> x3, waiting for transfers between devices: 0.01 us -> 1.78 us  [across(): return lax.ppermute(block, 'ty', [(0, 1), (1, 0)])]
    ppermute x1 -> x3, starting transfers between devices: 0.52 us -> 0.08 us  [across(): return lax.ppermute(block, 'ty', [(0, 1), (1, 0)])]
    ppermute x4, starting transfers between devices: 7.14 us -> 7.53 us  [moved(): return lax.ppermute(block, ('tx', 'ty'), pairs_of)]
    ppermute x4, waiting for transfers between devices: 6.38 us -> 6.69 us  [moved(): return lax.ppermute(block, ('tx', 'ty'), pairs_of)]
    unnamed x11 -> x14, local copies, waits for them, and re-layouts: 2.92 us -> 2.88 us
  transfers between devices with their start and end apart: 5 -> 7, of which waited for: 2 -> 5; matrix products, arithmetic and copies ran while one was open for 1% -> 1% of each run, Pallas kernels for 0% -> 0%
where the time goes in v6:
time: 25.8 us; the launch traced here: 25.6 us
  waiting for transfers between devices  8.47 us (33%)
  starting transfers between devices  7.61 us (29%)
  Pallas kernels  6.27 us (24%)
  local copies, waits for them, and re-layouts  3.11 us (12%)
    ppermute x4, starting transfers between devices, moved(): return lax.ppermute(block, ('tx', 'ty'), pairs_of)  7.53 us
    ppermute x4, waiting for transfers between devices, moved(): return lax.ppermute(block, ('tx', 'ty'), pairs_of)  6.69 us
    pallas_call x1, Pallas kernels, fast_on_device(): pl.pallas_call(functools.partial(step_kernel, cx, cy, count_x, full_rows,...  5.45 us
    unnamed x14, local copies, waits for them, and re-layouts  2.88 us
    ppermute x3, waiting for transfers between devices, across(): return lax.ppermute(block, 'ty', [(0, 1), (1, 0)])  1.78 us
    pallas_call x1, Pallas kernels, fast_on_device(): pl.pallas_call(functools.partial(pack_kernel, cx, cy, count_x, full_rows,...  0.82 us
  transfers between devices with their start and end apart: 7, of which 5 were waited for; matrix products, arithmetic and copies ran while one was open for 1% of the time, Pallas kernels for 0%

profile of v6, /device:TPU:0, one launch (start us, length us, event | category | flops | bytes accessed | tf_op | source)
XLA Modules:
  0.0 25.6 jit_solution(6098961038219622028)
XLA Ops:
  0.0 0.0 copy-start.2
  0.0 0.9 %copy-done.2 = f32[6,3,4,6,24]{4,2,3,1,0:T(4,128)S(1)} copy-done((f32[6,3,4,6,24]{4,2,3,1,0:T(4,128)S(1)}, f32[6,3,4,6,24]{4,2,3,1,0:T(4,128)}, u32[]{:S(2)}) %copy-start.2) | copy-done | bytes 41496
  0.9 0.0 copy-start.3
  0.9 0.7 %copy-done.3 = f32[6,6,24]{2,1,0:T(8,128)S(1)} copy-done((f32[6,6,24]{2,1,0:T(8,128)S(1)}, f32[6,6,24]{2,1,0:T(8,128)}, u32[]{:S(2)}) %copy-start.3) | copy-done | bytes 3480
  1.7 0.8 %pack.1 = (f32[216,128]{1,0:T(8,128)S(1)}, f32[96,128]{1,0:T(8,128)S(1)}, f32[48,128]{1,0:T(8,128)S(1)}) custom-call(f32[6,3,6,4,24]{4,3,2,1,0:T(4,128)S(1)} %bitcast.2, f32[6,6,24]{2,1,0:T(8,128)S(1)} %copy-done.3), custom_call_target="tpu_custom_call" | custom-call | tf_op jit(solution)/shard_map/pack/pallas_call | solution.py:419
  2.5 4.1 %collective-permute-start.5 = (f32[48,128]{1,0:T(8,128)S(1)}, f32[48,128]{1,0:T(8,128)S(1)}, u32[]{:S(2)}, u32[]{:S(2)}) collective-permute-start(f32[48,128]{1,0:T(8,128)S(1)} %get-tuple-element.14), channel_id=1, source_target_pairs={{0,8},{1,9},{2,10},{3,11},{4,12},{5,13},{6,14},{7,15},{8,0},{9,1},... | collective-permute-start | bytes 73736 | tf_op jit(solution)/shard_map/ppermute | solution.py:444
  6.6 0.0 collective-permute-start
  6.6 1.3 %collective-permute-done.other_ref = f32[216,128]{1,0:T(8,128)S(1)} collective-permute-done((f32[216,128]{1,0:T(8,128)S(1)}, f32[216,128]{1,0:T(8,128)S(1)}, u32[]{:S(2)}, u32[]{:S(2)}) %collective-permute-start) | collective-permute-done | bytes 110624 | tf_op jit(solution)/shard_map/ppermute | solution.py:447
  7.9 0.0 copy-start
  7.9 0.6 %copy-done = f32[216,128]{1,0:T(8,128)} copy-done((f32[216,128]{1,0:T(8,128)}, f32[216,128]{1,0:T(8,128)S(1)}, u32[]{:S(2)}) %copy-start) | copy-done | bytes 110616
  8.6 0.0 slice-start
  8.6 1.6 %collective-permute-start.3 = (f32[96,128]{1,0:T(8,128)S(1)}, f32[96,128]{1,0:T(8,128)S(1)}, u32[]{:S(2)}, u32[]{:S(2)}) collective-permute-start(f32[96,128]{1,0:T(8,128)S(1)} %pad_maximum_fusion.1), channel_id=1, source_target_pairs={{0,4},{1,13},{2,6},{3,15},{4,8},{5,1},{6,10},{7,3},{8,12},{9,5},{1... | collective-permute-start | bytes 147464 | tf_op jit(solution)/shard_map/ppermute | solution.py:444
  10.2 1.0 %collective-permute-start.4 = (f32[96,128]{1,0:T(8,128)S(1)}, f32[96,128]{1,0:T(8,128)S(1)}, u32[]{:S(2)}, u32[]{:S(2)}) collective-permute-start(f32[96,128]{1,0:T(8,128)S(1)} %pad_maximum_fusion.2), channel_id=1, source_target_pairs={{0,6},{1,11},{2,8},{3,13},{4,10},{5,15},{6,12},{7,1},{8,14},{9,3},... | collective-permute-start | bytes 147464 | tf_op jit(solution)/shard_map/ppermute | solution.py:444
  11.2 0.0 slice-done
  11.2 0.8 %collective-permute-start.1 = (f32[240,128]{1,0:T(8,128)S(1)}, f32[240,128]{1,0:T(8,128)S(1)}, u32[]{:S(2)}, u32[]{:S(2)}) collective-permute-start(f32[240,128]{1,0:T(8,128)S(1)} %pad_maximum_fusion), channel_id=1, source_target_pairs={{0,2},{1,15},{2,4},{3,1},{4,6},{5,3},{6,8},{7,5},{8,10},{9,7},{10,... | collective-permute-start | bytes 368648 | tf_op jit(solution)/shard_map/ppermute | solution.py:444
  12.0 2.7 %collective-permute-done.3 = f32[96,128]{1,0:T(8,128)S(1)} collective-permute-done((f32[96,128]{1,0:T(8,128)S(1)}, f32[96,128]{1,0:T(8,128)S(1)}, u32[]{:S(2)}, u32[]{:S(2)}) %collective-permute-start.3) | collective-permute-done | bytes 49184 | tf_op jit(solution)/shard_map/ppermute | solution.py:444
  14.7 0.0 copy-start.1
  14.7 1.9 %collective-permute-done.4 = f32[96,128]{1,0:T(8,128)S(1)} collective-permute-done((f32[96,128]{1,0:T(8,128)S(1)}, f32[96,128]{1,0:T(8,128)S(1)}, u32[]{:S(2)}, u32[]{:S(2)}) %collective-permute-start.4) | collective-permute-done | bytes 49184 | tf_op jit(solution)/shard_map/ppermute | solution.py:444
  16.6 0.0 copy-start.4
  16.6 0.0 collective-permute-done.5
  16.7 0.1 collective-permute-start.6
  16.7 2.1 %collective-permute-done.1.near_ref = f32[240,128]{1,0:T(8,128)S(1)} collective-permute-done((f32[240,128]{1,0:T(8,128)S(1)}, f32[240,128]{1,0:T(8,128)S(1)}, u32[]{:S(2)}, u32[]{:S(2)}) %collective-permute-start.1) | collective-permute-done | bytes 122912 | tf_op jit(solution)/shard_map/ppermute | solution.py:444
  18.8 0.0 collective-permute-start.2
  18.8 0.0 copy-done.4
  18.8 0.1 copy.6
  19.0 0.1 convert_element_type.7
  19.1 0.6 %copy-done.5 = f32[4]{0:T(128)S(1)} copy-done((f32[4]{0:T(128)S(1)}, f32[4]{0:T(128)}, u32[]{:S(2)}) %copy-start.5) | copy-done | bytes 40
  19.6 0.1 pad_maximum_fusion.3.table_ref
  19.7 0.0 collective-permute-done.6.far_other_ref
  19.7 0.5 %collective-permute-done.2.near_other_ref = f32[240,128]{1,0:T(8,128)S(1)} collective-permute-done((f32[240,128]{1,0:T(8,128)S(1)}, f32[240,128]{1,0:T(8,128)S(1)}, u32[]{:S(2)}, u32[]{:S(2)}) %collective-permute-start.2) | collective-permute-done | bytes 122912 | tf_op jit(solution)/shard_map/ppermute | solution.py:447
  20.2 0.0 copy-done.1
  20.2 5.5 %substeps.1 = f32[6,3,6,4,24]{4,3,2,1,0:T(4,128)} custom-call(f32[120,128]{1,0:T(8,128)S(1)} %slice.18.own_ref, f32[216,128]{1,0:T(8,128)S(1)} %copy-done.1, f32[240,128]{1,0:T(8,128)S(1)} %collective-permute-done.1.near_ref, f32[240,128]{1,0:T(8,128)S(1)} %collective-permute-done.2.near_other_ref, f32[240,128]{1,0:T(8,128)S(1)} %constant_dynamic-update-slice_fusion.far_ref, ...), custom_call_target="tpu_custom_call" | custom-call | tf_op jit(solution)/shard_map/substeps/pallas_call | solution.py:469
  (11 shorter events, 0.0 us)
Async XLA Ops:
  0.0 0.9 %copy-start.2 = (f32[6,3,4,6,24]{4,2,3,1,0:T(4,128)S(1)}, f32[6,3,4,6,24]{4,2,3,1,0:T(4,128)}, u32[]{:S(2)}) copy-start(f32[6,3,4,6,24]{4,2,3,1,0:T(4,128)} %param.4) | copy-start | bytes 124420
  0.9 0.7 %copy-start.3 = (f32[6,6,24]{2,1,0:T(8,128)S(1)}, f32[6,6,24]{2,1,0:T(8,128)}, u32[]{:S(2)}) copy-start(f32[6,6,24]{2,1,0:T(8,128)} %coriolis_hbm.1) | copy-start | bytes 10372
  2.5 14.1 %collective-permute-start.5 = (f32[48,128]{1,0:T(8,128)S(1)}, f32[48,128]{1,0:T(8,128)S(1)}, u32[]{:S(2)}, u32[]{:S(2)}) collective-permute-start(f32[48,128]{1,0:T(8,128)S(1)} %get-tuple-element.14), channel_id=1, source_target_pairs={{0,8},{1,9},{2,10},{3,11},{4,12},{5,13},{6,14},{7,15},{8,0},{9,1},... | collective-permute-start | bytes 73736 | tf_op jit(solution)/shard_map/ppermute | solution.py:444
  6.6 1.3 %collective-permute-start = (f32[216,128]{1,0:T(8,128)S(1)}, f32[216,128]{1,0:T(8,128)S(1)}, u32[]{:S(2)}, u32[]{:S(2)}) collective-permute-start(f32[216,128]{1,0:T(8,128)S(1)} %get-tuple-element.11), channel_id=1, source_target_pairs={{0,1},{1,0},{2,3},{3,2},{4,5},{5,4},{6,7},{7,6},{8,9},{9,8},{10,11... | collective-permute-start | bytes 331784 | tf_op jit(solution)/shard_map/ppermute | solution.py:447
  7.9 0.6 %copy-start = (f32[216,128]{1,0:T(8,128)}, f32[216,128]{1,0:T(8,128)S(1)}, u32[]{:S(2)}) copy-start(f32[216,128]{1,0:T(8,128)S(1)} %collective-permute-done.other_ref) | copy-start | bytes 331780
  8.6 2.6 %slice-start = ((f32[216,128]{1,0:T(8,128)}), f32[120,128]{1,0:T(8,128)S(1)}, s32[]{:S(2)}) async-start(f32[216,128]{1,0:T(8,128)} %copy-done), calls=%async_computation | async-start | bytes 122880 | tf_op jit(solution)/shard_map/slice | solution.py:452
  8.6 6.1 %collective-permute-start.3 = (f32[96,128]{1,0:T(8,128)S(1)}, f32[96,128]{1,0:T(8,128)S(1)}, u32[]{:S(2)}, u32[]{:S(2)}) collective-permute-start(f32[96,128]{1,0:T(8,128)S(1)} %pad_maximum_fusion.1), channel_id=1, source_target_pairs={{0,4},{1,13},{2,6},{3,15},{4,8},{5,1},{6,10},{7,3},{8,12},{9,5},{1... | collective-permute-start | bytes 147464 | tf_op jit(solution)/shard_map/ppermute | solution.py:444
  10.2 6.5 %collective-permute-start.4 = (f32[96,128]{1,0:T(8,128)S(1)}, f32[96,128]{1,0:T(8,128)S(1)}, u32[]{:S(2)}, u32[]{:S(2)}) collective-permute-start(f32[96,128]{1,0:T(8,128)S(1)} %pad_maximum_fusion.2), channel_id=1, source_target_pairs={{0,6},{1,11},{2,8},{3,13},{4,10},{5,15},{6,12},{7,1},{8,14},{9,3},... | collective-permute-start | bytes 147464 | tf_op jit(solution)/shard_map/ppermute | solution.py:444
  11.2 7.6 %collective-permute-start.1 = (f32[240,128]{1,0:T(8,128)S(1)}, f32[240,128]{1,0:T(8,128)S(1)}, u32[]{:S(2)}, u32[]{:S(2)}) collective-permute-start(f32[240,128]{1,0:T(8,128)S(1)} %pad_maximum_fusion), channel_id=1, source_target_pairs={{0,2},{1,15},{2,4},{3,1},{4,6},{5,3},{6,8},{7,5},{8,10},{9,7},{10,... | collective-permute-start | bytes 368648 | tf_op jit(solution)/shard_map/ppermute | solution.py:444
  14.7 5.5 %copy-start.1 = (f32[216,128]{1,0:T(8,128)S(1)}, f32[216,128]{1,0:T(8,128)}, u32[]{:S(2)}) copy-start(f32[216,128]{1,0:T(8,128)} %copy-done) | copy-start | bytes 331780
  16.6 2.2 %copy-start.4 = (s32[6,4,3]{0,1,2:T(4,128)S(1)}, s32[6,4,3]{0,1,2:T(4,128)}, u32[]{:S(2)}) copy-start(s32[6,4,3]{0,1,2:T(4,128)} %param.7) | copy-start | bytes 868
  16.7 3.0 %collective-permute-start.6 = (f32[240,128]{1,0:T(8,128)S(1)}, f32[240,128]{1,0:T(8,128)S(1)}, u32[]{:S(2)}, u32[]{:S(2)}) collective-permute-start(f32[240,128]{1,0:T(8,128)S(1)} %constant_dynamic-update-slice_fusion.far_ref), channel_id=1, source_target_pairs={{0,1},{1,0},{2,3},{3,2},{4,5},{5,4},{6,7},{7,6},{8,9},{9,8},{10,11... | collective-permute-start | bytes 368648 | tf_op jit(solution)/shard_map/ppermute | solution.py:447
  18.8 1.3 %collective-permute-start.2 = (f32[240,128]{1,0:T(8,128)S(1)}, f32[240,128]{1,0:T(8,128)S(1)}, u32[]{:S(2)}, u32[]{:S(2)}) collective-permute-start(f32[240,128]{1,0:T(8,128)S(1)} %collective-permute-done.1.near_ref), channel_id=1, source_target_pairs={{0,1},{1,0},{2,3},{3,2},{4,5},{5,4},{6,7},{7,6},{8,9},{9,8},{10,11... | collective-permute-start | bytes 368648 | tf_op jit(solution)/shard_map/ppermute | solution.py:447
  19.0 0.7 %copy-start.5 = (f32[4]{0:T(128)S(1)}, f32[4]{0:T(128)}, u32[]{:S(2)}) copy-start(f32[4]{0:T(128)} %param.6) | copy-start | bytes 52

commit v7 on v6

--- a/solution.py
+++ b/solution.py
@@ -105,9 +105,19 @@
             small_ref[top + row : top + row + group] = lines
 
 
+def mix_kernel(full_rows, small_rows, swap_ref, other_ref, keep_ref, near_ref, second_ref, third_ref):
+    near_ref[:full_rows] = swap_ref[:full_rows]
+    near_ref[full_rows:] = other_ref[:full_rows]
+    for place, far_ref in enumerate((second_ref, third_ref)):
+        at = place * small_rows
+        far_ref[:small_rows] = keep_ref[at : at + small_rows]
+        at += full_rows
+        far_ref[small_rows:] = other_ref[at : at + small_rows]
+
+
 def step_kernel(
-    cx, cy, count_x, full_rows, small_rows, own_ref, other_ref, near_ref, near_other_ref,
-    far_ref, far_other_ref, table_ref, out_ref, z_ref, cor_ref, pred_ref, store_ref, tile_ref, flip_ref, speed_ref,
+    cx, cy, count_x, full_rows, small_rows, own_ref, other_ref, got_ref, got_other_ref,
+    table_ref, out_ref, z_ref, cor_ref, pred_ref, store_ref, tile_ref, flip_ref, speed_ref,
 ):
     fields = z_ref.shape[0]
     levels = 4
@@ -183,9 +193,9 @@
     put_block(from_owner(0)[1], own_lines)
 
     sense = 1 - 2 * index_y
-    for block_ref, far_block_ref, toward, south_first in (
-        (near_ref, far_ref, sense, index_y),
-        (near_other_ref, far_other_ref, -sense, 1 - index_y),
+    for block_ref, toward, south_first in (
+        (got_ref, sense, index_y),
+        (got_other_ref, -sense, 1 - index_y),
     ):
         south_top = pl.multiple_of(south_first * full_rows, 8)
         north_top = pl.multiple_of((1 - south_first) * full_rows, 8)
@@ -199,13 +209,13 @@
 
         put_block(from_owner(toward)[1], near_lines)
         for place, distance in enumerate((2, 3)):
-            top = 2 * place * small_rows
+            top = 2 * full_rows + 2 * place * small_rows
             south_top = pl.multiple_of(top + south_first * small_rows, 8)
             north_top = pl.multiple_of(top + (1 - south_first) * small_rows, 8)
 
             def far_lines(
                 at, south_shift, north_shift,
-                block_ref=far_block_ref, south_top=south_top, north_top=north_top,
+                block_ref=block_ref, south_top=south_top, north_top=north_top,
             ):
                 south = block_ref[pl.ds(south_top + at, group)]
                 north = block_ref[pl.ds(north_top + at, group)]
@@ -215,11 +225,12 @@
             put_distant(*from_owner(toward * distance), far_lines)
 
     def middle_lines(at, south_shift, north_shift):
-        row = 4 * small_rows + at
+        row = 2 * full_rows + 4 * small_rows + at
         mine_shift = jnp.where(south_is_own, south_shift, north_shift)
         other_shift = jnp.where(south_is_own, north_shift, south_shift)
-        mine = pltpu.roll(far_ref[row : row + group], mine_shift, 1)
-        return jnp.where(own_half, mine, pltpu.roll(far_other_ref[row : row + group], other_shift, 1))
+        mine = pltpu.roll(got_ref[row : row + group], mine_shift, 1)
+        theirs = pltpu.roll(got_other_ref[row : row + group], other_shift, 1)
+        return jnp.where(own_half, mine, theirs)
 
     put_distant(*from_owner(count_x // 2), middle_lines)
 
@@ -446,24 +457,21 @@
     def across(block):
         return lax.ppermute(block, "ty", [(0, 1), (1, 0)])
 
-    own = swap[:full_rows]
     other = across(swap)
     wave_speed, edges, other = lax.optimization_barrier((wave_speed, edges, other))
-    first = moved(jnp.concatenate([own, other[:full_rows]]), 1)
-    seconds = [
-        moved(
-            jnp.concatenate(
-                [
-                    keep[place * small_rows : (place + 1) * small_rows],
-                    other[full_rows + place * small_rows : full_rows + (place + 1) * small_rows],
-                ]
-            ),
-            distance,
-        )
-        for place, distance in enumerate((2, 3))
-    ]
-    far = jnp.concatenate([*seconds, moved(middle, count_x // 2)])
-    pieces = (own, other, first, across(first), far, across(far))
+    messages = pl.pallas_call(
+        functools.partial(mix_kernel, full_rows, small_rows),
+        out_shape=[
+            jax.ShapeDtypeStruct((2 * rows, LANES), jnp.float32)
+            for rows in (full_rows, small_rows, small_rows)
+        ],
+        in_specs=[pl.BlockSpec(memory_space=pltpu.VMEM)] * 3,
+        out_specs=[pl.BlockSpec(memory_space=pltpu.VMEM)] * 3,
+        name="messages",
+    )(swap, other, keep)
+    got = [moved(block, place + 1) for place, block in enumerate(messages)]
+    got = jnp.concatenate([*got, moved(middle, count_x // 2)])
+    pieces = (swap, other, got, across(got))
     table = jnp.concatenate([wave_speed, edges.reshape(-1).astype(jnp.float32)])
     z_rows = (cells + 8) * group
     out = pl.pallas_call(
@@ -471,7 +479,7 @@
             step_kernel, cx, cy, count_x, full_rows, small_rows
         ),
         out_shape=jax.ShapeDtypeStruct((faces, fields, cx, levels, cy), jnp.float32),
-        in_specs=[pl.BlockSpec(memory_space=pltpu.VMEM)] * 6
+        in_specs=[pl.BlockSpec(memory_space=pltpu.VMEM)] * 4
         + [pl.BlockSpec(memory_space=pltpu.SMEM)],
         out_specs=pl.BlockSpec(memory_space=pltpu.VMEM),
         scratch_shapes=[

time: 25.8 us -> 27.8 us (1.078)
  Pallas kernels: 6.27 us -> 7.9 us
  local copies, waits for them, and re-layouts: 3.11 us -> 4.3 us
  waiting for transfers between devices: 8.47 us -> 7.35 us
    pallas_call x0 -> x1, Pallas kernels: none -> 1.63 us  [fast_on_device(): pl.pallas_call(functools.partial(mix_kernel, full_rows, small_rows), out_...]
    unnamed x14 -> x21, local copies, waits for them, and re-layouts: 2.88 us -> 4.08 us
    ppermute x3 -> x2, waiting for transfers between devices: 1.78 us -> 1.02 us  [across(): return lax.ppermute(block, 'ty', [(0, 1), (1, 0)])]
    ppermute x3 -> x2, starting transfers between devices: 0.08 us -> 0.52 us  [across(): return lax.ppermute(block, 'ty', [(0, 1), (1, 0)])]
    ppermute x4, waiting for transfers between devices: 6.69 us -> 6.33 us  [moved(): return lax.ppermute(block, ('tx', 'ty'), pairs_of)]
  transfers between devices with their start and end apart: 7 -> 6, of which waited for: 5 -> 5; matrix products, arithmetic and copies ran while one was open for 1% -> 1% of each run, Pallas kernels for 0% -> 0%
where the time goes in v7:
time: 27.8 us; the launch traced here: 27.5 us
  Pallas kernels  7.9 us (28%)
  starting transfers between devices  7.84 us (28%)
  waiting for transfers between devices  7.35 us (26%)
  local copies, waits for them, and re-layouts  4.3 us (15%)
    ppermute x4, starting transfers between devices, moved(): return lax.ppermute(block, ('tx', 'ty'), pairs_of)  7.32 us
    ppermute x4, waiting for transfers between devices, moved(): return lax.ppermute(block, ('tx', 'ty'), pairs_of)  6.33 us
    pallas_call x1, Pallas kernels, fast_on_device(): pl.pallas_call(functools.partial(step_kernel, cx, cy, count_x, full_rows,...  5.45 us
    unnamed x21, local copies, waits for them, and re-layouts  4.08 us
    pallas_call x1, Pallas kernels, fast_on_device(): pl.pallas_call(functools.partial(mix_kernel, full_rows, small_rows), out_...  1.63 us
    ppermute x2, waiting for transfers between devices, across(): return lax.ppermute(block, 'ty', [(0, 1), (1, 0)])  1.02 us
    pallas_call x1, Pallas kernels, fast_on_device(): pl.pallas_call(functools.partial(pack_kernel, cx, cy, count_x, full_rows,...  0.82 us
  transfers between devices with their start and end apart: 6, of which 5 were waited for; matrix products, arithmetic and copies ran while one was open for 1% of the time, Pallas kernels for 0%

profile of v7, /device:TPU:0, one launch (start us, length us, event | category | flops | bytes accessed | tf_op | source)
XLA Modules:
  0.0 27.5 jit_solution(3534496589047692890)
XLA Ops:
  0.0 0.0 copy-start.4
  0.0 0.9 %copy-done.4 = f32[6,3,4,6,24]{4,2,3,1,0:T(4,128)S(1)} copy-done((f32[6,3,4,6,24]{4,2,3,1,0:T(4,128)S(1)}, f32[6,3,4,6,24]{4,2,3,1,0:T(4,128)}, u32[]{:S(2)}) %copy-start.4) | copy-done | bytes 41496
  0.9 0.0 copy-start.6
  0.9 0.7 %copy-done.6 = f32[6,6,24]{2,1,0:T(8,128)S(1)} copy-done((f32[6,6,24]{2,1,0:T(8,128)S(1)}, f32[6,6,24]{2,1,0:T(8,128)}, u32[]{:S(2)}) %copy-start.6) | copy-done | bytes 3480
  1.7 0.8 %pack.1 = (f32[216,128]{1,0:T(8,128)S(1)}, f32[96,128]{1,0:T(8,128)S(1)}, f32[48,128]{1,0:T(8,128)S(1)}) custom-call(f32[6,3,6,4,24]{4,3,2,1,0:T(4,128)S(1)} %bitcast.2, f32[6,6,24]{2,1,0:T(8,128)S(1)} %copy-done.6), custom_call_target="tpu_custom_call" | custom-call | tf_op jit(solution)/shard_map/pack/pallas_call | solution.py:430
  2.5 0.0 copy-start.5
  2.5 0.6 %copy-done.5 = f32[96,128]{1,0:T(8,128)} copy-done((f32[96,128]{1,0:T(8,128)}, f32[96,128]{1,0:T(8,128)S(1)}, u32[]{:S(2)}) %copy-start.5) | copy-done | bytes 49176
  3.1 0.0 copy-start
  3.1 0.5 %collective-permute-start = (f32[216,128]{1,0:T(8,128)S(1)}, f32[216,128]{1,0:T(8,128)S(1)}, u32[]{:S(2)}, u32[]{:S(2)}) collective-permute-start(f32[216,128]{1,0:T(8,128)S(1)} %get-tuple-element.14.swap_ref.own_ref), channel_id=1, source_target_pairs={{0,1},{1,0},{2,3},{3,2},{4,5},{5,4},{6,7},{7,6},{8,9},{9,8},{10,11... | collective-permute-start | bytes 331784 | tf_op jit(solution)/shard_map/ppermute | solution.py:458
  3.6 1.0 %collective-permute-done.other_ref = f32[216,128]{1,0:T(8,128)S(1)} collective-permute-done((f32[216,128]{1,0:T(8,128)S(1)}, f32[216,128]{1,0:T(8,128)S(1)}, u32[]{:S(2)}, u32[]{:S(2)}) %collective-permute-start) | collective-permute-done | bytes 110624 | tf_op jit(solution)/shard_map/ppermute | solution.py:458
  4.5 0.0 copy-start.2
  4.5 0.0 copy-done
  4.5 0.6 %copy-done.2 = f32[216,128]{1,0:T(8,128)} copy-done((f32[216,128]{1,0:T(8,128)}, f32[216,128]{1,0:T(8,128)S(1)}, u32[]{:S(2)}) %copy-start.2) | copy-done | bytes 110616
  5.2 1.6 %messages.1 = (f32[240,128]{1,0:T(8,128)}, f32[96,128]{1,0:T(8,128)}, f32[96,128]{1,0:T(8,128)}) custom-call(f32[216,128]{1,0:T(8,128)} %copy-done, f32[216,128]{1,0:T(8,128)} %copy-done.2, f32[96,128]{1,0:T(8,128)} %copy-done.5), custom_call_target="tpu_custom_call" | custom-call | tf_op jit(solution)/shard_map/messages/pallas_call | solution.py:462
  6.8 2.9 %collective-permute-start.1 = (f32[240,128]{1,0:T(8,128)}, f32[240,128]{1,0:T(8,128)S(1)}, u32[]{:S(2)}, u32[]{:S(2)}) collective-permute-start(f32[240,128]{1,0:T(8,128)} %get-tuple-element.17), channel_id=1, source_target_pairs={{0,2},{1,15},{2,4},{3,1},{4,6},{5,3},{6,8},{7,5},{8,10},{9,7},{10,... | collective-permute-start | bytes 368648 | tf_op jit(solution)/shard_map/ppermute | solution.py:455
  9.7 2.6 %collective-permute-start.4 = (f32[48,128]{1,0:T(8,128)S(1)}, f32[48,128]{1,0:T(8,128)S(1)}, u32[]{:S(2)}, u32[]{:S(2)}) collective-permute-start(f32[48,128]{1,0:T(8,128)S(1)} %get-tuple-element.20), channel_id=1, source_target_pairs={{0,8},{1,9},{2,10},{3,11},{4,12},{5,13},{6,14},{7,15},{8,0},{9,1},... | collective-permute-start | bytes 73736 | tf_op jit(solution)/shard_map/ppermute | solution.py:455
  12.3 1.6 %collective-permute-start.2 = (f32[96,128]{1,0:T(8,128)}, f32[96,128]{1,0:T(8,128)S(1)}, u32[]{:S(2)}, u32[]{:S(2)}) collective-permute-start(f32[96,128]{1,0:T(8,128)} %get-tuple-element.18), channel_id=1, source_target_pairs={{0,4},{1,13},{2,6},{3,15},{4,8},{5,1},{6,10},{7,3},{8,12},{9,5},{1... | collective-permute-start | bytes 147464 | tf_op jit(solution)/shard_map/ppermute | solution.py:455
  13.8 0.3 %collective-permute-start.3 = (f32[96,128]{1,0:T(8,128)}, f32[96,128]{1,0:T(8,128)S(1)}, u32[]{:S(2)}, u32[]{:S(2)}) collective-permute-start(f32[96,128]{1,0:T(8,128)} %get-tuple-element.19), channel_id=1, source_target_pairs={{0,6},{1,11},{2,8},{3,13},{4,10},{5,15},{6,12},{7,1},{8,14},{9,3},... | collective-permute-start | bytes 147464 | tf_op jit(solution)/shard_map/ppermute | solution.py:455
  14.1 2.2 %collective-permute-done.1 = f32[240,128]{1,0:T(8,128)S(1)} collective-permute-done((f32[240,128]{1,0:T(8,128)}, f32[240,128]{1,0:T(8,128)S(1)}, u32[]{:S(2)}, u32[]{:S(2)}) %collective-permute-start.1) | collective-permute-done | bytes 122912 | tf_op jit(solution)/shard_map/ppermute | solution.py:455
  16.4 2.4 %collective-permute-done.2 = f32[96,128]{1,0:T(8,128)S(1)} collective-permute-done((f32[96,128]{1,0:T(8,128)}, f32[96,128]{1,0:T(8,128)S(1)}, u32[]{:S(2)}, u32[]{:S(2)}) %collective-permute-start.2) | collective-permute-done | bytes 49184 | tf_op jit(solution)/shard_map/ppermute | solution.py:455
  18.8 1.7 %collective-permute-done.3 = f32[96,128]{1,0:T(8,128)S(1)} collective-permute-done((f32[96,128]{1,0:T(8,128)}, f32[96,128]{1,0:T(8,128)S(1)}, u32[]{:S(2)}, u32[]{:S(2)}) %collective-permute-start.3) | collective-permute-done | bytes 49184 | tf_op jit(solution)/shard_map/ppermute | solution.py:455
  20.5 0.0 collective-permute-done.4
  20.5 0.1 collective-permute-start.5
  20.6 0.6 %copy-done.7 = s32[6,4,3]{0,1,2:T(4,128)S(1)} copy-done((s32[6,4,3]{0,1,2:T(4,128)S(1)}, s32[6,4,3]{0,1,2:T(4,128)}, u32[]{:S(2)}) %copy-start.7) | copy-done | bytes 312
  21.2 0.1 copy.6
  21.3 0.1 convert_element_type.7
  21.4 0.6 %copy-done.8 = f32[4]{0:T(128)S(1)} copy-done((f32[4]{0:T(128)S(1)}, f32[4]{0:T(128)}, u32[]{:S(2)}) %copy-start.8) | copy-done | bytes 40
  21.9 0.1 pad_maximum_fusion.table_ref
  22.0 0.1 collective-permute-done.5.got_other_ref
  22.1 0.0 copy-done.3
  22.1 0.0 copy-done.1
  22.1 5.4 %substeps.1 = f32[6,3,6,4,24]{4,3,2,1,0:T(4,128)} custom-call(f32[216,128]{1,0:T(8,128)S(1)} %copy-done.1, f32[216,128]{1,0:T(8,128)S(1)} %copy-done.3, f32[480,128]{1,0:T(8,128)S(1)} %constant_dynamic-update-slice_fusion.got_ref, f32[480,128]{1,0:T(8,128)S(1)} %collective-permute-done.5.got_other_ref, f32[76]{0:T(128)S(1)} %pad_maximum_fusion.table_ref), custom_call_target="tpu_custom_call" | custom-call | tf_op jit(solution)/shard_map/substeps/pallas_call | solution.py:477
  (9 shorter events, 0.0 us)
Async XLA Ops:
  0.0 0.9 %copy-start.4 = (f32[6,3,4,6,24]{4,2,3,1,0:T(4,128)S(1)}, f32[6,3,4,6,24]{4,2,3,1,0:T(4,128)}, u32[]{:S(2)}) copy-start(f32[6,3,4,6,24]{4,2,3,1,0:T(4,128)} %param.4) | copy-start | bytes 124420
  0.9 0.7 %copy-start.6 = (f32[6,6,24]{2,1,0:T(8,128)S(1)}, f32[6,6,24]{2,1,0:T(8,128)}, u32[]{:S(2)}) copy-start(f32[6,6,24]{2,1,0:T(8,128)} %coriolis_hbm.1) | copy-start | bytes 10372
  2.5 0.6 %copy-start.5 = (f32[96,128]{1,0:T(8,128)}, f32[96,128]{1,0:T(8,128)S(1)}, u32[]{:S(2)}) copy-start(f32[96,128]{1,0:T(8,128)S(1)} %get-tuple-element.16.keep_ref) | copy-start | bytes 147460
  3.1 1.4 %copy-start = (f32[216,128]{1,0:T(8,128)}, f32[216,128]{1,0:T(8,128)S(1)}, u32[]{:S(2)}) copy-start(f32[216,128]{1,0:T(8,128)S(1)} %get-tuple-element.14.swap_ref.own_ref) | copy-start | bytes 331780
  3.1 1.4 %collective-permute-start = (f32[216,128]{1,0:T(8,128)S(1)}, f32[216,128]{1,0:T(8,128)S(1)}, u32[]{:S(2)}, u32[]{:S(2)}) collective-permute-start(f32[216,128]{1,0:T(8,128)S(1)} %get-tuple-element.14.swap_ref.own_ref), channel_id=1, source_target_pairs={{0,1},{1,0},{2,3},{3,2},{4,5},{5,4},{6,7},{7,6},{8,9},{9,8},{10,11... | collective-permute-start | bytes 331784 | tf_op jit(solution)/shard_map/ppermute | solution.py:458
  4.5 0.6 %copy-start.2 = (f32[216,128]{1,0:T(8,128)}, f32[216,128]{1,0:T(8,128)S(1)}, u32[]{:S(2)}) copy-start(f32[216,128]{1,0:T(8,128)S(1)} %collective-permute-done.other_ref) | copy-start | bytes 331780
  6.8 9.6 %collective-permute-start.1 = (f32[240,128]{1,0:T(8,128)}, f32[240,128]{1,0:T(8,128)S(1)}, u32[]{:S(2)}, u32[]{:S(2)}) collective-permute-start(f32[240,128]{1,0:T(8,128)} %get-tuple-element.17), channel_id=1, source_target_pairs={{0,2},{1,15},{2,4},{3,1},{4,6},{5,3},{6,8},{7,5},{8,10},{9,7},{10,... | collective-permute-start | bytes 368648 | tf_op jit(solution)/shard_map/ppermute | solution.py:455
  9.7 10.8 %collective-permute-start.4 = (f32[48,128]{1,0:T(8,128)S(1)}, f32[48,128]{1,0:T(8,128)S(1)}, u32[]{:S(2)}, u32[]{:S(2)}) collective-permute-start(f32[48,128]{1,0:T(8,128)S(1)} %get-tuple-element.20), channel_id=1, source_target_pairs={{0,8},{1,9},{2,10},{3,11},{4,12},{5,13},{6,14},{7,15},{8,0},{9,1},... | collective-permute-start | bytes 73736 | tf_op jit(solution)/shard_map/ppermute | solution.py:455
  12.3 6.5 %collective-permute-start.2 = (f32[96,128]{1,0:T(8,128)}, f32[96,128]{1,0:T(8,128)S(1)}, u32[]{:S(2)}, u32[]{:S(2)}) collective-permute-start(f32[96,128]{1,0:T(8,128)} %get-tuple-element.18), channel_id=1, source_target_pairs={{0,4},{1,13},{2,6},{3,15},{4,8},{5,1},{6,10},{7,3},{8,12},{9,5},{1... | collective-permute-start | bytes 147464 | tf_op jit(solution)/shard_map/ppermute | solution.py:455
  13.8 6.6 %collective-permute-start.3 = (f32[96,128]{1,0:T(8,128)}, f32[96,128]{1,0:T(8,128)S(1)}, u32[]{:S(2)}, u32[]{:S(2)}) collective-permute-start(f32[96,128]{1,0:T(8,128)} %get-tuple-element.19), channel_id=1, source_target_pairs={{0,6},{1,11},{2,8},{3,13},{4,10},{5,15},{6,12},{7,1},{8,14},{9,3},... | collective-permute-start | bytes 147464 | tf_op jit(solution)/shard_map/ppermute | solution.py:455
  18.8 3.3 %copy-start.3 = (f32[216,128]{1,0:T(8,128)S(1)}, f32[216,128]{1,0:T(8,128)}, u32[]{:S(2)}) copy-start(f32[216,128]{1,0:T(8,128)} %copy-done.2) | copy-start | bytes 331780
  18.8 3.3 %copy-start.1 = (f32[216,128]{1,0:T(8,128)S(1)}, f32[216,128]{1,0:T(8,128)}, u32[]{:S(2)}) copy-start(f32[216,128]{1,0:T(8,128)} %copy-done) | copy-start | bytes 331780
  20.5 0.7 %copy-start.7 = (s32[6,4,3]{0,1,2:T(4,128)S(1)}, s32[6,4,3]{0,1,2:T(4,128)}, u32[]{:S(2)}) copy-start(s32[6,4,3]{0,1,2:T(4,128)} %param.7) | copy-start | bytes 868
  20.5 1.6 %collective-permute-start.5 = (f32[480,128]{1,0:T(8,128)S(1)}, f32[480,128]{1,0:T(8,128)S(1)}, u32[]{:S(2)}, u32[]{:S(2)}) collective-permute-start(f32[480,128]{1,0:T(8,128)S(1)} %constant_dynamic-update-slice_fusion.got_ref), channel_id=1, source_target_pairs={{0,1},{1,0},{2,3},{3,2},{4,5},{5,4},{6,7},{7,6},{8,9},{9,8},{10,11... | collective-permute-start | bytes 737288 | tf_op jit(solution)/shard_map/ppermute | solution.py:458
  21.3 0.7 %copy-start.8 = (f32[4]{0:T(128)S(1)}, f32[4]{0:T(128)}, u32[]{:S(2)}) copy-start(f32[4]{0:T(128)} %param.6) | copy-start | bytes 52

commit v8 on v7

--- a/solution.py
+++ b/solution.py
@@ -12,6 +12,7 @@
 WINDOW = 64
 MARGIN = 8
 VMEM_LIMIT = 32 * 1024 * 1024
+SMALL_VMEM_LIMIT = 8 * 1024 * 1024
 
 
 def window_start(source, target, count_x, index_y, cx, cy, far):
@@ -38,9 +39,8 @@
 
 def pack_kernel(
     cx, cy, count_x, full_rows, small_rows, state_hbm, coriolis_hbm,
-    swap_ref, keep_ref, middle_ref, state_ref, coriolis_ref, line_ref, sems,
+    swap_ref, line_ref, state_ref, coriolis_ref, sems,
 ):
-    full_ref = swap_ref.at[pl.ds(0, full_rows)]
     copies = [
         pltpu.make_async_copy(state_hbm, state_ref, sems.at[0]),
         pltpu.make_async_copy(coriolis_hbm, coriolis_ref, sems.at[1]),
@@ -52,11 +52,8 @@
     pairs = faces // 2
     group = pairs * levels
     half = cx // 2
-    width = 2 * cx
     base = fields * half * group
-    index_x = lax.axis_index("tx")
-    index_y = lax.axis_index("ty")
-    full_ref[...] = jnp.zeros(full_ref.shape, jnp.float32)
+    swap_ref[:full_rows] = jnp.zeros((full_rows, LANES), jnp.float32)
     line_ref[...] = jnp.zeros(line_ref.shape, jnp.float32)
     for copy in copies:
         copy.wait()
@@ -66,43 +63,59 @@
             for xp in range(half):
                 for field in range(fields):
                     row = field * half * group + xp * group + (face // 2) * levels
-                    full_ref[row : row + levels, lane : lane + cy] = state_ref[
+                    swap_ref[row : row + levels, lane : lane + cy] = state_ref[
                         face, field, 2 * xp + parity
                     ]
                 x = 2 * xp + parity
                 row = base + xp * pairs + face // 2
-                full_ref[row : row + 1, lane : lane + cy] = coriolis_ref[face, x : x + 1]
+                swap_ref[row : row + 1, lane : lane + cy] = coriolis_ref[face, x : x + 1]
                 row = (x // half) * 16 + (x % half) * pairs + face // 2
                 lane_at = (face % 2) * WINDOW + MARGIN
                 line_ref[row : row + 1, lane_at : lane_at + cy] = coriolis_ref[face, x : x + 1]
-    sense = 1 - 2 * index_y
-    wanted = [(middle_ref, 0, count_x // 2)]
+    sense = 1 - 2 * lax.axis_index("ty")
     for place, distance in enumerate((2, 3)):
-        wanted.append((keep_ref, place * small_rows, sense * distance))
-        wanted.append((swap_ref, full_rows + place * small_rows, -sense * distance))
-    for small_ref, top, offset in wanted:
-        target = (index_x + offset + count_x) % count_x
-        starts = windows(index_x, target, count_x, index_y, cx, cy)
-        blocks = {}
-
-        def put(row, lane, lines):
-            position = lax.broadcasted_iota(jnp.int32, lines.shape, 1) % WINDOW
-            here = (position >= lane) & (position < lane + width)
-            blocks[row] = jnp.where(here, lines, blocks.get(row, jnp.zeros_like(lines)))
-
-        for field in range(fields):
-            for x in range(cx):
-                row = field * half * group + (x // 2) * group
-                at, lane = unit_place(field, x, cx, group, width)
-                shift = lane - MARGIN - (x % 2) * cy - starts[x // half] + 2 * LANES
-                put(at, lane, pltpu.roll(full_ref[row : row + group], shift % LANES, 1))
-        for part in range(2):
-            at, lane = unit_place(fields, part, cx, group, width)
-            shift = lane - MARGIN - starts[part] + 2 * LANES
-            lines = line_ref[16 * part : 16 * part + group]
-            put(at, lane, pltpu.roll(lines, shift % LANES, 1))
-        for row, lines in blocks.items():
-            small_ref[top + row : top + row + group] = lines
+        top = full_rows + place * small_rows
+        put_chunk(cx, cy, count_x, swap_ref, line_ref, swap_ref, top, -sense * distance)
+
+
+def put_chunk(cx, cy, count_x, block_ref, line_ref, out_ref, top, offset):
+    pairs = 3
+    group = 4 * pairs
+    fields = 3
+    half = cx // 2
+    width = 2 * cx
+    index_x = lax.axis_index("tx")
+    index_y = lax.axis_index("ty")
+    target = (index_x + offset + count_x) % count_x
+    starts = windows(index_x, target, count_x, index_y, cx, cy)
+    blocks = {}
+
+    def put(row, lane, lines):
+        position = lax.broadcasted_iota(jnp.int32, lines.shape, 1) % WINDOW
+        here = (position >= lane) & (position < lane + width)
+        blocks[row] = jnp.where(here, lines, blocks.get(row, jnp.zeros_like(lines)))
+
+    for field in range(fields):
+        for x in range(cx):
+            row = field * half * group + (x // 2) * group
+            at, lane = unit_place(field, x, cx, group, width)
+            shift = lane - MARGIN - (x % 2) * cy - starts[x // half] + 2 * LANES
+            put(at, lane, pltpu.roll(block_ref[row : row + group], shift % LANES, 1))
+    for part in range(2):
+        at, lane = unit_place(fields, part, cx, group, width)
+        shift = lane - MARGIN - starts[part] + 2 * LANES
+        lines = line_ref[16 * part : 16 * part + group]
+        put(at, lane, pltpu.roll(lines, shift % LANES, 1))
+    for row, lines in blocks.items():
+        out_ref[top + row : top + row + group] = lines
+
+
+def keep_kernel(cx, cy, count_x, small_rows, swap_ref, line_ref, keep_ref, middle_ref):
+    sense = 1 - 2 * lax.axis_index("ty")
+    put_chunk(cx, cy, count_x, swap_ref, line_ref, middle_ref, 0, count_x // 2)
+    for place, distance in enumerate((2, 3)):
+        top = place * small_rows
+        put_chunk(cx, cy, count_x, swap_ref, line_ref, keep_ref, top, sense * distance)
 
 
 def mix_kernel(full_rows, small_rows, swap_ref, other_ref, keep_ref, near_ref, second_ref, third_ref):
@@ -427,24 +440,33 @@
     full_rows = fields * (cx // 2) * group + (cx // 2) * pairs
     full_rows = -(-full_rows // 8) * 8
     small_rows = unit_place(fields, 1, cx, group, 2 * cx)[0] + group
-    swap, keep, middle = pl.pallas_call(
+    swap, lines = pl.pallas_call(
         functools.partial(pack_kernel, cx, cy, count_x, full_rows, small_rows),
         out_shape=[
             jax.ShapeDtypeStruct((full_rows + 2 * small_rows, LANES), jnp.float32),
-            jax.ShapeDtypeStruct((2 * small_rows, LANES), jnp.float32),
-            jax.ShapeDtypeStruct((small_rows, LANES), jnp.float32),
+            jax.ShapeDtypeStruct((32, LANES), jnp.float32),
         ],
         in_specs=[pl.BlockSpec(memory_space=pltpu.HBM)] * 2,
-        out_specs=[pl.BlockSpec(memory_space=pltpu.VMEM)] * 3,
+        out_specs=[pl.BlockSpec(memory_space=pltpu.VMEM)] * 2,
         scratch_shapes=[
             pltpu.VMEM((faces, fields, cx, levels, cy), jnp.float32),
             pltpu.VMEM((faces, cx, cy), jnp.float32),
-            pltpu.VMEM((32, LANES), jnp.float32),
             pltpu.SemaphoreType.DMA((2,)),
         ],
         compiler_params=pltpu.CompilerParams(vmem_limit_bytes=VMEM_LIMIT),
         name="pack",
     )(jnp.swapaxes(state, 2, 3), coriolis)
+    keep, middle = pl.pallas_call(
+        functools.partial(keep_kernel, cx, cy, count_x, small_rows),
+        out_shape=[
+            jax.ShapeDtypeStruct((2 * small_rows, LANES), jnp.float32),
+            jax.ShapeDtypeStruct((small_rows, LANES), jnp.float32),
+        ],
+        in_specs=[pl.BlockSpec(memory_space=pltpu.VMEM)] * 2,
+        out_specs=[pl.BlockSpec(memory_space=pltpu.VMEM)] * 2,
+        compiler_params=pltpu.CompilerParams(vmem_limit_bytes=SMALL_VMEM_LIMIT),
+        name="keep",
+    )(swap, lines)
 
     def moved(block, distance):
         pairs_of = []
@@ -458,7 +480,6 @@
         return lax.ppermute(block, "ty", [(0, 1), (1, 0)])
 
     other = across(swap)
-    wave_speed, edges, other = lax.optimization_barrier((wave_speed, edges, other))
     messages = pl.pallas_call(
         functools.partial(mix_kernel, full_rows, small_rows),
         out_shape=[
@@ -467,12 +488,14 @@
         ],
         in_specs=[pl.BlockSpec(memory_space=pltpu.VMEM)] * 3,
         out_specs=[pl.BlockSpec(memory_space=pltpu.VMEM)] * 3,
+        compiler_params=pltpu.CompilerParams(vmem_limit_bytes=SMALL_VMEM_LIMIT),
         name="messages",
     )(swap, other, keep)
     got = [moved(block, place + 1) for place, block in enumerate(messages)]
     got = jnp.concatenate([*got, moved(middle, count_x // 2)])
+    table = jnp.concatenate([wave_speed, edges.reshape(-1).astype(jnp.float32)])
+    got, table = lax.optimization_barrier((got, table))
     pieces = (swap, other, got, across(got))
-    table = jnp.concatenate([wave_speed, edges.reshape(-1).astype(jnp.float32)])
     z_rows = (cells + 8) * group
     out = pl.pallas_call(
         functools.partial(

time: 27.8 us -> 25 us (0.90)
  local copies, waits for them, and re-layouts: 4.3 us -> 1.9 us
  Pallas kernels: 7.9 us -> 6.34 us
  waiting for transfers between devices: 7.35 us -> 8.39 us
    unnamed x21 -> x8, local copies, waits for them, and re-layouts: 4.08 us -> 1.68 us
    pallas_call x1, Pallas kernels: 1.63 us -> 0.02 us  [fast_on_device(): pl.pallas_call(functools.partial(mix_kernel, full_rows, small_rows), out_...]
    ppermute x2, waiting for transfers between devices: 1.02 us -> 2.26 us  [across(): return lax.ppermute(block, 'ty', [(0, 1), (1, 0)])]
  transfers between devices with their start and end apart: 6 -> 6, of which waited for: 5 -> 4; matrix products, arithmetic and copies ran while one was open for 1% -> 1% of each run, Pallas kernels for 0% -> 1%
where the time goes in v8:
time: 25 us; the launch traced here: 24.8 us
  waiting for transfers between devices  8.39 us (34%)
  starting transfers between devices  8.01 us (32%)
  Pallas kernels  6.34 us (25%)
  local copies, waits for them, and re-layouts  1.9 us (8%)
    ppermute x4, starting transfers between devices, moved(): return lax.ppermute(block, ('tx', 'ty'), pairs_of)  7.42 us
    ppermute x4, waiting for transfers between devices, moved(): return lax.ppermute(block, ('tx', 'ty'), pairs_of)  6.13 us
    pallas_call x1, Pallas kernels, fast_on_device(): pl.pallas_call(functools.partial(step_kernel, cx, cy, count_x, full_rows,...  5.45 us
    ppermute x2, waiting for transfers between devices, across(): return lax.ppermute(block, 'ty', [(0, 1), (1, 0)])  2.26 us
    unnamed x8, local copies, waits for them, and re-layouts  1.68 us
    pallas_call x1, Pallas kernels, fast_on_device(): pl.pallas_call(functools.partial(pack_kernel, cx, cy, count_x, full_rows,...  0.69 us
    ppermute x2, starting transfers between devices, across(): return lax.ppermute(block, 'ty', [(0, 1), (1, 0)])  0.59 us
  transfers between devices with their start and end apart: 6, of which 4 were waited for; matrix products, arithmetic and copies ran while one was open for 1% of the time, Pallas kernels for 1%

profile of v8, /device:TPU:0, one launch (start us, length us, event | category | flops | bytes accessed | tf_op | source)
XLA Modules:
  0.0 24.8 jit_solution(13476664903001335811)
XLA Ops:
  0.0 0.0 copy-start
  0.0 0.9 %copy-done = f32[6,3,4,6,24]{4,2,3,1,0:T(4,128)S(1)} copy-done((f32[6,3,4,6,24]{4,2,3,1,0:T(4,128)S(1)}, f32[6,3,4,6,24]{4,2,3,1,0:T(4,128)}, u32[]{:S(2)}) %copy-start) | copy-done | bytes 41496
  0.9 0.0 copy-start.1
  0.9 0.7 %copy-done.1 = f32[6,6,24]{2,1,0:T(8,128)S(1)} copy-done((f32[6,6,24]{2,1,0:T(8,128)S(1)}, f32[6,6,24]{2,1,0:T(8,128)}, u32[]{:S(2)}) %copy-start.1) | copy-done | bytes 3480
  1.7 0.7 %pack.1 = (f32[216,128]{1,0:T(8,128)S(1)}, f32[32,128]{1,0:T(8,128)S(1)}) custom-call(f32[6,3,6,4,24]{4,3,2,1,0:T(4,128)S(1)} %bitcast.2, f32[6,6,24]{2,1,0:T(8,128)S(1)} %copy-done.1), custom_call_target="tpu_custom_call" | custom-call | tf_op jit(solution)/shard_map/pack/pallas_call | solution.py:443
  2.4 0.5 %collective-permute-start = (f32[216,128]{1,0:T(8,128)S(1)}, f32[216,128]{1,0:T(8,128)S(1)}, u32[]{:S(2)}, u32[]{:S(2)}) collective-permute-start(f32[216,128]{1,0:T(8,128)S(1)} %get-tuple-element.14.swap_ref.own_ref), channel_id=1, source_target_pairs={{0,1},{1,0},{2,3},{3,2},{4,5},{5,4},{6,7},{7,6},{8,9},{9,8},{10,11... | collective-permute-start | bytes 331784 | tf_op jit(solution)/shard_map/ppermute | solution.py:480
  2.9 0.2 keep.1
  3.1 0.8 %collective-permute-done.other_ref = f32[216,128]{1,0:T(8,128)S(1)} collective-permute-done((f32[216,128]{1,0:T(8,128)S(1)}, f32[216,128]{1,0:T(8,128)S(1)}, u32[]{:S(2)}, u32[]{:S(2)}) %collective-permute-start) | collective-permute-done | bytes 110624 | tf_op jit(solution)/shard_map/ppermute | solution.py:480
  3.8 0.0 copy-start.2
  3.9 2.9 %collective-permute-start.1 = (f32[240,128]{1,0:T(8,128)S(1)}, f32[240,128]{1,0:T(8,128)S(1)}, u32[]{:S(2)}, u32[]{:S(2)}) collective-permute-start(f32[240,128]{1,0:T(8,128)S(1)} %get-tuple-element.17), channel_id=1, source_target_pairs={{0,2},{1,15},{2,4},{3,1},{4,6},{5,3},{6,8},{7,5},{8,10},{9,7},{10,... | collective-permute-start | bytes 368648 | tf_op jit(solution)/shard_map/ppermute | solution.py:477
  6.8 2.6 %collective-permute-start.4 = (f32[48,128]{1,0:T(8,128)S(1)}, f32[48,128]{1,0:T(8,128)S(1)}, u32[]{:S(2)}, u32[]{:S(2)}) collective-permute-start(f32[48,128]{1,0:T(8,128)S(1)} %get-tuple-element.20), channel_id=1, source_target_pairs={{0,8},{1,9},{2,10},{3,11},{4,12},{5,13},{6,14},{7,15},{8,0},{9,1},... | collective-permute-start | bytes 73736 | tf_op jit(solution)/shard_map/ppermute | solution.py:477
  9.4 0.0 copy-done.2
  9.4 0.1 copy.6
  9.5 0.1 convert_element_type.7
  9.6 0.0 copy-start.3
  9.6 1.6 %collective-permute-start.2 = (f32[96,128]{1,0:T(8,128)S(1)}, f32[96,128]{1,0:T(8,128)S(1)}, u32[]{:S(2)}, u32[]{:S(2)}) collective-permute-start(f32[96,128]{1,0:T(8,128)S(1)} %get-tuple-element.18), channel_id=1, source_target_pairs={{0,4},{1,13},{2,6},{3,15},{4,8},{5,1},{6,10},{7,3},{8,12},{9,5},{1... | collective-permute-start | bytes 147464 | tf_op jit(solution)/shard_map/ppermute | solution.py:477
  11.3 0.3 %collective-permute-start.3 = (f32[96,128]{1,0:T(8,128)S(1)}, f32[96,128]{1,0:T(8,128)S(1)}, u32[]{:S(2)}, u32[]{:S(2)}) collective-permute-start(f32[96,128]{1,0:T(8,128)S(1)} %get-tuple-element.19), channel_id=1, source_target_pairs={{0,6},{1,11},{2,8},{3,13},{4,10},{5,15},{6,12},{7,1},{8,14},{9,3},... | collective-permute-start | bytes 147464 | tf_op jit(solution)/shard_map/ppermute | solution.py:477
  11.5 0.0 copy-done.3
  11.5 0.1 pad_maximum_fusion.1.table_ref
  11.6 0.0 collective-permute-done.4
  11.6 4.4 %collective-permute-done.2 = f32[96,128]{1,0:T(8,128)S(1)} collective-permute-done((f32[96,128]{1,0:T(8,128)S(1)}, f32[96,128]{1,0:T(8,128)S(1)}, u32[]{:S(2)}, u32[]{:S(2)}) %collective-permute-start.2) | collective-permute-done | bytes 49184 | tf_op jit(solution)/shard_map/ppermute | solution.py:477
  16.0 1.7 %collective-permute-done.3 = f32[96,128]{1,0:T(8,128)S(1)} collective-permute-done((f32[96,128]{1,0:T(8,128)S(1)}, f32[96,128]{1,0:T(8,128)S(1)}, u32[]{:S(2)}, u32[]{:S(2)}) %collective-permute-start.3) | collective-permute-done | bytes 49184 | tf_op jit(solution)/shard_map/ppermute | solution.py:477
  17.7 0.0 collective-permute-done.1
  17.8 0.1 collective-permute-start.5
  17.8 1.5 %collective-permute-done.5.got_other_ref = f32[480,128]{1,0:T(8,128)S(1)} collective-permute-done((f32[480,128]{1,0:T(8,128)S(1)}, f32[480,128]{1,0:T(8,128)S(1)}, u32[]{:S(2)}, u32[]{:S(2)}) %collective-permute-start.5) | collective-permute-done | bytes 245792 | tf_op jit(solution)/shard_map/ppermute | solution.py:480
  19.3 5.5 %substeps.1 = f32[6,3,6,4,24]{4,3,2,1,0:T(4,128)} custom-call(f32[216,128]{1,0:T(8,128)S(1)} %get-tuple-element.14.swap_ref.own_ref, f32[216,128]{1,0:T(8,128)S(1)} %collective-permute-done.other_ref, f32[480,128]{1,0:T(8,128)S(1)} %pad_maximum_fusion.got_ref, f32[480,128]{1,0:T(8,128)S(1)} %collective-permute-done.5.got_other_ref, ...), custom_call_target="tpu_custom_call" | custom-call | tf_op jit(solution)/shard_map/substeps/pallas_call | solution.py:500
  (3 shorter events, 0.0 us)
Async XLA Ops:
  0.0 0.9 %copy-start = (f32[6,3,4,6,24]{4,2,3,1,0:T(4,128)S(1)}, f32[6,3,4,6,24]{4,2,3,1,0:T(4,128)}, u32[]{:S(2)}) copy-start(f32[6,3,4,6,24]{4,2,3,1,0:T(4,128)} %param.4) | copy-start | bytes 124420
  0.9 0.7 %copy-start.1 = (f32[6,6,24]{2,1,0:T(8,128)S(1)}, f32[6,6,24]{2,1,0:T(8,128)}, u32[]{:S(2)}) copy-start(f32[6,6,24]{2,1,0:T(8,128)} %coriolis_hbm.1) | copy-start | bytes 10372
  2.4 1.5 %collective-permute-start = (f32[216,128]{1,0:T(8,128)S(1)}, f32[216,128]{1,0:T(8,128)S(1)}, u32[]{:S(2)}, u32[]{:S(2)}) collective-permute-start(f32[216,128]{1,0:T(8,128)S(1)} %get-tuple-element.14.swap_ref.own_ref), channel_id=1, source_target_pairs={{0,1},{1,0},{2,3},{3,2},{4,5},{5,4},{6,7},{7,6},{8,9},{9,8},{10,11... | collective-permute-start | bytes 331784 | tf_op jit(solution)/shard_map/ppermute | solution.py:480
  3.8 5.5 %copy-start.2 = (s32[6,4,3]{0,1,2:T(4,128)S(1)}, s32[6,4,3]{0,1,2:T(4,128)}, u32[]{:S(2)}) copy-start(s32[6,4,3]{0,1,2:T(4,128)} %param.7) | copy-start | bytes 868
  3.9 13.9 %collective-permute-start.1 = (f32[240,128]{1,0:T(8,128)S(1)}, f32[240,128]{1,0:T(8,128)S(1)}, u32[]{:S(2)}, u32[]{:S(2)}) collective-permute-start(f32[240,128]{1,0:T(8,128)S(1)} %get-tuple-element.17), channel_id=1, source_target_pairs={{0,2},{1,15},{2,4},{3,1},{4,6},{5,3},{6,8},{7,5},{8,10},{9,7},{10,... | collective-permute-start | bytes 368648 | tf_op jit(solution)/shard_map/ppermute | solution.py:477
  6.8 4.8 %collective-permute-start.4 = (f32[48,128]{1,0:T(8,128)S(1)}, f32[48,128]{1,0:T(8,128)S(1)}, u32[]{:S(2)}, u32[]{:S(2)}) collective-permute-start(f32[48,128]{1,0:T(8,128)S(1)} %get-tuple-element.20), channel_id=1, source_target_pairs={{0,8},{1,9},{2,10},{3,11},{4,12},{5,13},{6,14},{7,15},{8,0},{9,1},... | collective-permute-start | bytes 73736 | tf_op jit(solution)/shard_map/ppermute | solution.py:477
  9.6 1.9 %copy-start.3 = (f32[4]{0:T(128)S(1)}, f32[4]{0:T(128)}, u32[]{:S(2)}) copy-start(f32[4]{0:T(128)} %param.6) | copy-start | bytes 52
  9.6 6.4 %collective-permute-start.2 = (f32[96,128]{1,0:T(8,128)S(1)}, f32[96,128]{1,0:T(8,128)S(1)}, u32[]{:S(2)}, u32[]{:S(2)}) collective-permute-start(f32[96,128]{1,0:T(8,128)S(1)} %get-tuple-element.18), channel_id=1, source_target_pairs={{0,4},{1,13},{2,6},{3,15},{4,8},{5,1},{6,10},{7,3},{8,12},{9,5},{1... | collective-permute-start | bytes 147464 | tf_op jit(solution)/shard_map/ppermute | solution.py:477
  11.3 6.5 %collective-permute-start.3 = (f32[96,128]{1,0:T(8,128)S(1)}, f32[96,128]{1,0:T(8,128)S(1)}, u32[]{:S(2)}, u32[]{:S(2)}) collective-permute-start(f32[96,128]{1,0:T(8,128)S(1)} %get-tuple-element.19), channel_id=1, source_target_pairs={{0,6},{1,11},{2,8},{3,13},{4,10},{5,15},{6,12},{7,1},{8,14},{9,3},... | collective-permute-start | bytes 147464 | tf_op jit(solution)/shard_map/ppermute | solution.py:477
  17.8 1.6 %collective-permute-start.5 = (f32[480,128]{1,0:T(8,128)S(1)}, f32[480,128]{1,0:T(8,128)S(1)}, u32[]{:S(2)}, u32[]{:S(2)}) collective-permute-start(f32[480,128]{1,0:T(8,128)S(1)} %pad_maximum_fusion.got_ref), channel_id=1, source_target_pairs={{0,1},{1,0},{2,3},{3,2},{4,5},{5,4},{6,7},{7,6},{8,9},{9,8},{10,11... | collective-permute-start | bytes 737288 | tf_op jit(solution)/shard_map/ppermute | solution.py:480

commit v9 on v8

--- a/solution.py
+++ b/solution.py
@@ -128,32 +128,21 @@
         far_ref[small_rows:] = other_ref[at : at + small_rows]
 
 
-def step_kernel(
-    cx, cy, count_x, full_rows, small_rows, own_ref, other_ref, got_ref, got_other_ref,
-    table_ref, out_ref, z_ref, cor_ref, pred_ref, store_ref, tile_ref, flip_ref, speed_ref,
-):
+def placer(cx, cy, count_x, full_rows, small_rows, z_ref, cor_ref):
     fields = z_ref.shape[0]
     levels = 4
-    slots = 16
-    cells = cx * count_x
-    faces = store_ref.shape[0] // 4
-    pairs = faces // 2
-    group = pairs * levels
+    group = z_ref.shape[1] // (cx * count_x + 8)
+    pairs = group // levels
     half = cx // 2
     chunk = cx * group
-    width = 2 * cx
     index_x = lax.axis_index("tx")
     index_y = lax.axis_index("ty")
+    south_half = lax.broadcasted_iota(jnp.int32, (group, LANES), 1) % WINDOW < MARGIN + cy
+    south_is_own = index_y == 0
+    own_half = south_half == south_is_own
 
     def row_of(x):
         return (x + 4) * group
-
-    def lanes_of(rows):
-        return lax.broadcasted_iota(jnp.int32, (rows, LANES), 1)
-
-    south_half = lanes_of(group) % WINDOW < MARGIN + cy
-    south_is_own = index_y == 0
-    own_half = south_half == south_is_own
 
     def from_owner(offset):
         source = (index_x - offset + 2 * count_x) % count_x
@@ -181,7 +170,7 @@
         starts_north = windows(source, index_x, count_x, 1, cx, cy)
 
         def lines_at(field, x, part):
-            at, lane = unit_place(field, x, cx, group, width)
+            at, lane = unit_place(field, x, cx, group, 2 * cx)
             south_shift = (MARGIN + starts_south[part] - lane + LANES) % LANES
             north_shift = (MARGIN + cy + starts_north[part] - lane + LANES) % LANES
             return lines_of(at, south_shift, north_shift)
@@ -194,26 +183,24 @@
             for x in range(half):
                 put_coriolis(start, part * half + x, values, x * pairs)
 
-    def own_lines(row, rows):
-        mine = own_ref[row : row + rows]
-        theirs = other_ref[row : row + rows]
-        up, down = index_y * cy, (1 - index_y) * cy
-        even = jnp.where(own_half[:rows], pltpu.roll(mine, up, 1), pltpu.roll(theirs, down, 1))
-        mine = pltpu.roll(mine, (LANES - down) % LANES, 1)
-        theirs = pltpu.roll(theirs, (LANES - up) % LANES, 1)
-        return even, jnp.where(own_half[:rows], mine, theirs)
-
-    put_block(from_owner(0)[1], own_lines)
-
-    sense = 1 - 2 * index_y
-    for block_ref, toward, south_first in (
-        (got_ref, sense, index_y),
-        (got_other_ref, -sense, 1 - index_y),
-    ):
+    def place_own(own_ref, other_ref):
+        def own_lines(row, rows):
+            mine = own_ref[row : row + rows]
+            theirs = other_ref[row : row + rows]
+            up, down = index_y * cy, (1 - index_y) * cy
+            keep = own_half[:rows]
+            even = jnp.where(keep, pltpu.roll(mine, up, 1), pltpu.roll(theirs, down, 1))
+            mine = pltpu.roll(mine, (LANES - down) % LANES, 1)
+            theirs = pltpu.roll(theirs, (LANES - up) % LANES, 1)
+            return even, jnp.where(keep, mine, theirs)
+
+        put_block(from_owner(0)[1], own_lines)
+
+    def place_got(block_ref, toward, south_first):
         south_top = pl.multiple_of(south_first * full_rows, 8)
         north_top = pl.multiple_of((1 - south_first) * full_rows, 8)
 
-        def near_lines(row, rows, block_ref=block_ref, south_top=south_top, north_top=north_top):
+        def near_lines(row, rows):
             south = block_ref[pl.ds(south_top + row, rows)]
             north = block_ref[pl.ds(north_top + row, rows)]
             low = south_half[:rows]
@@ -223,29 +210,63 @@
         put_block(from_owner(toward)[1], near_lines)
         for place, distance in enumerate((2, 3)):
             top = 2 * full_rows + 2 * place * small_rows
-            south_top = pl.multiple_of(top + south_first * small_rows, 8)
-            north_top = pl.multiple_of(top + (1 - south_first) * small_rows, 8)
-
-            def far_lines(
-                at, south_shift, north_shift,
-                block_ref=block_ref, south_top=south_top, north_top=north_top,
-            ):
-                south = block_ref[pl.ds(south_top + at, group)]
-                north = block_ref[pl.ds(north_top + at, group)]
-                south = pltpu.roll(south, south_shift, 1)
-                return jnp.where(south_half, south, pltpu.roll(north, north_shift, 1))
+            south_at = pl.multiple_of(top + south_first * small_rows, 8)
+            north_at = pl.multiple_of(top + (1 - south_first) * small_rows, 8)
+
+            def far_lines(at, south_shift, north_shift, south_at=south_at, north_at=north_at):
+                south = pltpu.roll(block_ref[pl.ds(south_at + at, group)], south_shift, 1)
+                north = pltpu.roll(block_ref[pl.ds(north_at + at, group)], north_shift, 1)
+                return jnp.where(south_half, south, north)
 
             put_distant(*from_owner(toward * distance), far_lines)
 
-    def middle_lines(at, south_shift, north_shift):
-        row = 2 * full_rows + 4 * small_rows + at
-        mine_shift = jnp.where(south_is_own, south_shift, north_shift)
-        other_shift = jnp.where(south_is_own, north_shift, south_shift)
-        mine = pltpu.roll(got_ref[row : row + group], mine_shift, 1)
-        theirs = pltpu.roll(got_other_ref[row : row + group], other_shift, 1)
-        return jnp.where(own_half, mine, theirs)
-
-    put_distant(*from_owner(count_x // 2), middle_lines)
+    def place_middle(got_ref, got_other_ref):
+        def middle_lines(at, south_shift, north_shift):
+            row = 2 * full_rows + 4 * small_rows + at
+            mine_shift = jnp.where(south_is_own, south_shift, north_shift)
+            other_shift = jnp.where(south_is_own, north_shift, south_shift)
+            mine = pltpu.roll(got_ref[row : row + group], mine_shift, 1)
+            theirs = pltpu.roll(got_other_ref[row : row + group], other_shift, 1)
+            return jnp.where(own_half, mine, theirs)
+
+        put_distant(*from_owner(count_x // 2), middle_lines)
+
+    return place_own, place_got, place_middle
+
+
+def own_kernel(sizes, own_ref, other_ref, z_ref, cor_ref):
+    placer(*sizes, z_ref, cor_ref)[0](own_ref, other_ref)
+
+
+def got_kernel(sizes, got_ref, z_in, cor_in, z_ref, cor_ref):
+    index_y = lax.axis_index("ty")
+    placer(*sizes, z_ref, cor_ref)[1](got_ref, 1 - 2 * index_y, index_y)
+
+
+def step_kernel(
+    sizes, got_ref, got_other_ref, table_ref, z_in, cor_in, out_ref, z_ref, cor_ref,
+    pred_ref, store_ref, tile_ref, flip_ref, speed_ref,
+):
+    cx, cy, count_x = sizes[:3]
+    levels = 4
+    slots = 16
+    cells = cx * count_x
+    faces = store_ref.shape[0] // 4
+    pairs = faces // 2
+    group = pairs * levels
+    chunk = cx * group
+    index_x = lax.axis_index("tx")
+    index_y = lax.axis_index("ty")
+
+    def row_of(x):
+        return (x + 4) * group
+
+    def lanes_of(rows):
+        return lax.broadcasted_iota(jnp.int32, (rows, LANES), 1)
+
+    _, place_got, place_middle = placer(*sizes, z_ref, cor_ref)
+    place_got(got_other_ref, 2 * index_y - 1, 1 - index_y)
+    place_middle(got_ref, got_other_ref)
 
     level_of = lax.broadcasted_iota(jnp.int32, speed_ref.shape, 0) % levels
     speeds = jnp.full(speed_ref.shape, table_ref[0], jnp.float32)
@@ -495,20 +516,41 @@
     got = jnp.concatenate([*got, moved(middle, count_x // 2)])
     table = jnp.concatenate([wave_speed, edges.reshape(-1).astype(jnp.float32)])
     got, table = lax.optimization_barrier((got, table))
-    pieces = (swap, other, got, across(got))
-    z_rows = (cells + 8) * group
-    out = pl.pallas_call(
-        functools.partial(
-            step_kernel, cx, cy, count_x, full_rows, small_rows
-        ),
-        out_shape=jax.ShapeDtypeStruct((faces, fields, cx, levels, cy), jnp.float32),
-        in_specs=[pl.BlockSpec(memory_space=pltpu.VMEM)] * 4
-        + [pl.BlockSpec(memory_space=pltpu.SMEM)],
-        out_specs=pl.BlockSpec(memory_space=pltpu.VMEM),
+    passed = across(got)
+
+    sizes = (cx, cy, count_x, full_rows, small_rows)
+    state_rows = [
+        jax.ShapeDtypeStruct((fields, (cells + 8) * group, LANES), jnp.float32),
+        jax.ShapeDtypeStruct((cells * group, LANES), jnp.float32),
+    ]
+    in_vmem = pl.BlockSpec(memory_space=pltpu.VMEM)
+    params = pltpu.CompilerParams(vmem_limit_bytes=SMALL_VMEM_LIMIT)
+    rows = pl.pallas_call(
+        functools.partial(own_kernel, sizes),
+        out_shape=state_rows,
+        in_specs=[in_vmem] * 2,
+        out_specs=[in_vmem] * 2,
+        compiler_params=params,
+        name="place_own",
+    )(swap, other)
+    rows = pl.pallas_call(
+        functools.partial(got_kernel, sizes),
+        out_shape=state_rows,
+        in_specs=[in_vmem] * 3,
+        out_specs=[in_vmem] * 2,
+        input_output_aliases={1: 0, 2: 1},
+        compiler_params=params,
+        name="place_got",
+    )(got, *rows)
+    out, _, _ = pl.pallas_call(
+        functools.partial(step_kernel, sizes),
+        out_shape=[jax.ShapeDtypeStruct((faces, fields, cx, levels, cy), jnp.float32)]
+        + state_rows,
+        in_specs=[in_vmem] * 2 + [pl.BlockSpec(memory_space=pltpu.SMEM)] + [in_vmem] * 2,
+        out_specs=[in_vmem] * 3,
+        input_output_aliases={3: 1, 4: 2},
         scratch_shapes=[
-            pltpu.VMEM((fields, z_rows, LANES), jnp.float32),
-            pltpu.VMEM((cells * group, LANES), jnp.float32),
-            pltpu.VMEM((z_rows, LANES), jnp.float32),
+            pltpu.VMEM(((cells + 8) * group, LANES), jnp.float32),
             pltpu.VMEM((faces * 4, 32, LANES), jnp.float32),
             pltpu.VMEM((faces, LANES, LANES), jnp.float32),
             pltpu.VMEM((pairs, LANES, LANES), jnp.float32),
@@ -516,7 +558,7 @@
         ],
         compiler_params=pltpu.CompilerParams(vmem_limit_bytes=VMEM_LIMIT),
         name="substeps",
-    )(*pieces, table)
+    )(got, passed, table, *rows)
     return jnp.swapaxes(out, 2, 3)
 
 

time: 25 us -> 24.7 us (0.988)
  waiting for transfers between devices: 8.39 us -> 7.95 us
    ppermute x2, waiting for transfers between devices: 2.26 us -> 1.81 us  [across(): return lax.ppermute(block, 'ty', [(0, 1), (1, 0)])]
    pallas_call x1 -> x3, Pallas kernels: 5.45 us -> 5.61 us  [the longest x1 5.17 us: fast_on_device(): pl.pallas_call(functools.partial(step_kernel, sizes), out_shape=[jax.Shap...]
  transfers between devices with their start and end apart: 6 -> 6, of which waited for: 4 -> 4; matrix products, arithmetic and copies ran while one was open for 1% -> 1% of each run, Pallas kernels for 1% -> 3%
where the time goes in v9:
time: 24.7 us; the launch traced here: 24.5 us
  starting transfers between devices  8.01 us (32%)
  waiting for transfers between devices  7.95 us (32%)
  Pallas kernels  6.5 us (26%)
  local copies, waits for them, and re-layouts  1.9 us (8%)
    ppermute x4, starting transfers between devices, moved(): return lax.ppermute(block, ('tx', 'ty'), pairs_of)  7.42 us
    ppermute x4, waiting for transfers between devices, moved(): return lax.ppermute(block, ('tx', 'ty'), pairs_of)  6.13 us
    pallas_call x1, Pallas kernels, fast_on_device(): pl.pallas_call(functools.partial(step_kernel, sizes), out_shape=[jax.Shap...  5.17 us
    ppermute x2, waiting for transfers between devices, across(): return lax.ppermute(block, 'ty', [(0, 1), (1, 0)])  1.81 us
    unnamed x8, local copies, waits for them, and re-layouts  1.68 us
    pallas_call x1, Pallas kernels, fast_on_device(): pl.pallas_call(functools.partial(pack_kernel, cx, cy, count_x, full_rows,...  0.69 us
    ppermute x2, starting transfers between devices, across(): return lax.ppermute(block, 'ty', [(0, 1), (1, 0)])  0.59 us
  transfers between devices with their start and end apart: 6, of which 4 were waited for; matrix products, arithmetic and copies ran while one was open for 1% of the time, Pallas kernels for 3%

profile of v9, /device:TPU:0, one launch (start us, length us, event | category | flops | bytes accessed | tf_op | source)
XLA Modules:
  0.0 24.5 jit_solution(16053180253092599430)
XLA Ops:
  0.0 0.0 copy-start
  0.0 0.9 %copy-done = f32[6,3,4,6,24]{4,2,3,1,0:T(4,128)S(1)} copy-done((f32[6,3,4,6,24]{4,2,3,1,0:T(4,128)S(1)}, f32[6,3,4,6,24]{4,2,3,1,0:T(4,128)}, u32[]{:S(2)}) %copy-start) | copy-done | bytes 41496
  0.9 0.0 copy-start.1
  0.9 0.7 %copy-done.1 = f32[6,6,24]{2,1,0:T(8,128)S(1)} copy-done((f32[6,6,24]{2,1,0:T(8,128)S(1)}, f32[6,6,24]{2,1,0:T(8,128)}, u32[]{:S(2)}) %copy-start.1) | copy-done | bytes 3480
  1.7 0.7 %pack.1 = (f32[216,128]{1,0:T(8,128)S(1)}, f32[32,128]{1,0:T(8,128)S(1)}) custom-call(f32[6,3,6,4,24]{4,3,2,1,0:T(4,128)S(1)} %bitcast.2, f32[6,6,24]{2,1,0:T(8,128)S(1)} %copy-done.1), custom_call_target="tpu_custom_call" | custom-call | tf_op jit(solution)/shard_map/pack/pallas_call | solution.py:464
  2.4 0.5 %collective-permute-start = (f32[216,128]{1,0:T(8,128)S(1)}, f32[216,128]{1,0:T(8,128)S(1)}, u32[]{:S(2)}, u32[]{:S(2)}) collective-permute-start(f32[216,128]{1,0:T(8,128)S(1)} %get-tuple-element.19.swap_ref.own_ref), channel_id=1, source_target_pairs={{0,1},{1,0},{2,3},{3,2},{4,5},{5,4},{6,7},{7,6},{8,9},{9,8},{10,11... | collective-permute-start | bytes 331784 | tf_op jit(solution)/shard_map/ppermute | solution.py:501
  2.9 0.2 keep.1
  3.1 0.8 %collective-permute-done.other_ref = f32[216,128]{1,0:T(8,128)S(1)} collective-permute-done((f32[216,128]{1,0:T(8,128)S(1)}, f32[216,128]{1,0:T(8,128)S(1)}, u32[]{:S(2)}, u32[]{:S(2)}) %collective-permute-start) | collective-permute-done | bytes 110624 | tf_op jit(solution)/shard_map/ppermute | solution.py:501
  3.8 0.0 copy-start.2
  3.9 2.9 %collective-permute-start.1 = (f32[240,128]{1,0:T(8,128)S(1)}, f32[240,128]{1,0:T(8,128)S(1)}, u32[]{:S(2)}, u32[]{:S(2)}) collective-permute-start(f32[240,128]{1,0:T(8,128)S(1)} %get-tuple-element.22), channel_id=1, source_target_pairs={{0,2},{1,15},{2,4},{3,1},{4,6},{5,3},{6,8},{7,5},{8,10},{9,7},{10,... | collective-permute-start | bytes 368648 | tf_op jit(solution)/shard_map/ppermute | solution.py:498
  6.8 2.6 %collective-permute-start.4 = (f32[48,128]{1,0:T(8,128)S(1)}, f32[48,128]{1,0:T(8,128)S(1)}, u32[]{:S(2)}, u32[]{:S(2)}) collective-permute-start(f32[48,128]{1,0:T(8,128)S(1)} %get-tuple-element.25), channel_id=1, source_target_pairs={{0,8},{1,9},{2,10},{3,11},{4,12},{5,13},{6,14},{7,15},{8,0},{9,1},... | collective-permute-start | bytes 73736 | tf_op jit(solution)/shard_map/ppermute | solution.py:498
  9.4 0.0 copy-done.2
  9.4 0.1 copy.10
  9.5 0.1 convert_element_type.7
  9.6 0.0 copy-start.3
  9.6 1.6 %collective-permute-start.2 = (f32[96,128]{1,0:T(8,128)S(1)}, f32[96,128]{1,0:T(8,128)S(1)}, u32[]{:S(2)}, u32[]{:S(2)}) collective-permute-start(f32[96,128]{1,0:T(8,128)S(1)} %get-tuple-element.23), channel_id=1, source_target_pairs={{0,4},{1,13},{2,6},{3,15},{4,8},{5,1},{6,10},{7,3},{8,12},{9,5},{1... | collective-permute-start | bytes 147464 | tf_op jit(solution)/shard_map/ppermute | solution.py:498
  11.3 0.3 %collective-permute-start.3 = (f32[96,128]{1,0:T(8,128)S(1)}, f32[96,128]{1,0:T(8,128)S(1)}, u32[]{:S(2)}, u32[]{:S(2)}) collective-permute-start(f32[96,128]{1,0:T(8,128)S(1)} %get-tuple-element.24), channel_id=1, source_target_pairs={{0,6},{1,11},{2,8},{3,13},{4,10},{5,15},{6,12},{7,1},{8,14},{9,3},... | collective-permute-start | bytes 147464 | tf_op jit(solution)/shard_map/ppermute | solution.py:498
  11.5 0.0 copy-done.3
  11.5 0.1 pad_maximum_fusion.1.table_ref
  11.6 0.0 collective-permute-done.4
  11.6 4.4 %collective-permute-done.2 = f32[96,128]{1,0:T(8,128)S(1)} collective-permute-done((f32[96,128]{1,0:T(8,128)S(1)}, f32[96,128]{1,0:T(8,128)S(1)}, u32[]{:S(2)}, u32[]{:S(2)}) %collective-permute-start.2) | collective-permute-done | bytes 49184 | tf_op jit(solution)/shard_map/ppermute | solution.py:498
  16.0 1.7 %collective-permute-done.3 = f32[96,128]{1,0:T(8,128)S(1)} collective-permute-done((f32[96,128]{1,0:T(8,128)S(1)}, f32[96,128]{1,0:T(8,128)S(1)}, u32[]{:S(2)}, u32[]{:S(2)}) %collective-permute-start.3) | collective-permute-done | bytes 49184 | tf_op jit(solution)/shard_map/ppermute | solution.py:498
  17.7 0.0 collective-permute-done.1
  17.8 0.1 collective-permute-start.5
  17.8 0.2 place_own.1
  18.0 0.3 %place_got.1 = (f32[3,672,128]{2,1,0:T(8,128)S(1)}, f32[576,128]{1,0:T(8,128)S(1)}) custom-call(f32[480,128]{1,0:T(8,128)S(1)} %pad_maximum_fusion.got_ref, f32[3,672,128]{2,1,0:T(8,128)S(1)} %get-tuple-element.28.z_in, f32[576,128]{1,0:T(8,128)S(1)} %get-tuple-element.29.cor_in), custom_call_target="tpu_custom_call", output_to_operand_aliasing={{0}: (1, {}), {1}: (2, {})} | custom-call | tf_op jit(solution)/shard_map/place_got/pallas_call | solution.py:536
  18.3 1.1 %collective-permute-done.5.got_other_ref = f32[480,128]{1,0:T(8,128)S(1)} collective-permute-done((f32[480,128]{1,0:T(8,128)S(1)}, f32[480,128]{1,0:T(8,128)S(1)}, u32[]{:S(2)}, u32[]{:S(2)}) %collective-permute-start.5) | collective-permute-done | bytes 245792 | tf_op jit(solution)/shard_map/ppermute | solution.py:501
  19.3 5.2 %substeps.1 = (f32[6,3,6,4,24]{4,3,2,1,0:T(4,128)}, f32[3,672,128]{2,1,0:T(8,128)S(1)}, f32[576,128]{1,0:T(8,128)S(1)}) custom-call(f32[480,128]{1,0:T(8,128)S(1)} %pad_maximum_fusion.got_ref, f32[480,128]{1,0:T(8,128)S(1)} %collective-permute-done.5.got_other_ref, f32[76]{0:T(128)S(1)} %pad_maximum_fusion.1.table_ref, ...), custom_call_target="tpu_custom_call", output_to_operand_aliasing={{1}: (3, {}), {2}: (4, {})} | custom-call | tf_op jit(solution)/shard_map/substeps/pallas_call | solution.py:545
  (3 shorter events, 0.0 us)
Async XLA Ops:
  0.0 0.9 %copy-start = (f32[6,3,4,6,24]{4,2,3,1,0:T(4,128)S(1)}, f32[6,3,4,6,24]{4,2,3,1,0:T(4,128)}, u32[]{:S(2)}) copy-start(f32[6,3,4,6,24]{4,2,3,1,0:T(4,128)} %param.4) | copy-start | bytes 124420
  0.9 0.7 %copy-start.1 = (f32[6,6,24]{2,1,0:T(8,128)S(1)}, f32[6,6,24]{2,1,0:T(8,128)}, u32[]{:S(2)}) copy-start(f32[6,6,24]{2,1,0:T(8,128)} %coriolis_hbm.1) | copy-start | bytes 10372
  2.4 1.5 %collective-permute-start = (f32[216,128]{1,0:T(8,128)S(1)}, f32[216,128]{1,0:T(8,128)S(1)}, u32[]{:S(2)}, u32[]{:S(2)}) collective-permute-start(f32[216,128]{1,0:T(8,128)S(1)} %get-tuple-element.19.swap_ref.own_ref), channel_id=1, source_target_pairs={{0,1},{1,0},{2,3},{3,2},{4,5},{5,4},{6,7},{7,6},{8,9},{9,8},{10,11... | collective-permute-start | bytes 331784 | tf_op jit(solution)/shard_map/ppermute | solution.py:501
  3.8 5.5 %copy-start.2 = (s32[6,4,3]{0,1,2:T(4,128)S(1)}, s32[6,4,3]{0,1,2:T(4,128)}, u32[]{:S(2)}) copy-start(s32[6,4,3]{0,1,2:T(4,128)} %param.7) | copy-start | bytes 868
  3.9 13.9 %collective-permute-start.1 = (f32[240,128]{1,0:T(8,128)S(1)}, f32[240,128]{1,0:T(8,128)S(1)}, u32[]{:S(2)}, u32[]{:S(2)}) collective-permute-start(f32[240,128]{1,0:T(8,128)S(1)} %get-tuple-element.22), channel_id=1, source_target_pairs={{0,2},{1,15},{2,4},{3,1},{4,6},{5,3},{6,8},{7,5},{8,10},{9,7},{10,... | collective-permute-start | bytes 368648 | tf_op jit(solution)/shard_map/ppermute | solution.py:498
  6.8 4.8 %collective-permute-start.4 = (f32[48,128]{1,0:T(8,128)S(1)}, f32[48,128]{1,0:T(8,128)S(1)}, u32[]{:S(2)}, u32[]{:S(2)}) collective-permute-start(f32[48,128]{1,0:T(8,128)S(1)} %get-tuple-element.25), channel_id=1, source_target_pairs={{0,8},{1,9},{2,10},{3,11},{4,12},{5,13},{6,14},{7,15},{8,0},{9,1},... | collective-permute-start | bytes 73736 | tf_op jit(solution)/shard_map/ppermute | solution.py:498
  9.6 1.9 %copy-start.3 = (f32[4]{0:T(128)S(1)}, f32[4]{0:T(128)}, u32[]{:S(2)}) copy-start(f32[4]{0:T(128)} %param.6) | copy-start | bytes 52
  9.6 6.4 %collective-permute-start.2 = (f32[96,128]{1,0:T(8,128)S(1)}, f32[96,128]{1,0:T(8,128)S(1)}, u32[]{:S(2)}, u32[]{:S(2)}) collective-permute-start(f32[96,128]{1,0:T(8,128)S(1)} %get-tuple-element.23), channel_id=1, source_target_pairs={{0,4},{1,13},{2,6},{3,15},{4,8},{5,1},{6,10},{7,3},{8,12},{9,5},{1... | collective-permute-start | bytes 147464 | tf_op jit(solution)/shard_map/ppermute | solution.py:498
  11.3 6.5 %collective-permute-start.3 = (f32[96,128]{1,0:T(8,128)S(1)}, f32[96,128]{1,0:T(8,128)S(1)}, u32[]{:S(2)}, u32[]{:S(2)}) collective-permute-start(f32[96,128]{1,0:T(8,128)S(1)} %get-tuple-element.24), channel_id=1, source_target_pairs={{0,6},{1,11},{2,8},{3,13},{4,10},{5,15},{6,12},{7,1},{8,14},{9,3},... | collective-permute-start | bytes 147464 | tf_op jit(solution)/shard_map/ppermute | solution.py:498
  17.8 1.6 %collective-permute-start.5 = (f32[480,128]{1,0:T(8,128)S(1)}, f32[480,128]{1,0:T(8,128)S(1)}, u32[]{:S(2)}, u32[]{:S(2)}) collective-permute-start(f32[480,128]{1,0:T(8,128)S(1)} %pad_maximum_fusion.got_ref), channel_id=1, source_target_pairs={{0,1},{1,0},{2,3},{3,2},{4,5},{5,4},{6,7},{7,6},{8,9},{9,8},{10,11... | collective-permute-start | bytes 737288 | tf_op jit(solution)/shard_map/ppermute | solution.py:501

commit v10 on v9

--- a/solution.py
+++ b/solution.py
@@ -11,6 +11,7 @@
 LANES = 128
 WINDOW = 64
 MARGIN = 8
+STRIDE = 13
 VMEM_LIMIT = 32 * 1024 * 1024
 SMALL_VMEM_LIMIT = 8 * 1024 * 1024
 
@@ -131,10 +132,9 @@
 def placer(cx, cy, count_x, full_rows, small_rows, z_ref, cor_ref):
     fields = z_ref.shape[0]
     levels = 4
-    group = z_ref.shape[1] // (cx * count_x + 8)
-    pairs = group // levels
+    pairs = 3
+    group = pairs * levels
     half = cx // 2
-    chunk = cx * group
     index_x = lax.axis_index("tx")
     index_y = lax.axis_index("ty")
     south_half = lax.broadcasted_iota(jnp.int32, (group, LANES), 1) % WINDOW < MARGIN + cy
@@ -142,16 +142,16 @@
     own_half = south_half == south_is_own
 
     def row_of(x):
-        return (x + 4) * group
+        return (x + 4) * STRIDE
 
     def from_owner(offset):
         source = (index_x - offset + 2 * count_x) % count_x
-        return source, pl.multiple_of(source * chunk, 8)
+        return source, source * (cx * STRIDE)
 
     def put_coriolis(start, x, values, at):
         for pair in range(pairs):
             line = values[at + pair : at + pair + 1]
-            rows = pl.ds(start + x * group + pair * levels, levels)
+            rows = pl.ds(start + x * STRIDE + pair * levels, levels)
             cor_ref[rows] = jnp.broadcast_to(line, (levels, LANES))
 
     def put_block(start, lines_of):
@@ -253,7 +253,7 @@
     cells = cx * count_x
     faces = store_ref.shape[0] // 4
     pairs = faces // 2
-    group = pairs * levels
+    group = STRIDE
     chunk = cx * group
     index_x = lax.axis_index("tx")
     index_y = lax.axis_index("ty")
@@ -268,7 +268,7 @@
     place_got(got_other_ref, 2 * index_y - 1, 1 - index_y)
     place_middle(got_ref, got_other_ref)
 
-    level_of = lax.broadcasted_iota(jnp.int32, speed_ref.shape, 0) % levels
+    level_of = lax.broadcasted_iota(jnp.int32, speed_ref.shape, 0) % group % levels
     speeds = jnp.full(speed_ref.shape, table_ref[0], jnp.float32)
     for index in range(1, levels):
         speeds = jnp.where(level_of == index, table_ref[index], speeds)
@@ -345,19 +345,21 @@
                     row = row_of(x) + pair * levels
                     z_ref[slot, row : row + levels] = both[at : at + levels]
 
-    def tile_rows(odd, side, depth):
+    wide = WINDOW - cells - 3 + 3 * levels
+
+    def tile_rows(odd, side, depth, base=0):
         if side == 3:
-            return pl.ds(odd * WINDOW + depth, levels, 16)
-        return pl.ds(((odd + 1) % 2) * WINDOW + 15 - depth, levels, 16)
-
-    def put_columns(lines, field, start, pair):
+            return pl.ds(base + odd * WINDOW + depth, levels, 3)
+        return pl.ds(base + ((odd + 1) % 2) * WINDOW + wide - 3 * levels + 2 - depth, levels, 3)
+
+    def put_columns(lines, field, start, pair, base=0):
         count = lines.shape[0]
         position = lanes_of(count) % WINDOW
         rim = ((position >= MARGIN - 3) & (position < MARGIN)) | (
             (position >= MARGIN + cells) & (position < MARGIN + cells + 3)
         )
         for level in range(levels):
-            rolled = pltpu.roll(lines, (MARGIN + cells - 16 * level) % LANES, 1)
+            rolled = pltpu.roll(lines, (MARGIN + cells - base - 3 * level) % LANES, 1)
             at = pl.ds(row_of(start) + pair * levels + level, count, group)
             z_ref[field, at] = jnp.where(rim, rolled, z_ref[field, at])
 
@@ -369,11 +371,11 @@
                     for slot in range(2):
                         for depth in range(3):
                             at = slot * slots + depth * levels
-                            tile_ref[2 * pair + slot, tile_rows(odd, side, depth)] = block[
-                                at : at + levels
-                            ]
+                            rows = tile_rows(odd, side, depth, slot * wide)
+                            tile_ref[pair, rows] = block[at : at + levels]
+            turned = tile_ref[pair].T[:cells]
             for slot, field in ((0, 0), (1, 2)):
-                put_columns(tile_ref[2 * pair + slot].T[:cells], field, 0, pair)
+                put_columns(turned, field, 0, pair, slot * wide)
 
     def rim_columns_own():
         lane = lanes_of(2 * slots)
@@ -440,7 +442,7 @@
         rim_rows(1)
 
     rim_columns_own()
-    at = pl.multiple_of(row_of(0) + index_x * chunk, 8)
+    at = row_of(0) + index_x * chunk
     predict(at - 2 * group, chunk + 4 * group)
     for field, values in enumerate(update(at, chunk)):
         for odd in range(2):
@@ -520,8 +522,8 @@
 
     sizes = (cx, cy, count_x, full_rows, small_rows)
     state_rows = [
-        jax.ShapeDtypeStruct((fields, (cells + 8) * group, LANES), jnp.float32),
-        jax.ShapeDtypeStruct((cells * group, LANES), jnp.float32),
+        jax.ShapeDtypeStruct((fields, (cells + 8) * STRIDE, LANES), jnp.float32),
+        jax.ShapeDtypeStruct((cells * STRIDE, LANES), jnp.float32),
     ]
     in_vmem = pl.BlockSpec(memory_space=pltpu.VMEM)
     params = pltpu.CompilerParams(vmem_limit_bytes=SMALL_VMEM_LIMIT)
@@ -550,11 +552,11 @@
         out_specs=[in_vmem] * 3,
         input_output_aliases={3: 1, 4: 2},
         scratch_shapes=[
-            pltpu.VMEM(((cells + 8) * group, LANES), jnp.float32),
+            pltpu.VMEM(((cells + 8) * STRIDE, LANES), jnp.float32),
             pltpu.VMEM((faces * 4, 32, LANES), jnp.float32),
-            pltpu.VMEM((faces, LANES, LANES), jnp.float32),
             pltpu.VMEM((pairs, LANES, LANES), jnp.float32),
-            pltpu.VMEM(((cx + 4) * group, LANES), jnp.float32),
+            pltpu.VMEM((pairs, LANES, LANES), jnp.float32),
+            pltpu.VMEM(((cx + 4) * STRIDE, LANES), jnp.float32),
         ],
         compiler_params=pltpu.CompilerParams(vmem_limit_bytes=VMEM_LIMIT),
         name="substeps",

time: 24.7 us -> 25.5 us (1.032)
  other arithmetic: 0.09 us -> 1.44 us
  waiting for transfers between devices: 7.95 us -> 7.3 us
    convert_element_type x1, other arithmetic: 0.01 us -> 0.69 us  [fast_on_device(): table = jnp.concatenate([wave_speed, edges.reshape(-1).astype(jnp.float32)])]
    concatenate x1, other arithmetic: 0.07 us -> 0.73 us  [fast_on_device(): table = jnp.concatenate([wave_speed, edges.reshape(-1).astype(jnp.float32)])]
    ppermute x4, waiting for transfers between devices: 6.13 us -> 5.48 us  [moved(): return lax.ppermute(block, ('tx', 'ty'), pairs_of)]
    unnamed x8 -> x4, local copies, waits for them, and re-layouts: 1.68 us -> 1.67 us
  transfers between devices with their start and end apart: 6 -> 6, of which waited for: 4 -> 4; matrix products, arithmetic and copies ran while one was open for 1% -> 6% of each run, Pallas kernels for 3% -> 2%
where the time goes in v10:
time: 25.5 us; the launch traced here: 25.3 us
  starting transfers between devices  8.01 us (31%)
  waiting for transfers between devices  7.3 us (29%)
  Pallas kernels  6.6 us (26%)
  local copies, waits for them, and re-layouts  1.89 us (7%)
  other arithmetic  1.44 us (6%)
    ppermute x4, starting transfers between devices, moved(): return lax.ppermute(block, ('tx', 'ty'), pairs_of)  7.42 us
    ppermute x4, waiting for transfers between devices, moved(): return lax.ppermute(block, ('tx', 'ty'), pairs_of)  5.48 us
    pallas_call x1, Pallas kernels, fast_on_device(): pl.pallas_call(functools.partial(step_kernel, sizes), out_shape=[jax.Shap...  5.27 us
    ppermute x2, waiting for transfers between devices, across(): return lax.ppermute(block, 'ty', [(0, 1), (1, 0)])  1.81 us
    unnamed x4, local copies, waits for them, and re-layouts  1.67 us
    concatenate x1, other arithmetic, fast_on_device(): table = jnp.concatenate([wave_speed, edges.reshape(-1).astype(jnp.float32)])  0.73 us
    convert_element_type x1, other arithmetic, fast_on_device(): table = jnp.concatenate([wave_speed, edges.reshape(-1).astype(jnp.float32)])  0.69 us
    pallas_call x1, Pallas kernels, fast_on_device(): pl.pallas_call(functools.partial(pack_kernel, cx, cy, count_x, full_rows,...  0.69 us
  transfers between devices with their start and end apart: 6, of which 4 were waited for; matrix products, arithmetic and copies ran while one was open for 6% of the time, Pallas kernels for 2%

profile of v10, /device:TPU:0, one launch (start us, length us, event | category | flops | bytes accessed | tf_op | source)
XLA Modules:
  0.0 25.3 jit_solution(8172106949771516252)
XLA Ops:
  0.0 0.0 copy-start
  0.0 0.9 %copy-done = f32[6,3,4,6,24]{4,2,3,1,0:T(4,128)S(1)} copy-done((f32[6,3,4,6,24]{4,2,3,1,0:T(4,128)S(1)}, f32[6,3,4,6,24]{4,2,3,1,0:T(4,128)}, u32[]{:S(2)}) %copy-start) | copy-done | bytes 41496
  0.9 0.0 copy-start.1
  0.9 0.7 %copy-done.1 = f32[6,6,24]{2,1,0:T(8,128)S(1)} copy-done((f32[6,6,24]{2,1,0:T(8,128)S(1)}, f32[6,6,24]{2,1,0:T(8,128)}, u32[]{:S(2)}) %copy-start.1) | copy-done | bytes 3480
  1.7 0.7 %pack.1 = (f32[216,128]{1,0:T(8,128)S(1)}, f32[32,128]{1,0:T(8,128)S(1)}) custom-call(f32[6,3,6,4,24]{4,3,2,1,0:T(4,128)S(1)} %bitcast.2, f32[6,6,24]{2,1,0:T(8,128)S(1)} %copy-done.1), custom_call_target="tpu_custom_call" | custom-call | tf_op jit(solution)/shard_map/pack/pallas_call | solution.py:466
  2.4 0.5 %collective-permute-start = (f32[216,128]{1,0:T(8,128)S(1)}, f32[216,128]{1,0:T(8,128)S(1)}, u32[]{:S(2)}, u32[]{:S(2)}) collective-permute-start(f32[216,128]{1,0:T(8,128)S(1)} %get-tuple-element.19.swap_ref.own_ref), channel_id=1, source_target_pairs={{0,1},{1,0},{2,3},{3,2},{4,5},{5,4},{6,7},{7,6},{8,9},{9,8},{10,11... | collective-permute-start | bytes 331784 | tf_op jit(solution)/shard_map/ppermute | solution.py:503
  2.9 0.2 keep.1
  3.1 0.8 %collective-permute-done.other_ref = f32[216,128]{1,0:T(8,128)S(1)} collective-permute-done((f32[216,128]{1,0:T(8,128)S(1)}, f32[216,128]{1,0:T(8,128)S(1)}, u32[]{:S(2)}, u32[]{:S(2)}) %collective-permute-start) | collective-permute-done | bytes 110624 | tf_op jit(solution)/shard_map/ppermute | solution.py:503
  3.9 2.9 %collective-permute-start.1 = (f32[240,128]{1,0:T(8,128)S(1)}, f32[240,128]{1,0:T(8,128)S(1)}, u32[]{:S(2)}, u32[]{:S(2)}) collective-permute-start(f32[240,128]{1,0:T(8,128)S(1)} %get-tuple-element.22), channel_id=1, source_target_pairs={{0,2},{1,15},{2,4},{3,1},{4,6},{5,3},{6,8},{7,5},{8,10},{9,7},{10,... | collective-permute-start | bytes 368648 | tf_op jit(solution)/shard_map/ppermute | solution.py:500
  6.8 2.6 %collective-permute-start.4 = (f32[48,128]{1,0:T(8,128)S(1)}, f32[48,128]{1,0:T(8,128)S(1)}, u32[]{:S(2)}, u32[]{:S(2)}) collective-permute-start(f32[48,128]{1,0:T(8,128)S(1)} %get-tuple-element.25), channel_id=1, source_target_pairs={{0,8},{1,9},{2,10},{3,11},{4,12},{5,13},{6,14},{7,15},{8,0},{9,1},... | collective-permute-start | bytes 73736 | tf_op jit(solution)/shard_map/ppermute | solution.py:500
  9.4 0.7 %convert_element_type.6 = f32[6,4,3]{0,1,2:T(4,128)S(1)} convert(s32[6,4,3]{0,1,2:T(4,128)} %param.7) | non-fusion elementwise | flops 72 | bytes 576 | tf_op jit(solution)/shard_map/convert_element_type | solution.py:519
  10.1 0.1 copy.10
  10.2 0.1 convert_element_type.7
  10.3 1.6 %collective-permute-start.2 = (f32[96,128]{1,0:T(8,128)S(1)}, f32[96,128]{1,0:T(8,128)S(1)}, u32[]{:S(2)}, u32[]{:S(2)}) collective-permute-start(f32[96,128]{1,0:T(8,128)S(1)} %get-tuple-element.23), channel_id=1, source_target_pairs={{0,4},{1,13},{2,6},{3,15},{4,8},{5,1},{6,10},{7,3},{8,12},{9,5},{1... | collective-permute-start | bytes 147464 | tf_op jit(solution)/shard_map/ppermute | solution.py:500
  11.9 0.3 %collective-permute-start.3 = (f32[96,128]{1,0:T(8,128)S(1)}, f32[96,128]{1,0:T(8,128)S(1)}, u32[]{:S(2)}, u32[]{:S(2)}) collective-permute-start(f32[96,128]{1,0:T(8,128)S(1)} %get-tuple-element.24), channel_id=1, source_target_pairs={{0,6},{1,11},{2,8},{3,13},{4,10},{5,15},{6,12},{7,1},{8,14},{9,3},... | collective-permute-start | bytes 147464 | tf_op jit(solution)/shard_map/ppermute | solution.py:500
  12.2 0.7 %pad_maximum_fusion.1.table_ref = f32[76]{0:T(128)S(1)} fusion(f32[72]{0:T(128)S(1)} %convert_element_type.7, f32[4]{0:T(128)} %param.6), kind=kLoop, calls=%fused_computation.1 | loop fusion | flops 76 | bytes 608 | tf_op jit(solution)/shard_map/concatenate | solution.py:519
  12.9 0.0 collective-permute-done.4
  12.9 3.7 %collective-permute-done.2 = f32[96,128]{1,0:T(8,128)S(1)} collective-permute-done((f32[96,128]{1,0:T(8,128)S(1)}, f32[96,128]{1,0:T(8,128)S(1)}, u32[]{:S(2)}, u32[]{:S(2)}) %collective-permute-start.2) | collective-permute-done | bytes 49184 | tf_op jit(solution)/shard_map/ppermute | solution.py:500
  16.7 1.7 %collective-permute-done.3 = f32[96,128]{1,0:T(8,128)S(1)} collective-permute-done((f32[96,128]{1,0:T(8,128)S(1)}, f32[96,128]{1,0:T(8,128)S(1)}, u32[]{:S(2)}, u32[]{:S(2)}) %collective-permute-start.3) | collective-permute-done | bytes 49184 | tf_op jit(solution)/shard_map/ppermute | solution.py:500
  18.4 0.0 collective-permute-done.1
  18.4 0.1 collective-permute-start.5
  18.5 0.2 place_own.1
  18.7 0.3 %place_got.1 = (f32[3,728,128]{2,1,0:T(8,128)S(1)}, f32[624,128]{1,0:T(8,128)S(1)}) custom-call(f32[480,128]{1,0:T(8,128)S(1)} %pad_maximum_fusion.got_ref, f32[3,728,128]{2,1,0:T(8,128)S(1)} %get-tuple-element.28.z_in, f32[624,128]{1,0:T(8,128)S(1)} %get-tuple-element.29.cor_in), custom_call_target="tpu_custom_call", output_to_operand_aliasing={{0}: (1, {}), {1}: (2, {})} | custom-call | tf_op jit(solution)/shard_map/place_got/pallas_call | solution.py:538
  19.0 1.1 %collective-permute-done.5.got_other_ref = f32[480,128]{1,0:T(8,128)S(1)} collective-permute-done((f32[480,128]{1,0:T(8,128)S(1)}, f32[480,128]{1,0:T(8,128)S(1)}, u32[]{:S(2)}, u32[]{:S(2)}) %collective-permute-start.5) | collective-permute-done | bytes 245792 | tf_op jit(solution)/shard_map/ppermute | solution.py:503
  20.0 5.3 %substeps.1 = (f32[6,3,6,4,24]{4,3,2,1,0:T(4,128)}, f32[3,728,128]{2,1,0:T(8,128)S(1)}, f32[624,128]{1,0:T(8,128)S(1)}) custom-call(f32[480,128]{1,0:T(8,128)S(1)} %pad_maximum_fusion.got_ref, f32[480,128]{1,0:T(8,128)S(1)} %collective-permute-done.5.got_other_ref, f32[76]{0:T(128)S(1)} %pad_maximum_fusion.1.table_ref, ...), custom_call_target="tpu_custom_call", output_to_operand_aliasing={{1}: (3, {}), {2}: (4, {})} | custom-call | tf_op jit(solution)/shard_map/substeps/pallas_call | solution.py:547
  (2 shorter events, 0.0 us)
Async XLA Ops:
  0.0 0.9 %copy-start = (f32[6,3,4,6,24]{4,2,3,1,0:T(4,128)S(1)}, f32[6,3,4,6,24]{4,2,3,1,0:T(4,128)}, u32[]{:S(2)}) copy-start(f32[6,3,4,6,24]{4,2,3,1,0:T(4,128)} %param.4) | copy-start | bytes 124420
  0.9 0.7 %copy-start.1 = (f32[6,6,24]{2,1,0:T(8,128)S(1)}, f32[6,6,24]{2,1,0:T(8,128)}, u32[]{:S(2)}) copy-start(f32[6,6,24]{2,1,0:T(8,128)} %coriolis_hbm.1) | copy-start | bytes 10372
  2.4 1.5 %collective-permute-start = (f32[216,128]{1,0:T(8,128)S(1)}, f32[216,128]{1,0:T(8,128)S(1)}, u32[]{:S(2)}, u32[]{:S(2)}) collective-permute-start(f32[216,128]{1,0:T(8,128)S(1)} %get-tuple-element.19.swap_ref.own_ref), channel_id=1, source_target_pairs={{0,1},{1,0},{2,3},{3,2},{4,5},{5,4},{6,7},{7,6},{8,9},{9,8},{10,11... | collective-permute-start | bytes 331784 | tf_op jit(solution)/shard_map/ppermute | solution.py:503
  3.9 14.5 %collective-permute-start.1 = (f32[240,128]{1,0:T(8,128)S(1)}, f32[240,128]{1,0:T(8,128)S(1)}, u32[]{:S(2)}, u32[]{:S(2)}) collective-permute-start(f32[240,128]{1,0:T(8,128)S(1)} %get-tuple-element.22), channel_id=1, source_target_pairs={{0,2},{1,15},{2,4},{3,1},{4,6},{5,3},{6,8},{7,5},{8,10},{9,7},{10,... | collective-permute-start | bytes 368648 | tf_op jit(solution)/shard_map/ppermute | solution.py:500
  6.8 6.1 %collective-permute-start.4 = (f32[48,128]{1,0:T(8,128)S(1)}, f32[48,128]{1,0:T(8,128)S(1)}, u32[]{:S(2)}, u32[]{:S(2)}) collective-permute-start(f32[48,128]{1,0:T(8,128)S(1)} %get-tuple-element.25), channel_id=1, source_target_pairs={{0,8},{1,9},{2,10},{3,11},{4,12},{5,13},{6,14},{7,15},{8,0},{9,1},... | collective-permute-start | bytes 73736 | tf_op jit(solution)/shard_map/ppermute | solution.py:500
  10.3 6.4 %collective-permute-start.2 = (f32[96,128]{1,0:T(8,128)S(1)}, f32[96,128]{1,0:T(8,128)S(1)}, u32[]{:S(2)}, u32[]{:S(2)}) collective-permute-start(f32[96,128]{1,0:T(8,128)S(1)} %get-tuple-element.23), channel_id=1, source_target_pairs={{0,4},{1,13},{2,6},{3,15},{4,8},{5,1},{6,10},{7,3},{8,12},{9,5},{1... | collective-permute-start | bytes 147464 | tf_op jit(solution)/shard_map/ppermute | solution.py:500
  11.9 6.5 %collective-permute-start.3 = (f32[96,128]{1,0:T(8,128)S(1)}, f32[96,128]{1,0:T(8,128)S(1)}, u32[]{:S(2)}, u32[]{:S(2)}) collective-permute-start(f32[96,128]{1,0:T(8,128)S(1)} %get-tuple-element.24), channel_id=1, source_target_pairs={{0,6},{1,11},{2,8},{3,13},{4,10},{5,15},{6,12},{7,1},{8,14},{9,3},... | collective-permute-start | bytes 147464 | tf_op jit(solution)/shard_map/ppermute | solution.py:500
  18.4 1.6 %collective-permute-start.5 = (f32[480,128]{1,0:T(8,128)S(1)}, f32[480,128]{1,0:T(8,128)S(1)}, u32[]{:S(2)}, u32[]{:S(2)}) collective-permute-start(f32[480,128]{1,0:T(8,128)S(1)} %pad_maximum_fusion.got_ref), channel_id=1, source_target_pairs={{0,1},{1,0},{2,3},{3,2},{4,5},{5,4},{6,7},{7,6},{8,9},{9,8},{10,11... | collective-permute-start | bytes 737288 | tf_op jit(solution)/shard_map/ppermute | solution.py:503

commit v11 on v9

--- a/solution.py
+++ b/solution.py
@@ -11,6 +11,8 @@
 LANES = 128
 WINDOW = 64
 MARGIN = 8
+ROWS = 64
+EDGE = 8
 VMEM_LIMIT = 32 * 1024 * 1024
 SMALL_VMEM_LIMIT = 8 * 1024 * 1024
 
@@ -131,39 +133,36 @@
 def placer(cx, cy, count_x, full_rows, small_rows, z_ref, cor_ref):
     fields = z_ref.shape[0]
     levels = 4
-    group = z_ref.shape[1] // (cx * count_x + 8)
-    pairs = group // levels
+    pairs = cor_ref.shape[0]
+    group = pairs * levels
     half = cx // 2
-    chunk = cx * group
     index_x = lax.axis_index("tx")
     index_y = lax.axis_index("ty")
     south_half = lax.broadcasted_iota(jnp.int32, (group, LANES), 1) % WINDOW < MARGIN + cy
     south_is_own = index_y == 0
     own_half = south_half == south_is_own
 
-    def row_of(x):
-        return (x + 4) * group
-
     def from_owner(offset):
         source = (index_x - offset + 2 * count_x) % count_x
-        return source, pl.multiple_of(source * chunk, 8)
-
-    def put_coriolis(start, x, values, at):
+        return source, source * cx
+
+    def put_state(field, x, values):
+        z_ref[field, pl.ds(x + EDGE, group, ROWS)] = values
+
+    def put_coriolis(x, values, at):
         for pair in range(pairs):
-            line = values[at + pair : at + pair + 1]
-            rows = pl.ds(start + x * group + pair * levels, levels)
-            cor_ref[rows] = jnp.broadcast_to(line, (levels, LANES))
+            cor_ref[pair, pl.ds(x, 1)] = values[at + pair : at + pair + 1]
 
     def put_block(start, lines_of):
         base = fields * half * group
         for field in range(fields):
             for xp in range(half):
                 even, odd = lines_of(field * half * group + xp * group, group)
-                z_ref[field, pl.ds(start + row_of(2 * xp), group)] = even
-                z_ref[field, pl.ds(start + row_of(2 * xp + 1), group)] = odd
+                put_state(field, start + 2 * xp, even)
+                put_state(field, start + 2 * xp + 1, odd)
         for parity, values in enumerate(lines_of(base, half * pairs)):
             for xp in range(half):
-                put_coriolis(start, 2 * xp + parity, values, xp * pairs)
+                put_coriolis(start + 2 * xp + parity, values, xp * pairs)
 
     def put_distant(source, start, lines_of):
         starts_south = windows(source, index_x, count_x, 0, cx, cy)
@@ -177,11 +176,11 @@
 
         for field in range(fields):
             for x in range(cx):
-                z_ref[field, pl.ds(start + row_of(x), group)] = lines_at(field, x, x // half)
+                put_state(field, start + x, lines_at(field, x, x // half))
         for part in range(2):
             values = lines_at(fields, part, part)
             for x in range(half):
-                put_coriolis(start, part * half + x, values, x * pairs)
+                put_coriolis(start + part * half + x, values, x * pairs)
 
     def place_own(own_ref, other_ref):
         def own_lines(row, rows):
@@ -245,77 +244,65 @@
 
 def step_kernel(
     sizes, got_ref, got_other_ref, table_ref, z_in, cor_in, out_ref, z_ref, cor_ref,
-    pred_ref, store_ref, tile_ref, flip_ref, speed_ref,
+    pred_ref, store_ref, tile_ref, flip_ref, result_ref,
 ):
     cx, cy, count_x = sizes[:3]
     levels = 4
-    slots = 16
+    slots = 4 * levels
     cells = cx * count_x
     faces = store_ref.shape[0] // 4
     pairs = faces // 2
-    group = pairs * levels
-    chunk = cx * group
     index_x = lax.axis_index("tx")
     index_y = lax.axis_index("ty")
 
-    def row_of(x):
-        return (x + 4) * group
-
     def lanes_of(rows):
         return lax.broadcasted_iota(jnp.int32, (rows, LANES), 1)
+
+    def rows_of(rows):
+        return lax.broadcasted_iota(jnp.int32, (rows, LANES), 0)
+
+    def top_of(pair, level):
+        return (pair * levels + level) * ROWS
 
     _, place_got, place_middle = placer(*sizes, z_ref, cor_ref)
     place_got(got_other_ref, 2 * index_y - 1, 1 - index_y)
     place_middle(got_ref, got_other_ref)
 
-    level_of = lax.broadcasted_iota(jnp.int32, speed_ref.shape, 0) % levels
-    speeds = jnp.full(speed_ref.shape, table_ref[0], jnp.float32)
-    for index in range(1, levels):
-        speeds = jnp.where(level_of == index, table_ref[index], speeds)
-    speed_ref[...] = speeds
-
     def collect():
         position = lanes_of(cells) % WINDOW
         gap = WINDOW - cells + 3
-        wide = gap + 3 * levels
         for pair in range(pairs):
-            merged = jnp.zeros((cells, LANES), jnp.float32)
             for slot, field in ((0, 0), (1, 2)):
+                merged = jnp.zeros((cells, LANES), jnp.float32)
                 for level in range(levels):
-                    lines = z_ref[field, pl.ds(row_of(0) + pair * levels + level, cells, group)]
-                    offset = slot * wide + 3 * level
-                    here = position - offset
+                    at = top_of(pair, level) + EDGE
+                    here = position - 4 * level
                     wanted = ((here >= 0) & (here < 3)) | ((here >= gap) & (here < gap + 3))
-                    shift = (offset - (MARGIN + cells - 3)) % LANES
-                    merged = jnp.where(wanted, pltpu.roll(lines, shift, 1), merged)
-            merged = jnp.concatenate(
-                [merged, jnp.zeros((LANES - cells, LANES), jnp.float32)], axis=0
-            )
-            flip_ref[pair] = merged.T
+                    shift = (4 * level - (MARGIN + cells - 3)) % LANES
+                    lines = pltpu.roll(z_ref[field, at : at + cells], shift, 1)
+                    merged = jnp.where(wanted, lines, merged)
+                merged = jnp.concatenate(
+                    [merged, jnp.zeros((LANES - cells, LANES), jnp.float32)], axis=0
+                )
+                flip = 2 * pair + slot
+                flip_ref[flip] = merged.T
+                for odd in range(2):
+                    for side in (2, 3):
+                        if side == 3:
+                            base = odd * WINDOW
+                        else:
+                            base = ((odd + 1) % 2) * WINDOW + gap
+                        store_ref[(2 * pair + odd) * 4 + side, slot * slots : (slot + 1) * slots] = (
+                            flip_ref[flip, base : base + slots]
+                        )
             for slot in range(2):
-                for side in (2, 3):
-                    for odd in range(2):
-                        for depth in range(3):
-                            base = slot * wide
-                            if side == 3:
-                                base += odd * WINDOW + 2 - depth
-                            else:
-                                base += ((odd + 1) % 2) * WINDOW + gap + depth
-                            at = slot * slots + depth * levels
-                            store_ref[(2 * pair + odd) * 4 + side, at : at + levels] = flip_ref[
-                                pair, pl.ds(base, levels, 3)
-                            ]
-            for slot in range(2):
-                for side in (0, 1):
-                    for depth in range(3):
-                        x = depth if side == 0 else cells - 1 - depth
-                        row = row_of(x) + pair * levels
-                        lines = z_ref[slot, row : row + levels]
-                        at = slot * slots + depth * levels
+                for level in range(levels):
+                    for side in (0, 1):
+                        at = top_of(pair, level) + EDGE + (0 if side == 0 else cells - 3)
+                        lines = z_ref[slot, at : at + 4]
+                        row = slot * slots + 4 * level
                         for odd in range(2):
-                            store_ref[(2 * pair + odd) * 4 + side, at : at + levels] = pltpu.roll(
-                                lines, LANES - MARGIN - odd * WINDOW, 1
-                            )
+                            store_ref[(2 * pair + odd) * 4 + side, row : row + 4] = lines
 
     def fetch(face, side, position):
         at = levels + (face * 4 + side) * 3
@@ -325,30 +312,43 @@
         block = store_ref[neighbour * 4 + far_side]
         order = jnp.where(flipped == 1, cells - 1 - position, position)
         order = jnp.where((position >= 0) & (position < cells), order, 0)
+        order = order + jnp.where(far_side < 2, MARGIN + WINDOW * (neighbour % 2), 0)
         block = jnp.take_along_axis(block, order, axis=1)
+        turned = far_side % 2 == side % 2
+        place = rows_of(8) % 4
+        parts = []
+        for part in range(4):
+            lines = block[8 * part : 8 * part + 8]
+            swapped = jnp.where(place == 0, pltpu.roll(lines, 6, 0), pltpu.roll(lines, 2, 0))
+            parts.append(jnp.where(turned & (place != 1), swapped, lines))
         sign_here = 2 * (side % 2) - 1
         sign_there = 2 * (far_side % 2) - 1
         sign = (-sign_here * sign_there).astype(jnp.float32)
-        normal = lax.broadcasted_iota(jnp.int32, block.shape, 0) >= slots
-        return jnp.where(normal, sign * block, block)
+        return parts[:2], [sign * lines for lines in parts[2:]]
+
+    def level_rows(parts, level, rows):
+        at = 4 * (level % 2)
+        return parts[level // 2][at : at + rows]
 
     def rim_rows(side):
         lane = lanes_of(2 * slots)
+        left = lanes_of(8) < WINDOW
         for pair in range(pairs):
             first = fetch(2 * pair, side, lane - MARGIN)
             second = fetch(2 * pair + 1, side, lane - (MARGIN + WINDOW))
-            both = jnp.where(lane < WINDOW, first, second)
             for slot in range(2):
-                for depth in range(3):
-                    x = -1 - depth if side == 0 else cells + depth
-                    at = slot * slots + depth * levels
-                    row = row_of(x) + pair * levels
-                    z_ref[slot, row : row + levels] = both[at : at + levels]
-
-    def tile_rows(odd, side, depth):
-        if side == 3:
-            return pl.ds(odd * WINDOW + depth, levels, 16)
-        return pl.ds(((odd + 1) % 2) * WINDOW + 15 - depth, levels, 16)
+                both = [jnp.where(left, a, b) for a, b in zip(first[slot], second[slot])]
+                for level in range(levels):
+                    at = top_of(pair, level) + EDGE + (-3 if side == 0 else cells)
+                    z_ref[slot, at : at + 3] = level_rows(both, level, 3)
+
+    def put_tile(tile, parts, odd, side):
+        for level in range(levels):
+            if side == 3:
+                at = odd * WINDOW + 16 * level
+            else:
+                at = ((odd + 1) % 2) * WINDOW + 16 * level + 13
+            tile_ref[tile, at : at + 3] = level_rows(parts, level, 3)
 
     def put_columns(lines, field, start, pair):
         count = lines.shape[0]
@@ -358,76 +358,69 @@
         )
         for level in range(levels):
             rolled = pltpu.roll(lines, (MARGIN + cells - 16 * level) % LANES, 1)
-            at = pl.ds(row_of(start) + pair * levels + level, count, group)
+            at = pl.ds(start + top_of(pair, level) + EDGE, count)
             z_ref[field, at] = jnp.where(rim, rolled, z_ref[field, at])
 
     def rim_columns_all():
         for pair in range(pairs):
             for odd in range(2):
                 for side in (2, 3):
-                    block = fetch(2 * pair + odd, side, lanes_of(2 * slots))
-                    for slot in range(2):
-                        for depth in range(3):
-                            at = slot * slots + depth * levels
-                            tile_ref[2 * pair + slot, tile_rows(odd, side, depth)] = block[
-                                at : at + levels
-                            ]
+                    for slot, parts in enumerate(fetch(2 * pair + odd, side, lanes_of(2 * slots))):
+                        put_tile(2 * pair + slot, parts, odd, side)
             for slot, field in ((0, 0), (1, 2)):
                 put_columns(tile_ref[2 * pair + slot].T[:cells], field, 0, pair)
 
     def rim_columns_own():
         lane = lanes_of(2 * slots)
-        second = lax.broadcasted_iota(jnp.int32, lane.shape, 0) >= slots
+        second = rows_of(2 * slots) >= slots
         for odd in range(2):
             for side in (2, 3):
-                total = jnp.zeros((slots, LANES), jnp.float32)
+                total = [jnp.zeros((8, LANES), jnp.float32)] * 2
                 for pair in range(pairs):
                     local = lane - jnp.where(second, 8 * (pairs + pair), 8 * pair)
-                    block = fetch(2 * pair + odd, side, index_x * cx + local)
-                    block = jnp.where((local >= 0) & (local < 8), block, 0.0)
-                    total = total + block[:slots] + block[slots:]
-                for depth in range(3):
-                    at = depth * levels
-                    tile_ref[0, tile_rows(odd, side, depth)] = total[at : at + levels]
+                    fetched = fetch(2 * pair + odd, side, index_x * cx + local)
+                    for slot, parts in enumerate(fetched):
+                        local = lanes_of(8) - 8 * (slot * pairs + pair)
+                        here = (local >= 0) & (local < 8)
+                        total = [jnp.where(here, a, b) for a, b in zip(parts, total)]
+                put_tile(0, total, odd, side)
         turned = tile_ref[0].T
         for slot, field in ((0, 0), (1, 2)):
             for pair in range(pairs):
                 at = 8 * (slot * pairs + pair)
-                put_columns(turned[at : at + cx], field, index_x * cx, pair)
-
-    def predict(at, rows):
-        speed = speed_ref[:rows]
-        ahead = z_ref[0, pl.ds(at + group, rows)]
-        behind = z_ref[0, pl.ds(at - group, rows)]
-        pred_ref[pl.ds(at, rows)] = z_ref[1, pl.ds(at, rows)] - speed * (0.5 * (ahead - behind))
-
-    def update(at, rows):
-        speed = speed_ref[:rows]
-        height = z_ref[0, pl.ds(at, rows)]
-        north_pred = z_ref[2, pl.ds(at, rows)] - speed * (
+                put_columns(turned[at : at + 8], field, index_x * cx, pair)
+
+    def advance_rows(pair, level, start, count, before, rows):
+        top = top_of(pair, level) + EDGE + start
+        speed = table_ref[level]
+        ahead = z_ref[0, pl.ds(top - before + 1, rows)]
+        behind = z_ref[0, pl.ds(top - before - 1, rows)]
+        east = z_ref[1, pl.ds(top - before, rows)]
+        pred_ref[pl.ds(top - before, rows)] = east - speed * (0.5 * (ahead - behind))
+        height = z_ref[0, pl.ds(top, count)]
+        north_pred = z_ref[2, pl.ds(top, count)] - speed * (
             0.5 * (pltpu.roll(height, LANES - 1, 1) - pltpu.roll(height, 1, 1))
         )
-        east_pred = pred_ref[pl.ds(at, rows)]
-        flux_east = 8.0 * (
-            pred_ref[pl.ds(at + group, rows)] - pred_ref[pl.ds(at - group, rows)]
-        ) - (pred_ref[pl.ds(at + 2 * group, rows)] - pred_ref[pl.ds(at - 2 * group, rows)])
+        east_pred = pred_ref[pl.ds(top, count)]
+        flux_east = 8.0 * (pred_ref[pl.ds(top + 1, count)] - pred_ref[pl.ds(top - 1, count)]) - (
+            pred_ref[pl.ds(top + 2, count)] - pred_ref[pl.ds(top - 2, count)]
+        )
         flux_north = 8.0 * (
             pltpu.roll(north_pred, LANES - 1, 1) - pltpu.roll(north_pred, 1, 1)
         ) - (pltpu.roll(north_pred, LANES - 2, 1) - pltpu.roll(north_pred, 2, 1))
         height = height - speed * ((flux_east + flux_north) * (1.0 / 12.0))
-        turning = cor_ref[pl.ds(at - row_of(0), rows)]
+        turning = cor_ref[pair, pl.ds(start, count)]
         return height, east_pred + turning * north_pred, north_pred - turning * east_pred
 
     collect()
     rim_rows(0)
     rim_rows(1)
     rim_columns_all()
-    for first in range(-2, cells + 2, 4):
-        predict(row_of(first), 4 * group)
-    for index in range(count_x):
-        at = row_of(0) + index * chunk
-        for field, values in enumerate(update(at, chunk)):
-            z_ref[field, at : at + chunk] = values
+    for pair in range(pairs):
+        for level in range(levels):
+            at = top_of(pair, level) + EDGE
+            for field, values in enumerate(advance_rows(pair, level, 0, cells, 4, cells + 8)):
+                z_ref[field, at : at + cells] = values
 
     collect()
 
@@ -440,16 +433,19 @@
         rim_rows(1)
 
     rim_columns_own()
-    at = pl.multiple_of(row_of(0) + index_x * chunk, 8)
-    predict(at - 2 * group, chunk + 4 * group)
-    for field, values in enumerate(update(at, chunk)):
-        for odd in range(2):
-            shift = LANES - (MARGIN + odd * WINDOW) - index_y * cy
-            rolled = pltpu.roll(values, shift, 1)
+    for pair in range(pairs):
+        for level in range(levels):
+            fields = advance_rows(pair, level, index_x * cx, 8, 2, 16)
+            at = 8 * (pair * levels + level)
+            for field, values in enumerate(fields):
+                for odd in range(2):
+                    shift = LANES - (MARGIN + odd * WINDOW) - index_y * cy
+                    result_ref[2 * field + odd, at : at + 8] = pltpu.roll(values, shift, 1)
+    for field in range(3):
+        for face in range(faces):
             for x in range(cx):
-                for pair in range(pairs):
-                    row = x * group + pair * levels
-                    out_ref[2 * pair + odd, field, x] = rolled[row : row + levels, :cy]
+                rows = pl.ds((face // 2) * levels * 8 + x, levels, 8)
+                out_ref[face, field, x] = result_ref[2 * field + face % 2, rows][:, :cy]
 
 
 def fast_on_device(state, coriolis, wave_speed, edges):
@@ -520,8 +516,8 @@
 
     sizes = (cx, cy, count_x, full_rows, small_rows)
     state_rows = [
-        jax.ShapeDtypeStruct((fields, (cells + 8) * group, LANES), jnp.float32),
-        jax.ShapeDtypeStruct((cells * group, LANES), jnp.float32),
+        jax.ShapeDtypeStruct((fields, group * ROWS + 8, LANES), jnp.float32),
+        jax.ShapeDtypeStruct((pairs, cells + 8, LANES), jnp.float32),
     ]
     in_vmem = pl.BlockSpec(memory_space=pltpu.VMEM)
     params = pltpu.CompilerParams(vmem_limit_bytes=SMALL_VMEM_LIMIT)
@@ -550,11 +546,11 @@
         out_specs=[in_vmem] * 3,
         input_output_aliases={3: 1, 4: 2},
         scratch_shapes=[
-            pltpu.VMEM(((cells + 8) * group, LANES), jnp.float32),
+            pltpu.VMEM((group * ROWS + 8, LANES), jnp.float32),
             pltpu.VMEM((faces * 4, 32, LANES), jnp.float32),
             pltpu.VMEM((faces, LANES, LANES), jnp.float32),
-            pltpu.VMEM((pairs, LANES, LANES), jnp.float32),
-            pltpu.VMEM(((cx + 4) * group, LANES), jnp.float32),
+            pltpu.VMEM((faces, LANES, LANES), jnp.float32),
+            pltpu.VMEM((2 * fields, 8 * group, LANES), jnp.float32),
         ],
         compiler_params=pltpu.CompilerParams(vmem_limit_bytes=VMEM_LIMIT),
         name="substeps",

time: 24.7 us -> 25.6 us (1.036)
  other arithmetic: 0.09 us -> 1.44 us
  waiting for transfers between devices: 7.95 us -> 7.17 us
  Pallas kernels: 6.5 us -> 6.81 us
    convert_element_type x1, other arithmetic: 0.01 us -> 0.69 us  [fast_on_device(): table = jnp.concatenate([wave_speed, edges.reshape(-1).astype(jnp.float32)])]
    concatenate x1, other arithmetic: 0.07 us -> 0.73 us  [fast_on_device(): table = jnp.concatenate([wave_speed, edges.reshape(-1).astype(jnp.float32)])]
    ppermute x4, waiting for transfers between devices: 6.13 us -> 5.48 us  [moved(): return lax.ppermute(block, ('tx', 'ty'), pairs_of)]
    unnamed x8 -> x4, local copies, waits for them, and re-layouts: 1.68 us -> 1.67 us
  transfers between devices with their start and end apart: 6 -> 6, of which waited for: 4 -> 4; matrix products, arithmetic and copies ran while one was open for 1% -> 6% of each run, Pallas kernels for 3% -> 3%
where the time goes in v11:
time: 25.6 us; the launch traced here: 25.4 us
  starting transfers between devices  8.01 us (31%)
  waiting for transfers between devices  7.17 us (28%)
  Pallas kernels  6.81 us (27%)
  local copies, waits for them, and re-layouts  1.89 us (7%)
  other arithmetic  1.44 us (6%)
    ppermute x4, starting transfers between devices, moved(): return lax.ppermute(block, ('tx', 'ty'), pairs_of)  7.42 us
    ppermute x4, waiting for transfers between devices, moved(): return lax.ppermute(block, ('tx', 'ty'), pairs_of)  5.48 us
    pallas_call x1, Pallas kernels, fast_on_device(): pl.pallas_call(functools.partial(step_kernel, sizes), out_shape=[jax.Shap...  5.37 us
    ppermute x2, waiting for transfers between devices, across(): return lax.ppermute(block, 'ty', [(0, 1), (1, 0)])  1.69 us
    unnamed x4, local copies, waits for them, and re-layouts  1.67 us
    concatenate x1, other arithmetic, fast_on_device(): table = jnp.concatenate([wave_speed, edges.reshape(-1).astype(jnp.float32)])  0.73 us
    convert_element_type x1, other arithmetic, fast_on_device(): table = jnp.concatenate([wave_speed, edges.reshape(-1).astype(jnp.float32)])  0.69 us
    pallas_call x1, Pallas kernels, fast_on_device(): pl.pallas_call(functools.partial(pack_kernel, cx, cy, count_x, full_rows,...  0.69 us
  transfers between devices with their start and end apart: 6, of which 4 were waited for; matrix products, arithmetic and copies ran while one was open for 6% of the time, Pallas kernels for 3%

profile of v11, /device:TPU:0, one launch (start us, length us, event | category | flops | bytes accessed | tf_op | source)
XLA Modules:
  0.0 25.4 jit_solution(4011978002279195848)
XLA Ops:
  0.0 0.0 copy-start
  0.0 0.9 %copy-done = f32[6,3,4,6,24]{4,2,3,1,0:T(4,128)S(1)} copy-done((f32[6,3,4,6,24]{4,2,3,1,0:T(4,128)S(1)}, f32[6,3,4,6,24]{4,2,3,1,0:T(4,128)}, u32[]{:S(2)}) %copy-start) | copy-done | bytes 41496
  0.9 0.0 copy-start.1
  0.9 0.7 %copy-done.1 = f32[6,6,24]{2,1,0:T(8,128)S(1)} copy-done((f32[6,6,24]{2,1,0:T(8,128)S(1)}, f32[6,6,24]{2,1,0:T(8,128)}, u32[]{:S(2)}) %copy-start.1) | copy-done | bytes 3480
  1.7 0.7 %pack.1 = (f32[216,128]{1,0:T(8,128)S(1)}, f32[32,128]{1,0:T(8,128)S(1)}) custom-call(f32[6,3,6,4,24]{4,3,2,1,0:T(4,128)S(1)} %bitcast.2, f32[6,6,24]{2,1,0:T(8,128)S(1)} %copy-done.1), custom_call_target="tpu_custom_call" | custom-call | tf_op jit(solution)/shard_map/pack/pallas_call | solution.py:460
  2.4 0.5 %collective-permute-start = (f32[216,128]{1,0:T(8,128)S(1)}, f32[216,128]{1,0:T(8,128)S(1)}, u32[]{:S(2)}, u32[]{:S(2)}) collective-permute-start(f32[216,128]{1,0:T(8,128)S(1)} %get-tuple-element.19.swap_ref.own_ref), channel_id=1, source_target_pairs={{0,1},{1,0},{2,3},{3,2},{4,5},{5,4},{6,7},{7,6},{8,9},{9,8},{10,11... | collective-permute-start | bytes 331784 | tf_op jit(solution)/shard_map/ppermute | solution.py:497
  2.9 0.2 keep.1
  3.1 0.8 %collective-permute-done.other_ref = f32[216,128]{1,0:T(8,128)S(1)} collective-permute-done((f32[216,128]{1,0:T(8,128)S(1)}, f32[216,128]{1,0:T(8,128)S(1)}, u32[]{:S(2)}, u32[]{:S(2)}) %collective-permute-start) | collective-permute-done | bytes 110624 | tf_op jit(solution)/shard_map/ppermute | solution.py:497
  3.9 2.9 %collective-permute-start.1 = (f32[240,128]{1,0:T(8,128)S(1)}, f32[240,128]{1,0:T(8,128)S(1)}, u32[]{:S(2)}, u32[]{:S(2)}) collective-permute-start(f32[240,128]{1,0:T(8,128)S(1)} %get-tuple-element.22), channel_id=1, source_target_pairs={{0,2},{1,15},{2,4},{3,1},{4,6},{5,3},{6,8},{7,5},{8,10},{9,7},{10,... | collective-permute-start | bytes 368648 | tf_op jit(solution)/shard_map/ppermute | solution.py:494
  6.8 2.6 %collective-permute-start.4 = (f32[48,128]{1,0:T(8,128)S(1)}, f32[48,128]{1,0:T(8,128)S(1)}, u32[]{:S(2)}, u32[]{:S(2)}) collective-permute-start(f32[48,128]{1,0:T(8,128)S(1)} %get-tuple-element.25), channel_id=1, source_target_pairs={{0,8},{1,9},{2,10},{3,11},{4,12},{5,13},{6,14},{7,15},{8,0},{9,1},... | collective-permute-start | bytes 73736 | tf_op jit(solution)/shard_map/ppermute | solution.py:494
  9.4 0.7 %convert_element_type.6 = f32[6,4,3]{0,1,2:T(4,128)S(1)} convert(s32[6,4,3]{0,1,2:T(4,128)} %param.7) | non-fusion elementwise | flops 72 | bytes 576 | tf_op jit(solution)/shard_map/convert_element_type | solution.py:513
  10.1 0.1 copy.10
  10.2 0.1 convert_element_type.7
  10.3 1.6 %collective-permute-start.2 = (f32[96,128]{1,0:T(8,128)S(1)}, f32[96,128]{1,0:T(8,128)S(1)}, u32[]{:S(2)}, u32[]{:S(2)}) collective-permute-start(f32[96,128]{1,0:T(8,128)S(1)} %get-tuple-element.23), channel_id=1, source_target_pairs={{0,4},{1,13},{2,6},{3,15},{4,8},{5,1},{6,10},{7,3},{8,12},{9,5},{1... | collective-permute-start | bytes 147464 | tf_op jit(solution)/shard_map/ppermute | solution.py:494
  11.9 0.3 %collective-permute-start.3 = (f32[96,128]{1,0:T(8,128)S(1)}, f32[96,128]{1,0:T(8,128)S(1)}, u32[]{:S(2)}, u32[]{:S(2)}) collective-permute-start(f32[96,128]{1,0:T(8,128)S(1)} %get-tuple-element.24), channel_id=1, source_target_pairs={{0,6},{1,11},{2,8},{3,13},{4,10},{5,15},{6,12},{7,1},{8,14},{9,3},... | collective-permute-start | bytes 147464 | tf_op jit(solution)/shard_map/ppermute | solution.py:494
  12.2 0.7 %pad_maximum_fusion.1.table_ref = f32[76]{0:T(128)S(1)} fusion(f32[72]{0:T(128)S(1)} %convert_element_type.7, f32[4]{0:T(128)} %param.6), kind=kLoop, calls=%fused_computation.1 | loop fusion | flops 76 | bytes 608 | tf_op jit(solution)/shard_map/concatenate | solution.py:513
  12.9 0.0 collective-permute-done.4
  12.9 3.7 %collective-permute-done.2 = f32[96,128]{1,0:T(8,128)S(1)} collective-permute-done((f32[96,128]{1,0:T(8,128)S(1)}, f32[96,128]{1,0:T(8,128)S(1)}, u32[]{:S(2)}, u32[]{:S(2)}) %collective-permute-start.2) | collective-permute-done | bytes 49184 | tf_op jit(solution)/shard_map/ppermute | solution.py:494
  16.7 1.7 %collective-permute-done.3 = f32[96,128]{1,0:T(8,128)S(1)} collective-permute-done((f32[96,128]{1,0:T(8,128)S(1)}, f32[96,128]{1,0:T(8,128)S(1)}, u32[]{:S(2)}, u32[]{:S(2)}) %collective-permute-start.3) | collective-permute-done | bytes 49184 | tf_op jit(solution)/shard_map/ppermute | solution.py:494
  18.4 0.0 collective-permute-done.1
  18.4 0.1 collective-permute-start.5
  18.5 0.2 place_own.1
  18.7 0.4 %place_got.1 = (f32[3,776,128]{2,1,0:T(8,128)S(1)}, f32[3,56,128]{2,1,0:T(8,128)S(1)}) custom-call(f32[480,128]{1,0:T(8,128)S(1)} %pad_maximum_fusion.got_ref, f32[3,776,128]{2,1,0:T(8,128)S(1)} %get-tuple-element.28.z_in, f32[3,56,128]{2,1,0:T(8,128)S(1)} %get-tuple-element.29.cor_in), custom_call_target="tpu_custom_call", output_to_operand_aliasing={{0}: (1, {}), {1}: (2, {})} | custom-call | tf_op jit(solution)/shard_map/place_got/pallas_call | solution.py:532
  19.1 0.9 %collective-permute-done.5.got_other_ref = f32[480,128]{1,0:T(8,128)S(1)} collective-permute-done((f32[480,128]{1,0:T(8,128)S(1)}, f32[480,128]{1,0:T(8,128)S(1)}, u32[]{:S(2)}, u32[]{:S(2)}) %collective-permute-start.5) | collective-permute-done | bytes 245792 | tf_op jit(solution)/shard_map/ppermute | solution.py:497
  20.0 5.4 %substeps.1 = (f32[6,3,6,4,24]{4,3,2,1,0:T(4,128)}, f32[3,776,128]{2,1,0:T(8,128)S(1)}, f32[3,56,128]{2,1,0:T(8,128)S(1)}) custom-call(f32[480,128]{1,0:T(8,128)S(1)} %pad_maximum_fusion.got_ref, f32[480,128]{1,0:T(8,128)S(1)} %collective-permute-done.5.got_other_ref, ...), custom_call_target="tpu_custom_call", output_to_operand_aliasing={{1}: (3, {}), {2}: (4, {})} | custom-call | tf_op jit(solution)/shard_map/substeps/pallas_call | solution.py:541
  (2 shorter events, 0.0 us)
Async XLA Ops:
  0.0 0.9 %copy-start = (f32[6,3,4,6,24]{4,2,3,1,0:T(4,128)S(1)}, f32[6,3,4,6,24]{4,2,3,1,0:T(4,128)}, u32[]{:S(2)}) copy-start(f32[6,3,4,6,24]{4,2,3,1,0:T(4,128)} %param.4) | copy-start | bytes 124420
  0.9 0.7 %copy-start.1 = (f32[6,6,24]{2,1,0:T(8,128)S(1)}, f32[6,6,24]{2,1,0:T(8,128)}, u32[]{:S(2)}) copy-start(f32[6,6,24]{2,1,0:T(8,128)} %coriolis_hbm.1) | copy-start | bytes 10372
  2.4 1.5 %collective-permute-start = (f32[216,128]{1,0:T(8,128)S(1)}, f32[216,128]{1,0:T(8,128)S(1)}, u32[]{:S(2)}, u32[]{:S(2)}) collective-permute-start(f32[216,128]{1,0:T(8,128)S(1)} %get-tuple-element.19.swap_ref.own_ref), channel_id=1, source_target_pairs={{0,1},{1,0},{2,3},{3,2},{4,5},{5,4},{6,7},{7,6},{8,9},{9,8},{10,11... | collective-permute-start | bytes 331784 | tf_op jit(solution)/shard_map/ppermute | solution.py:497
  3.9 14.5 %collective-permute-start.1 = (f32[240,128]{1,0:T(8,128)S(1)}, f32[240,128]{1,0:T(8,128)S(1)}, u32[]{:S(2)}, u32[]{:S(2)}) collective-permute-start(f32[240,128]{1,0:T(8,128)S(1)} %get-tuple-element.22), channel_id=1, source_target_pairs={{0,2},{1,15},{2,4},{3,1},{4,6},{5,3},{6,8},{7,5},{8,10},{9,7},{10,... | collective-permute-start | bytes 368648 | tf_op jit(solution)/shard_map/ppermute | solution.py:494
  6.8 6.1 %collective-permute-start.4 = (f32[48,128]{1,0:T(8,128)S(1)}, f32[48,128]{1,0:T(8,128)S(1)}, u32[]{:S(2)}, u32[]{:S(2)}) collective-permute-start(f32[48,128]{1,0:T(8,128)S(1)} %get-tuple-element.25), channel_id=1, source_target_pairs={{0,8},{1,9},{2,10},{3,11},{4,12},{5,13},{6,14},{7,15},{8,0},{9,1},... | collective-permute-start | bytes 73736 | tf_op jit(solution)/shard_map/ppermute | solution.py:494
  10.3 6.4 %collective-permute-start.2 = (f32[96,128]{1,0:T(8,128)S(1)}, f32[96,128]{1,0:T(8,128)S(1)}, u32[]{:S(2)}, u32[]{:S(2)}) collective-permute-start(f32[96,128]{1,0:T(8,128)S(1)} %get-tuple-element.23), channel_id=1, source_target_pairs={{0,4},{1,13},{2,6},{3,15},{4,8},{5,1},{6,10},{7,3},{8,12},{9,5},{1... | collective-permute-start | bytes 147464 | tf_op jit(solution)/shard_map/ppermute | solution.py:494
  11.9 6.5 %collective-permute-start.3 = (f32[96,128]{1,0:T(8,128)S(1)}, f32[96,128]{1,0:T(8,128)S(1)}, u32[]{:S(2)}, u32[]{:S(2)}) collective-permute-start(f32[96,128]{1,0:T(8,128)S(1)} %get-tuple-element.24), channel_id=1, source_target_pairs={{0,6},{1,11},{2,8},{3,13},{4,10},{5,15},{6,12},{7,1},{8,14},{9,3},... | collective-permute-start | bytes 147464 | tf_op jit(solution)/shard_map/ppermute | solution.py:494
  18.4 1.6 %collective-permute-start.5 = (f32[480,128]{1,0:T(8,128)S(1)}, f32[480,128]{1,0:T(8,128)S(1)}, u32[]{:S(2)}, u32[]{:S(2)}) collective-permute-start(f32[480,128]{1,0:T(8,128)S(1)} %pad_maximum_fusion.got_ref), channel_id=1, source_target_pairs={{0,1},{1,0},{2,3},{3,2},{4,5},{5,4},{6,7},{7,6},{8,9},{9,8},{10,11... | collective-permute-start | bytes 737288 | tf_op jit(solution)/shard_map/ppermute | solution.py:497

commit v12 on v9

--- a/solution.py
+++ b/solution.py
@@ -244,9 +244,11 @@
 
 
 def step_kernel(
-    sizes, got_ref, got_other_ref, table_ref, z_in, cor_in, out_ref, z_ref, cor_ref,
-    pred_ref, store_ref, tile_ref, flip_ref, speed_ref,
+    sizes, got_ref, got_other_ref, table_in, z_in, cor_in, out_hbm, z_ref, cor_ref,
+    pred_ref, store_ref, tile_ref, flip_ref, speed_ref, table_ref, out_ref, sems,
 ):
+    table_copy = pltpu.make_async_copy(table_in, table_ref, sems.at[0])
+    table_copy.start()
     cx, cy, count_x = sizes[:3]
     levels = 4
     slots = 16
@@ -268,6 +270,7 @@
     place_got(got_other_ref, 2 * index_y - 1, 1 - index_y)
     place_middle(got_ref, got_other_ref)
 
+    table_copy.wait()
     level_of = lax.broadcasted_iota(jnp.int32, speed_ref.shape, 0) % levels
     speeds = jnp.full(speed_ref.shape, table_ref[0], jnp.float32)
     for index in range(1, levels):
@@ -288,10 +291,7 @@
                     wanted = ((here >= 0) & (here < 3)) | ((here >= gap) & (here < gap + 3))
                     shift = (offset - (MARGIN + cells - 3)) % LANES
                     merged = jnp.where(wanted, pltpu.roll(lines, shift, 1), merged)
-            merged = jnp.concatenate(
-                [merged, jnp.zeros((LANES - cells, LANES), jnp.float32)], axis=0
-            )
-            flip_ref[pair] = merged.T
+            flip_ref[pair, :, :cells] = merged.T
             for slot in range(2):
                 for side in (2, 3):
                     for odd in range(2):
@@ -345,19 +345,21 @@
                     row = row_of(x) + pair * levels
                     z_ref[slot, row : row + levels] = both[at : at + levels]
 
-    def tile_rows(odd, side, depth):
+    wide = WINDOW - cells - 3 + 3 * levels
+
+    def tile_rows(odd, side, depth, base=0):
         if side == 3:
-            return pl.ds(odd * WINDOW + depth, levels, 16)
-        return pl.ds(((odd + 1) % 2) * WINDOW + 15 - depth, levels, 16)
-
-    def put_columns(lines, field, start, pair):
+            return pl.ds(base + odd * WINDOW + depth, levels, 3)
+        return pl.ds(base + ((odd + 1) % 2) * WINDOW + wide - 3 * levels + 2 - depth, levels, 3)
+
+    def put_columns(lines, field, start, pair, base=0):
         count = lines.shape[0]
         position = lanes_of(count) % WINDOW
         rim = ((position >= MARGIN - 3) & (position < MARGIN)) | (
             (position >= MARGIN + cells) & (position < MARGIN + cells + 3)
         )
         for level in range(levels):
-            rolled = pltpu.roll(lines, (MARGIN + cells - 16 * level) % LANES, 1)
+            rolled = pltpu.roll(lines, (MARGIN + cells - base - 3 * level) % LANES, 1)
             at = pl.ds(row_of(start) + pair * levels + level, count, group)
             z_ref[field, at] = jnp.where(rim, rolled, z_ref[field, at])
 
@@ -369,11 +371,11 @@
                     for slot in range(2):
                         for depth in range(3):
                             at = slot * slots + depth * levels
-                            tile_ref[2 * pair + slot, tile_rows(odd, side, depth)] = block[
-                                at : at + levels
-                            ]
+                            rows = tile_rows(odd, side, depth, slot * wide)
+                            tile_ref[pair, rows] = block[at : at + levels]
+            turned = tile_ref[pair].T[:cells]
             for slot, field in ((0, 0), (1, 2)):
-                put_columns(tile_ref[2 * pair + slot].T[:cells], field, 0, pair)
+                put_columns(turned, field, 0, pair, slot * wide)
 
     def rim_columns_own():
         lane = lanes_of(2 * slots)
@@ -442,6 +444,7 @@
     rim_columns_own()
     at = pl.multiple_of(row_of(0) + index_x * chunk, 8)
     predict(at - 2 * group, chunk + 4 * group)
+    copies = []
     for field, values in enumerate(update(at, chunk)):
         for odd in range(2):
             shift = LANES - (MARGIN + odd * WINDOW) - index_y * cy
@@ -449,7 +452,12 @@
             for x in range(cx):
                 for pair in range(pairs):
                     row = x * group + pair * levels
-                    out_ref[2 * pair + odd, field, x] = rolled[row : row + levels, :cy]
+                    out_ref[field, 2 * pair + odd, x] = rolled[row : row + levels, :cy]
+        copy = pltpu.make_async_copy(out_ref.at[field], out_hbm.at[:, field], sems.at[1 + field])
+        copy.start()
+        copies.append(copy)
+    for copy in copies:
+        copy.wait()
 
 
 def fast_on_device(state, coriolis, wave_speed, edges):
@@ -546,15 +554,18 @@
         functools.partial(step_kernel, sizes),
         out_shape=[jax.ShapeDtypeStruct((faces, fields, cx, levels, cy), jnp.float32)]
         + state_rows,
-        in_specs=[in_vmem] * 2 + [pl.BlockSpec(memory_space=pltpu.SMEM)] + [in_vmem] * 2,
-        out_specs=[in_vmem] * 3,
+        in_specs=[in_vmem] * 5,
+        out_specs=[pl.BlockSpec(memory_space=pltpu.HBM)] + [in_vmem] * 2,
         input_output_aliases={3: 1, 4: 2},
         scratch_shapes=[
             pltpu.VMEM(((cells + 8) * group, LANES), jnp.float32),
             pltpu.VMEM((faces * 4, 32, LANES), jnp.float32),
-            pltpu.VMEM((faces, LANES, LANES), jnp.float32),
+            pltpu.VMEM((pairs, LANES, LANES), jnp.float32),
             pltpu.VMEM((pairs, LANES, LANES), jnp.float32),
             pltpu.VMEM(((cx + 4) * group, LANES), jnp.float32),
+            pltpu.SMEM(table.shape, jnp.float32),
+            pltpu.VMEM((fields, faces, cx, levels, cy), jnp.float32),
+            pltpu.SemaphoreType.DMA((1 + fields,)),
         ],
         compiler_params=pltpu.CompilerParams(vmem_limit_bytes=VMEM_LIMIT),
         name="substeps",

time: 24.7 us -> 24.7 us (level)
  no operation moved by 1% of the time
where the time goes in v12:
time: 24.7 us; the launch traced here: 24.5 us
  starting transfers between devices  8.01 us (32%)
  waiting for transfers between devices  7.95 us (32%)
  Pallas kernels  6.49 us (26%)
  local copies, waits for them, and re-layouts  1.9 us (8%)
    ppermute x4, starting transfers between devices, moved(): return lax.ppermute(block, ('tx', 'ty'), pairs_of)  7.42 us
    ppermute x4, waiting for transfers between devices, moved(): return lax.ppermute(block, ('tx', 'ty'), pairs_of)  6.13 us
    pallas_call x1, Pallas kernels, fast_on_device(): pl.pallas_call(functools.partial(step_kernel, sizes), out_shape=[jax.Shap...  5.15 us
    ppermute x2, waiting for transfers between devices, across(): return lax.ppermute(block, 'ty', [(0, 1), (1, 0)])  1.81 us
    unnamed x8, local copies, waits for them, and re-layouts  1.68 us
    pallas_call x1, Pallas kernels, fast_on_device(): pl.pallas_call(functools.partial(pack_kernel, cx, cy, count_x, full_rows,...  0.69 us
    ppermute x2, starting transfers between devices, across(): return lax.ppermute(block, 'ty', [(0, 1), (1, 0)])  0.59 us
  transfers between devices with their start and end apart: 6, of which 4 were waited for; matrix products, arithmetic and copies ran while one was open for 1% of the time, Pallas kernels for 3%

profile of v12, /device:TPU:0, one launch (start us, length us, event | category | flops | bytes accessed | tf_op | source)
XLA Modules:
  0.0 24.5 jit_solution(1961463152897542071)
XLA Ops:
  0.0 0.0 copy-start
  0.0 0.9 %copy-done = f32[6,3,4,6,24]{4,2,3,1,0:T(4,128)S(1)} copy-done((f32[6,3,4,6,24]{4,2,3,1,0:T(4,128)S(1)}, f32[6,3,4,6,24]{4,2,3,1,0:T(4,128)}, u32[]{:S(2)}) %copy-start) | copy-done | bytes 41496
  0.9 0.0 copy-start.1
  0.9 0.7 %copy-done.1 = f32[6,6,24]{2,1,0:T(8,128)S(1)} copy-done((f32[6,6,24]{2,1,0:T(8,128)S(1)}, f32[6,6,24]{2,1,0:T(8,128)}, u32[]{:S(2)}) %copy-start.1) | copy-done | bytes 3480
  1.7 0.7 %pack.1 = (f32[216,128]{1,0:T(8,128)S(1)}, f32[32,128]{1,0:T(8,128)S(1)}) custom-call(f32[6,3,6,4,24]{4,3,2,1,0:T(4,128)S(1)} %bitcast.2, f32[6,6,24]{2,1,0:T(8,128)S(1)} %copy-done.1), custom_call_target="tpu_custom_call" | custom-call | tf_op jit(solution)/shard_map/pack/pallas_call | solution.py:472
  2.4 0.5 %collective-permute-start = (f32[216,128]{1,0:T(8,128)S(1)}, f32[216,128]{1,0:T(8,128)S(1)}, u32[]{:S(2)}, u32[]{:S(2)}) collective-permute-start(f32[216,128]{1,0:T(8,128)S(1)} %get-tuple-element.19.swap_ref.own_ref), channel_id=1, source_target_pairs={{0,1},{1,0},{2,3},{3,2},{4,5},{5,4},{6,7},{7,6},{8,9},{9,8},{10,11... | collective-permute-start | bytes 331784 | tf_op jit(solution)/shard_map/ppermute | solution.py:509
  2.9 0.2 keep.1
  3.1 0.8 %collective-permute-done.other_ref = f32[216,128]{1,0:T(8,128)S(1)} collective-permute-done((f32[216,128]{1,0:T(8,128)S(1)}, f32[216,128]{1,0:T(8,128)S(1)}, u32[]{:S(2)}, u32[]{:S(2)}) %collective-permute-start) | collective-permute-done | bytes 110624 | tf_op jit(solution)/shard_map/ppermute | solution.py:509
  3.8 0.0 copy-start.2
  3.9 2.9 %collective-permute-start.1 = (f32[240,128]{1,0:T(8,128)S(1)}, f32[240,128]{1,0:T(8,128)S(1)}, u32[]{:S(2)}, u32[]{:S(2)}) collective-permute-start(f32[240,128]{1,0:T(8,128)S(1)} %get-tuple-element.22), channel_id=1, source_target_pairs={{0,2},{1,15},{2,4},{3,1},{4,6},{5,3},{6,8},{7,5},{8,10},{9,7},{10,... | collective-permute-start | bytes 368648 | tf_op jit(solution)/shard_map/ppermute | solution.py:506
  6.8 2.6 %collective-permute-start.4 = (f32[48,128]{1,0:T(8,128)S(1)}, f32[48,128]{1,0:T(8,128)S(1)}, u32[]{:S(2)}, u32[]{:S(2)}) collective-permute-start(f32[48,128]{1,0:T(8,128)S(1)} %get-tuple-element.25), channel_id=1, source_target_pairs={{0,8},{1,9},{2,10},{3,11},{4,12},{5,13},{6,14},{7,15},{8,0},{9,1},... | collective-permute-start | bytes 73736 | tf_op jit(solution)/shard_map/ppermute | solution.py:506
  9.4 0.0 copy-done.2
  9.4 0.1 copy.10
  9.5 0.1 convert_element_type.7
  9.6 0.0 copy-start.3
  9.6 1.6 %collective-permute-start.2 = (f32[96,128]{1,0:T(8,128)S(1)}, f32[96,128]{1,0:T(8,128)S(1)}, u32[]{:S(2)}, u32[]{:S(2)}) collective-permute-start(f32[96,128]{1,0:T(8,128)S(1)} %get-tuple-element.23), channel_id=1, source_target_pairs={{0,4},{1,13},{2,6},{3,15},{4,8},{5,1},{6,10},{7,3},{8,12},{9,5},{1... | collective-permute-start | bytes 147464 | tf_op jit(solution)/shard_map/ppermute | solution.py:506
  11.3 0.3 %collective-permute-start.3 = (f32[96,128]{1,0:T(8,128)S(1)}, f32[96,128]{1,0:T(8,128)S(1)}, u32[]{:S(2)}, u32[]{:S(2)}) collective-permute-start(f32[96,128]{1,0:T(8,128)S(1)} %get-tuple-element.24), channel_id=1, source_target_pairs={{0,6},{1,11},{2,8},{3,13},{4,10},{5,15},{6,12},{7,1},{8,14},{9,3},... | collective-permute-start | bytes 147464 | tf_op jit(solution)/shard_map/ppermute | solution.py:506
  11.5 0.0 copy-done.3
  11.5 0.1 pad_maximum_fusion.1.table_in
  11.6 0.0 collective-permute-done.4
  11.6 4.4 %collective-permute-done.2 = f32[96,128]{1,0:T(8,128)S(1)} collective-permute-done((f32[96,128]{1,0:T(8,128)S(1)}, f32[96,128]{1,0:T(8,128)S(1)}, u32[]{:S(2)}, u32[]{:S(2)}) %collective-permute-start.2) | collective-permute-done | bytes 49184 | tf_op jit(solution)/shard_map/ppermute | solution.py:506
  16.0 1.7 %collective-permute-done.3 = f32[96,128]{1,0:T(8,128)S(1)} collective-permute-done((f32[96,128]{1,0:T(8,128)S(1)}, f32[96,128]{1,0:T(8,128)S(1)}, u32[]{:S(2)}, u32[]{:S(2)}) %collective-permute-start.3) | collective-permute-done | bytes 49184 | tf_op jit(solution)/shard_map/ppermute | solution.py:506
  17.7 0.0 collective-permute-done.1
  17.8 0.1 collective-permute-start.5
  17.8 0.2 place_own.1
  18.0 0.3 %place_got.1 = (f32[3,672,128]{2,1,0:T(8,128)S(1)}, f32[576,128]{1,0:T(8,128)S(1)}) custom-call(f32[480,128]{1,0:T(8,128)S(1)} %pad_maximum_fusion.got_ref, f32[3,672,128]{2,1,0:T(8,128)S(1)} %get-tuple-element.28.z_in, f32[576,128]{1,0:T(8,128)S(1)} %get-tuple-element.29.cor_in), custom_call_target="tpu_custom_call", output_to_operand_aliasing={{0}: (1, {}), {1}: (2, {})} | custom-call | tf_op jit(solution)/shard_map/place_got/pallas_call | solution.py:544
  18.3 1.1 %collective-permute-done.5.got_other_ref = f32[480,128]{1,0:T(8,128)S(1)} collective-permute-done((f32[480,128]{1,0:T(8,128)S(1)}, f32[480,128]{1,0:T(8,128)S(1)}, u32[]{:S(2)}, u32[]{:S(2)}) %collective-permute-start.5) | collective-permute-done | bytes 245792 | tf_op jit(solution)/shard_map/ppermute | solution.py:509
  19.3 5.2 %substeps.1 = (f32[6,3,6,4,24]{4,3,2,1,0:T(4,128)}, f32[3,672,128]{2,1,0:T(8,128)S(1)}, f32[576,128]{1,0:T(8,128)S(1)}) custom-call(f32[480,128]{1,0:T(8,128)S(1)} %pad_maximum_fusion.got_ref, f32[480,128]{1,0:T(8,128)S(1)} %collective-permute-done.5.got_other_ref, f32[76]{0:T(128)S(1)} %pad_maximum_fusion.1.table_in, ...), custom_call_target="tpu_custom_call", output_to_operand_aliasing={{1}: (3, {}), {2}: (4, {})} | custom-call | tf_op jit(solution)/shard_map/substeps/pallas_call | solution.py:553
  (3 shorter events, 0.0 us)
Async XLA Ops:
  0.0 0.9 %copy-start = (f32[6,3,4,6,24]{4,2,3,1,0:T(4,128)S(1)}, f32[6,3,4,6,24]{4,2,3,1,0:T(4,128)}, u32[]{:S(2)}) copy-start(f32[6,3,4,6,24]{4,2,3,1,0:T(4,128)} %param.4) | copy-start | bytes 124420
  0.9 0.7 %copy-start.1 = (f32[6,6,24]{2,1,0:T(8,128)S(1)}, f32[6,6,24]{2,1,0:T(8,128)}, u32[]{:S(2)}) copy-start(f32[6,6,24]{2,1,0:T(8,128)} %coriolis_hbm.1) | copy-start | bytes 10372
  2.4 1.5 %collective-permute-start = (f32[216,128]{1,0:T(8,128)S(1)}, f32[216,128]{1,0:T(8,128)S(1)}, u32[]{:S(2)}, u32[]{:S(2)}) collective-permute-start(f32[216,128]{1,0:T(8,128)S(1)} %get-tuple-element.19.swap_ref.own_ref), channel_id=1, source_target_pairs={{0,1},{1,0},{2,3},{3,2},{4,5},{5,4},{6,7},{7,6},{8,9},{9,8},{10,11... | collective-permute-start | bytes 331784 | tf_op jit(solution)/shard_map/ppermute | solution.py:509
  3.8 5.5 %copy-start.2 = (s32[6,4,3]{0,1,2:T(4,128)S(1)}, s32[6,4,3]{0,1,2:T(4,128)}, u32[]{:S(2)}) copy-start(s32[6,4,3]{0,1,2:T(4,128)} %param.7) | copy-start | bytes 868
  3.9 13.9 %collective-permute-start.1 = (f32[240,128]{1,0:T(8,128)S(1)}, f32[240,128]{1,0:T(8,128)S(1)}, u32[]{:S(2)}, u32[]{:S(2)}) collective-permute-start(f32[240,128]{1,0:T(8,128)S(1)} %get-tuple-element.22), channel_id=1, source_target_pairs={{0,2},{1,15},{2,4},{3,1},{4,6},{5,3},{6,8},{7,5},{8,10},{9,7},{10,... | collective-permute-start | bytes 368648 | tf_op jit(solution)/shard_map/ppermute | solution.py:506
  6.8 4.8 %collective-permute-start.4 = (f32[48,128]{1,0:T(8,128)S(1)}, f32[48,128]{1,0:T(8,128)S(1)}, u32[]{:S(2)}, u32[]{:S(2)}) collective-permute-start(f32[48,128]{1,0:T(8,128)S(1)} %get-tuple-element.25), channel_id=1, source_target_pairs={{0,8},{1,9},{2,10},{3,11},{4,12},{5,13},{6,14},{7,15},{8,0},{9,1},... | collective-permute-start | bytes 73736 | tf_op jit(solution)/shard_map/ppermute | solution.py:506
  9.6 1.9 %copy-start.3 = (f32[4]{0:T(128)S(1)}, f32[4]{0:T(128)}, u32[]{:S(2)}) copy-start(f32[4]{0:T(128)} %param.6) | copy-start | bytes 52
  9.6 6.4 %collective-permute-start.2 = (f32[96,128]{1,0:T(8,128)S(1)}, f32[96,128]{1,0:T(8,128)S(1)}, u32[]{:S(2)}, u32[]{:S(2)}) collective-permute-start(f32[96,128]{1,0:T(8,128)S(1)} %get-tuple-element.23), channel_id=1, source_target_pairs={{0,4},{1,13},{2,6},{3,15},{4,8},{5,1},{6,10},{7,3},{8,12},{9,5},{1... | collective-permute-start | bytes 147464 | tf_op jit(solution)/shard_map/ppermute | solution.py:506
  11.3 6.5 %collective-permute-start.3 = (f32[96,128]{1,0:T(8,128)S(1)}, f32[96,128]{1,0:T(8,128)S(1)}, u32[]{:S(2)}, u32[]{:S(2)}) collective-permute-start(f32[96,128]{1,0:T(8,128)S(1)} %get-tuple-element.24), channel_id=1, source_target_pairs={{0,6},{1,11},{2,8},{3,13},{4,10},{5,15},{6,12},{7,1},{8,14},{9,3},... | collective-permute-start | bytes 147464 | tf_op jit(solution)/shard_map/ppermute | solution.py:506
  17.8 1.6 %collective-permute-start.5 = (f32[480,128]{1,0:T(8,128)S(1)}, f32[480,128]{1,0:T(8,128)S(1)}, u32[]{:S(2)}, u32[]{:S(2)}) collective-permute-start(f32[480,128]{1,0:T(8,128)S(1)} %pad_maximum_fusion.got_ref), channel_id=1, source_target_pairs={{0,1},{1,0},{2,3},{3,2},{4,5},{5,4},{6,7},{7,6},{8,9},{9,8},{10,11... | collective-permute-start | bytes 737288 | tf_op jit(solution)/shard_map/ppermute | solution.py:509

commit v13 on v12

--- a/solution.py
+++ b/solution.py
@@ -497,12 +497,17 @@
         name="keep",
     )(swap, lines)
 
+    def read(source, target):
+        ends = (0, count_x - 1)
+        return source in ends or target in ends or abs(source + target - ends[1]) <= 1
+
     def moved(block, distance):
         pairs_of = []
         for index in range(count_x):
             for core in range(2):
                 target = (index + distance * (1 - 2 * core)) % count_x
-                pairs_of.append((2 * index + core, 2 * target + core))
+                if distance == 1 or read(index, target):
+                    pairs_of.append((2 * index + core, 2 * target + core))
         return lax.ppermute(block, ("tx", "ty"), pairs_of)
 
     def across(block):

time: 24.7 us -> 27.9 us (1.13)
  starting transfers between devices: 8.01 us -> 11.8 us
  waiting for transfers between devices: 7.95 us -> 7.32 us
    ppermute x4, starting transfers between devices: 7.42 us -> 11.2 us  [moved(): return lax.ppermute(block, ('tx', 'ty'), pairs_of)]
    ppermute x4, waiting for transfers between devices: 6.13 us -> 5.5 us  [moved(): return lax.ppermute(block, ('tx', 'ty'), pairs_of)]
  transfers between devices with their start and end apart: 6 -> 6, of which waited for: 4 -> 4; matrix products, arithmetic and copies ran while one was open for 1% -> 1% of each run, Pallas kernels for 3% -> 2%
where the time goes in v13:
time: 27.9 us; the launch traced here: 27.6 us
  starting transfers between devices  11.8 us (42%)
  waiting for transfers between devices  7.32 us (26%)
  Pallas kernels  6.48 us (23%)
  local copies, waits for them, and re-layouts  1.9 us (7%)
    ppermute x4, starting transfers between devices, moved(): return lax.ppermute(block, ('tx', 'ty'), pairs_of)  11.2 us
    ppermute x4, waiting for transfers between devices, moved(): return lax.ppermute(block, ('tx', 'ty'), pairs_of)  5.5 us
    pallas_call x1, Pallas kernels, fast_on_device(): pl.pallas_call(functools.partial(step_kernel, sizes), out_shape=[jax.Shap...  5.15 us
    ppermute x2, waiting for transfers between devices, across(): return lax.ppermute(block, 'ty', [(0, 1), (1, 0)])  1.81 us
    unnamed x8, local copies, waits for them, and re-layouts  1.68 us
    pallas_call x1, Pallas kernels, fast_on_device(): pl.pallas_call(functools.partial(pack_kernel, cx, cy, count_x, full_rows,...  0.69 us
    ppermute x2, starting transfers between devices, across(): return lax.ppermute(block, 'ty', [(0, 1), (1, 0)])  0.59 us
  transfers between devices with their start and end apart: 6, of which 4 were waited for; matrix products, arithmetic and copies ran while one was open for 1% of the time, Pallas kernels for 2%

profile of v13, /device:TPU:0, one launch (start us, length us, event | category | flops | bytes accessed | tf_op | source)
XLA Modules:
  0.0 27.6 jit_solution(3358848971976977420)
XLA Ops:
  0.0 0.0 copy-start
  0.0 0.9 %copy-done = f32[6,3,4,6,24]{4,2,3,1,0:T(4,128)S(1)} copy-done((f32[6,3,4,6,24]{4,2,3,1,0:T(4,128)S(1)}, f32[6,3,4,6,24]{4,2,3,1,0:T(4,128)}, u32[]{:S(2)}) %copy-start) | copy-done | bytes 41496
  0.9 0.0 copy-start.1
  0.9 0.7 %copy-done.1 = f32[6,6,24]{2,1,0:T(8,128)S(1)} copy-done((f32[6,6,24]{2,1,0:T(8,128)S(1)}, f32[6,6,24]{2,1,0:T(8,128)}, u32[]{:S(2)}) %copy-start.1) | copy-done | bytes 3480
  1.7 0.7 %pack.1 = (f32[216,128]{1,0:T(8,128)S(1)}, f32[32,128]{1,0:T(8,128)S(1)}) custom-call(f32[6,3,6,4,24]{4,3,2,1,0:T(4,128)S(1)} %bitcast.2, f32[6,6,24]{2,1,0:T(8,128)S(1)} %copy-done.1), custom_call_target="tpu_custom_call" | custom-call | tf_op jit(solution)/shard_map/pack/pallas_call | solution.py:472
  2.4 0.5 %collective-permute-start = (f32[216,128]{1,0:T(8,128)S(1)}, f32[216,128]{1,0:T(8,128)S(1)}, u32[]{:S(2)}, u32[]{:S(2)}) collective-permute-start(f32[216,128]{1,0:T(8,128)S(1)} %get-tuple-element.19.swap_ref.own_ref), channel_id=1, source_target_pairs={{0,1},{1,0},{2,3},{3,2},{4,5},{5,4},{6,7},{7,6},{8,9},{9,8},{10,11... | collective-permute-start | bytes 331784 | tf_op jit(solution)/shard_map/ppermute | solution.py:514
  2.9 0.2 keep.1
  3.1 0.8 %collective-permute-done.other_ref = f32[216,128]{1,0:T(8,128)S(1)} collective-permute-done((f32[216,128]{1,0:T(8,128)S(1)}, f32[216,128]{1,0:T(8,128)S(1)}, u32[]{:S(2)}, u32[]{:S(2)}) %collective-permute-start) | collective-permute-done | bytes 110624 | tf_op jit(solution)/shard_map/ppermute | solution.py:514
  3.8 0.0 copy-start.2
  3.9 2.9 %collective-permute-start.1 = (f32[240,128]{1,0:T(8,128)S(1)}, f32[240,128]{1,0:T(8,128)S(1)}, u32[]{:S(2)}, u32[]{:S(2)}) collective-permute-start(f32[240,128]{1,0:T(8,128)S(1)} %get-tuple-element.22), channel_id=1, source_target_pairs={{0,2},{1,15},{2,4},{3,1},{4,6},{5,3},{6,8},{7,5},{8,10},{9,7},{10,... | collective-permute-start | bytes 368648 | tf_op jit(solution)/shard_map/ppermute | solution.py:511
  6.8 2.6 %collective-permute-start.4 = (f32[48,128]{1,0:T(8,128)S(1)}, f32[48,128]{1,0:T(8,128)S(1)}, u32[]{:S(2)}, u32[]{:S(2)}) collective-permute-start(f32[48,128]{1,0:T(8,128)S(1)} %get-tuple-element.25), channel_id=1, source_target_pairs={{0,8},{1,9},{2,10},{3,11},{4,12},{5,13},{6,14},{7,15},{8,0},{9,1},... | collective-permute-start | bytes 73736 | tf_op jit(solution)/shard_map/ppermute | solution.py:511
  9.4 0.0 copy-done.2
  9.4 0.1 copy.10
  9.5 0.1 convert_element_type.7
  9.6 0.0 copy-start.3
  9.6 3.5 %collective-permute-start.2 = (f32[96,128]{1,0:T(8,128)S(1)}, f32[96,128]{1,0:T(8,128)S(1)}, u32[]{:S(2)}, u32[]{:S(2)}) collective-permute-start(f32[96,128]{1,0:T(8,128)S(1)} %get-tuple-element.23), channel_id=1, source_target_pairs={{0,4},{1,13},{3,15},{4,8},{5,1},{6,10},{9,5},{10,14},{11,7},{12,0}... | collective-permute-start | bytes 147464 | tf_op jit(solution)/shard_map/ppermute | solution.py:511
  13.1 2.2 %collective-permute-start.3 = (f32[96,128]{1,0:T(8,128)S(1)}, f32[96,128]{1,0:T(8,128)S(1)}, u32[]{:S(2)}, u32[]{:S(2)}) collective-permute-start(f32[96,128]{1,0:T(8,128)S(1)} %get-tuple-element.24), channel_id=1, source_target_pairs={{0,6},{1,11},{3,13},{4,10},{5,15},{7,1},{8,14},{10,0},{11,5},{12,2... | collective-permute-start | bytes 147464 | tf_op jit(solution)/shard_map/ppermute | solution.py:511
  15.3 0.0 copy-done.3
  15.3 0.1 pad_maximum_fusion.1.table_in
  15.4 0.0 collective-permute-done.4
  15.4 2.0 %collective-permute-done.2 = f32[96,128]{1,0:T(8,128)S(1)} collective-permute-done((f32[96,128]{1,0:T(8,128)S(1)}, f32[96,128]{1,0:T(8,128)S(1)}, u32[]{:S(2)}, u32[]{:S(2)}) %collective-permute-start.2) | collective-permute-done | bytes 49184 | tf_op jit(solution)/shard_map/ppermute | solution.py:511
  17.4 3.5 %collective-permute-done.3 = f32[96,128]{1,0:T(8,128)S(1)} collective-permute-done((f32[96,128]{1,0:T(8,128)S(1)}, f32[96,128]{1,0:T(8,128)S(1)}, u32[]{:S(2)}, u32[]{:S(2)}) %collective-permute-start.3) | collective-permute-done | bytes 49184 | tf_op jit(solution)/shard_map/ppermute | solution.py:511
  20.9 0.0 collective-permute-done.1
  20.9 0.1 collective-permute-start.5
  21.0 0.2 place_own.1
  21.2 0.3 %place_got.1 = (f32[3,672,128]{2,1,0:T(8,128)S(1)}, f32[576,128]{1,0:T(8,128)S(1)}) custom-call(f32[480,128]{1,0:T(8,128)S(1)} %pad_maximum_fusion.got_ref, f32[3,672,128]{2,1,0:T(8,128)S(1)} %get-tuple-element.28.z_in, f32[576,128]{1,0:T(8,128)S(1)} %get-tuple-element.29.cor_in), custom_call_target="tpu_custom_call", output_to_operand_aliasing={{0}: (1, {}), {1}: (2, {})} | custom-call | tf_op jit(solution)/shard_map/place_got/pallas_call | solution.py:549
  21.4 1.1 %collective-permute-done.5.got_other_ref = f32[480,128]{1,0:T(8,128)S(1)} collective-permute-done((f32[480,128]{1,0:T(8,128)S(1)}, f32[480,128]{1,0:T(8,128)S(1)}, u32[]{:S(2)}, u32[]{:S(2)}) %collective-permute-start.5) | collective-permute-done | bytes 245792 | tf_op jit(solution)/shard_map/ppermute | solution.py:514
  22.5 5.2 %substeps.1 = (f32[6,3,6,4,24]{4,3,2,1,0:T(4,128)}, f32[3,672,128]{2,1,0:T(8,128)S(1)}, f32[576,128]{1,0:T(8,128)S(1)}) custom-call(f32[480,128]{1,0:T(8,128)S(1)} %pad_maximum_fusion.got_ref, f32[480,128]{1,0:T(8,128)S(1)} %collective-permute-done.5.got_other_ref, f32[76]{0:T(128)S(1)} %pad_maximum_fusion.1.table_in, ...), custom_call_target="tpu_custom_call", output_to_operand_aliasing={{1}: (3, {}), {2}: (4, {})} | custom-call | tf_op jit(solution)/shard_map/substeps/pallas_call | solution.py:558
  (3 shorter events, 0.0 us)
Async XLA Ops:
  0.0 0.9 %copy-start = (f32[6,3,4,6,24]{4,2,3,1,0:T(4,128)S(1)}, f32[6,3,4,6,24]{4,2,3,1,0:T(4,128)}, u32[]{:S(2)}) copy-start(f32[6,3,4,6,24]{4,2,3,1,0:T(4,128)} %param.4) | copy-start | bytes 124420
  0.9 0.7 %copy-start.1 = (f32[6,6,24]{2,1,0:T(8,128)S(1)}, f32[6,6,24]{2,1,0:T(8,128)}, u32[]{:S(2)}) copy-start(f32[6,6,24]{2,1,0:T(8,128)} %coriolis_hbm.1) | copy-start | bytes 10372
  2.4 1.5 %collective-permute-start = (f32[216,128]{1,0:T(8,128)S(1)}, f32[216,128]{1,0:T(8,128)S(1)}, u32[]{:S(2)}, u32[]{:S(2)}) collective-permute-start(f32[216,128]{1,0:T(8,128)S(1)} %get-tuple-element.19.swap_ref.own_ref), channel_id=1, source_target_pairs={{0,1},{1,0},{2,3},{3,2},{4,5},{5,4},{6,7},{7,6},{8,9},{9,8},{10,11... | collective-permute-start | bytes 331784 | tf_op jit(solution)/shard_map/ppermute | solution.py:514
  3.8 5.5 %copy-start.2 = (s32[6,4,3]{0,1,2:T(4,128)S(1)}, s32[6,4,3]{0,1,2:T(4,128)}, u32[]{:S(2)}) copy-start(s32[6,4,3]{0,1,2:T(4,128)} %param.7) | copy-start | bytes 868
  3.9 17.0 %collective-permute-start.1 = (f32[240,128]{1,0:T(8,128)S(1)}, f32[240,128]{1,0:T(8,128)S(1)}, u32[]{:S(2)}, u32[]{:S(2)}) collective-permute-start(f32[240,128]{1,0:T(8,128)S(1)} %get-tuple-element.22), channel_id=1, source_target_pairs={{0,2},{1,15},{2,4},{3,1},{4,6},{5,3},{6,8},{7,5},{8,10},{9,7},{10,... | collective-permute-start | bytes 368648 | tf_op jit(solution)/shard_map/ppermute | solution.py:511
  6.8 8.6 %collective-permute-start.4 = (f32[48,128]{1,0:T(8,128)S(1)}, f32[48,128]{1,0:T(8,128)S(1)}, u32[]{:S(2)}, u32[]{:S(2)}) collective-permute-start(f32[48,128]{1,0:T(8,128)S(1)} %get-tuple-element.25), channel_id=1, source_target_pairs={{0,8},{1,9},{2,10},{3,11},{4,12},{5,13},{6,14},{7,15},{8,0},{9,1},... | collective-permute-start | bytes 73736 | tf_op jit(solution)/shard_map/ppermute | solution.py:511
  9.6 5.7 %copy-start.3 = (f32[4]{0:T(128)S(1)}, f32[4]{0:T(128)}, u32[]{:S(2)}) copy-start(f32[4]{0:T(128)} %param.6) | copy-start | bytes 52
  9.6 7.8 %collective-permute-start.2 = (f32[96,128]{1,0:T(8,128)S(1)}, f32[96,128]{1,0:T(8,128)S(1)}, u32[]{:S(2)}, u32[]{:S(2)}) collective-permute-start(f32[96,128]{1,0:T(8,128)S(1)} %get-tuple-element.23), channel_id=1, source_target_pairs={{0,4},{1,13},{3,15},{4,8},{5,1},{6,10},{9,5},{10,14},{11,7},{12,0}... | collective-permute-start | bytes 147464 | tf_op jit(solution)/shard_map/ppermute | solution.py:511
  13.1 7.8 %collective-permute-start.3 = (f32[96,128]{1,0:T(8,128)S(1)}, f32[96,128]{1,0:T(8,128)S(1)}, u32[]{:S(2)}, u32[]{:S(2)}) collective-permute-start(f32[96,128]{1,0:T(8,128)S(1)} %get-tuple-element.24), channel_id=1, source_target_pairs={{0,6},{1,11},{3,13},{4,10},{5,15},{7,1},{8,14},{10,0},{11,5},{12,2... | collective-permute-start | bytes 147464 | tf_op jit(solution)/shard_map/ppermute | solution.py:511
  20.9 1.6 %collective-permute-start.5 = (f32[480,128]{1,0:T(8,128)S(1)}, f32[480,128]{1,0:T(8,128)S(1)}, u32[]{:S(2)}, u32[]{:S(2)}) collective-permute-start(f32[480,128]{1,0:T(8,128)S(1)} %pad_maximum_fusion.got_ref), channel_id=1, source_target_pairs={{0,1},{1,0},{2,3},{3,2},{4,5},{5,4},{6,7},{7,6},{8,9},{9,8},{10,11... | collective-permute-start | bytes 737288 | tf_op jit(solution)/shard_map/ppermute | solution.py:514

commit v14 on v12

--- a/solution.py
+++ b/solution.py
@@ -15,20 +15,27 @@
 SMALL_VMEM_LIMIT = 8 * 1024 * 1024
 
 
-def window_start(source, target, count_x, index_y, cx, cy, far):
-    width = 2 * cx
+def wrap(index, count):
+    index = jnp.where(index < 0, index + count, index)
+    return jnp.where(index >= count, index - count, index)
+
+
+def lane_shift(amount):
+    return amount & (LANES - 1)
+
+
+def windows(source, target, count_x, index_y, cx, cy):
+    spare = cy - 2 * cx
     near = jnp.minimum(target, count_x - 1 - target)
-    inward = jnp.minimum(cx * near - jnp.where(far, cx, cx // 2), cy - width)
     rim = (source == 0) | (source == count_x - 1)
-    start = jnp.where(rim, jnp.maximum(inward, 0), 0)
-    return jnp.where(index_y == 0, start, cy - width - start)
-
-
-def windows(source, target, count_x, index_y, cx, cy):
-    low_far = source == count_x - 1
-    lower = window_start(source, target, count_x, index_y, cx, cy, low_far)
-    upper = window_start(source, target, count_x, index_y, cx, cy, ~low_far)
-    return lower, upper
+    starts = []
+    for inward in (cx // 2, cx):
+        start = jnp.maximum(jnp.minimum(cx * near - inward, spare), 0)
+        start = jnp.where(rim, start, 0)
+        starts.append(jnp.where(index_y == 0, start, spare - start))
+    close, far = starts
+    upside = source == count_x - 1
+    return jnp.where(upside, far, close), jnp.where(upside, close, far)
 
 
 def unit_place(field, x, cx, group, width):
@@ -37,26 +44,55 @@
     return (index // per_row) * group, (index % per_row) * width
 
 
-def pack_kernel(
-    cx, cy, count_x, full_rows, small_rows, state_hbm, coriolis_hbm,
-    swap_ref, line_ref, state_ref, coriolis_ref, sems,
-):
-    copies = [
-        pltpu.make_async_copy(state_hbm, state_ref, sems.at[0]),
-        pltpu.make_async_copy(coriolis_hbm, coriolis_ref, sems.at[1]),
+def chunk_targets(count_x, full_rows, small_rows):
+    sense = 1 - 2 * lax.axis_index("ty")
+    return [
+        (full_rows + place * small_rows, -sense * distance)
+        for place, distance in enumerate((2, 3))
     ]
-    for copy in copies:
-        copy.start()
+
+
+def put_chunk(cx, cy, count_x, block_ref, line_ref, out_ref, top, offset):
+    pairs = 3
+    group = 4 * pairs
+    fields = 3
+    half = cx // 2
+    width = 2 * cx
+    index_x = lax.axis_index("tx")
+    target = wrap(index_x + offset, count_x)
+    starts = windows(index_x, target, count_x, lax.axis_index("ty"), cx, cy)
+    position = lax.broadcasted_iota(jnp.int32, (group, LANES), 1) % WINDOW
+    from_lane = {lane: position >= lane for lane in range(0, 60, width)}
+    blocks = {}
+
+    def put(row, lane, lines):
+        blocks[row] = lines if row not in blocks else jnp.where(from_lane[lane], lines, blocks[row])
+
+    if block_ref is not None:
+        for field in range(fields):
+            for x in range(cx):
+                row = field * half * group + (x // 2) * group
+                at, lane = unit_place(field, x, cx, group, width)
+                shift = lane_shift(lane - MARGIN - (x % 2) * cy - starts[x // half])
+                put(at, lane, pltpu.roll(block_ref[row : row + group], shift, 1))
+    else:
+        at = unit_place(fields, 0, cx, group, width)[0]
+        blocks[at] = out_ref[top + at : top + at + group]
+    if line_ref is not None:
+        for part in range(2):
+            at, lane = unit_place(fields, part, cx, group, width)
+            shift = lane_shift(lane - MARGIN - starts[part])
+            put(at, lane, pltpu.roll(line_ref[16 * part : 16 * part + group], shift, 1))
+    for row, lines in blocks.items():
+        out_ref[top + row : top + row + group] = lines
+
+
+def pack_kernel(cx, cy, count_x, full_rows, small_rows, state_ref, swap_ref):
     faces, fields = state_ref.shape[:2]
     levels = state_ref.shape[3]
-    pairs = faces // 2
-    group = pairs * levels
+    group = (faces // 2) * levels
     half = cx // 2
-    base = fields * half * group
     swap_ref[:full_rows] = jnp.zeros((full_rows, LANES), jnp.float32)
-    line_ref[...] = jnp.zeros(line_ref.shape, jnp.float32)
-    for copy in copies:
-        copy.wait()
     for face in range(faces):
         for parity in range(2):
             lane = (face % 2) * WINDOW + MARGIN + parity * cy
@@ -66,48 +102,29 @@
                     swap_ref[row : row + levels, lane : lane + cy] = state_ref[
                         face, field, 2 * xp + parity
                     ]
-                x = 2 * xp + parity
-                row = base + xp * pairs + face // 2
-                swap_ref[row : row + 1, lane : lane + cy] = coriolis_ref[face, x : x + 1]
-                row = (x // half) * 16 + (x % half) * pairs + face // 2
-                lane_at = (face % 2) * WINDOW + MARGIN
-                line_ref[row : row + 1, lane_at : lane_at + cy] = coriolis_ref[face, x : x + 1]
-    sense = 1 - 2 * lax.axis_index("ty")
-    for place, distance in enumerate((2, 3)):
-        top = full_rows + place * small_rows
-        put_chunk(cx, cy, count_x, swap_ref, line_ref, swap_ref, top, -sense * distance)
-
-
-def put_chunk(cx, cy, count_x, block_ref, line_ref, out_ref, top, offset):
-    pairs = 3
-    group = 4 * pairs
-    fields = 3
+    for top, offset in chunk_targets(count_x, full_rows, small_rows):
+        put_chunk(cx, cy, count_x, swap_ref, None, swap_ref, top, offset)
+
+
+def pack_coriolis_kernel(
+    cx, cy, count_x, full_rows, small_rows, coriolis_ref, swap_in, swap_ref, line_ref
+):
+    faces = coriolis_ref.shape[0]
+    pairs = faces // 2
     half = cx // 2
-    width = 2 * cx
-    index_x = lax.axis_index("tx")
-    index_y = lax.axis_index("ty")
-    target = (index_x + offset + count_x) % count_x
-    starts = windows(index_x, target, count_x, index_y, cx, cy)
-    blocks = {}
-
-    def put(row, lane, lines):
-        position = lax.broadcasted_iota(jnp.int32, lines.shape, 1) % WINDOW
-        here = (position >= lane) & (position < lane + width)
-        blocks[row] = jnp.where(here, lines, blocks.get(row, jnp.zeros_like(lines)))
-
-    for field in range(fields):
+    base = 3 * half * 4 * pairs
+    line_ref[...] = jnp.zeros(line_ref.shape, jnp.float32)
+    for face in range(faces):
+        lane = (face % 2) * WINDOW + MARGIN
         for x in range(cx):
-            row = field * half * group + (x // 2) * group
-            at, lane = unit_place(field, x, cx, group, width)
-            shift = lane - MARGIN - (x % 2) * cy - starts[x // half] + 2 * LANES
-            put(at, lane, pltpu.roll(block_ref[row : row + group], shift % LANES, 1))
-    for part in range(2):
-        at, lane = unit_place(fields, part, cx, group, width)
-        shift = lane - MARGIN - starts[part] + 2 * LANES
-        lines = line_ref[16 * part : 16 * part + group]
-        put(at, lane, pltpu.roll(lines, shift % LANES, 1))
-    for row, lines in blocks.items():
-        out_ref[top + row : top + row + group] = lines
+            line = coriolis_ref[face, x : x + 1]
+            row = base + (x // 2) * pairs + face // 2
+            at = lane + (x % 2) * cy
+            swap_ref[row : row + 1, at : at + cy] = line
+            row = (x // half) * 16 + (x % half) * pairs + face // 2
+            line_ref[row : row + 1, lane : lane + cy] = line
+    for top, offset in chunk_targets(count_x, full_rows, small_rows):
+        put_chunk(cx, cy, count_x, None, line_ref, swap_ref, top, offset)
 
 
 def keep_kernel(cx, cy, count_x, small_rows, swap_ref, line_ref, keep_ref, middle_ref):
@@ -145,7 +162,7 @@
         return (x + 4) * group
 
     def from_owner(offset):
-        source = (index_x - offset + 2 * count_x) % count_x
+        source = wrap(index_x - offset, count_x)
         return source, pl.multiple_of(source * chunk, 8)
 
     def put_coriolis(start, x, values, at):
@@ -167,13 +184,21 @@
 
     def put_distant(source, start, lines_of):
         starts_south = windows(source, index_x, count_x, 0, cx, cy)
-        starts_north = windows(source, index_x, count_x, 1, cx, cy)
+        starts_north = [cy - 2 * cx - start for start in starts_south]
+        is_rim = (source == 0) | (source == count_x - 1)
+        starts_north = [jnp.where(is_rim, start, cy - 2 * cx) for start in starts_north]
+        shifts = {
+            (part, lane): (
+                lane_shift(MARGIN + starts_south[part] - lane),
+                lane_shift(MARGIN + cy + starts_north[part] - lane),
+            )
+            for part in range(2)
+            for lane in range(0, 60, 2 * cx)
+        }
 
         def lines_at(field, x, part):
             at, lane = unit_place(field, x, cx, group, 2 * cx)
-            south_shift = (MARGIN + starts_south[part] - lane + LANES) % LANES
-            north_shift = (MARGIN + cy + starts_north[part] - lane + LANES) % LANES
-            return lines_of(at, south_shift, north_shift)
+            return lines_of(at, *shifts[part, lane])
 
         for field in range(fields):
             for x in range(cx):
@@ -190,8 +215,8 @@
             up, down = index_y * cy, (1 - index_y) * cy
             keep = own_half[:rows]
             even = jnp.where(keep, pltpu.roll(mine, up, 1), pltpu.roll(theirs, down, 1))
-            mine = pltpu.roll(mine, (LANES - down) % LANES, 1)
-            theirs = pltpu.roll(theirs, (LANES - up) % LANES, 1)
+            mine = pltpu.roll(mine, lane_shift(-down), 1)
+            theirs = pltpu.roll(theirs, lane_shift(-up), 1)
             return even, jnp.where(keep, mine, theirs)
 
         put_block(from_owner(0)[1], own_lines)
@@ -277,21 +302,31 @@
         speeds = jnp.where(level_of == index, table_ref[index], speeds)
     speed_ref[...] = speeds
 
+    lane_8 = lanes_of(8)
+    place_8 = lane_8 % WINDOW
+    gap = WINDOW - cells + 3
+    wide = gap + 3 * levels
+    row_tiles = range(0, cells, 8)
+    rim_8 = ((place_8 >= MARGIN - 3) & (place_8 < MARGIN)) | (
+        (place_8 >= MARGIN + cells) & (place_8 < MARGIN + cells + 3)
+    )
+
     def collect():
-        position = lanes_of(cells) % WINDOW
-        gap = WINDOW - cells + 3
-        wide = gap + 3 * levels
         for pair in range(pairs):
-            merged = jnp.zeros((cells, LANES), jnp.float32)
+            merged = [jnp.zeros((8, LANES), jnp.float32)] * len(row_tiles)
             for slot, field in ((0, 0), (1, 2)):
                 for level in range(levels):
-                    lines = z_ref[field, pl.ds(row_of(0) + pair * levels + level, cells, group)]
                     offset = slot * wide + 3 * level
-                    here = position - offset
+                    here = place_8 - offset
                     wanted = ((here >= 0) & (here < 3)) | ((here >= gap) & (here < gap + 3))
                     shift = (offset - (MARGIN + cells - 3)) % LANES
-                    merged = jnp.where(wanted, pltpu.roll(lines, shift, 1), merged)
-            flip_ref[pair, :, :cells] = merged.T
+                    lines = z_ref[field, pl.ds(row_of(0) + pair * levels + level, cells, group)]
+                    lines = pltpu.roll(lines, shift, 1)
+                    merged = [
+                        jnp.where(wanted, lines[row : row + 8], old)
+                        for row, old in zip(row_tiles, merged)
+                    ]
+            flip_ref[pair, :, :cells] = jnp.concatenate(merged, axis=0).T
             for slot in range(2):
                 for side in (2, 3):
                     for odd in range(2):
@@ -313,89 +348,94 @@
                         lines = z_ref[slot, row : row + levels]
                         at = slot * slots + depth * levels
                         for odd in range(2):
-                            store_ref[(2 * pair + odd) * 4 + side, at : at + levels] = pltpu.roll(
-                                lines, LANES - MARGIN - odd * WINDOW, 1
-                            )
-
-    def fetch(face, side, position):
+                            store_ref[(2 * pair + odd) * 4 + side, at : at + levels] = lines
+
+    def fetch(face, side, positions):
         at = levels + (face * 4 + side) * 3
         neighbour = table_ref[at].astype(jnp.int32)
         far_side = table_ref[at + 1].astype(jnp.int32)
         flipped = table_ref[at + 2].astype(jnp.int32)
-        block = store_ref[neighbour * 4 + far_side]
-        order = jnp.where(flipped == 1, cells - 1 - position, position)
-        order = jnp.where((position >= 0) & (position < cells), order, 0)
-        block = jnp.take_along_axis(block, order, axis=1)
-        sign_here = 2 * (side % 2) - 1
-        sign_there = 2 * (far_side % 2) - 1
-        sign = (-sign_here * sign_there).astype(jnp.float32)
-        normal = lax.broadcasted_iota(jnp.int32, block.shape, 0) >= slots
-        return jnp.where(normal, sign * block, block)
+        first = jnp.where(far_side < 2, MARGIN + WINDOW * (neighbour & 1), 0)
+        start = first + jnp.where(flipped == 1, cells - 1, 0)
+        step = 1 - 2 * flipped
+        sign = ((1 - 2 * (side % 2)) * (2 * (far_side & 1) - 1)).astype(jnp.float32)
+        index = neighbour * 4 + far_side
+        parts = []
+        for slot, position in enumerate(positions):
+            order = (start + step * position) & (LANES - 1)
+            for half_at in (0, 8):
+                at = slot * slots + half_at
+                lines = jnp.take_along_axis(store_ref[index, at : at + 8], order, axis=1)
+                parts.append(lines if slot == 0 else sign * lines)
+        return parts[:2], parts[2:]
+
+    def depth_rows(parts, depth):
+        at = (depth % 2) * levels
+        return parts[depth // 2][at : at + levels]
 
     def rim_rows(side):
-        lane = lanes_of(2 * slots)
+        left = lane_8 < WINDOW
         for pair in range(pairs):
-            first = fetch(2 * pair, side, lane - MARGIN)
-            second = fetch(2 * pair + 1, side, lane - (MARGIN + WINDOW))
-            both = jnp.where(lane < WINDOW, first, second)
+            first = fetch(2 * pair, side, [lane_8 - MARGIN] * 2)
+            second = fetch(2 * pair + 1, side, [lane_8 - (MARGIN + WINDOW)] * 2)
             for slot in range(2):
+                both = [jnp.where(left, a, b) for a, b in zip(first[slot], second[slot])]
                 for depth in range(3):
                     x = -1 - depth if side == 0 else cells + depth
-                    at = slot * slots + depth * levels
                     row = row_of(x) + pair * levels
-                    z_ref[slot, row : row + levels] = both[at : at + levels]
-
-    wide = WINDOW - cells - 3 + 3 * levels
-
-    def tile_rows(odd, side, depth, base=0):
-        if side == 3:
-            return pl.ds(base + odd * WINDOW + depth, levels, 3)
-        return pl.ds(base + ((odd + 1) % 2) * WINDOW + wide - 3 * levels + 2 - depth, levels, 3)
-
-    def put_columns(lines, field, start, pair, base=0):
-        count = lines.shape[0]
-        position = lanes_of(count) % WINDOW
-        rim = ((position >= MARGIN - 3) & (position < MARGIN)) | (
-            (position >= MARGIN + cells) & (position < MARGIN + cells + 3)
-        )
-        for level in range(levels):
-            rolled = pltpu.roll(lines, (MARGIN + cells - base - 3 * level) % LANES, 1)
-            at = pl.ds(row_of(start) + pair * levels + level, count, group)
-            z_ref[field, at] = jnp.where(rim, rolled, z_ref[field, at])
+                    z_ref[slot, row : row + levels] = depth_rows(both, depth)
+
+    tile_wide = WINDOW - cells - 3 + 3 * levels
+
+    def put_tile(tile, parts, odd, side, base=0):
+        for depth in range(3):
+            if side == 3:
+                at = base + odd * WINDOW + depth
+            else:
+                at = base + ((odd + 1) % 2) * WINDOW + tile_wide - 3 * levels + 2 - depth
+            tile_ref[tile, pl.ds(at, levels, 3)] = depth_rows(parts, depth)
 
     def rim_columns_all():
         for pair in range(pairs):
             for odd in range(2):
                 for side in (2, 3):
-                    block = fetch(2 * pair + odd, side, lanes_of(2 * slots))
-                    for slot in range(2):
-                        for depth in range(3):
-                            at = slot * slots + depth * levels
-                            rows = tile_rows(odd, side, depth, slot * wide)
-                            tile_ref[pair, rows] = block[at : at + levels]
+                    for slot, parts in enumerate(fetch(2 * pair + odd, side, [lane_8] * 2)):
+                        put_tile(pair, parts, odd, side, slot * tile_wide)
             turned = tile_ref[pair].T[:cells]
             for slot, field in ((0, 0), (1, 2)):
-                put_columns(turned, field, 0, pair, slot * wide)
+                for level in range(levels):
+                    shift = (MARGIN + cells - slot * tile_wide - 3 * level) % LANES
+                    rolled = pltpu.roll(turned, shift, 1)
+                    at = pl.ds(row_of(0) + pair * levels + level, cells, group)
+                    lines = z_ref[field, at]
+                    lines = [
+                        jnp.where(rim_8, rolled[row : row + 8], lines[row : row + 8])
+                        for row in row_tiles
+                    ]
+                    z_ref[field, at] = jnp.concatenate(lines, axis=0)
 
     def rim_columns_own():
-        lane = lanes_of(2 * slots)
-        second = lax.broadcasted_iota(jnp.int32, lane.shape, 0) >= slots
         for odd in range(2):
             for side in (2, 3):
-                total = jnp.zeros((slots, LANES), jnp.float32)
+                total = [jnp.zeros((8, LANES), jnp.float32)] * 2
                 for pair in range(pairs):
-                    local = lane - jnp.where(second, 8 * (pairs + pair), 8 * pair)
-                    block = fetch(2 * pair + odd, side, index_x * cx + local)
-                    block = jnp.where((local >= 0) & (local < 8), block, 0.0)
-                    total = total + block[:slots] + block[slots:]
-                for depth in range(3):
-                    at = depth * levels
-                    tile_ref[0, tile_rows(odd, side, depth)] = total[at : at + levels]
+                    places = [8 * pair, 8 * (pairs + pair)]
+                    positions = [lane_8 + (index_x * cx - place) for place in places]
+                    fetched = fetch(2 * pair + odd, side, positions)
+                    for place, parts in zip(places, fetched):
+                        here = (lane_8 >= place) & (lane_8 < place + 8)
+                        total = [jnp.where(here, a, b) for a, b in zip(parts, total)]
+                put_tile(0, total, odd, side)
         turned = tile_ref[0].T
         for slot, field in ((0, 0), (1, 2)):
             for pair in range(pairs):
-                at = 8 * (slot * pairs + pair)
-                put_columns(turned[at : at + cx], field, index_x * cx, pair)
+                row = 8 * (slot * pairs + pair)
+                for level in range(levels):
+                    shift = (MARGIN + cells - 3 * level) % LANES
+                    rolled = pltpu.roll(turned[row : row + 8], shift, 1)[:cx]
+                    start = row_of(0) + index_x * chunk + pair * levels + level
+                    at = pl.ds(start, cx, group)
+                    z_ref[field, at] = jnp.where(rim_8[:cx], rolled, z_ref[field, at])
 
     def predict(at, rows):
         speed = speed_ref[:rows]
@@ -469,22 +509,26 @@
     full_rows = fields * (cx // 2) * group + (cx // 2) * pairs
     full_rows = -(-full_rows // 8) * 8
     small_rows = unit_place(fields, 1, cx, group, 2 * cx)[0] + group
+    in_vmem = pl.BlockSpec(memory_space=pltpu.VMEM)
+    params = pltpu.CompilerParams(vmem_limit_bytes=SMALL_VMEM_LIMIT)
+    swap_shape = jax.ShapeDtypeStruct((full_rows + 2 * small_rows, LANES), jnp.float32)
+    swap = pl.pallas_call(
+        functools.partial(pack_kernel, cx, cy, count_x, full_rows, small_rows),
+        out_shape=swap_shape,
+        in_specs=[in_vmem],
+        out_specs=in_vmem,
+        compiler_params=params,
+        name="pack",
+    )(jnp.swapaxes(state, 2, 3))
     swap, lines = pl.pallas_call(
-        functools.partial(pack_kernel, cx, cy, count_x, full_rows, small_rows),
-        out_shape=[
-            jax.ShapeDtypeStruct((full_rows + 2 * small_rows, LANES), jnp.float32),
-            jax.ShapeDtypeStruct((32, LANES), jnp.float32),
-        ],
-        in_specs=[pl.BlockSpec(memory_space=pltpu.HBM)] * 2,
-        out_specs=[pl.BlockSpec(memory_space=pltpu.VMEM)] * 2,
-        scratch_shapes=[
-            pltpu.VMEM((faces, fields, cx, levels, cy), jnp.float32),
-            pltpu.VMEM((faces, cx, cy), jnp.float32),
-            pltpu.SemaphoreType.DMA((2,)),
-        ],
-        compiler_params=pltpu.CompilerParams(vmem_limit_bytes=VMEM_LIMIT),
-        name="pack",
-    )(jnp.swapaxes(state, 2, 3), coriolis)
+        functools.partial(pack_coriolis_kernel, cx, cy, count_x, full_rows, small_rows),
+        out_shape=[swap_shape, jax.ShapeDtypeStruct((32, LANES), jnp.float32)],
+        in_specs=[in_vmem] * 2,
+        out_specs=[in_vmem] * 2,
+        input_output_aliases={1: 0},
+        compiler_params=params,
+        name="pack_coriolis",
+    )(coriolis, swap)
     keep, middle = pl.pallas_call(
         functools.partial(keep_kernel, cx, cy, count_x, small_rows),
         out_shape=[
@@ -531,8 +575,6 @@
         jax.ShapeDtypeStruct((fields, (cells + 8) * group, LANES), jnp.float32),
         jax.ShapeDtypeStruct((cells * group, LANES), jnp.float32),
     ]
-    in_vmem = pl.BlockSpec(memory_space=pltpu.VMEM)
-    params = pltpu.CompilerParams(vmem_limit_bytes=SMALL_VMEM_LIMIT)
     rows = pl.pallas_call(
         functools.partial(own_kernel, sizes),
         out_shape=state_rows,

time: 24.7 us -> 24.1 us (0.976)
  local copies, waits for them, and re-layouts: 1.9 us -> 1.57 us
  Pallas kernels: 6.49 us -> 6.22 us
    pallas_call x1, Pallas kernels: 0.69 us -> 0.32 us  [fast_on_device(): pl.pallas_call(functools.partial(pack_kernel, cx, cy, count_x, full_rows,...]
    unnamed x8, local copies, waits for them, and re-layouts: 1.68 us -> 1.36 us
where the time goes in v14:
time: 24.1 us; the launch traced here: 23.9 us
  starting transfers between devices  7.97 us (33%)
  waiting for transfers between devices  7.95 us (33%)
  Pallas kernels  6.22 us (26%)
  local copies, waits for them, and re-layouts  1.57 us (7%)
    ppermute x4, starting transfers between devices, moved(): return lax.ppermute(block, ('tx', 'ty'), pairs_of)  7.42 us
    ppermute x4, waiting for transfers between devices, moved(): return lax.ppermute(block, ('tx', 'ty'), pairs_of)  6.13 us
    pallas_call x1, Pallas kernels, fast_on_device(): pl.pallas_call(functools.partial(step_kernel, sizes), out_shape=[jax.Shap...  5.09 us
    ppermute x2, waiting for transfers between devices, across(): return lax.ppermute(block, 'ty', [(0, 1), (1, 0)])  1.82 us
    unnamed x8, local copies, waits for them, and re-layouts  1.36 us
    ppermute x2, starting transfers between devices, across(): return lax.ppermute(block, 'ty', [(0, 1), (1, 0)])  0.54 us
  transfers between devices with their start and end apart: 6, of which 4 were waited for; matrix products, arithmetic and copies ran while one was open for 1% of the time, Pallas kernels for 3%

profile of v14, /device:TPU:0, one launch (start us, length us, event | category | flops | bytes accessed | tf_op | source)
XLA Modules:
  0.0 23.9 jit_solution(11927187674173776930)
XLA Ops:
  0.0 0.0 copy-start
  0.0 0.9 %copy-done = f32[6,3,4,6,24]{4,2,3,1,0:T(4,128)S(1)} copy-done((f32[6,3,4,6,24]{4,2,3,1,0:T(4,128)S(1)}, f32[6,3,4,6,24]{4,2,3,1,0:T(4,128)}, u32[]{:S(2)}) %copy-start) | copy-done | bytes 41496
  0.9 0.0 copy-start.1
  0.9 0.3 %pack.1.swap_in = f32[216,128]{1,0:T(8,128)S(1)} custom-call(f32[6,3,6,4,24]{4,3,2,1,0:T(4,128)S(1)} %bitcast.2), custom_call_target="tpu_custom_call" | custom-call | tf_op jit(solution)/shard_map/pack/pallas_call | solution.py:515
  1.3 0.4 %copy-done.1 = f32[6,6,24]{2,1,0:T(8,128)S(1)} copy-done((f32[6,6,24]{2,1,0:T(8,128)S(1)}, f32[6,6,24]{2,1,0:T(8,128)}, u32[]{:S(2)}) %copy-start.1) | copy-done | bytes 3480
  1.7 0.2 pack_coriolis.1
  1.9 0.5 %collective-permute-start = (f32[216,128]{1,0:T(8,128)S(1)}, f32[216,128]{1,0:T(8,128)S(1)}, u32[]{:S(2)}, u32[]{:S(2)}) collective-permute-start(f32[216,128]{1,0:T(8,128)S(1)} %get-tuple-element.19.swap_ref.own_ref), channel_id=1, source_target_pairs={{0,1},{1,0},{2,3},{3,2},{4,5},{5,4},{6,7},{7,6},{8,9},{9,8},{10,11... | collective-permute-start | bytes 331784 | tf_op jit(solution)/shard_map/ppermute | solution.py:553
  2.3 0.2 keep.1
  2.5 0.8 %collective-permute-done.other_ref = f32[216,128]{1,0:T(8,128)S(1)} collective-permute-done((f32[216,128]{1,0:T(8,128)S(1)}, f32[216,128]{1,0:T(8,128)S(1)}, u32[]{:S(2)}, u32[]{:S(2)}) %collective-permute-start) | collective-permute-done | bytes 110624 | tf_op jit(solution)/shard_map/ppermute | solution.py:553
  3.3 0.0 copy-start.2
  3.3 2.9 %collective-permute-start.1 = (f32[240,128]{1,0:T(8,128)S(1)}, f32[240,128]{1,0:T(8,128)S(1)}, u32[]{:S(2)}, u32[]{:S(2)}) collective-permute-start(f32[240,128]{1,0:T(8,128)S(1)} %get-tuple-element.22), channel_id=1, source_target_pairs={{0,2},{1,15},{2,4},{3,1},{4,6},{5,3},{6,8},{7,5},{8,10},{9,7},{10,... | collective-permute-start | bytes 368648 | tf_op jit(solution)/shard_map/ppermute | solution.py:550
  6.2 2.6 %collective-permute-start.4 = (f32[48,128]{1,0:T(8,128)S(1)}, f32[48,128]{1,0:T(8,128)S(1)}, u32[]{:S(2)}, u32[]{:S(2)}) collective-permute-start(f32[48,128]{1,0:T(8,128)S(1)} %get-tuple-element.25), channel_id=1, source_target_pairs={{0,8},{1,9},{2,10},{3,11},{4,12},{5,13},{6,14},{7,15},{8,0},{9,1},... | collective-permute-start | bytes 73736 | tf_op jit(solution)/shard_map/ppermute | solution.py:550
  8.8 0.0 copy-done.2
  8.8 0.1 copy.11
  8.9 0.1 convert_element_type.7
  9.0 0.0 copy-start.3
  9.1 1.6 %collective-permute-start.2 = (f32[96,128]{1,0:T(8,128)S(1)}, f32[96,128]{1,0:T(8,128)S(1)}, u32[]{:S(2)}, u32[]{:S(2)}) collective-permute-start(f32[96,128]{1,0:T(8,128)S(1)} %get-tuple-element.23), channel_id=1, source_target_pairs={{0,4},{1,13},{2,6},{3,15},{4,8},{5,1},{6,10},{7,3},{8,12},{9,5},{1... | collective-permute-start | bytes 147464 | tf_op jit(solution)/shard_map/ppermute | solution.py:550
  10.7 0.3 %collective-permute-start.3 = (f32[96,128]{1,0:T(8,128)S(1)}, f32[96,128]{1,0:T(8,128)S(1)}, u32[]{:S(2)}, u32[]{:S(2)}) collective-permute-start(f32[96,128]{1,0:T(8,128)S(1)} %get-tuple-element.24), channel_id=1, source_target_pairs={{0,6},{1,11},{2,8},{3,13},{4,10},{5,15},{6,12},{7,1},{8,14},{9,3},... | collective-permute-start | bytes 147464 | tf_op jit(solution)/shard_map/ppermute | solution.py:550
  11.0 0.0 copy-done.3
  11.0 0.1 pad_maximum_fusion.1.table_in
  11.0 0.0 collective-permute-done.4
  11.1 4.4 %collective-permute-done.2 = f32[96,128]{1,0:T(8,128)S(1)} collective-permute-done((f32[96,128]{1,0:T(8,128)S(1)}, f32[96,128]{1,0:T(8,128)S(1)}, u32[]{:S(2)}, u32[]{:S(2)}) %collective-permute-start.2) | collective-permute-done | bytes 49184 | tf_op jit(solution)/shard_map/ppermute | solution.py:550
  15.4 1.7 %collective-permute-done.3 = f32[96,128]{1,0:T(8,128)S(1)} collective-permute-done((f32[96,128]{1,0:T(8,128)S(1)}, f32[96,128]{1,0:T(8,128)S(1)}, u32[]{:S(2)}, u32[]{:S(2)}) %collective-permute-start.3) | collective-permute-done | bytes 49184 | tf_op jit(solution)/shard_map/ppermute | solution.py:550
  17.2 0.0 collective-permute-done.1
  17.2 0.1 collective-permute-start.5
  17.3 0.2 place_own.1
  17.4 0.3 %place_got.1 = (f32[3,672,128]{2,1,0:T(8,128)S(1)}, f32[576,128]{1,0:T(8,128)S(1)}) custom-call(f32[480,128]{1,0:T(8,128)S(1)} %pad_maximum_fusion.got_ref, f32[3,672,128]{2,1,0:T(8,128)S(1)} %get-tuple-element.28.z_in, f32[576,128]{1,0:T(8,128)S(1)} %get-tuple-element.29.cor_in), custom_call_target="tpu_custom_call", output_to_operand_aliasing={{0}: (1, {}), {1}: (2, {})} | custom-call | tf_op jit(solution)/shard_map/place_got/pallas_call | solution.py:586
  17.7 1.1 %collective-permute-done.5.got_other_ref = f32[480,128]{1,0:T(8,128)S(1)} collective-permute-done((f32[480,128]{1,0:T(8,128)S(1)}, f32[480,128]{1,0:T(8,128)S(1)}, u32[]{:S(2)}, u32[]{:S(2)}) %collective-permute-start.5) | collective-permute-done | bytes 245792 | tf_op jit(solution)/shard_map/ppermute | solution.py:553
  18.8 5.1 %substeps.1 = (f32[6,3,6,4,24]{4,3,2,1,0:T(4,128)}, f32[3,672,128]{2,1,0:T(8,128)S(1)}, f32[576,128]{1,0:T(8,128)S(1)}) custom-call(f32[480,128]{1,0:T(8,128)S(1)} %pad_maximum_fusion.got_ref, f32[480,128]{1,0:T(8,128)S(1)} %collective-permute-done.5.got_other_ref, f32[76]{0:T(128)S(1)} %pad_maximum_fusion.1.table_in, ...), custom_call_target="tpu_custom_call", output_to_operand_aliasing={{1}: (3, {}), {2}: (4, {})} | custom-call | tf_op jit(solution)/shard_map/substeps/pallas_call | solution.py:595
  (3 shorter events, 0.0 us)
Async XLA Ops:
  0.0 0.9 %copy-start = (f32[6,3,4,6,24]{4,2,3,1,0:T(4,128)S(1)}, f32[6,3,4,6,24]{4,2,3,1,0:T(4,128)}, u32[]{:S(2)}) copy-start(f32[6,3,4,6,24]{4,2,3,1,0:T(4,128)} %param.4) | copy-start | bytes 124420
  0.9 0.7 %copy-start.1 = (f32[6,6,24]{2,1,0:T(8,128)S(1)}, f32[6,6,24]{2,1,0:T(8,128)}, u32[]{:S(2)}) copy-start(f32[6,6,24]{2,1,0:T(8,128)} %coriolis_ref.1) | copy-start | bytes 10372
  1.9 1.4 %collective-permute-start = (f32[216,128]{1,0:T(8,128)S(1)}, f32[216,128]{1,0:T(8,128)S(1)}, u32[]{:S(2)}, u32[]{:S(2)}) collective-permute-start(f32[216,128]{1,0:T(8,128)S(1)} %get-tuple-element.19.swap_ref.own_ref), channel_id=1, source_target_pairs={{0,1},{1,0},{2,3},{3,2},{4,5},{5,4},{6,7},{7,6},{8,9},{9,8},{10,11... | collective-permute-start | bytes 331784 | tf_op jit(solution)/shard_map/ppermute | solution.py:553
  3.3 5.5 %copy-start.2 = (s32[6,4,3]{0,1,2:T(4,128)S(1)}, s32[6,4,3]{0,1,2:T(4,128)}, u32[]{:S(2)}) copy-start(s32[6,4,3]{0,1,2:T(4,128)} %param.7) | copy-start | bytes 868
  3.3 13.9 %collective-permute-start.1 = (f32[240,128]{1,0:T(8,128)S(1)}, f32[240,128]{1,0:T(8,128)S(1)}, u32[]{:S(2)}, u32[]{:S(2)}) collective-permute-start(f32[240,128]{1,0:T(8,128)S(1)} %get-tuple-element.22), channel_id=1, source_target_pairs={{0,2},{1,15},{2,4},{3,1},{4,6},{5,3},{6,8},{7,5},{8,10},{9,7},{10,... | collective-permute-start | bytes 368648 | tf_op jit(solution)/shard_map/ppermute | solution.py:550
  6.2 4.8 %collective-permute-start.4 = (f32[48,128]{1,0:T(8,128)S(1)}, f32[48,128]{1,0:T(8,128)S(1)}, u32[]{:S(2)}, u32[]{:S(2)}) collective-permute-start(f32[48,128]{1,0:T(8,128)S(1)} %get-tuple-element.25), channel_id=1, source_target_pairs={{0,8},{1,9},{2,10},{3,11},{4,12},{5,13},{6,14},{7,15},{8,0},{9,1},... | collective-permute-start | bytes 73736 | tf_op jit(solution)/shard_map/ppermute | solution.py:550
  9.0 1.9 %copy-start.3 = (f32[4]{0:T(128)S(1)}, f32[4]{0:T(128)}, u32[]{:S(2)}) copy-start(f32[4]{0:T(128)} %param.6) | copy-start | bytes 52
  9.1 6.4 %collective-permute-start.2 = (f32[96,128]{1,0:T(8,128)S(1)}, f32[96,128]{1,0:T(8,128)S(1)}, u32[]{:S(2)}, u32[]{:S(2)}) collective-permute-start(f32[96,128]{1,0:T(8,128)S(1)} %get-tuple-element.23), channel_id=1, source_target_pairs={{0,4},{1,13},{2,6},{3,15},{4,8},{5,1},{6,10},{7,3},{8,12},{9,5},{1... | collective-permute-start | bytes 147464 | tf_op jit(solution)/shard_map/ppermute | solution.py:550
  10.7 6.5 %collective-permute-start.3 = (f32[96,128]{1,0:T(8,128)S(1)}, f32[96,128]{1,0:T(8,128)S(1)}, u32[]{:S(2)}, u32[]{:S(2)}) collective-permute-start(f32[96,128]{1,0:T(8,128)S(1)} %get-tuple-element.24), channel_id=1, source_target_pairs={{0,6},{1,11},{2,8},{3,13},{4,10},{5,15},{6,12},{7,1},{8,14},{9,3},... | collective-permute-start | bytes 147464 | tf_op jit(solution)/shard_map/ppermute | solution.py:550
  17.2 1.6 %collective-permute-start.5 = (f32[480,128]{1,0:T(8,128)S(1)}, f32[480,128]{1,0:T(8,128)S(1)}, u32[]{:S(2)}, u32[]{:S(2)}) collective-permute-start(f32[480,128]{1,0:T(8,128)S(1)} %pad_maximum_fusion.got_ref), channel_id=1, source_target_pairs={{0,1},{1,0},{2,3},{3,2},{4,5},{5,4},{6,7},{7,6},{8,9},{9,8},{10,11... | collective-permute-start | bytes 737288 | tf_op jit(solution)/shard_map/ppermute | solution.py:553

commit v15 on v14

--- a/solution.py
+++ b/solution.py
@@ -460,44 +460,55 @@
         turning = cor_ref[pl.ds(at - row_of(0), rows)]
         return height, east_pred + turning * north_pred, north_pred - turning * east_pred
 
-    collect()
-    rim_rows(0)
-    rim_rows(1)
-    rim_columns_all()
-    for first in range(-2, cells + 2, 4):
-        predict(row_of(first), 4 * group)
-    for index in range(count_x):
-        at = row_of(0) + index * chunk
+    def all_faces():
+        rim_rows(0)
+        rim_rows(1)
+        rim_columns_all()
+        for first in range(-2, cells + 2, 4):
+            predict(row_of(first), 4 * group)
+        def update_part(index, carry):
+            at = pl.multiple_of(row_of(0) + index * (2 * chunk), 8)
+            for field, values in enumerate(update(at, 2 * chunk)):
+                z_ref[field, pl.ds(at, 2 * chunk)] = values
+            return carry
+
+        lax.fori_loop(0, count_x // 2, update_part, 0)
+
+    def own_rows():
+
+        @pl.when(index_x == 0)
+        def _():
+            rim_rows(0)
+
+        @pl.when(index_x == count_x - 1)
+        def _():
+            rim_rows(1)
+
+        rim_columns_own()
+        at = pl.multiple_of(row_of(0) + index_x * chunk, 8)
+        predict(at - 2 * group, chunk + 4 * group)
+        copies = []
         for field, values in enumerate(update(at, chunk)):
-            z_ref[field, at : at + chunk] = values
-
-    collect()
-
-    @pl.when(index_x == 0)
-    def _():
-        rim_rows(0)
-
-    @pl.when(index_x == count_x - 1)
-    def _():
-        rim_rows(1)
-
-    rim_columns_own()
-    at = pl.multiple_of(row_of(0) + index_x * chunk, 8)
-    predict(at - 2 * group, chunk + 4 * group)
-    copies = []
-    for field, values in enumerate(update(at, chunk)):
-        for odd in range(2):
-            shift = LANES - (MARGIN + odd * WINDOW) - index_y * cy
-            rolled = pltpu.roll(values, shift, 1)
-            for x in range(cx):
-                for pair in range(pairs):
-                    row = x * group + pair * levels
-                    out_ref[field, 2 * pair + odd, x] = rolled[row : row + levels, :cy]
-        copy = pltpu.make_async_copy(out_ref.at[field], out_hbm.at[:, field], sems.at[1 + field])
-        copy.start()
-        copies.append(copy)
-    for copy in copies:
-        copy.wait()
+            for odd in range(2):
+                shift = LANES - (MARGIN + odd * WINDOW) - index_y * cy
+                rolled = pltpu.roll(values, shift, 1)
+                for x in range(cx):
+                    for pair in range(pairs):
+                        row = x * group + pair * levels
+                        out_ref[field, 2 * pair + odd, x] = rolled[row : row + levels, :cy]
+            copy = pltpu.make_async_copy(out_ref.at[field], out_hbm.at[:, field], sems.at[1 + field])
+            copy.start()
+            copies.append(copy)
+        for copy in copies:
+            copy.wait()
+
+    def substep(index, carry):
+        collect()
+        pl.when(index == 0)(all_faces)
+        pl.when(index == SUBSTEPS - 1)(own_rows)
+        return carry
+
+    lax.fori_loop(0, SUBSTEPS, substep, 0)
 
 
 def fast_on_device(state, coriolis, wave_speed, edges):
@@ -604,7 +615,7 @@
             pltpu.VMEM((faces * 4, 32, LANES), jnp.float32),
             pltpu.VMEM((pairs, LANES, LANES), jnp.float32),
             pltpu.VMEM((pairs, LANES, LANES), jnp.float32),
-            pltpu.VMEM(((cx + 4) * group, LANES), jnp.float32),
+            pltpu.VMEM((2 * cx * group, LANES), jnp.float32),
             pltpu.SMEM(table.shape, jnp.float32),
             pltpu.VMEM((fields, faces, cx, levels, cy), jnp.float32),
             pltpu.SemaphoreType.DMA((1 + fields,)),

time: 24.1 us -> 24.1 us (level)
  no operation moved by 1% of the time
where the time goes in v15:
time: 24.1 us; the launch traced here: 23.9 us
  starting transfers between devices  7.97 us (33%)
  waiting for transfers between devices  7.95 us (33%)
  Pallas kernels  6.21 us (26%)
  local copies, waits for them, and re-layouts  1.57 us (7%)
    ppermute x4, starting transfers between devices, moved(): return lax.ppermute(block, ('tx', 'ty'), pairs_of)  7.42 us
    ppermute x4, waiting for transfers between devices, moved(): return lax.ppermute(block, ('tx', 'ty'), pairs_of)  6.13 us
    pallas_call x1, Pallas kernels, fast_on_device(): pl.pallas_call(functools.partial(step_kernel, sizes), out_shape=[jax.Shap...  5.07 us
    ppermute x2, waiting for transfers between devices, across(): return lax.ppermute(block, 'ty', [(0, 1), (1, 0)])  1.82 us
    unnamed x8, local copies, waits for them, and re-layouts  1.36 us
    ppermute x2, starting transfers between devices, across(): return lax.ppermute(block, 'ty', [(0, 1), (1, 0)])  0.54 us
  transfers between devices with their start and end apart: 6, of which 4 were waited for; matrix products, arithmetic and copies ran while one was open for 1% of the time, Pallas kernels for 3%

profile of v15, /device:TPU:0, one launch (start us, length us, event | category | flops | bytes accessed | tf_op | source)
XLA Modules:
  0.0 23.9 jit_solution(12083720368021825111)
XLA Ops:
  0.0 0.0 copy-start
  0.0 0.9 %copy-done = f32[6,3,4,6,24]{4,2,3,1,0:T(4,128)S(1)} copy-done((f32[6,3,4,6,24]{4,2,3,1,0:T(4,128)S(1)}, f32[6,3,4,6,24]{4,2,3,1,0:T(4,128)}, u32[]{:S(2)}) %copy-start) | copy-done | bytes 41496
  0.9 0.0 copy-start.1
  0.9 0.3 %pack.1.swap_in = f32[216,128]{1,0:T(8,128)S(1)} custom-call(f32[6,3,6,4,24]{4,3,2,1,0:T(4,128)S(1)} %bitcast.2), custom_call_target="tpu_custom_call" | custom-call | tf_op jit(solution)/shard_map/pack/pallas_call | solution.py:526
  1.3 0.4 %copy-done.1 = f32[6,6,24]{2,1,0:T(8,128)S(1)} copy-done((f32[6,6,24]{2,1,0:T(8,128)S(1)}, f32[6,6,24]{2,1,0:T(8,128)}, u32[]{:S(2)}) %copy-start.1) | copy-done | bytes 3480
  1.7 0.2 pack_coriolis.1
  1.9 0.5 %collective-permute-start = (f32[216,128]{1,0:T(8,128)S(1)}, f32[216,128]{1,0:T(8,128)S(1)}, u32[]{:S(2)}, u32[]{:S(2)}) collective-permute-start(f32[216,128]{1,0:T(8,128)S(1)} %get-tuple-element.19.swap_ref.own_ref), channel_id=1, source_target_pairs={{0,1},{1,0},{2,3},{3,2},{4,5},{5,4},{6,7},{7,6},{8,9},{9,8},{10,11... | collective-permute-start | bytes 331784 | tf_op jit(solution)/shard_map/ppermute | solution.py:564
  2.3 0.2 keep.1
  2.5 0.8 %collective-permute-done.other_ref = f32[216,128]{1,0:T(8,128)S(1)} collective-permute-done((f32[216,128]{1,0:T(8,128)S(1)}, f32[216,128]{1,0:T(8,128)S(1)}, u32[]{:S(2)}, u32[]{:S(2)}) %collective-permute-start) | collective-permute-done | bytes 110624 | tf_op jit(solution)/shard_map/ppermute | solution.py:564
  3.3 0.0 copy-start.2
  3.3 2.9 %collective-permute-start.1 = (f32[240,128]{1,0:T(8,128)S(1)}, f32[240,128]{1,0:T(8,128)S(1)}, u32[]{:S(2)}, u32[]{:S(2)}) collective-permute-start(f32[240,128]{1,0:T(8,128)S(1)} %get-tuple-element.22), channel_id=1, source_target_pairs={{0,2},{1,15},{2,4},{3,1},{4,6},{5,3},{6,8},{7,5},{8,10},{9,7},{10,... | collective-permute-start | bytes 368648 | tf_op jit(solution)/shard_map/ppermute | solution.py:561
  6.2 2.6 %collective-permute-start.4 = (f32[48,128]{1,0:T(8,128)S(1)}, f32[48,128]{1,0:T(8,128)S(1)}, u32[]{:S(2)}, u32[]{:S(2)}) collective-permute-start(f32[48,128]{1,0:T(8,128)S(1)} %get-tuple-element.25), channel_id=1, source_target_pairs={{0,8},{1,9},{2,10},{3,11},{4,12},{5,13},{6,14},{7,15},{8,0},{9,1},... | collective-permute-start | bytes 73736 | tf_op jit(solution)/shard_map/ppermute | solution.py:561
  8.8 0.0 copy-done.2
  8.8 0.1 copy.11
  8.9 0.1 convert_element_type.7
  9.0 0.0 copy-start.3
  9.1 1.6 %collective-permute-start.2 = (f32[96,128]{1,0:T(8,128)S(1)}, f32[96,128]{1,0:T(8,128)S(1)}, u32[]{:S(2)}, u32[]{:S(2)}) collective-permute-start(f32[96,128]{1,0:T(8,128)S(1)} %get-tuple-element.23), channel_id=1, source_target_pairs={{0,4},{1,13},{2,6},{3,15},{4,8},{5,1},{6,10},{7,3},{8,12},{9,5},{1... | collective-permute-start | bytes 147464 | tf_op jit(solution)/shard_map/ppermute | solution.py:561
  10.7 0.3 %collective-permute-start.3 = (f32[96,128]{1,0:T(8,128)S(1)}, f32[96,128]{1,0:T(8,128)S(1)}, u32[]{:S(2)}, u32[]{:S(2)}) collective-permute-start(f32[96,128]{1,0:T(8,128)S(1)} %get-tuple-element.24), channel_id=1, source_target_pairs={{0,6},{1,11},{2,8},{3,13},{4,10},{5,15},{6,12},{7,1},{8,14},{9,3},... | collective-permute-start | bytes 147464 | tf_op jit(solution)/shard_map/ppermute | solution.py:561
  11.0 0.0 copy-done.3
  11.0 0.1 pad_maximum_fusion.1.table_in
  11.0 0.0 collective-permute-done.4
  11.1 4.4 %collective-permute-done.2 = f32[96,128]{1,0:T(8,128)S(1)} collective-permute-done((f32[96,128]{1,0:T(8,128)S(1)}, f32[96,128]{1,0:T(8,128)S(1)}, u32[]{:S(2)}, u32[]{:S(2)}) %collective-permute-start.2) | collective-permute-done | bytes 49184 | tf_op jit(solution)/shard_map/ppermute | solution.py:561
  15.4 1.7 %collective-permute-done.3 = f32[96,128]{1,0:T(8,128)S(1)} collective-permute-done((f32[96,128]{1,0:T(8,128)S(1)}, f32[96,128]{1,0:T(8,128)S(1)}, u32[]{:S(2)}, u32[]{:S(2)}) %collective-permute-start.3) | collective-permute-done | bytes 49184 | tf_op jit(solution)/shard_map/ppermute | solution.py:561
  17.2 0.0 collective-permute-done.1
  17.2 0.1 collective-permute-start.5
  17.3 0.2 place_own.1
  17.4 0.3 %place_got.1 = (f32[3,672,128]{2,1,0:T(8,128)S(1)}, f32[576,128]{1,0:T(8,128)S(1)}) custom-call(f32[480,128]{1,0:T(8,128)S(1)} %pad_maximum_fusion.got_ref, f32[3,672,128]{2,1,0:T(8,128)S(1)} %get-tuple-element.28.z_in, f32[576,128]{1,0:T(8,128)S(1)} %get-tuple-element.29.cor_in), custom_call_target="tpu_custom_call", output_to_operand_aliasing={{0}: (1, {}), {1}: (2, {})} | custom-call | tf_op jit(solution)/shard_map/place_got/pallas_call | solution.py:597
  17.7 1.1 %collective-permute-done.5.got_other_ref = f32[480,128]{1,0:T(8,128)S(1)} collective-permute-done((f32[480,128]{1,0:T(8,128)S(1)}, f32[480,128]{1,0:T(8,128)S(1)}, u32[]{:S(2)}, u32[]{:S(2)}) %collective-permute-start.5) | collective-permute-done | bytes 245792 | tf_op jit(solution)/shard_map/ppermute | solution.py:564
  18.8 5.1 %substeps.1 = (f32[6,3,6,4,24]{4,3,2,1,0:T(4,128)}, f32[3,672,128]{2,1,0:T(8,128)S(1)}, f32[576,128]{1,0:T(8,128)S(1)}) custom-call(f32[480,128]{1,0:T(8,128)S(1)} %pad_maximum_fusion.got_ref, f32[480,128]{1,0:T(8,128)S(1)} %collective-permute-done.5.got_other_ref, f32[76]{0:T(128)S(1)} %pad_maximum_fusion.1.table_in, ...), custom_call_target="tpu_custom_call", output_to_operand_aliasing={{1}: (3, {}), {2}: (4, {})} | custom-call | tf_op jit(solution)/shard_map/substeps/pallas_call | solution.py:606
  (3 shorter events, 0.0 us)
Async XLA Ops:
  0.0 0.9 %copy-start = (f32[6,3,4,6,24]{4,2,3,1,0:T(4,128)S(1)}, f32[6,3,4,6,24]{4,2,3,1,0:T(4,128)}, u32[]{:S(2)}) copy-start(f32[6,3,4,6,24]{4,2,3,1,0:T(4,128)} %param.4) | copy-start | bytes 124420
  0.9 0.7 %copy-start.1 = (f32[6,6,24]{2,1,0:T(8,128)S(1)}, f32[6,6,24]{2,1,0:T(8,128)}, u32[]{:S(2)}) copy-start(f32[6,6,24]{2,1,0:T(8,128)} %coriolis_ref.1) | copy-start | bytes 10372
  1.9 1.4 %collective-permute-start = (f32[216,128]{1,0:T(8,128)S(1)}, f32[216,128]{1,0:T(8,128)S(1)}, u32[]{:S(2)}, u32[]{:S(2)}) collective-permute-start(f32[216,128]{1,0:T(8,128)S(1)} %get-tuple-element.19.swap_ref.own_ref), channel_id=1, source_target_pairs={{0,1},{1,0},{2,3},{3,2},{4,5},{5,4},{6,7},{7,6},{8,9},{9,8},{10,11... | collective-permute-start | bytes 331784 | tf_op jit(solution)/shard_map/ppermute | solution.py:564
  3.3 5.5 %copy-start.2 = (s32[6,4,3]{0,1,2:T(4,128)S(1)}, s32[6,4,3]{0,1,2:T(4,128)}, u32[]{:S(2)}) copy-start(s32[6,4,3]{0,1,2:T(4,128)} %param.7) | copy-start | bytes 868
  3.3 13.9 %collective-permute-start.1 = (f32[240,128]{1,0:T(8,128)S(1)}, f32[240,128]{1,0:T(8,128)S(1)}, u32[]{:S(2)}, u32[]{:S(2)}) collective-permute-start(f32[240,128]{1,0:T(8,128)S(1)} %get-tuple-element.22), channel_id=1, source_target_pairs={{0,2},{1,15},{2,4},{3,1},{4,6},{5,3},{6,8},{7,5},{8,10},{9,7},{10,... | collective-permute-start | bytes 368648 | tf_op jit(solution)/shard_map/ppermute | solution.py:561
  6.2 4.8 %collective-permute-start.4 = (f32[48,128]{1,0:T(8,128)S(1)}, f32[48,128]{1,0:T(8,128)S(1)}, u32[]{:S(2)}, u32[]{:S(2)}) collective-permute-start(f32[48,128]{1,0:T(8,128)S(1)} %get-tuple-element.25), channel_id=1, source_target_pairs={{0,8},{1,9},{2,10},{3,11},{4,12},{5,13},{6,14},{7,15},{8,0},{9,1},... | collective-permute-start | bytes 73736 | tf_op jit(solution)/shard_map/ppermute | solution.py:561
  9.0 1.9 %copy-start.3 = (f32[4]{0:T(128)S(1)}, f32[4]{0:T(128)}, u32[]{:S(2)}) copy-start(f32[4]{0:T(128)} %param.6) | copy-start | bytes 52
  9.1 6.4 %collective-permute-start.2 = (f32[96,128]{1,0:T(8,128)S(1)}, f32[96,128]{1,0:T(8,128)S(1)}, u32[]{:S(2)}, u32[]{:S(2)}) collective-permute-start(f32[96,128]{1,0:T(8,128)S(1)} %get-tuple-element.23), channel_id=1, source_target_pairs={{0,4},{1,13},{2,6},{3,15},{4,8},{5,1},{6,10},{7,3},{8,12},{9,5},{1... | collective-permute-start | bytes 147464 | tf_op jit(solution)/shard_map/ppermute | solution.py:561
  10.7 6.5 %collective-permute-start.3 = (f32[96,128]{1,0:T(8,128)S(1)}, f32[96,128]{1,0:T(8,128)S(1)}, u32[]{:S(2)}, u32[]{:S(2)}) collective-permute-start(f32[96,128]{1,0:T(8,128)S(1)} %get-tuple-element.24), channel_id=1, source_target_pairs={{0,6},{1,11},{2,8},{3,13},{4,10},{5,15},{6,12},{7,1},{8,14},{9,3},... | collective-permute-start | bytes 147464 | tf_op jit(solution)/shard_map/ppermute | solution.py:561
  17.2 1.6 %collective-permute-start.5 = (f32[480,128]{1,0:T(8,128)S(1)}, f32[480,128]{1,0:T(8,128)S(1)}, u32[]{:S(2)}, u32[]{:S(2)}) collective-permute-start(f32[480,128]{1,0:T(8,128)S(1)} %pad_maximum_fusion.got_ref), channel_id=1, source_target_pairs={{0,1},{1,0},{2,3},{3,2},{4,5},{5,4},{6,7},{7,6},{8,9},{9,8},{10,11... | collective-permute-start | bytes 737288 | tf_op jit(solution)/shard_map/ppermute | solution.py:564

commit v16 on v15

--- a/solution.py
+++ b/solution.py
@@ -135,7 +135,10 @@
         put_chunk(cx, cy, count_x, swap_ref, line_ref, keep_ref, top, sense * distance)
 
 
-def mix_kernel(full_rows, small_rows, swap_ref, other_ref, keep_ref, near_ref, second_ref, third_ref):
+def mix_kernel(
+    full_rows, small_rows, swap_ref, other_ref, keep_ref, middle_ref,
+    near_ref, third_ref, second_ref, fourth_ref,
+):
     near_ref[:full_rows] = swap_ref[:full_rows]
     near_ref[full_rows:] = other_ref[:full_rows]
     for place, far_ref in enumerate((second_ref, third_ref)):
@@ -143,6 +146,7 @@
         far_ref[:small_rows] = keep_ref[at : at + small_rows]
         at += full_rows
         far_ref[small_rows:] = other_ref[at : at + small_rows]
+    fourth_ref[...] = middle_ref[...]
 
 
 def placer(cx, cy, count_x, full_rows, small_rows, z_ref, cor_ref):
@@ -233,7 +237,7 @@
             return even, jnp.where(low, pltpu.roll(south, LANES - cy, 1), north)
 
         put_block(from_owner(toward)[1], near_lines)
-        for place, distance in enumerate((2, 3)):
+        for place, distance in enumerate((3, 2)):
             top = 2 * full_rows + 2 * place * small_rows
             south_at = pl.multiple_of(top + south_first * small_rows, 8)
             north_at = pl.multiple_of(top + (1 - south_first) * small_rows, 8)
@@ -567,16 +571,16 @@
     messages = pl.pallas_call(
         functools.partial(mix_kernel, full_rows, small_rows),
         out_shape=[
-            jax.ShapeDtypeStruct((2 * rows, LANES), jnp.float32)
-            for rows in (full_rows, small_rows, small_rows)
+            jax.ShapeDtypeStruct((rows, LANES), jnp.float32)
+            for rows in (2 * full_rows, 2 * small_rows, 2 * small_rows, small_rows)
         ],
-        in_specs=[pl.BlockSpec(memory_space=pltpu.VMEM)] * 3,
-        out_specs=[pl.BlockSpec(memory_space=pltpu.VMEM)] * 3,
-        compiler_params=pltpu.CompilerParams(vmem_limit_bytes=SMALL_VMEM_LIMIT),
+        in_specs=[in_vmem] * 4,
+        out_specs=[in_vmem] * 4,
+        compiler_params=params,
         name="messages",
-    )(swap, other, keep)
-    got = [moved(block, place + 1) for place, block in enumerate(messages)]
-    got = jnp.concatenate([*got, moved(middle, count_x // 2)])
+    )(swap, other, keep, middle)
+    got = [moved(block, distance) for block, distance in zip(messages, (1, 3, 2, count_x // 2))]
+    got = jnp.concatenate(got)
     table = jnp.concatenate([wave_speed, edges.reshape(-1).astype(jnp.float32)])
     got, table = lax.optimization_barrier((got, table))
     passed = across(got)

time: 24.1 us -> 23.5 us (0.975)
  waiting for transfers between devices: 7.95 us -> 7.4 us
    ppermute x4, waiting for transfers between devices: 6.13 us -> 5.58 us  [moved(): return lax.ppermute(block, ('tx', 'ty'), pairs_of)]
  transfers between devices with their start and end apart: 6 -> 6, of which waited for: 4 -> 5; matrix products, arithmetic and copies ran while one was open for 1% -> 1% of each run, Pallas kernels for 3% -> 3%
where the time goes in v16:
time: 23.5 us; the launch traced here: 23.3 us
  starting transfers between devices  7.98 us (34%)
  waiting for transfers between devices  7.4 us (31%)
  Pallas kernels  6.21 us (26%)
  local copies, waits for them, and re-layouts  1.57 us (7%)
    ppermute x4, starting transfers between devices, moved(): return lax.ppermute(block, ('tx', 'ty'), pairs_of)  7.44 us
    ppermute x4, waiting for transfers between devices, moved(): return lax.ppermute(block, ('tx', 'ty'), pairs_of)  5.58 us
    pallas_call x1, Pallas kernels, fast_on_device(): pl.pallas_call(functools.partial(step_kernel, sizes), out_shape=[jax.Shap...  5.07 us
    ppermute x2, waiting for transfers between devices, across(): return lax.ppermute(block, 'ty', [(0, 1), (1, 0)])  1.82 us
    unnamed x8, local copies, waits for them, and re-layouts  1.35 us
    ppermute x2, starting transfers between devices, across(): return lax.ppermute(block, 'ty', [(0, 1), (1, 0)])  0.54 us
  transfers between devices with their start and end apart: 6, of which 5 were waited for; matrix products, arithmetic and copies ran while one was open for 1% of the time, Pallas kernels for 3%

profile of v16, /device:TPU:0, one launch (start us, length us, event | category | flops | bytes accessed | tf_op | source)
XLA Modules:
  0.0 23.3 jit_solution(12768776252241918613)
XLA Ops:
  0.0 0.0 copy-start
  0.0 0.9 %copy-done = f32[6,3,4,6,24]{4,2,3,1,0:T(4,128)S(1)} copy-done((f32[6,3,4,6,24]{4,2,3,1,0:T(4,128)S(1)}, f32[6,3,4,6,24]{4,2,3,1,0:T(4,128)}, u32[]{:S(2)}) %copy-start) | copy-done | bytes 41496
  0.9 0.0 copy-start.1
  0.9 0.3 %pack.1.swap_in = f32[216,128]{1,0:T(8,128)S(1)} custom-call(f32[6,3,6,4,24]{4,3,2,1,0:T(4,128)S(1)} %bitcast.2), custom_call_target="tpu_custom_call" | custom-call | tf_op jit(solution)/shard_map/pack/pallas_call | solution.py:530
  1.3 0.4 %copy-done.1 = f32[6,6,24]{2,1,0:T(8,128)S(1)} copy-done((f32[6,6,24]{2,1,0:T(8,128)S(1)}, f32[6,6,24]{2,1,0:T(8,128)}, u32[]{:S(2)}) %copy-start.1) | copy-done | bytes 3480
  1.7 0.2 pack_coriolis.1
  1.9 0.5 %collective-permute-start = (f32[216,128]{1,0:T(8,128)S(1)}, f32[216,128]{1,0:T(8,128)S(1)}, u32[]{:S(2)}, u32[]{:S(2)}) collective-permute-start(f32[216,128]{1,0:T(8,128)S(1)} %get-tuple-element.20.swap_ref.own_ref), channel_id=1, source_target_pairs={{0,1},{1,0},{2,3},{3,2},{4,5},{5,4},{6,7},{7,6},{8,9},{9,8},{10,11... | collective-permute-start | bytes 331784 | tf_op jit(solution)/shard_map/ppermute | solution.py:568
  2.3 0.2 keep.1
  2.5 0.8 %collective-permute-done.other_ref = f32[216,128]{1,0:T(8,128)S(1)} collective-permute-done((f32[216,128]{1,0:T(8,128)S(1)}, f32[216,128]{1,0:T(8,128)S(1)}, u32[]{:S(2)}, u32[]{:S(2)}) %collective-permute-start) | collective-permute-done | bytes 110624 | tf_op jit(solution)/shard_map/ppermute | solution.py:568
  3.3 0.0 copy-start.2
  3.3 2.9 %collective-permute-start.1 = (f32[240,128]{1,0:T(8,128)S(1)}, f32[240,128]{1,0:T(8,128)S(1)}, u32[]{:S(2)}, u32[]{:S(2)}) collective-permute-start(f32[240,128]{1,0:T(8,128)S(1)} %get-tuple-element.24), channel_id=1, source_target_pairs={{0,2},{1,15},{2,4},{3,1},{4,6},{5,3},{6,8},{7,5},{8,10},{9,7},{10,... | collective-permute-start | bytes 368648 | tf_op jit(solution)/shard_map/ppermute | solution.py:565
  6.2 0.0 copy-done.2
  6.2 0.1 copy.11
  6.4 0.1 convert_element_type.7
  6.5 2.7 %collective-permute-start.4 = (f32[48,128]{1,0:T(8,128)S(1)}, f32[48,128]{1,0:T(8,128)S(1)}, u32[]{:S(2)}, u32[]{:S(2)}) collective-permute-start(f32[48,128]{1,0:T(8,128)S(1)} %get-tuple-element.27), channel_id=1, source_target_pairs={{0,8},{1,9},{2,10},{3,11},{4,12},{5,13},{6,14},{7,15},{8,0},{9,1},... | collective-permute-start | bytes 73736 | tf_op jit(solution)/shard_map/ppermute | solution.py:565
  9.1 0.0 copy-start.3
  9.1 1.6 %collective-permute-start.2 = (f32[96,128]{1,0:T(8,128)S(1)}, f32[96,128]{1,0:T(8,128)S(1)}, u32[]{:S(2)}, u32[]{:S(2)}) collective-permute-start(f32[96,128]{1,0:T(8,128)S(1)} %get-tuple-element.25), channel_id=1, source_target_pairs={{0,6},{1,11},{2,8},{3,13},{4,10},{5,15},{6,12},{7,1},{8,14},{9,3},... | collective-permute-start | bytes 147464 | tf_op jit(solution)/shard_map/ppermute | solution.py:565
  10.7 0.2 collective-permute-start.3
  11.0 0.0 copy-done.3
  11.0 0.1 pad_maximum_fusion.1.table_in
  11.1 0.2 collective-permute-done.4
  11.3 4.0 %collective-permute-done.2 = f32[96,128]{1,0:T(8,128)S(1)} collective-permute-done((f32[96,128]{1,0:T(8,128)S(1)}, f32[96,128]{1,0:T(8,128)S(1)}, u32[]{:S(2)}, u32[]{:S(2)}) %collective-permute-start.2) | collective-permute-done | bytes 49184 | tf_op jit(solution)/shard_map/ppermute | solution.py:565
  15.2 1.4 %collective-permute-done.3 = f32[96,128]{1,0:T(8,128)S(1)} collective-permute-done((f32[96,128]{1,0:T(8,128)S(1)}, f32[96,128]{1,0:T(8,128)S(1)}, u32[]{:S(2)}, u32[]{:S(2)}) %collective-permute-start.3) | collective-permute-done | bytes 49184 | tf_op jit(solution)/shard_map/ppermute | solution.py:565
  16.6 0.0 collective-permute-done.1
  16.7 0.1 collective-permute-start.5
  16.7 0.2 place_own.1
  16.9 0.3 %place_got.1 = (f32[3,672,128]{2,1,0:T(8,128)S(1)}, f32[576,128]{1,0:T(8,128)S(1)}) custom-call(f32[480,128]{1,0:T(8,128)S(1)} %pad_maximum_fusion.got_ref, f32[3,672,128]{2,1,0:T(8,128)S(1)} %get-tuple-element.30.z_in, f32[576,128]{1,0:T(8,128)S(1)} %get-tuple-element.31.cor_in), custom_call_target="tpu_custom_call", output_to_operand_aliasing={{0}: (1, {}), {1}: (2, {})} | custom-call | tf_op jit(solution)/shard_map/place_got/pallas_call | solution.py:601
  17.2 1.1 %collective-permute-done.5.got_other_ref = f32[480,128]{1,0:T(8,128)S(1)} collective-permute-done((f32[480,128]{1,0:T(8,128)S(1)}, f32[480,128]{1,0:T(8,128)S(1)}, u32[]{:S(2)}, u32[]{:S(2)}) %collective-permute-start.5) | collective-permute-done | bytes 245792 | tf_op jit(solution)/shard_map/ppermute | solution.py:568
  18.2 5.1 %substeps.1 = (f32[6,3,6,4,24]{4,3,2,1,0:T(4,128)}, f32[3,672,128]{2,1,0:T(8,128)S(1)}, f32[576,128]{1,0:T(8,128)S(1)}) custom-call(f32[480,128]{1,0:T(8,128)S(1)} %pad_maximum_fusion.got_ref, f32[480,128]{1,0:T(8,128)S(1)} %collective-permute-done.5.got_other_ref, f32[76]{0:T(128)S(1)} %pad_maximum_fusion.1.table_in, ...), custom_call_target="tpu_custom_call", output_to_operand_aliasing={{1}: (3, {}), {2}: (4, {})} | custom-call | tf_op jit(solution)/shard_map/substeps/pallas_call | solution.py:610
  (3 shorter events, 0.0 us)
Async XLA Ops:
  0.0 0.9 %copy-start = (f32[6,3,4,6,24]{4,2,3,1,0:T(4,128)S(1)}, f32[6,3,4,6,24]{4,2,3,1,0:T(4,128)}, u32[]{:S(2)}) copy-start(f32[6,3,4,6,24]{4,2,3,1,0:T(4,128)} %param.4) | copy-start | bytes 124420
  0.9 0.7 %copy-start.1 = (f32[6,6,24]{2,1,0:T(8,128)S(1)}, f32[6,6,24]{2,1,0:T(8,128)}, u32[]{:S(2)}) copy-start(f32[6,6,24]{2,1,0:T(8,128)} %coriolis_ref.1) | copy-start | bytes 10372
  1.9 1.4 %collective-permute-start = (f32[216,128]{1,0:T(8,128)S(1)}, f32[216,128]{1,0:T(8,128)S(1)}, u32[]{:S(2)}, u32[]{:S(2)}) collective-permute-start(f32[216,128]{1,0:T(8,128)S(1)} %get-tuple-element.20.swap_ref.own_ref), channel_id=1, source_target_pairs={{0,1},{1,0},{2,3},{3,2},{4,5},{5,4},{6,7},{7,6},{8,9},{9,8},{10,11... | collective-permute-start | bytes 331784 | tf_op jit(solution)/shard_map/ppermute | solution.py:568
  3.3 3.0 %copy-start.2 = (s32[6,4,3]{0,1,2:T(4,128)S(1)}, s32[6,4,3]{0,1,2:T(4,128)}, u32[]{:S(2)}) copy-start(s32[6,4,3]{0,1,2:T(4,128)} %param.7) | copy-start | bytes 868
  3.3 13.3 %collective-permute-start.1 = (f32[240,128]{1,0:T(8,128)S(1)}, f32[240,128]{1,0:T(8,128)S(1)}, u32[]{:S(2)}, u32[]{:S(2)}) collective-permute-start(f32[240,128]{1,0:T(8,128)S(1)} %get-tuple-element.24), channel_id=1, source_target_pairs={{0,2},{1,15},{2,4},{3,1},{4,6},{5,3},{6,8},{7,5},{8,10},{9,7},{10,... | collective-permute-start | bytes 368648 | tf_op jit(solution)/shard_map/ppermute | solution.py:565
  6.5 4.8 %collective-permute-start.4 = (f32[48,128]{1,0:T(8,128)S(1)}, f32[48,128]{1,0:T(8,128)S(1)}, u32[]{:S(2)}, u32[]{:S(2)}) collective-permute-start(f32[48,128]{1,0:T(8,128)S(1)} %get-tuple-element.27), channel_id=1, source_target_pairs={{0,8},{1,9},{2,10},{3,11},{4,12},{5,13},{6,14},{7,15},{8,0},{9,1},... | collective-permute-start | bytes 73736 | tf_op jit(solution)/shard_map/ppermute | solution.py:565
  9.1 1.9 %copy-start.3 = (f32[4]{0:T(128)S(1)}, f32[4]{0:T(128)}, u32[]{:S(2)}) copy-start(f32[4]{0:T(128)} %param.6) | copy-start | bytes 52
  9.1 6.1 %collective-permute-start.2 = (f32[96,128]{1,0:T(8,128)S(1)}, f32[96,128]{1,0:T(8,128)S(1)}, u32[]{:S(2)}, u32[]{:S(2)}) collective-permute-start(f32[96,128]{1,0:T(8,128)S(1)} %get-tuple-element.25), channel_id=1, source_target_pairs={{0,6},{1,11},{2,8},{3,13},{4,10},{5,15},{6,12},{7,1},{8,14},{9,3},... | collective-permute-start | bytes 147464 | tf_op jit(solution)/shard_map/ppermute | solution.py:565
  10.7 5.9 %collective-permute-start.3 = (f32[96,128]{1,0:T(8,128)S(1)}, f32[96,128]{1,0:T(8,128)S(1)}, u32[]{:S(2)}, u32[]{:S(2)}) collective-permute-start(f32[96,128]{1,0:T(8,128)S(1)} %get-tuple-element.26), channel_id=1, source_target_pairs={{0,4},{1,13},{2,6},{3,15},{4,8},{5,1},{6,10},{7,3},{8,12},{9,5},{1... | collective-permute-start | bytes 147464 | tf_op jit(solution)/shard_map/ppermute | solution.py:565
  16.7 1.6 %collective-permute-start.5 = (f32[480,128]{1,0:T(8,128)S(1)}, f32[480,128]{1,0:T(8,128)S(1)}, u32[]{:S(2)}, u32[]{:S(2)}) collective-permute-start(f32[480,128]{1,0:T(8,128)S(1)} %pad_maximum_fusion.got_ref), channel_id=1, source_target_pairs={{0,1},{1,0},{2,3},{3,2},{4,5},{5,4},{6,7},{7,6},{8,9},{9,8},{10,11... | collective-permute-start | bytes 737288 | tf_op jit(solution)/shard_map/ppermute | solution.py:568

commit v17 on v16

--- a/solution.py
+++ b/solution.py
@@ -225,7 +225,7 @@
 
         put_block(from_owner(0)[1], own_lines)
 
-    def place_got(block_ref, toward, south_first):
+    def place_near(block_ref, toward, south_first):
         south_top = pl.multiple_of(south_first * full_rows, 8)
         north_top = pl.multiple_of((1 - south_first) * full_rows, 8)
 
@@ -237,8 +237,10 @@
             return even, jnp.where(low, pltpu.roll(south, LANES - cy, 1), north)
 
         put_block(from_owner(toward)[1], near_lines)
+
+    def place_far(block_ref, toward, south_first):
         for place, distance in enumerate((3, 2)):
-            top = 2 * full_rows + 2 * place * small_rows
+            top = 2 * place * small_rows
             south_at = pl.multiple_of(top + south_first * small_rows, 8)
             north_at = pl.multiple_of(top + (1 - south_first) * small_rows, 8)
 
@@ -249,31 +251,37 @@
 
             put_distant(*from_owner(toward * distance), far_lines)
 
-    def place_middle(got_ref, got_other_ref):
+    def place_middle(got_ref, passed_ref):
         def middle_lines(at, south_shift, north_shift):
-            row = 2 * full_rows + 4 * small_rows + at
+            row = 4 * small_rows + at
             mine_shift = jnp.where(south_is_own, south_shift, north_shift)
             other_shift = jnp.where(south_is_own, north_shift, south_shift)
             mine = pltpu.roll(got_ref[row : row + group], mine_shift, 1)
-            theirs = pltpu.roll(got_other_ref[row : row + group], other_shift, 1)
+            theirs = pltpu.roll(passed_ref[row : row + group], other_shift, 1)
             return jnp.where(own_half, mine, theirs)
 
         put_distant(*from_owner(count_x // 2), middle_lines)
 
-    return place_own, place_got, place_middle
-
-
-def own_kernel(sizes, own_ref, other_ref, z_ref, cor_ref):
-    placer(*sizes, z_ref, cor_ref)[0](own_ref, other_ref)
-
-
-def got_kernel(sizes, got_ref, z_in, cor_in, z_ref, cor_ref):
+    return place_own, place_near, place_far, place_middle
+
+
+def own_kernel(sizes, own_ref, other_ref, far_ref, z_ref, cor_ref):
+    place_own, _, place_far, _ = placer(*sizes, z_ref, cor_ref)
     index_y = lax.axis_index("ty")
-    placer(*sizes, z_ref, cor_ref)[1](got_ref, 1 - 2 * index_y, index_y)
+    place_own(own_ref, other_ref)
+    place_far(far_ref, 1 - 2 * index_y, index_y)
+
+
+def got_kernel(sizes, near_ref, far_ref, passed_ref, z_in, cor_in, z_ref, cor_ref):
+    _, place_near, place_far, place_middle = placer(*sizes, z_ref, cor_ref)
+    index_y = lax.axis_index("ty")
+    place_near(near_ref, 1 - 2 * index_y, index_y)
+    place_far(passed_ref, 2 * index_y - 1, 1 - index_y)
+    place_middle(far_ref, passed_ref)
 
 
 def step_kernel(
-    sizes, got_ref, got_other_ref, table_in, z_in, cor_in, out_hbm, z_ref, cor_ref,
+    sizes, passed_ref, table_in, z_in, cor_in, out_hbm, z_ref, cor_ref,
     pred_ref, store_ref, tile_ref, flip_ref, speed_ref, table_ref, out_ref, sems,
 ):
     table_copy = pltpu.make_async_copy(table_in, table_ref, sems.at[0])
@@ -295,9 +303,8 @@
     def lanes_of(rows):
         return lax.broadcasted_iota(jnp.int32, (rows, LANES), 1)
 
-    _, place_got, place_middle = placer(*sizes, z_ref, cor_ref)
-    place_got(got_other_ref, 2 * index_y - 1, 1 - index_y)
-    place_middle(got_ref, got_other_ref)
+    place_near = placer(*sizes, z_ref, cor_ref)[1]
+    place_near(passed_ref, 2 * index_y - 1, 1 - index_y)
 
     table_copy.wait()
     level_of = lax.broadcasted_iota(jnp.int32, speed_ref.shape, 0) % levels
@@ -579,11 +586,14 @@
         compiler_params=params,
         name="messages",
     )(swap, other, keep, middle)
-    got = [moved(block, distance) for block, distance in zip(messages, (1, 3, 2, count_x // 2))]
-    got = jnp.concatenate(got)
+    near, *far = [
+        moved(block, distance) for block, distance in zip(messages, (1, 3, 2, count_x // 2))
+    ]
+    far = jnp.concatenate(far)
     table = jnp.concatenate([wave_speed, edges.reshape(-1).astype(jnp.float32)])
-    got, table = lax.optimization_barrier((got, table))
-    passed = across(got)
+    near, table = lax.optimization_barrier((near, table))
+    far_passed = across(far)
+    near_passed = across(near)
 
     sizes = (cx, cy, count_x, full_rows, small_rows)
     state_rows = [
@@ -593,27 +603,27 @@
     rows = pl.pallas_call(
         functools.partial(own_kernel, sizes),
         out_shape=state_rows,
-        in_specs=[in_vmem] * 2,
+        in_specs=[in_vmem] * 3,
         out_specs=[in_vmem] * 2,
         compiler_params=params,
         name="place_own",
-    )(swap, other)
+    )(swap, other, far)
     rows = pl.pallas_call(
         functools.partial(got_kernel, sizes),
         out_shape=state_rows,
-        in_specs=[in_vmem] * 3,
+        in_specs=[in_vmem] * 5,
         out_specs=[in_vmem] * 2,
-        input_output_aliases={1: 0, 2: 1},
+        input_output_aliases={3: 0, 4: 1},
         compiler_params=params,
         name="place_got",
-    )(got, *rows)
+    )(near, far, far_passed, *rows)
     out, _, _ = pl.pallas_call(
         functools.partial(step_kernel, sizes),
         out_shape=[jax.ShapeDtypeStruct((faces, fields, cx, levels, cy), jnp.float32)]
         + state_rows,
-        in_specs=[in_vmem] * 5,
+        in_specs=[in_vmem] * 4,
         out_specs=[pl.BlockSpec(memory_space=pltpu.HBM)] + [in_vmem] * 2,
-        input_output_aliases={3: 1, 4: 2},
+        input_output_aliases={2: 1, 3: 2},
         scratch_shapes=[
             pltpu.VMEM(((cells + 8) * group, LANES), jnp.float32),
             pltpu.VMEM((faces * 4, 32, LANES), jnp.float32),
@@ -626,7 +636,7 @@
         ],
         compiler_params=pltpu.CompilerParams(vmem_limit_bytes=VMEM_LIMIT),
         name="substeps",
-    )(got, passed, table, *rows)
+    )(near_passed, table, *rows)
     return jnp.swapaxes(out, 2, 3)
 
 

time: 23.5 us -> 24.1 us (1.026)
  local copies, waits for them, and re-layouts: 1.57 us -> 2.08 us
    ppermute x2 -> x3, waiting for transfers between devices: 1.82 us -> 0.67 us  [across(): return lax.ppermute(block, 'ty', [(0, 1), (1, 0)])]
    ppermute x4, waiting for transfers between devices: 5.58 us -> 6.63 us  [moved(): return lax.ppermute(block, ('tx', 'ty'), pairs_of)]
    unnamed x8 -> x10, local copies, waits for them, and re-layouts: 1.35 us -> 1.86 us
    pallas_call x1, Pallas kernels: 5.07 us -> 4.78 us  [fast_on_device(): pl.pallas_call(functools.partial(step_kernel, sizes), out_shape=[jax.Shap...]
    ppermute x4, starting transfers between devices: 7.44 us -> 7.68 us  [moved(): return lax.ppermute(block, ('tx', 'ty'), pairs_of)]
    ppermute x2 -> x3, starting transfers between devices: 0.54 us -> 0.48 us  [across(): return lax.ppermute(block, 'ty', [(0, 1), (1, 0)])]
  transfers between devices with their start and end apart: 6 -> 7, of which waited for: 5 -> 4; matrix products, arithmetic and copies ran while one was open for 1% -> 1% of each run, Pallas kernels for 3% -> 4%
where the time goes in v17:
time: 24.1 us; the launch traced here: 23.8 us
  starting transfers between devices  8.16 us (34%)
  waiting for transfers between devices  7.3 us (30%)
  Pallas kernels  6.17 us (26%)
  local copies, waits for them, and re-layouts  2.08 us (9%)
    ppermute x4, starting transfers between devices, moved(): return lax.ppermute(block, ('tx', 'ty'), pairs_of)  7.68 us
    ppermute x4, waiting for transfers between devices, moved(): return lax.ppermute(block, ('tx', 'ty'), pairs_of)  6.63 us
    pallas_call x1, Pallas kernels, fast_on_device(): pl.pallas_call(functools.partial(step_kernel, sizes), out_shape=[jax.Shap...  4.78 us
    unnamed x10, local copies, waits for them, and re-layouts  1.86 us
    ppermute x3, waiting for transfers between devices, across(): return lax.ppermute(block, 'ty', [(0, 1), (1, 0)])  0.67 us
  transfers between devices with their start and end apart: 7, of which 4 were waited for; matrix products, arithmetic and copies ran while one was open for 1% of the time, Pallas kernels for 4%

profile of v17, /device:TPU:0, one launch (start us, length us, event | category | flops | bytes accessed | tf_op | source)
XLA Modules:
  0.0 23.8 jit_solution(3083311660891869257)
XLA Ops:
  0.0 0.0 copy-start
  0.0 0.9 %copy-done = f32[6,3,4,6,24]{4,2,3,1,0:T(4,128)S(1)} copy-done((f32[6,3,4,6,24]{4,2,3,1,0:T(4,128)S(1)}, f32[6,3,4,6,24]{4,2,3,1,0:T(4,128)}, u32[]{:S(2)}) %copy-start) | copy-done | bytes 41496
  0.9 0.0 copy-start.1
  0.9 0.3 %pack.1.swap_in = f32[216,128]{1,0:T(8,128)S(1)} custom-call(f32[6,3,6,4,24]{4,3,2,1,0:T(4,128)S(1)} %bitcast.2), custom_call_target="tpu_custom_call" | custom-call | tf_op jit(solution)/shard_map/pack/pallas_call | solution.py:537
  1.3 0.4 %copy-done.1 = f32[6,6,24]{2,1,0:T(8,128)S(1)} copy-done((f32[6,6,24]{2,1,0:T(8,128)S(1)}, f32[6,6,24]{2,1,0:T(8,128)}, u32[]{:S(2)}) %copy-start.1) | copy-done | bytes 3480
  1.7 0.2 pack_coriolis.1
  1.9 0.5 %collective-permute-start = (f32[216,128]{1,0:T(8,128)S(1)}, f32[216,128]{1,0:T(8,128)S(1)}, u32[]{:S(2)}, u32[]{:S(2)}) collective-permute-start(f32[216,128]{1,0:T(8,128)S(1)} %get-tuple-element.20.swap_ref.own_ref), channel_id=1, source_target_pairs={{0,1},{1,0},{2,3},{3,2},{4,5},{5,4},{6,7},{7,6},{8,9},{9,8},{10,11... | collective-permute-start | bytes 331784 | tf_op jit(solution)/shard_map/ppermute | solution.py:575
  2.3 0.0 copy-start.2
  2.3 0.2 keep.1
  2.5 0.5 %copy-done.2 = s32[6,4,3]{0,1,2:T(4,128)S(1)} copy-done((s32[6,4,3]{0,1,2:T(4,128)S(1)}, s32[6,4,3]{0,1,2:T(4,128)}, u32[]{:S(2)}) %copy-start.2) | copy-done | bytes 312
  3.0 0.1 copy.11
  3.1 0.1 convert_element_type.7
  3.2 0.0 collective-permute-done.other_ref
  3.3 0.0 copy-start.3
  3.3 3.9 %collective-permute-start.3 = (f32[96,128]{1,0:T(8,128)S(1)}, f32[96,128]{1,0:T(8,128)S(1)}, u32[]{:S(2)}, u32[]{:S(2)}) collective-permute-start(f32[96,128]{1,0:T(8,128)S(1)} %get-tuple-element.27), channel_id=1, source_target_pairs={{0,6},{1,11},{2,8},{3,13},{4,10},{5,15},{6,12},{7,1},{8,14},{9,3},... | collective-permute-start | bytes 147464 | tf_op jit(solution)/shard_map/ppermute | solution.py:572
  7.3 0.0 copy-done.3
  7.3 0.1 pad_maximum_fusion.table_in
  7.3 1.6 %collective-permute-start.4 = (f32[96,128]{1,0:T(8,128)S(1)}, f32[96,128]{1,0:T(8,128)S(1)}, u32[]{:S(2)}, u32[]{:S(2)}) collective-permute-start(f32[96,128]{1,0:T(8,128)S(1)} %get-tuple-element.28), channel_id=1, source_target_pairs={{0,4},{1,13},{2,6},{3,15},{4,8},{5,1},{6,10},{7,3},{8,12},{9,5},{1... | collective-permute-start | bytes 147464 | tf_op jit(solution)/shard_map/ppermute | solution.py:572
  8.9 1.2 %collective-permute-start.5 = (f32[48,128]{1,0:T(8,128)S(1)}, f32[48,128]{1,0:T(8,128)S(1)}, u32[]{:S(2)}, u32[]{:S(2)}) collective-permute-start(f32[48,128]{1,0:T(8,128)S(1)} %get-tuple-element.29), channel_id=1, source_target_pairs={{0,8},{1,9},{2,10},{3,11},{4,12},{5,13},{6,14},{7,15},{8,0},{9,1},... | collective-permute-start | bytes 73736 | tf_op jit(solution)/shard_map/ppermute | solution.py:572
  10.1 0.9 %collective-permute-start.1 = (f32[240,128]{1,0:T(8,128)S(1)}, f32[240,128]{1,0:T(8,128)S(1)}, u32[]{:S(2)}, u32[]{:S(2)}) collective-permute-start(f32[240,128]{1,0:T(8,128)S(1)} %get-tuple-element.24), channel_id=1, source_target_pairs={{0,2},{1,15},{2,4},{3,1},{4,6},{5,3},{6,8},{7,5},{8,10},{9,7},{10,... | collective-permute-start | bytes 368648 | tf_op jit(solution)/shard_map/ppermute | solution.py:572
  11.1 0.0 collective-permute-done.3
  11.1 2.5 %collective-permute-done.4 = f32[96,128]{1,0:T(8,128)S(1)} collective-permute-done((f32[96,128]{1,0:T(8,128)S(1)}, f32[96,128]{1,0:T(8,128)S(1)}, u32[]{:S(2)}, u32[]{:S(2)}) %collective-permute-start.4) | collective-permute-done | bytes 49184 | tf_op jit(solution)/shard_map/ppermute | solution.py:572
  13.6 0.5 %collective-permute-done.5 = f32[48,128]{1,0:T(8,128)S(1)} collective-permute-done((f32[48,128]{1,0:T(8,128)S(1)}, f32[48,128]{1,0:T(8,128)S(1)}, u32[]{:S(2)}, u32[]{:S(2)}) %collective-permute-start.5) | collective-permute-done | bytes 24608 | tf_op jit(solution)/shard_map/ppermute | solution.py:572
  14.1 0.0 collective-permute-start.6
  14.1 3.6 %collective-permute-done.1.near_ref = f32[240,128]{1,0:T(8,128)S(1)} collective-permute-done((f32[240,128]{1,0:T(8,128)S(1)}, f32[240,128]{1,0:T(8,128)S(1)}, u32[]{:S(2)}, u32[]{:S(2)}) %collective-permute-start.1) | collective-permute-done | bytes 122912 | tf_op jit(solution)/shard_map/ppermute | solution.py:572
  17.7 0.0 collective-permute-start.2
  17.7 0.3 %place_own.1 = (f32[3,672,128]{2,1,0:T(8,128)S(1)}, f32[576,128]{1,0:T(8,128)S(1)}) custom-call(f32[216,128]{1,0:T(8,128)S(1)} %get-tuple-element.20.swap_ref.own_ref, f32[216,128]{1,0:T(8,128)S(1)} %collective-permute-done.other_ref, f32[240,128]{1,0:T(8,128)S(1)} %constant_dynamic-update-slice_fusion.far_ref), custom_call_target="tpu_custom_call" | custom-call | tf_op jit(solution)/shard_map/place_own/pallas_call | solution.py:603
  18.1 0.0 collective-permute-done.6.passed_ref
  18.1 0.4 %place_got.1 = (f32[3,672,128]{2,1,0:T(8,128)S(1)}, f32[576,128]{1,0:T(8,128)S(1)}) custom-call(f32[240,128]{1,0:T(8,128)S(1)} %collective-permute-done.1.near_ref, f32[240,128]{1,0:T(8,128)S(1)} %constant_dynamic-update-slice_fusion.far_ref, f32[240,128]{1,0:T(8,128)S(1)} %collective-permute-done.6.passed_ref, ...), custom_call_target="tpu_custom_call", output_to_operand_aliasing={{0}: (3, {}), {1}: (4, {})} | custom-call | tf_op jit(solution)/shard_map/place_got/pallas_call | solution.py:611
  18.4 0.6 %collective-permute-done.2.passed_ref = f32[240,128]{1,0:T(8,128)S(1)} collective-permute-done((f32[240,128]{1,0:T(8,128)S(1)}, f32[240,128]{1,0:T(8,128)S(1)}, u32[]{:S(2)}, u32[]{:S(2)}) %collective-permute-start.2) | collective-permute-done | bytes 122912 | tf_op jit(solution)/shard_map/ppermute | solution.py:575
  19.1 4.8 %substeps.1 = (f32[6,3,6,4,24]{4,3,2,1,0:T(4,128)}, f32[3,672,128]{2,1,0:T(8,128)S(1)}, f32[576,128]{1,0:T(8,128)S(1)}) custom-call(f32[240,128]{1,0:T(8,128)S(1)} %collective-permute-done.2.passed_ref, f32[76]{0:T(128)S(1)} %pad_maximum_fusion.table_in, f32[3,672,128]{2,1,0:T(8,128)S(1)} %get-tuple-element.32.z_in, ...), custom_call_target="tpu_custom_call", output_to_operand_aliasing={{1}: (2, {}), {2}: (3, {})} | custom-call | tf_op jit(solution)/shard_map/substeps/pallas_call | solution.py:620
  (5 shorter events, 0.0 us)
Async XLA Ops:
  0.0 0.9 %copy-start = (f32[6,3,4,6,24]{4,2,3,1,0:T(4,128)S(1)}, f32[6,3,4,6,24]{4,2,3,1,0:T(4,128)}, u32[]{:S(2)}) copy-start(f32[6,3,4,6,24]{4,2,3,1,0:T(4,128)} %param.4) | copy-start | bytes 124420
  0.9 0.7 %copy-start.1 = (f32[6,6,24]{2,1,0:T(8,128)S(1)}, f32[6,6,24]{2,1,0:T(8,128)}, u32[]{:S(2)}) copy-start(f32[6,6,24]{2,1,0:T(8,128)} %coriolis_ref.1) | copy-start | bytes 10372
  1.9 1.4 %collective-permute-start = (f32[216,128]{1,0:T(8,128)S(1)}, f32[216,128]{1,0:T(8,128)S(1)}, u32[]{:S(2)}, u32[]{:S(2)}) collective-permute-start(f32[216,128]{1,0:T(8,128)S(1)} %get-tuple-element.20.swap_ref.own_ref), channel_id=1, source_target_pairs={{0,1},{1,0},{2,3},{3,2},{4,5},{5,4},{6,7},{7,6},{8,9},{9,8},{10,11... | collective-permute-start | bytes 331784 | tf_op jit(solution)/shard_map/ppermute | solution.py:575
  2.3 0.7 %copy-start.2 = (s32[6,4,3]{0,1,2:T(4,128)S(1)}, s32[6,4,3]{0,1,2:T(4,128)}, u32[]{:S(2)}) copy-start(s32[6,4,3]{0,1,2:T(4,128)} %param.7) | copy-start | bytes 868
  3.3 4.0 %copy-start.3 = (f32[4]{0:T(128)S(1)}, f32[4]{0:T(128)}, u32[]{:S(2)}) copy-start(f32[4]{0:T(128)} %param.6) | copy-start | bytes 52
  3.3 7.8 %collective-permute-start.3 = (f32[96,128]{1,0:T(8,128)S(1)}, f32[96,128]{1,0:T(8,128)S(1)}, u32[]{:S(2)}, u32[]{:S(2)}) collective-permute-start(f32[96,128]{1,0:T(8,128)S(1)} %get-tuple-element.27), channel_id=1, source_target_pairs={{0,6},{1,11},{2,8},{3,13},{4,10},{5,15},{6,12},{7,1},{8,14},{9,3},... | collective-permute-start | bytes 147464 | tf_op jit(solution)/shard_map/ppermute | solution.py:572
  7.3 6.2 %collective-permute-start.4 = (f32[96,128]{1,0:T(8,128)S(1)}, f32[96,128]{1,0:T(8,128)S(1)}, u32[]{:S(2)}, u32[]{:S(2)}) collective-permute-start(f32[96,128]{1,0:T(8,128)S(1)} %get-tuple-element.28), channel_id=1, source_target_pairs={{0,4},{1,13},{2,6},{3,15},{4,8},{5,1},{6,10},{7,3},{8,12},{9,5},{1... | collective-permute-start | bytes 147464 | tf_op jit(solution)/shard_map/ppermute | solution.py:572
  8.9 5.2 %collective-permute-start.5 = (f32[48,128]{1,0:T(8,128)S(1)}, f32[48,128]{1,0:T(8,128)S(1)}, u32[]{:S(2)}, u32[]{:S(2)}) collective-permute-start(f32[48,128]{1,0:T(8,128)S(1)} %get-tuple-element.29), channel_id=1, source_target_pairs={{0,8},{1,9},{2,10},{3,11},{4,12},{5,13},{6,14},{7,15},{8,0},{9,1},... | collective-permute-start | bytes 73736 | tf_op jit(solution)/shard_map/ppermute | solution.py:572
  10.1 7.6 %collective-permute-start.1 = (f32[240,128]{1,0:T(8,128)S(1)}, f32[240,128]{1,0:T(8,128)S(1)}, u32[]{:S(2)}, u32[]{:S(2)}) collective-permute-start(f32[240,128]{1,0:T(8,128)S(1)} %get-tuple-element.24), channel_id=1, source_target_pairs={{0,2},{1,15},{2,4},{3,1},{4,6},{5,3},{6,8},{7,5},{8,10},{9,7},{10,... | collective-permute-start | bytes 368648 | tf_op jit(solution)/shard_map/ppermute | solution.py:572
  14.1 4.0 %collective-permute-start.6 = (f32[240,128]{1,0:T(8,128)S(1)}, f32[240,128]{1,0:T(8,128)S(1)}, u32[]{:S(2)}, u32[]{:S(2)}) collective-permute-start(f32[240,128]{1,0:T(8,128)S(1)} %constant_dynamic-update-slice_fusion.far_ref), channel_id=1, source_target_pairs={{0,1},{1,0},{2,3},{3,2},{4,5},{5,4},{6,7},{7,6},{8,9},{9,8},{10,11... | collective-permute-start | bytes 368648 | tf_op jit(solution)/shard_map/ppermute | solution.py:575
  17.7 1.3 %collective-permute-start.2 = (f32[240,128]{1,0:T(8,128)S(1)}, f32[240,128]{1,0:T(8,128)S(1)}, u32[]{:S(2)}, u32[]{:S(2)}) collective-permute-start(f32[240,128]{1,0:T(8,128)S(1)} %collective-permute-done.1.near_ref), channel_id=1, source_target_pairs={{0,1},{1,0},{2,3},{3,2},{4,5},{5,4},{6,7},{7,6},{8,9},{9,8},{10,11... | collective-permute-start | bytes 368648 | tf_op jit(solution)/shard_map/ppermute | solution.py:575

commit v18 on v17

--- a/solution.py
+++ b/solution.py
@@ -265,23 +265,22 @@
     return place_own, place_near, place_far, place_middle
 
 
-def own_kernel(sizes, own_ref, other_ref, far_ref, z_ref, cor_ref):
-    place_own, _, place_far, _ = placer(*sizes, z_ref, cor_ref)
+def own_kernel(sizes, own_ref, other_ref, near_ref, z_ref, cor_ref):
+    place_own, place_near = placer(*sizes, z_ref, cor_ref)[:2]
     index_y = lax.axis_index("ty")
     place_own(own_ref, other_ref)
+    place_near(near_ref, 1 - 2 * index_y, index_y)
+
+
+def got_kernel(sizes, far_ref, passed_ref, z_in, cor_in, z_ref, cor_ref):
+    _, place_near, place_far, _ = placer(*sizes, z_ref, cor_ref)
+    index_y = lax.axis_index("ty")
     place_far(far_ref, 1 - 2 * index_y, index_y)
-
-
-def got_kernel(sizes, near_ref, far_ref, passed_ref, z_in, cor_in, z_ref, cor_ref):
-    _, place_near, place_far, place_middle = placer(*sizes, z_ref, cor_ref)
-    index_y = lax.axis_index("ty")
-    place_near(near_ref, 1 - 2 * index_y, index_y)
-    place_far(passed_ref, 2 * index_y - 1, 1 - index_y)
-    place_middle(far_ref, passed_ref)
+    place_near(passed_ref, 2 * index_y - 1, 1 - index_y)
 
 
 def step_kernel(
-    sizes, passed_ref, table_in, z_in, cor_in, out_hbm, z_ref, cor_ref,
+    sizes, far_ref, passed_ref, table_in, z_in, cor_in, out_hbm, z_ref, cor_ref,
     pred_ref, store_ref, tile_ref, flip_ref, speed_ref, table_ref, out_ref, sems,
 ):
     table_copy = pltpu.make_async_copy(table_in, table_ref, sems.at[0])
@@ -303,8 +302,9 @@
     def lanes_of(rows):
         return lax.broadcasted_iota(jnp.int32, (rows, LANES), 1)
 
-    place_near = placer(*sizes, z_ref, cor_ref)[1]
-    place_near(passed_ref, 2 * index_y - 1, 1 - index_y)
+    place_far, place_middle = placer(*sizes, z_ref, cor_ref)[2:]
+    place_far(passed_ref, 2 * index_y - 1, 1 - index_y)
+    place_middle(far_ref, passed_ref)
 
     table_copy.wait()
     level_of = lax.broadcasted_iota(jnp.int32, speed_ref.shape, 0) % levels
@@ -586,14 +586,15 @@
         compiler_params=params,
         name="messages",
     )(swap, other, keep, middle)
-    near, *far = [
+    near, third, second, fourth = [
         moved(block, distance) for block, distance in zip(messages, (1, 3, 2, count_x // 2))
     ]
-    far = jnp.concatenate(far)
+    near, fourth = lax.optimization_barrier((near, fourth))
+    far = jnp.concatenate([third, second, fourth])
     table = jnp.concatenate([wave_speed, edges.reshape(-1).astype(jnp.float32)])
-    near, table = lax.optimization_barrier((near, table))
+    far, table = lax.optimization_barrier((far, table))
+    near_passed = across(near)
     far_passed = across(far)
-    near_passed = across(near)
 
     sizes = (cx, cy, count_x, full_rows, small_rows)
     state_rows = [
@@ -607,23 +608,23 @@
         out_specs=[in_vmem] * 2,
         compiler_params=params,
         name="place_own",
-    )(swap, other, far)
+    )(swap, other, near)
     rows = pl.pallas_call(
         functools.partial(got_kernel, sizes),
         out_shape=state_rows,
-        in_specs=[in_vmem] * 5,
+        in_specs=[in_vmem] * 4,
         out_specs=[in_vmem] * 2,
-        input_output_aliases={3: 0, 4: 1},
+        input_output_aliases={2: 0, 3: 1},
         compiler_params=params,
         name="place_got",
-    )(near, far, far_passed, *rows)
+    )(far, near_passed, *rows)
     out, _, _ = pl.pallas_call(
         functools.partial(step_kernel, sizes),
         out_shape=[jax.ShapeDtypeStruct((faces, fields, cx, levels, cy), jnp.float32)]
         + state_rows,
-        in_specs=[in_vmem] * 4,
+        in_specs=[in_vmem] * 5,
         out_specs=[pl.BlockSpec(memory_space=pltpu.HBM)] + [in_vmem] * 2,
-        input_output_aliases={2: 1, 3: 2},
+        input_output_aliases={3: 1, 4: 2},
         scratch_shapes=[
             pltpu.VMEM(((cells + 8) * group, LANES), jnp.float32),
             pltpu.VMEM((faces * 4, 32, LANES), jnp.float32),
@@ -636,7 +637,7 @@
         ],
         compiler_params=pltpu.CompilerParams(vmem_limit_bytes=VMEM_LIMIT),
         name="substeps",
-    )(near_passed, table, *rows)
+    )(far, far_passed, table, *rows)
     return jnp.swapaxes(out, 2, 3)
 
 

time: 24.1 us -> 23.3 us (0.967)
  waiting for transfers between devices: 7.3 us -> 6.58 us
  local copies, waits for them, and re-layouts: 2.08 us -> 1.57 us
  starting transfers between devices: 8.16 us -> 8.55 us
    ppermute x4, waiting for transfers between devices: 6.63 us -> 5 us  [moved(): return lax.ppermute(block, ('tx', 'ty'), pairs_of)]
    ppermute x3, waiting for transfers between devices: 0.67 us -> 1.57 us  [across(): return lax.ppermute(block, 'ty', [(0, 1), (1, 0)])]
    ppermute x3, starting transfers between devices: 0.48 us -> 1.12 us  [across(): return lax.ppermute(block, 'ty', [(0, 1), (1, 0)])]
    unnamed x10 -> x8, local copies, waits for them, and re-layouts: 1.86 us -> 1.35 us
    pallas_call x1, Pallas kernels: 4.78 us -> 5.03 us  [fast_on_device(): pl.pallas_call(functools.partial(step_kernel, sizes), out_shape=[jax.Shap...]
    ppermute x4, starting transfers between devices: 7.68 us -> 7.44 us  [moved(): return lax.ppermute(block, ('tx', 'ty'), pairs_of)]
  transfers between devices with their start and end apart: 7 -> 7, of which waited for: 4 -> 6; matrix products, arithmetic and copies ran while one was open for 1% -> 1% of each run, Pallas kernels for 4% -> 3%
where the time goes in v18:
time: 23.3 us; the launch traced here: 23.1 us
  starting transfers between devices  8.55 us (37%)
  waiting for transfers between devices  6.58 us (28%)
  Pallas kernels  6.23 us (27%)
  local copies, waits for them, and re-layouts  1.57 us (7%)
    ppermute x4, starting transfers between devices, moved(): return lax.ppermute(block, ('tx', 'ty'), pairs_of)  7.44 us
    pallas_call x1, Pallas kernels, fast_on_device(): pl.pallas_call(functools.partial(step_kernel, sizes), out_shape=[jax.Shap...  5.03 us
    ppermute x4, waiting for transfers between devices, moved(): return lax.ppermute(block, ('tx', 'ty'), pairs_of)  5 us
    ppermute x3, waiting for transfers between devices, across(): return lax.ppermute(block, 'ty', [(0, 1), (1, 0)])  1.57 us
    unnamed x8, local copies, waits for them, and re-layouts  1.35 us
    ppermute x3, starting transfers between devices, across(): return lax.ppermute(block, 'ty', [(0, 1), (1, 0)])  1.12 us
  transfers between devices with their start and end apart: 7, of which 6 were waited for; matrix products, arithmetic and copies ran while one was open for 1% of the time, Pallas kernels for 3%

profile of v18, /device:TPU:0, one launch (start us, length us, event | category | flops | bytes accessed | tf_op | source)
XLA Modules:
  0.0 23.1 jit_solution(15043500686758175571)
XLA Ops:
  0.0 0.0 copy-start
  0.0 0.9 %copy-done = f32[6,3,4,6,24]{4,2,3,1,0:T(4,128)S(1)} copy-done((f32[6,3,4,6,24]{4,2,3,1,0:T(4,128)S(1)}, f32[6,3,4,6,24]{4,2,3,1,0:T(4,128)}, u32[]{:S(2)}) %copy-start) | copy-done | bytes 41496
  0.9 0.0 copy-start.1
  0.9 0.3 %pack.1.swap_in = f32[216,128]{1,0:T(8,128)S(1)} custom-call(f32[6,3,6,4,24]{4,3,2,1,0:T(4,128)S(1)} %bitcast.2), custom_call_target="tpu_custom_call" | custom-call | tf_op jit(solution)/shard_map/pack/pallas_call | solution.py:537
  1.3 0.4 %copy-done.1 = f32[6,6,24]{2,1,0:T(8,128)S(1)} copy-done((f32[6,6,24]{2,1,0:T(8,128)S(1)}, f32[6,6,24]{2,1,0:T(8,128)}, u32[]{:S(2)}) %copy-start.1) | copy-done | bytes 3480
  1.7 0.2 pack_coriolis.1
  1.9 0.5 %collective-permute-start = (f32[216,128]{1,0:T(8,128)S(1)}, f32[216,128]{1,0:T(8,128)S(1)}, u32[]{:S(2)}, u32[]{:S(2)}) collective-permute-start(f32[216,128]{1,0:T(8,128)S(1)} %get-tuple-element.22.swap_ref.own_ref), channel_id=1, source_target_pairs={{0,1},{1,0},{2,3},{3,2},{4,5},{5,4},{6,7},{7,6},{8,9},{9,8},{10,11... | collective-permute-start | bytes 331784 | tf_op jit(solution)/shard_map/ppermute | solution.py:575
  2.3 0.2 keep.1
  2.5 0.8 %collective-permute-done.other_ref = f32[216,128]{1,0:T(8,128)S(1)} collective-permute-done((f32[216,128]{1,0:T(8,128)S(1)}, f32[216,128]{1,0:T(8,128)S(1)}, u32[]{:S(2)}, u32[]{:S(2)}) %collective-permute-start) | collective-permute-done | bytes 110624 | tf_op jit(solution)/shard_map/ppermute | solution.py:575
  3.3 0.0 copy-start.2
  3.3 2.9 %collective-permute-start.3 = (f32[240,128]{1,0:T(8,128)S(1)}, f32[240,128]{1,0:T(8,128)S(1)}, u32[]{:S(2)}, u32[]{:S(2)}) collective-permute-start(f32[240,128]{1,0:T(8,128)S(1)} %get-tuple-element.28), channel_id=1, source_target_pairs={{0,2},{1,15},{2,4},{3,1},{4,6},{5,3},{6,8},{7,5},{8,10},{9,7},{10,... | collective-permute-start | bytes 368648 | tf_op jit(solution)/shard_map/ppermute | solution.py:572
  6.2 0.0 copy-done.2
  6.2 0.1 copy.11
  6.4 0.1 convert_element_type.7
  6.5 2.7 %collective-permute-start.4 = (f32[48,128]{1,0:T(8,128)S(1)}, f32[48,128]{1,0:T(8,128)S(1)}, u32[]{:S(2)}, u32[]{:S(2)}) collective-permute-start(f32[48,128]{1,0:T(8,128)S(1)} %get-tuple-element.29), channel_id=1, source_target_pairs={{0,8},{1,9},{2,10},{3,11},{4,12},{5,13},{6,14},{7,15},{8,0},{9,1},... | collective-permute-start | bytes 73736 | tf_op jit(solution)/shard_map/ppermute | solution.py:572
  9.1 0.0 copy-start.3
  9.1 1.6 %collective-permute-start.1 = (f32[96,128]{1,0:T(8,128)S(1)}, f32[96,128]{1,0:T(8,128)S(1)}, u32[]{:S(2)}, u32[]{:S(2)}) collective-permute-start(f32[96,128]{1,0:T(8,128)S(1)} %get-tuple-element.26), channel_id=1, source_target_pairs={{0,6},{1,11},{2,8},{3,13},{4,10},{5,15},{6,12},{7,1},{8,14},{9,3},... | collective-permute-start | bytes 147464 | tf_op jit(solution)/shard_map/ppermute | solution.py:572
  10.7 0.2 collective-permute-start.2
  11.0 0.0 copy-done.3
  11.0 0.1 pad_maximum_fusion.1.table_in
  11.1 0.2 collective-permute-done.4
  11.3 1.2 %collective-permute-done.3.near_ref = f32[240,128]{1,0:T(8,128)S(1)} collective-permute-done((f32[240,128]{1,0:T(8,128)S(1)}, f32[240,128]{1,0:T(8,128)S(1)}, u32[]{:S(2)}, u32[]{:S(2)}) %collective-permute-start.3) | collective-permute-done | bytes 122912 | tf_op jit(solution)/shard_map/ppermute | solution.py:572
  12.4 0.6 %collective-permute-start.6 = (f32[240,128]{1,0:T(8,128)S(1)}, f32[240,128]{1,0:T(8,128)S(1)}, u32[]{:S(2)}, u32[]{:S(2)}) collective-permute-start(f32[240,128]{1,0:T(8,128)S(1)} %collective-permute-done.3.near_ref), channel_id=1, source_target_pairs={{0,1},{1,0},{2,3},{3,2},{4,5},{5,4},{6,7},{7,6},{8,9},{9,8},{10,11... | collective-permute-start | bytes 368648 | tf_op jit(solution)/shard_map/ppermute | solution.py:575
  13.0 2.2 %collective-permute-done.1 = f32[96,128]{1,0:T(8,128)S(1)} collective-permute-done((f32[96,128]{1,0:T(8,128)S(1)}, f32[96,128]{1,0:T(8,128)S(1)}, u32[]{:S(2)}, u32[]{:S(2)}) %collective-permute-start.1) | collective-permute-done | bytes 49184 | tf_op jit(solution)/shard_map/ppermute | solution.py:572
  15.2 1.4 %collective-permute-done.2 = f32[96,128]{1,0:T(8,128)S(1)} collective-permute-done((f32[96,128]{1,0:T(8,128)S(1)}, f32[96,128]{1,0:T(8,128)S(1)}, u32[]{:S(2)}, u32[]{:S(2)}) %collective-permute-start.2) | collective-permute-done | bytes 49184 | tf_op jit(solution)/shard_map/ppermute | solution.py:572
  16.6 0.1 collective-permute-start.5
  16.7 0.2 place_own.1
  16.9 0.0 collective-permute-done.6.passed_ref
  16.9 0.3 %place_got.1 = (f32[3,672,128]{2,1,0:T(8,128)S(1)}, f32[576,128]{1,0:T(8,128)S(1)}) custom-call(f32[240,128]{1,0:T(8,128)S(1)} %pad_maximum_fusion.far_ref, f32[240,128]{1,0:T(8,128)S(1)} %collective-permute-done.6.passed_ref, f32[3,672,128]{2,1,0:T(8,128)S(1)} %get-tuple-element.34.z_in, ...), custom_call_target="tpu_custom_call", output_to_operand_aliasing={{0}: (2, {}), {1}: (3, {})} | custom-call | tf_op jit(solution)/shard_map/place_got/pallas_call | solution.py:612
  17.2 0.8 %collective-permute-done.5.passed_ref = f32[240,128]{1,0:T(8,128)S(1)} collective-permute-done((f32[240,128]{1,0:T(8,128)S(1)}, f32[240,128]{1,0:T(8,128)S(1)}, u32[]{:S(2)}, u32[]{:S(2)}) %collective-permute-start.5) | collective-permute-done | bytes 122912 | tf_op jit(solution)/shard_map/ppermute | solution.py:575
  18.0 5.0 %substeps.1 = (f32[6,3,6,4,24]{4,3,2,1,0:T(4,128)}, f32[3,672,128]{2,1,0:T(8,128)S(1)}, f32[576,128]{1,0:T(8,128)S(1)}) custom-call(f32[240,128]{1,0:T(8,128)S(1)} %pad_maximum_fusion.far_ref, f32[240,128]{1,0:T(8,128)S(1)} %collective-permute-done.5.passed_ref, f32[76]{0:T(128)S(1)} %pad_maximum_fusion.1.table_in, ...), custom_call_target="tpu_custom_call", output_to_operand_aliasing={{1}: (3, {}), {2}: (4, {})} | custom-call | tf_op jit(solution)/shard_map/substeps/pallas_call | solution.py:621
  (3 shorter events, 0.0 us)
Async XLA Ops:
  0.0 0.9 %copy-start = (f32[6,3,4,6,24]{4,2,3,1,0:T(4,128)S(1)}, f32[6,3,4,6,24]{4,2,3,1,0:T(4,128)}, u32[]{:S(2)}) copy-start(f32[6,3,4,6,24]{4,2,3,1,0:T(4,128)} %param.4) | copy-start | bytes 124420
  0.9 0.7 %copy-start.1 = (f32[6,6,24]{2,1,0:T(8,128)S(1)}, f32[6,6,24]{2,1,0:T(8,128)}, u32[]{:S(2)}) copy-start(f32[6,6,24]{2,1,0:T(8,128)} %coriolis_ref.1) | copy-start | bytes 10372
  1.9 1.4 %collective-permute-start = (f32[216,128]{1,0:T(8,128)S(1)}, f32[216,128]{1,0:T(8,128)S(1)}, u32[]{:S(2)}, u32[]{:S(2)}) collective-permute-start(f32[216,128]{1,0:T(8,128)S(1)} %get-tuple-element.22.swap_ref.own_ref), channel_id=1, source_target_pairs={{0,1},{1,0},{2,3},{3,2},{4,5},{5,4},{6,7},{7,6},{8,9},{9,8},{10,11... | collective-permute-start | bytes 331784 | tf_op jit(solution)/shard_map/ppermute | solution.py:575
  3.3 3.0 %copy-start.2 = (s32[6,4,3]{0,1,2:T(4,128)S(1)}, s32[6,4,3]{0,1,2:T(4,128)}, u32[]{:S(2)}) copy-start(s32[6,4,3]{0,1,2:T(4,128)} %param.7) | copy-start | bytes 868
  3.3 9.1 %collective-permute-start.3 = (f32[240,128]{1,0:T(8,128)S(1)}, f32[240,128]{1,0:T(8,128)S(1)}, u32[]{:S(2)}, u32[]{:S(2)}) collective-permute-start(f32[240,128]{1,0:T(8,128)S(1)} %get-tuple-element.28), channel_id=1, source_target_pairs={{0,2},{1,15},{2,4},{3,1},{4,6},{5,3},{6,8},{7,5},{8,10},{9,7},{10,... | collective-permute-start | bytes 368648 | tf_op jit(solution)/shard_map/ppermute | solution.py:572
  6.5 4.8 %collective-permute-start.4 = (f32[48,128]{1,0:T(8,128)S(1)}, f32[48,128]{1,0:T(8,128)S(1)}, u32[]{:S(2)}, u32[]{:S(2)}) collective-permute-start(f32[48,128]{1,0:T(8,128)S(1)} %get-tuple-element.29), channel_id=1, source_target_pairs={{0,8},{1,9},{2,10},{3,11},{4,12},{5,13},{6,14},{7,15},{8,0},{9,1},... | collective-permute-start | bytes 73736 | tf_op jit(solution)/shard_map/ppermute | solution.py:572
  9.1 1.9 %copy-start.3 = (f32[4]{0:T(128)S(1)}, f32[4]{0:T(128)}, u32[]{:S(2)}) copy-start(f32[4]{0:T(128)} %param.6) | copy-start | bytes 52
  9.1 6.1 %collective-permute-start.1 = (f32[96,128]{1,0:T(8,128)S(1)}, f32[96,128]{1,0:T(8,128)S(1)}, u32[]{:S(2)}, u32[]{:S(2)}) collective-permute-start(f32[96,128]{1,0:T(8,128)S(1)} %get-tuple-element.26), channel_id=1, source_target_pairs={{0,6},{1,11},{2,8},{3,13},{4,10},{5,15},{6,12},{7,1},{8,14},{9,3},... | collective-permute-start | bytes 147464 | tf_op jit(solution)/shard_map/ppermute | solution.py:572
  10.7 5.9 %collective-permute-start.2 = (f32[96,128]{1,0:T(8,128)S(1)}, f32[96,128]{1,0:T(8,128)S(1)}, u32[]{:S(2)}, u32[]{:S(2)}) collective-permute-start(f32[96,128]{1,0:T(8,128)S(1)} %get-tuple-element.27), channel_id=1, source_target_pairs={{0,4},{1,13},{2,6},{3,15},{4,8},{5,1},{6,10},{7,3},{8,12},{9,5},{1... | collective-permute-start | bytes 147464 | tf_op jit(solution)/shard_map/ppermute | solution.py:572
  12.4 4.5 %collective-permute-start.6 = (f32[240,128]{1,0:T(8,128)S(1)}, f32[240,128]{1,0:T(8,128)S(1)}, u32[]{:S(2)}, u32[]{:S(2)}) collective-permute-start(f32[240,128]{1,0:T(8,128)S(1)} %collective-permute-done.3.near_ref), channel_id=1, source_target_pairs={{0,1},{1,0},{2,3},{3,2},{4,5},{5,4},{6,7},{7,6},{8,9},{9,8},{10,11... | collective-permute-start | bytes 368648 | tf_op jit(solution)/shard_map/ppermute | solution.py:575
  16.6 1.4 %collective-permute-start.5 = (f32[240,128]{1,0:T(8,128)S(1)}, f32[240,128]{1,0:T(8,128)S(1)}, u32[]{:S(2)}, u32[]{:S(2)}) collective-permute-start(f32[240,128]{1,0:T(8,128)S(1)} %pad_maximum_fusion.far_ref), channel_id=1, source_target_pairs={{0,1},{1,0},{2,3},{3,2},{4,5},{5,4},{6,7},{7,6},{8,9},{9,8},{10,11... | collective-permute-start | bytes 368648 | tf_op jit(solution)/shard_map/ppermute | solution.py:575

commit v19 on v18

--- a/solution.py
+++ b/solution.py
@@ -253,7 +253,7 @@
 
     def place_middle(got_ref, passed_ref):
         def middle_lines(at, south_shift, north_shift):
-            row = 4 * small_rows + at
+            row = 2 * full_rows + at
             mine_shift = jnp.where(south_is_own, south_shift, north_shift)
             other_shift = jnp.where(south_is_own, north_shift, south_shift)
             mine = pltpu.roll(got_ref[row : row + group], mine_shift, 1)
@@ -272,15 +272,16 @@
     place_near(near_ref, 1 - 2 * index_y, index_y)
 
 
-def got_kernel(sizes, far_ref, passed_ref, z_in, cor_in, z_ref, cor_ref):
-    _, place_near, place_far, _ = placer(*sizes, z_ref, cor_ref)
+def got_kernel(sizes, near_ref, far_ref, passed_ref, z_in, cor_in, z_ref, cor_ref):
+    _, place_near, place_far, place_middle = placer(*sizes, z_ref, cor_ref)
     index_y = lax.axis_index("ty")
     place_far(far_ref, 1 - 2 * index_y, index_y)
     place_near(passed_ref, 2 * index_y - 1, 1 - index_y)
+    place_middle(near_ref, passed_ref)
 
 
 def step_kernel(
-    sizes, far_ref, passed_ref, table_in, z_in, cor_in, out_hbm, z_ref, cor_ref,
+    sizes, passed_ref, table_in, z_in, cor_in, out_hbm, z_ref, cor_ref,
     pred_ref, store_ref, tile_ref, flip_ref, speed_ref, table_ref, out_ref, sems,
 ):
     table_copy = pltpu.make_async_copy(table_in, table_ref, sems.at[0])
@@ -302,9 +303,8 @@
     def lanes_of(rows):
         return lax.broadcasted_iota(jnp.int32, (rows, LANES), 1)
 
-    place_far, place_middle = placer(*sizes, z_ref, cor_ref)[2:]
+    place_far = placer(*sizes, z_ref, cor_ref)[2]
     place_far(passed_ref, 2 * index_y - 1, 1 - index_y)
-    place_middle(far_ref, passed_ref)
 
     table_copy.wait()
     level_of = lax.broadcasted_iota(jnp.int32, speed_ref.shape, 0) % levels
@@ -589,8 +589,8 @@
     near, third, second, fourth = [
         moved(block, distance) for block, distance in zip(messages, (1, 3, 2, count_x // 2))
     ]
-    near, fourth = lax.optimization_barrier((near, fourth))
-    far = jnp.concatenate([third, second, fourth])
+    near = jnp.concatenate([near, fourth])
+    far = jnp.concatenate([third, second])
     table = jnp.concatenate([wave_speed, edges.reshape(-1).astype(jnp.float32)])
     far, table = lax.optimization_barrier((far, table))
     near_passed = across(near)
@@ -612,19 +612,19 @@
     rows = pl.pallas_call(
         functools.partial(got_kernel, sizes),
         out_shape=state_rows,
-        in_specs=[in_vmem] * 4,
+        in_specs=[in_vmem] * 5,
         out_specs=[in_vmem] * 2,
-        input_output_aliases={2: 0, 3: 1},
+        input_output_aliases={3: 0, 4: 1},
         compiler_params=params,
         name="place_got",
-    )(far, near_passed, *rows)
+    )(near, far, near_passed, *rows)
     out, _, _ = pl.pallas_call(
         functools.partial(step_kernel, sizes),
         out_shape=[jax.ShapeDtypeStruct((faces, fields, cx, levels, cy), jnp.float32)]
         + state_rows,
-        in_specs=[in_vmem] * 5,
+        in_specs=[in_vmem] * 4,
         out_specs=[pl.BlockSpec(memory_space=pltpu.HBM)] + [in_vmem] * 2,
-        input_output_aliases={3: 1, 4: 2},
+        input_output_aliases={2: 1, 3: 2},
         scratch_shapes=[
             pltpu.VMEM(((cells + 8) * group, LANES), jnp.float32),
             pltpu.VMEM((faces * 4, 32, LANES), jnp.float32),
@@ -637,7 +637,7 @@
         ],
         compiler_params=pltpu.CompilerParams(vmem_limit_bytes=VMEM_LIMIT),
         name="substeps",
-    )(far, far_passed, table, *rows)
+    )(far_passed, table, *rows)
     return jnp.swapaxes(out, 2, 3)
 
 

time: 23.3 us -> 23.7 us (1.017)
  local copies, waits for them, and re-layouts: 1.57 us -> 2.13 us
  waiting for transfers between devices: 6.58 us -> 6.03 us
  starting transfers between devices: 8.55 us -> 8.96 us
    unnamed x8 -> x9, local copies, waits for them, and re-layouts: 1.35 us -> 1.91 us
    ppermute x3, starting transfers between devices: 1.12 us -> 1.59 us  [across(): return lax.ppermute(block, 'ty', [(0, 1), (1, 0)])]
    ppermute x4, waiting for transfers between devices: 5 us -> 4.58 us  [moved(): return lax.ppermute(block, ('tx', 'ty'), pairs_of)]
  transfers between devices with their start and end apart: 7 -> 7, of which waited for: 6 -> 5; matrix products, arithmetic and copies ran while one was open for 1% -> 1% of each run, Pallas kernels for 3% -> 3%
where the time goes in v19:
time: 23.7 us; the launch traced here: 23.5 us
  starting transfers between devices  8.96 us (38%)
  Pallas kernels  6.21 us (26%)
  waiting for transfers between devices  6.03 us (25%)
  local copies, waits for them, and re-layouts  2.13 us (9%)
    ppermute x4, starting transfers between devices, moved(): return lax.ppermute(block, ('tx', 'ty'), pairs_of)  7.37 us
    pallas_call x1, Pallas kernels, fast_on_device(): pl.pallas_call(functools.partial(step_kernel, sizes), out_shape=[jax.Shap...  4.93 us
    ppermute x4, waiting for transfers between devices, moved(): return lax.ppermute(block, ('tx', 'ty'), pairs_of)  4.58 us
    unnamed x9, local copies, waits for them, and re-layouts  1.91 us
    ppermute x3, starting transfers between devices, across(): return lax.ppermute(block, 'ty', [(0, 1), (1, 0)])  1.59 us
    ppermute x3, waiting for transfers between devices, across(): return lax.ppermute(block, 'ty', [(0, 1), (1, 0)])  1.45 us
  transfers between devices with their start and end apart: 7, of which 5 were waited for; matrix products, arithmetic and copies ran while one was open for 1% of the time, Pallas kernels for 3%

profile of v19, /device:TPU:0, one launch (start us, length us, event | category | flops | bytes accessed | tf_op | source)
XLA Modules:
  0.0 23.5 jit_solution(8401575388360411417)
XLA Ops:
  0.0 0.0 copy-start
  0.0 0.9 %copy-done = f32[6,3,4,6,24]{4,2,3,1,0:T(4,128)S(1)} copy-done((f32[6,3,4,6,24]{4,2,3,1,0:T(4,128)S(1)}, f32[6,3,4,6,24]{4,2,3,1,0:T(4,128)}, u32[]{:S(2)}) %copy-start) | copy-done | bytes 41496
  0.9 0.0 copy-start.1
  0.9 0.3 %pack.1.swap_in = f32[216,128]{1,0:T(8,128)S(1)} custom-call(f32[6,3,6,4,24]{4,3,2,1,0:T(4,128)S(1)} %bitcast.2), custom_call_target="tpu_custom_call" | custom-call | tf_op jit(solution)/shard_map/pack/pallas_call | solution.py:537
  1.3 0.4 %copy-done.1 = f32[6,6,24]{2,1,0:T(8,128)S(1)} copy-done((f32[6,6,24]{2,1,0:T(8,128)S(1)}, f32[6,6,24]{2,1,0:T(8,128)}, u32[]{:S(2)}) %copy-start.1) | copy-done | bytes 3480
  1.7 0.2 pack_coriolis.1
  1.9 0.5 %collective-permute-start = (f32[216,128]{1,0:T(8,128)S(1)}, f32[216,128]{1,0:T(8,128)S(1)}, u32[]{:S(2)}, u32[]{:S(2)}) collective-permute-start(f32[216,128]{1,0:T(8,128)S(1)} %get-tuple-element.20.swap_ref.own_ref), channel_id=1, source_target_pairs={{0,1},{1,0},{2,3},{3,2},{4,5},{5,4},{6,7},{7,6},{8,9},{9,8},{10,11... | collective-permute-start | bytes 331784 | tf_op jit(solution)/shard_map/ppermute | solution.py:575
  2.3 0.2 keep.1
  2.5 0.8 %collective-permute-done.other_ref = f32[216,128]{1,0:T(8,128)S(1)} collective-permute-done((f32[216,128]{1,0:T(8,128)S(1)}, f32[216,128]{1,0:T(8,128)S(1)}, u32[]{:S(2)}, u32[]{:S(2)}) %collective-permute-start) | collective-permute-done | bytes 110624 | tf_op jit(solution)/shard_map/ppermute | solution.py:575
  3.3 0.0 copy-start.2
  3.3 2.9 %collective-permute-start.4 = (f32[240,128]{1,0:T(8,128)S(1)}, f32[240,128]{1,0:T(8,128)S(1)}, u32[]{:S(2)}, u32[]{:S(2)}) collective-permute-start(f32[240,128]{1,0:T(8,128)S(1)} %get-tuple-element.28), channel_id=1, source_target_pairs={{0,2},{1,15},{2,4},{3,1},{4,6},{5,3},{6,8},{7,5},{8,10},{9,7},{10,... | collective-permute-start | bytes 368648 | tf_op jit(solution)/shard_map/ppermute | solution.py:572
  6.2 0.0 copy-done.2
  6.2 0.1 copy.11
  6.4 0.0 copy-start.3
  6.4 0.1 convert_element_type.7
  6.5 0.6 %copy-done.3 = f32[4]{0:T(128)S(1)} copy-done((f32[4]{0:T(128)S(1)}, f32[4]{0:T(128)}, u32[]{:S(2)}) %copy-start.3) | copy-done | bytes 40
  7.0 0.1 pad_maximum_fusion.1.table_in
  7.1 2.6 %collective-permute-start.5 = (f32[48,128]{1,0:T(8,128)S(1)}, f32[48,128]{1,0:T(8,128)S(1)}, u32[]{:S(2)}, u32[]{:S(2)}) collective-permute-start(f32[48,128]{1,0:T(8,128)S(1)} %get-tuple-element.29), channel_id=1, source_target_pairs={{0,8},{1,9},{2,10},{3,11},{4,12},{5,13},{6,14},{7,15},{8,0},{9,1},... | collective-permute-start | bytes 73736 | tf_op jit(solution)/shard_map/ppermute | solution.py:572
  9.7 1.6 %collective-permute-start.1 = (f32[96,128]{1,0:T(8,128)S(1)}, f32[96,128]{1,0:T(8,128)S(1)}, u32[]{:S(2)}, u32[]{:S(2)}) collective-permute-start(f32[96,128]{1,0:T(8,128)S(1)} %get-tuple-element.24), channel_id=1, source_target_pairs={{0,6},{1,11},{2,8},{3,13},{4,10},{5,15},{6,12},{7,1},{8,14},{9,3},... | collective-permute-start | bytes 147464 | tf_op jit(solution)/shard_map/ppermute | solution.py:572
  11.3 0.2 collective-permute-start.2
  11.5 1.0 %collective-permute-done.4 = f32[240,128]{1,0:T(8,128)S(1)} collective-permute-done((f32[240,128]{1,0:T(8,128)S(1)}, f32[240,128]{1,0:T(8,128)S(1)}, u32[]{:S(2)}, u32[]{:S(2)}) %collective-permute-start.4) | collective-permute-done | bytes 122912 | tf_op jit(solution)/shard_map/ppermute | solution.py:572
  12.5 0.0 collective-permute-done.5
  12.5 1.0 %collective-permute-start.6 = (f32[288,128]{1,0:T(8,128)S(1)}, f32[288,128]{1,0:T(8,128)S(1)}, u32[]{:S(2)}, u32[]{:S(2)}) collective-permute-start(f32[288,128]{1,0:T(8,128)S(1)} %constant_dynamic-update-slice_fusion.near_ref), channel_id=1, source_target_pairs={{0,1},{1,0},{2,3},{3,2},{4,5},{5,4},{6,7},{7,6},{8,9},{9,8},{10,11... | collective-permute-start | bytes 442376 | tf_op jit(solution)/shard_map/ppermute | solution.py:575
  13.6 2.2 %collective-permute-done.1 = f32[96,128]{1,0:T(8,128)S(1)} collective-permute-done((f32[96,128]{1,0:T(8,128)S(1)}, f32[96,128]{1,0:T(8,128)S(1)}, u32[]{:S(2)}, u32[]{:S(2)}) %collective-permute-start.1) | collective-permute-done | bytes 49184 | tf_op jit(solution)/shard_map/ppermute | solution.py:572
  15.8 1.4 %collective-permute-done.2 = f32[96,128]{1,0:T(8,128)S(1)} collective-permute-done((f32[96,128]{1,0:T(8,128)S(1)}, f32[96,128]{1,0:T(8,128)S(1)}, u32[]{:S(2)}, u32[]{:S(2)}) %collective-permute-start.2) | collective-permute-done | bytes 49184 | tf_op jit(solution)/shard_map/ppermute | solution.py:572
  17.2 0.1 collective-permute-start.3
  17.3 0.2 place_own.1
  17.5 0.0 collective-permute-done.6.passed_ref
  17.5 0.4 %place_got.1 = (f32[3,672,128]{2,1,0:T(8,128)S(1)}, f32[576,128]{1,0:T(8,128)S(1)}) custom-call(f32[288,128]{1,0:T(8,128)S(1)} %constant_dynamic-update-slice_fusion.near_ref, f32[192,128]{1,0:T(8,128)S(1)} %pad_maximum_fusion.far_ref, f32[288,128]{1,0:T(8,128)S(1)} %collective-permute-done.6.passed_ref, ...), custom_call_target="tpu_custom_call", output_to_operand_aliasing={{0}: (3, {}), {1}: (4, {})} | custom-call | tf_op jit(solution)/shard_map/place_got/pallas_call | solution.py:612
  17.9 0.7 %collective-permute-done.3.passed_ref = f32[192,128]{1,0:T(8,128)S(1)} collective-permute-done((f32[192,128]{1,0:T(8,128)S(1)}, f32[192,128]{1,0:T(8,128)S(1)}, u32[]{:S(2)}, u32[]{:S(2)}) %collective-permute-start.3) | collective-permute-done | bytes 98336 | tf_op jit(solution)/shard_map/ppermute | solution.py:575
  18.6 4.9 %substeps.1 = (f32[6,3,6,4,24]{4,3,2,1,0:T(4,128)}, f32[3,672,128]{2,1,0:T(8,128)S(1)}, f32[576,128]{1,0:T(8,128)S(1)}) custom-call(f32[192,128]{1,0:T(8,128)S(1)} %collective-permute-done.3.passed_ref, f32[76]{0:T(128)S(1)} %pad_maximum_fusion.1.table_in, f32[3,672,128]{2,1,0:T(8,128)S(1)} %get-tuple-element.32.z_in, ...), custom_call_target="tpu_custom_call", output_to_operand_aliasing={{1}: (2, {}), {2}: (3, {})} | custom-call | tf_op jit(solution)/shard_map/substeps/pallas_call | solution.py:621
  (5 shorter events, 0.0 us)
Async XLA Ops:
  0.0 0.9 %copy-start = (f32[6,3,4,6,24]{4,2,3,1,0:T(4,128)S(1)}, f32[6,3,4,6,24]{4,2,3,1,0:T(4,128)}, u32[]{:S(2)}) copy-start(f32[6,3,4,6,24]{4,2,3,1,0:T(4,128)} %param.4) | copy-start | bytes 124420
  0.9 0.7 %copy-start.1 = (f32[6,6,24]{2,1,0:T(8,128)S(1)}, f32[6,6,24]{2,1,0:T(8,128)}, u32[]{:S(2)}) copy-start(f32[6,6,24]{2,1,0:T(8,128)} %coriolis_ref.1) | copy-start | bytes 10372
  1.9 1.4 %collective-permute-start = (f32[216,128]{1,0:T(8,128)S(1)}, f32[216,128]{1,0:T(8,128)S(1)}, u32[]{:S(2)}, u32[]{:S(2)}) collective-permute-start(f32[216,128]{1,0:T(8,128)S(1)} %get-tuple-element.20.swap_ref.own_ref), channel_id=1, source_target_pairs={{0,1},{1,0},{2,3},{3,2},{4,5},{5,4},{6,7},{7,6},{8,9},{9,8},{10,11... | collective-permute-start | bytes 331784 | tf_op jit(solution)/shard_map/ppermute | solution.py:575
  3.3 3.0 %copy-start.2 = (s32[6,4,3]{0,1,2:T(4,128)S(1)}, s32[6,4,3]{0,1,2:T(4,128)}, u32[]{:S(2)}) copy-start(s32[6,4,3]{0,1,2:T(4,128)} %param.7) | copy-start | bytes 868
  3.3 9.2 %collective-permute-start.4 = (f32[240,128]{1,0:T(8,128)S(1)}, f32[240,128]{1,0:T(8,128)S(1)}, u32[]{:S(2)}, u32[]{:S(2)}) collective-permute-start(f32[240,128]{1,0:T(8,128)S(1)} %get-tuple-element.28), channel_id=1, source_target_pairs={{0,2},{1,15},{2,4},{3,1},{4,6},{5,3},{6,8},{7,5},{8,10},{9,7},{10,... | collective-permute-start | bytes 368648 | tf_op jit(solution)/shard_map/ppermute | solution.py:572
  6.4 0.7 %copy-start.3 = (f32[4]{0:T(128)S(1)}, f32[4]{0:T(128)}, u32[]{:S(2)}) copy-start(f32[4]{0:T(128)} %param.6) | copy-start | bytes 52
  7.1 5.4 %collective-permute-start.5 = (f32[48,128]{1,0:T(8,128)S(1)}, f32[48,128]{1,0:T(8,128)S(1)}, u32[]{:S(2)}, u32[]{:S(2)}) collective-permute-start(f32[48,128]{1,0:T(8,128)S(1)} %get-tuple-element.29), channel_id=1, source_target_pairs={{0,8},{1,9},{2,10},{3,11},{4,12},{5,13},{6,14},{7,15},{8,0},{9,1},... | collective-permute-start | bytes 73736 | tf_op jit(solution)/shard_map/ppermute | solution.py:572
  9.7 6.1 %collective-permute-start.1 = (f32[96,128]{1,0:T(8,128)S(1)}, f32[96,128]{1,0:T(8,128)S(1)}, u32[]{:S(2)}, u32[]{:S(2)}) collective-permute-start(f32[96,128]{1,0:T(8,128)S(1)} %get-tuple-element.24), channel_id=1, source_target_pairs={{0,6},{1,11},{2,8},{3,13},{4,10},{5,15},{6,12},{7,1},{8,14},{9,3},... | collective-permute-start | bytes 147464 | tf_op jit(solution)/shard_map/ppermute | solution.py:572
  11.3 5.9 %collective-permute-start.2 = (f32[96,128]{1,0:T(8,128)S(1)}, f32[96,128]{1,0:T(8,128)S(1)}, u32[]{:S(2)}, u32[]{:S(2)}) collective-permute-start(f32[96,128]{1,0:T(8,128)S(1)} %get-tuple-element.25), channel_id=1, source_target_pairs={{0,4},{1,13},{2,6},{3,15},{4,8},{5,1},{6,10},{7,3},{8,12},{9,5},{1... | collective-permute-start | bytes 147464 | tf_op jit(solution)/shard_map/ppermute | solution.py:572
  12.5 5.0 %collective-permute-start.6 = (f32[288,128]{1,0:T(8,128)S(1)}, f32[288,128]{1,0:T(8,128)S(1)}, u32[]{:S(2)}, u32[]{:S(2)}) collective-permute-start(f32[288,128]{1,0:T(8,128)S(1)} %constant_dynamic-update-slice_fusion.near_ref), channel_id=1, source_target_pairs={{0,1},{1,0},{2,3},{3,2},{4,5},{5,4},{6,7},{7,6},{8,9},{9,8},{10,11... | collective-permute-start | bytes 442376 | tf_op jit(solution)/shard_map/ppermute | solution.py:575
  17.2 1.4 %collective-permute-start.3 = (f32[192,128]{1,0:T(8,128)S(1)}, f32[192,128]{1,0:T(8,128)S(1)}, u32[]{:S(2)}, u32[]{:S(2)}) collective-permute-start(f32[192,128]{1,0:T(8,128)S(1)} %pad_maximum_fusion.far_ref), channel_id=1, source_target_pairs={{0,1},{1,0},{2,3},{3,2},{4,5},{5,4},{6,7},{7,6},{8,9},{9,8},{10,11... | collective-permute-start | bytes 294920 | tf_op jit(solution)/shard_map/ppermute | solution.py:575

commit v20 on v18

--- a/solution.py
+++ b/solution.py
@@ -266,6 +266,8 @@
 
 
 def own_kernel(sizes, own_ref, other_ref, near_ref, z_ref, cor_ref):
+    z_ref[...] = jnp.zeros(z_ref.shape, jnp.float32)
+    cor_ref[...] = jnp.zeros(cor_ref.shape, jnp.float32)
     place_own, place_near = placer(*sizes, z_ref, cor_ref)[:2]
     index_y = lax.axis_index("ty")
     place_own(own_ref, other_ref)
@@ -386,11 +388,13 @@
 
     def rim_rows(side):
         left = lane_8 < WINDOW
+        cells_8 = (place_8 >= MARGIN) & (place_8 < MARGIN + cells)
         for pair in range(pairs):
             first = fetch(2 * pair, side, [lane_8 - MARGIN] * 2)
             second = fetch(2 * pair + 1, side, [lane_8 - (MARGIN + WINDOW)] * 2)
             for slot in range(2):
                 both = [jnp.where(left, a, b) for a, b in zip(first[slot], second[slot])]
+                both = [jnp.where(cells_8, lines, 0.0) for lines in both]
                 for depth in range(3):
                     x = -1 - depth if side == 0 else cells + depth
                     row = row_of(x) + pair * levels
@@ -454,19 +458,31 @@
         behind = z_ref[0, pl.ds(at - group, rows)]
         pred_ref[pl.ds(at, rows)] = z_ref[1, pl.ds(at, rows)] - speed * (0.5 * (ahead - behind))
 
+    ahead_by = lax.broadcasted_iota(jnp.int32, (LANES, LANES), 0) - lanes_of(LANES)
+
+    def band(entries):
+        matrix = jnp.zeros((LANES, LANES), jnp.float32)
+        for offset, value in entries:
+            matrix = jnp.where(ahead_by == offset, value, matrix)
+        return matrix
+
+    slope = band(((1, 0.5), (-1, -0.5)))
+    flux = band(((1, 8.0), (-1, -8.0), (2, -1.0), (-2, 1.0)))
+
+    def times(values, matrix):
+        return jnp.dot(
+            values, matrix, precision=lax.Precision.HIGHEST, preferred_element_type=jnp.float32
+        )
+
     def update(at, rows):
         speed = speed_ref[:rows]
         height = z_ref[0, pl.ds(at, rows)]
-        north_pred = z_ref[2, pl.ds(at, rows)] - speed * (
-            0.5 * (pltpu.roll(height, LANES - 1, 1) - pltpu.roll(height, 1, 1))
-        )
+        north_pred = z_ref[2, pl.ds(at, rows)] - speed * times(height, slope)
         east_pred = pred_ref[pl.ds(at, rows)]
         flux_east = 8.0 * (
             pred_ref[pl.ds(at + group, rows)] - pred_ref[pl.ds(at - group, rows)]
         ) - (pred_ref[pl.ds(at + 2 * group, rows)] - pred_ref[pl.ds(at - 2 * group, rows)])
-        flux_north = 8.0 * (
-            pltpu.roll(north_pred, LANES - 1, 1) - pltpu.roll(north_pred, 1, 1)
-        ) - (pltpu.roll(north_pred, LANES - 2, 1) - pltpu.roll(north_pred, 2, 1))
+        flux_north = times(north_pred, flux)
         height = height - speed * ((flux_east + flux_north) * (1.0 / 12.0))
         turning = cor_ref[pl.ds(at - row_of(0), rows)]
         return height, east_pred + turning * north_pred, north_pred - turning * east_pred

time: 23.3 us -> 24.5 us (1.052)
  Pallas kernels: 6.23 us -> 7.45 us
    pallas_call x1, Pallas kernels: 5.03 us -> 6.25 us  [fast_on_device(): pl.pallas_call(functools.partial(step_kernel, sizes), out_shape=[jax.Shap...]
where the time goes in v20:
time: 24.5 us; the launch traced here: 24.3 us
  starting transfers between devices  8.55 us (35%)
  Pallas kernels  7.45 us (30%)
  waiting for transfers between devices  6.57 us (27%)
  local copies, waits for them, and re-layouts  1.57 us (6%)
    ppermute x4, starting transfers between devices, moved(): return lax.ppermute(block, ('tx', 'ty'), pairs_of)  7.44 us
    pallas_call x1, Pallas kernels, fast_on_device(): pl.pallas_call(functools.partial(step_kernel, sizes), out_shape=[jax.Shap...  6.25 us
    ppermute x4, waiting for transfers between devices, moved(): return lax.ppermute(block, ('tx', 'ty'), pairs_of)  5 us
    ppermute x3, waiting for transfers between devices, across(): return lax.ppermute(block, 'ty', [(0, 1), (1, 0)])  1.57 us
    unnamed x8, local copies, waits for them, and re-layouts  1.35 us
    ppermute x3, starting transfers between devices, across(): return lax.ppermute(block, 'ty', [(0, 1), (1, 0)])  1.12 us
  transfers between devices with their start and end apart: 7, of which 6 were waited for; matrix products, arithmetic and copies ran while one was open for 1% of the time, Pallas kernels for 3%

profile of v20, /device:TPU:0, one launch (start us, length us, event | category | flops | bytes accessed | tf_op | source)
XLA Modules:
  0.0 24.3 jit_solution(6226950666548086074)
XLA Ops:
  0.0 0.0 copy-start
  0.0 0.9 %copy-done = f32[6,3,4,6,24]{4,2,3,1,0:T(4,128)S(1)} copy-done((f32[6,3,4,6,24]{4,2,3,1,0:T(4,128)S(1)}, f32[6,3,4,6,24]{4,2,3,1,0:T(4,128)}, u32[]{:S(2)}) %copy-start) | copy-done | bytes 41496
  0.9 0.0 copy-start.1
  0.9 0.3 %pack.1.swap_in = f32[216,128]{1,0:T(8,128)S(1)} custom-call(f32[6,3,6,4,24]{4,3,2,1,0:T(4,128)S(1)} %bitcast.2), custom_call_target="tpu_custom_call" | custom-call | tf_op jit(solution)/shard_map/pack/pallas_call | solution.py:553
  1.3 0.4 %copy-done.1 = f32[6,6,24]{2,1,0:T(8,128)S(1)} copy-done((f32[6,6,24]{2,1,0:T(8,128)S(1)}, f32[6,6,24]{2,1,0:T(8,128)}, u32[]{:S(2)}) %copy-start.1) | copy-done | bytes 3480
  1.7 0.2 pack_coriolis.1
  1.9 0.5 %collective-permute-start = (f32[216,128]{1,0:T(8,128)S(1)}, f32[216,128]{1,0:T(8,128)S(1)}, u32[]{:S(2)}, u32[]{:S(2)}) collective-permute-start(f32[216,128]{1,0:T(8,128)S(1)} %get-tuple-element.22.swap_ref.own_ref), channel_id=1, source_target_pairs={{0,1},{1,0},{2,3},{3,2},{4,5},{5,4},{6,7},{7,6},{8,9},{9,8},{10,11... | collective-permute-start | bytes 331784 | tf_op jit(solution)/shard_map/ppermute | solution.py:591
  2.3 0.2 keep.1
  2.5 0.8 %collective-permute-done.other_ref = f32[216,128]{1,0:T(8,128)S(1)} collective-permute-done((f32[216,128]{1,0:T(8,128)S(1)}, f32[216,128]{1,0:T(8,128)S(1)}, u32[]{:S(2)}, u32[]{:S(2)}) %collective-permute-start) | collective-permute-done | bytes 110624 | tf_op jit(solution)/shard_map/ppermute | solution.py:591
  3.3 0.0 copy-start.2
  3.3 2.9 %collective-permute-start.3 = (f32[240,128]{1,0:T(8,128)S(1)}, f32[240,128]{1,0:T(8,128)S(1)}, u32[]{:S(2)}, u32[]{:S(2)}) collective-permute-start(f32[240,128]{1,0:T(8,128)S(1)} %get-tuple-element.28), channel_id=1, source_target_pairs={{0,2},{1,15},{2,4},{3,1},{4,6},{5,3},{6,8},{7,5},{8,10},{9,7},{10,... | collective-permute-start | bytes 368648 | tf_op jit(solution)/shard_map/ppermute | solution.py:588
  6.2 0.0 copy-done.2
  6.2 0.1 copy.11
  6.4 0.1 convert_element_type.7
  6.5 2.7 %collective-permute-start.4 = (f32[48,128]{1,0:T(8,128)S(1)}, f32[48,128]{1,0:T(8,128)S(1)}, u32[]{:S(2)}, u32[]{:S(2)}) collective-permute-start(f32[48,128]{1,0:T(8,128)S(1)} %get-tuple-element.29), channel_id=1, source_target_pairs={{0,8},{1,9},{2,10},{3,11},{4,12},{5,13},{6,14},{7,15},{8,0},{9,1},... | collective-permute-start | bytes 73736 | tf_op jit(solution)/shard_map/ppermute | solution.py:588
  9.1 0.0 copy-start.3
  9.1 1.6 %collective-permute-start.1 = (f32[96,128]{1,0:T(8,128)S(1)}, f32[96,128]{1,0:T(8,128)S(1)}, u32[]{:S(2)}, u32[]{:S(2)}) collective-permute-start(f32[96,128]{1,0:T(8,128)S(1)} %get-tuple-element.26), channel_id=1, source_target_pairs={{0,6},{1,11},{2,8},{3,13},{4,10},{5,15},{6,12},{7,1},{8,14},{9,3},... | collective-permute-start | bytes 147464 | tf_op jit(solution)/shard_map/ppermute | solution.py:588
  10.7 0.2 collective-permute-start.2
  11.0 0.0 copy-done.3
  11.0 0.1 pad_maximum_fusion.1.table_in
  11.1 0.2 collective-permute-done.4
  11.3 1.2 %collective-permute-done.3.near_ref = f32[240,128]{1,0:T(8,128)S(1)} collective-permute-done((f32[240,128]{1,0:T(8,128)S(1)}, f32[240,128]{1,0:T(8,128)S(1)}, u32[]{:S(2)}, u32[]{:S(2)}) %collective-permute-start.3) | collective-permute-done | bytes 122912 | tf_op jit(solution)/shard_map/ppermute | solution.py:588
  12.4 0.6 %collective-permute-start.6 = (f32[240,128]{1,0:T(8,128)S(1)}, f32[240,128]{1,0:T(8,128)S(1)}, u32[]{:S(2)}, u32[]{:S(2)}) collective-permute-start(f32[240,128]{1,0:T(8,128)S(1)} %collective-permute-done.3.near_ref), channel_id=1, source_target_pairs={{0,1},{1,0},{2,3},{3,2},{4,5},{5,4},{6,7},{7,6},{8,9},{9,8},{10,11... | collective-permute-start | bytes 368648 | tf_op jit(solution)/shard_map/ppermute | solution.py:591
  13.0 2.2 %collective-permute-done.1 = f32[96,128]{1,0:T(8,128)S(1)} collective-permute-done((f32[96,128]{1,0:T(8,128)S(1)}, f32[96,128]{1,0:T(8,128)S(1)}, u32[]{:S(2)}, u32[]{:S(2)}) %collective-permute-start.1) | collective-permute-done | bytes 49184 | tf_op jit(solution)/shard_map/ppermute | solution.py:588
  15.2 1.4 %collective-permute-done.2 = f32[96,128]{1,0:T(8,128)S(1)} collective-permute-done((f32[96,128]{1,0:T(8,128)S(1)}, f32[96,128]{1,0:T(8,128)S(1)}, u32[]{:S(2)}, u32[]{:S(2)}) %collective-permute-start.2) | collective-permute-done | bytes 49184 | tf_op jit(solution)/shard_map/ppermute | solution.py:588
  16.6 0.1 collective-permute-start.5
  16.7 0.2 place_own.1
  16.9 0.0 collective-permute-done.6.passed_ref
  16.9 0.3 %place_got.1 = (f32[3,672,128]{2,1,0:T(8,128)S(1)}, f32[576,128]{1,0:T(8,128)S(1)}) custom-call(f32[240,128]{1,0:T(8,128)S(1)} %pad_maximum_fusion.far_ref, f32[240,128]{1,0:T(8,128)S(1)} %collective-permute-done.6.passed_ref, f32[3,672,128]{2,1,0:T(8,128)S(1)} %get-tuple-element.34.z_in, ...), custom_call_target="tpu_custom_call", output_to_operand_aliasing={{0}: (2, {}), {1}: (3, {})} | custom-call | tf_op jit(solution)/shard_map/place_got/pallas_call | solution.py:628
  17.2 0.8 %collective-permute-done.5.passed_ref = f32[240,128]{1,0:T(8,128)S(1)} collective-permute-done((f32[240,128]{1,0:T(8,128)S(1)}, f32[240,128]{1,0:T(8,128)S(1)}, u32[]{:S(2)}, u32[]{:S(2)}) %collective-permute-start.5) | collective-permute-done | bytes 122912 | tf_op jit(solution)/shard_map/ppermute | solution.py:591
  18.0 6.2 %substeps.1 = (f32[6,3,6,4,24]{4,3,2,1,0:T(4,128)}, f32[3,672,128]{2,1,0:T(8,128)S(1)}, f32[576,128]{1,0:T(8,128)S(1)}) custom-call(f32[240,128]{1,0:T(8,128)S(1)} %pad_maximum_fusion.far_ref, f32[240,128]{1,0:T(8,128)S(1)} %collective-permute-done.5.passed_ref, f32[76]{0:T(128)S(1)} %pad_maximum_fusion.1.table_in, ...), custom_call_target="tpu_custom_call", output_to_operand_aliasing={{1}: (3, {}), {2}: (4, {})} | custom-call | tf_op jit(solution)/shard_map/substeps/pallas_call | solution.py:637
  (3 shorter events, 0.0 us)
Async XLA Ops:
  0.0 0.9 %copy-start = (f32[6,3,4,6,24]{4,2,3,1,0:T(4,128)S(1)}, f32[6,3,4,6,24]{4,2,3,1,0:T(4,128)}, u32[]{:S(2)}) copy-start(f32[6,3,4,6,24]{4,2,3,1,0:T(4,128)} %param.4) | copy-start | bytes 124420
  0.9 0.7 %copy-start.1 = (f32[6,6,24]{2,1,0:T(8,128)S(1)}, f32[6,6,24]{2,1,0:T(8,128)}, u32[]{:S(2)}) copy-start(f32[6,6,24]{2,1,0:T(8,128)} %coriolis_ref.1) | copy-start | bytes 10372
  1.9 1.4 %collective-permute-start = (f32[216,128]{1,0:T(8,128)S(1)}, f32[216,128]{1,0:T(8,128)S(1)}, u32[]{:S(2)}, u32[]{:S(2)}) collective-permute-start(f32[216,128]{1,0:T(8,128)S(1)} %get-tuple-element.22.swap_ref.own_ref), channel_id=1, source_target_pairs={{0,1},{1,0},{2,3},{3,2},{4,5},{5,4},{6,7},{7,6},{8,9},{9,8},{10,11... | collective-permute-start | bytes 331784 | tf_op jit(solution)/shard_map/ppermute | solution.py:591
  3.3 3.0 %copy-start.2 = (s32[6,4,3]{0,1,2:T(4,128)S(1)}, s32[6,4,3]{0,1,2:T(4,128)}, u32[]{:S(2)}) copy-start(s32[6,4,3]{0,1,2:T(4,128)} %param.7) | copy-start | bytes 868
  3.3 9.1 %collective-permute-start.3 = (f32[240,128]{1,0:T(8,128)S(1)}, f32[240,128]{1,0:T(8,128)S(1)}, u32[]{:S(2)}, u32[]{:S(2)}) collective-permute-start(f32[240,128]{1,0:T(8,128)S(1)} %get-tuple-element.28), channel_id=1, source_target_pairs={{0,2},{1,15},{2,4},{3,1},{4,6},{5,3},{6,8},{7,5},{8,10},{9,7},{10,... | collective-permute-start | bytes 368648 | tf_op jit(solution)/shard_map/ppermute | solution.py:588
  6.5 4.8 %collective-permute-start.4 = (f32[48,128]{1,0:T(8,128)S(1)}, f32[48,128]{1,0:T(8,128)S(1)}, u32[]{:S(2)}, u32[]{:S(2)}) collective-permute-start(f32[48,128]{1,0:T(8,128)S(1)} %get-tuple-element.29), channel_id=1, source_target_pairs={{0,8},{1,9},{2,10},{3,11},{4,12},{5,13},{6,14},{7,15},{8,0},{9,1},... | collective-permute-start | bytes 73736 | tf_op jit(solution)/shard_map/ppermute | solution.py:588
  9.1 1.9 %copy-start.3 = (f32[4]{0:T(128)S(1)}, f32[4]{0:T(128)}, u32[]{:S(2)}) copy-start(f32[4]{0:T(128)} %param.6) | copy-start | bytes 52
  9.1 6.1 %collective-permute-start.1 = (f32[96,128]{1,0:T(8,128)S(1)}, f32[96,128]{1,0:T(8,128)S(1)}, u32[]{:S(2)}, u32[]{:S(2)}) collective-permute-start(f32[96,128]{1,0:T(8,128)S(1)} %get-tuple-element.26), channel_id=1, source_target_pairs={{0,6},{1,11},{2,8},{3,13},{4,10},{5,15},{6,12},{7,1},{8,14},{9,3},... | collective-permute-start | bytes 147464 | tf_op jit(solution)/shard_map/ppermute | solution.py:588
  10.7 5.9 %collective-permute-start.2 = (f32[96,128]{1,0:T(8,128)S(1)}, f32[96,128]{1,0:T(8,128)S(1)}, u32[]{:S(2)}, u32[]{:S(2)}) collective-permute-start(f32[96,128]{1,0:T(8,128)S(1)} %get-tuple-element.27), channel_id=1, source_target_pairs={{0,4},{1,13},{2,6},{3,15},{4,8},{5,1},{6,10},{7,3},{8,12},{9,5},{1... | collective-permute-start | bytes 147464 | tf_op jit(solution)/shard_map/ppermute | solution.py:588
  12.4 4.5 %collective-permute-start.6 = (f32[240,128]{1,0:T(8,128)S(1)}, f32[240,128]{1,0:T(8,128)S(1)}, u32[]{:S(2)}, u32[]{:S(2)}) collective-permute-start(f32[240,128]{1,0:T(8,128)S(1)} %collective-permute-done.3.near_ref), channel_id=1, source_target_pairs={{0,1},{1,0},{2,3},{3,2},{4,5},{5,4},{6,7},{7,6},{8,9},{9,8},{10,11... | collective-permute-start | bytes 368648 | tf_op jit(solution)/shard_map/ppermute | solution.py:591
  16.6 1.4 %collective-permute-start.5 = (f32[240,128]{1,0:T(8,128)S(1)}, f32[240,128]{1,0:T(8,128)S(1)}, u32[]{:S(2)}, u32[]{:S(2)}) collective-permute-start(f32[240,128]{1,0:T(8,128)S(1)} %pad_maximum_fusion.far_ref), channel_id=1, source_target_pairs={{0,1},{1,0},{2,3},{3,2},{4,5},{5,4},{6,7},{7,6},{8,9},{9,8},{10,11... | collective-permute-start | bytes 368648 | tf_op jit(solution)/shard_map/ppermute | solution.py:591

commit v21 on v19

--- a/solution.py
+++ b/solution.py
@@ -594,7 +594,7 @@
     table = jnp.concatenate([wave_speed, edges.reshape(-1).astype(jnp.float32)])
     far, table = lax.optimization_barrier((far, table))
     near_passed = across(near)
-    far_passed = across(far)
+    far_passed = jnp.concatenate([across(third), across(second)])
 
     sizes = (cx, cy, count_x, full_rows, small_rows)
     state_rows = [

time: 23.7 us -> 22.6 us (0.954)
  local copies, waits for them, and re-layouts: 2.13 us -> 1.58 us
  waiting for transfers between devices: 6.03 us -> 5.52 us
    ppermute x3 -> x4, starting transfers between devices: 1.59 us -> 0.59 us  [across(): return lax.ppermute(block, 'ty', [(0, 1), (1, 0)])]
    ppermute x4, waiting for transfers between devices: 4.58 us -> 3.62 us  [moved(): return lax.ppermute(block, ('tx', 'ty'), pairs_of)]
    ppermute x4, starting transfers between devices: 7.37 us -> 8.32 us  [moved(): return lax.ppermute(block, ('tx', 'ty'), pairs_of)]
    unnamed x9, local copies, waits for them, and re-layouts: 1.91 us -> 1.37 us
    ppermute x3 -> x4, waiting for transfers between devices: 1.45 us -> 1.9 us  [across(): return lax.ppermute(block, 'ty', [(0, 1), (1, 0)])]
  transfers between devices with their start and end apart: 7 -> 8, of which waited for: 5 -> 6; matrix products, arithmetic and copies ran while one was open for 1% -> 1% of each run, Pallas kernels for 3% -> 2%
where the time goes in v21:
time: 22.6 us; the launch traced here: 22.4 us
  starting transfers between devices  8.92 us (39%)
  Pallas kernels  6.21 us (27%)
  waiting for transfers between devices  5.52 us (24%)
  local copies, waits for them, and re-layouts  1.58 us (7%)
    ppermute x4, starting transfers between devices, moved(): return lax.ppermute(block, ('tx', 'ty'), pairs_of)  8.32 us
    pallas_call x1, Pallas kernels, fast_on_device(): pl.pallas_call(functools.partial(step_kernel, sizes), out_shape=[jax.Shap...  4.94 us
    ppermute x4, waiting for transfers between devices, moved(): return lax.ppermute(block, ('tx', 'ty'), pairs_of)  3.62 us
    ppermute x4, waiting for transfers between devices, across(): return lax.ppermute(block, 'ty', [(0, 1), (1, 0)])  1.9 us
    unnamed x9, local copies, waits for them, and re-layouts  1.37 us
    ppermute x4, starting transfers between devices, across(): return lax.ppermute(block, 'ty', [(0, 1), (1, 0)])  0.59 us
  transfers between devices with their start and end apart: 8, of which 6 were waited for; matrix products, arithmetic and copies ran while one was open for 1% of the time, Pallas kernels for 2%

profile of v21, /device:TPU:0, one launch (start us, length us, event | category | flops | bytes accessed | tf_op | source)
XLA Modules:
  0.0 22.4 jit_solution(3454647144667916001)
XLA Ops:
  0.0 0.0 copy-start
  0.0 0.9 %copy-done = f32[6,3,4,6,24]{4,2,3,1,0:T(4,128)S(1)} copy-done((f32[6,3,4,6,24]{4,2,3,1,0:T(4,128)S(1)}, f32[6,3,4,6,24]{4,2,3,1,0:T(4,128)}, u32[]{:S(2)}) %copy-start) | copy-done | bytes 41496
  0.9 0.0 copy-start.1
  0.9 0.3 %pack.1.swap_in = f32[216,128]{1,0:T(8,128)S(1)} custom-call(f32[6,3,6,4,24]{4,3,2,1,0:T(4,128)S(1)} %bitcast.2), custom_call_target="tpu_custom_call" | custom-call | tf_op jit(solution)/shard_map/pack/pallas_call | solution.py:537
  1.3 0.4 %copy-done.1 = f32[6,6,24]{2,1,0:T(8,128)S(1)} copy-done((f32[6,6,24]{2,1,0:T(8,128)S(1)}, f32[6,6,24]{2,1,0:T(8,128)}, u32[]{:S(2)}) %copy-start.1) | copy-done | bytes 3480
  1.7 0.2 pack_coriolis.1
  1.9 0.5 %collective-permute-start = (f32[216,128]{1,0:T(8,128)S(1)}, f32[216,128]{1,0:T(8,128)S(1)}, u32[]{:S(2)}, u32[]{:S(2)}) collective-permute-start(f32[216,128]{1,0:T(8,128)S(1)} %get-tuple-element.20.swap_ref.own_ref), channel_id=1, source_target_pairs={{0,1},{1,0},{2,3},{3,2},{4,5},{5,4},{6,7},{7,6},{8,9},{9,8},{10,11... | collective-permute-start | bytes 331784 | tf_op jit(solution)/shard_map/ppermute | solution.py:575
  2.3 0.2 keep.1
  2.5 0.8 %collective-permute-done.other_ref = f32[216,128]{1,0:T(8,128)S(1)} collective-permute-done((f32[216,128]{1,0:T(8,128)S(1)}, f32[216,128]{1,0:T(8,128)S(1)}, u32[]{:S(2)}, u32[]{:S(2)}) %collective-permute-start) | collective-permute-done | bytes 110624 | tf_op jit(solution)/shard_map/ppermute | solution.py:575
  3.3 2.9 %collective-permute-start.5 = (f32[240,128]{1,0:T(8,128)S(1)}, f32[240,128]{1,0:T(8,128)S(1)}, u32[]{:S(2)}, u32[]{:S(2)}) collective-permute-start(f32[240,128]{1,0:T(8,128)S(1)} %get-tuple-element.27), channel_id=1, source_target_pairs={{0,2},{1,15},{2,4},{3,1},{4,6},{5,3},{6,8},{7,5},{8,10},{9,7},{10,... | collective-permute-start | bytes 368648 | tf_op jit(solution)/shard_map/ppermute | solution.py:572
  6.2 0.0 copy-done.2
  6.2 0.1 copy.11
  6.4 0.1 convert_element_type.7
  6.5 0.0 copy-start.3
  6.5 2.6 %collective-permute-start.1 = (f32[96,128]{1,0:T(8,128)S(1)}, f32[96,128]{1,0:T(8,128)S(1)}, u32[]{:S(2)}, u32[]{:S(2)}) collective-permute-start(f32[96,128]{1,0:T(8,128)S(1)} %get-tuple-element.24), channel_id=1, source_target_pairs={{0,6},{1,11},{2,8},{3,13},{4,10},{5,15},{6,12},{7,1},{8,14},{9,3},... | collective-permute-start | bytes 147464 | tf_op jit(solution)/shard_map/ppermute | solution.py:572
  9.1 1.6 %collective-permute-start.3 = (f32[96,128]{1,0:T(8,128)S(1)}, f32[96,128]{1,0:T(8,128)S(1)}, u32[]{:S(2)}, u32[]{:S(2)}) collective-permute-start(f32[96,128]{1,0:T(8,128)S(1)} %get-tuple-element.25), channel_id=1, source_target_pairs={{0,4},{1,13},{2,6},{3,15},{4,8},{5,1},{6,10},{7,3},{8,12},{9,5},{1... | collective-permute-start | bytes 147464 | tf_op jit(solution)/shard_map/ppermute | solution.py:572
  10.6 0.0 copy-done.3
  10.6 0.1 pad_maximum_fusion.2.table_in
  10.7 1.2 %collective-permute-start.6 = (f32[48,128]{1,0:T(8,128)S(1)}, f32[48,128]{1,0:T(8,128)S(1)}, u32[]{:S(2)}, u32[]{:S(2)}) collective-permute-start(f32[48,128]{1,0:T(8,128)S(1)} %get-tuple-element.28), channel_id=1, source_target_pairs={{0,8},{1,9},{2,10},{3,11},{4,12},{5,13},{6,14},{7,15},{8,0},{9,1},... | collective-permute-start | bytes 73736 | tf_op jit(solution)/shard_map/ppermute | solution.py:572
  11.9 1.4 %collective-permute-done.1 = f32[96,128]{1,0:T(8,128)S(1)} collective-permute-done((f32[96,128]{1,0:T(8,128)S(1)}, f32[96,128]{1,0:T(8,128)S(1)}, u32[]{:S(2)}, u32[]{:S(2)}) %collective-permute-start.1) | collective-permute-done | bytes 49184 | tf_op jit(solution)/shard_map/ppermute | solution.py:572
  13.4 0.1 collective-permute-start.2
  13.5 1.5 %collective-permute-done.3 = f32[96,128]{1,0:T(8,128)S(1)} collective-permute-done((f32[96,128]{1,0:T(8,128)S(1)}, f32[96,128]{1,0:T(8,128)S(1)}, u32[]{:S(2)}, u32[]{:S(2)}) %collective-permute-start.3) | collective-permute-done | bytes 49184 | tf_op jit(solution)/shard_map/ppermute | solution.py:572
  15.0 0.0 collective-permute-start.4
  15.0 0.0 collective-permute-done.5
  15.1 0.6 %collective-permute-done.6 = f32[48,128]{1,0:T(8,128)S(1)} collective-permute-done((f32[48,128]{1,0:T(8,128)S(1)}, f32[48,128]{1,0:T(8,128)S(1)}, u32[]{:S(2)}, u32[]{:S(2)}) %collective-permute-start.6) | collective-permute-done | bytes 24608 | tf_op jit(solution)/shard_map/ppermute | solution.py:572
  15.7 0.0 collective-permute-start.7
  15.7 0.0 collective-permute-done.2
  15.7 0.5 %collective-permute-done.4 = f32[96,128]{1,0:T(8,128)S(1)} collective-permute-done((f32[96,128]{1,0:T(8,128)S(1)}, f32[96,128]{1,0:T(8,128)S(1)}, u32[]{:S(2)}, u32[]{:S(2)}) %collective-permute-start.4) | collective-permute-done | bytes 49184 | tf_op jit(solution)/shard_map/ppermute | solution.py:575
  16.3 0.2 place_own.1
  16.5 0.6 %collective-permute-done.7.passed_ref = f32[288,128]{1,0:T(8,128)S(1)} collective-permute-done((f32[288,128]{1,0:T(8,128)S(1)}, f32[288,128]{1,0:T(8,128)S(1)}, u32[]{:S(2)}, u32[]{:S(2)}) %collective-permute-start.7) | collective-permute-done | bytes 147488 | tf_op jit(solution)/shard_map/ppermute | solution.py:575
  17.1 0.4 %place_got.1 = (f32[3,672,128]{2,1,0:T(8,128)S(1)}, f32[576,128]{1,0:T(8,128)S(1)}) custom-call(f32[288,128]{1,0:T(8,128)S(1)} %constant_dynamic-update-slice_fusion.near_ref, f32[192,128]{1,0:T(8,128)S(1)} %pad_maximum_fusion.1.far_ref, f32[288,128]{1,0:T(8,128)S(1)} %collective-permute-done.7.passed_ref, ...), custom_call_target="tpu_custom_call", output_to_operand_aliasing={{0}: (3, {}), {1}: (4, {})} | custom-call | tf_op jit(solution)/shard_map/place_got/pallas_call | solution.py:612
  17.4 4.9 %substeps.1 = (f32[6,3,6,4,24]{4,3,2,1,0:T(4,128)}, f32[3,672,128]{2,1,0:T(8,128)S(1)}, f32[576,128]{1,0:T(8,128)S(1)}) custom-call(f32[192,128]{1,0:T(8,128)S(1)} %pad_maximum_fusion.passed_ref, f32[76]{0:T(128)S(1)} %pad_maximum_fusion.2.table_in, f32[3,672,128]{2,1,0:T(8,128)S(1)} %get-tuple-element.32.z_in, ...), custom_call_target="tpu_custom_call", output_to_operand_aliasing={{1}: (2, {}), {2}: (3, {})} | custom-call | tf_op jit(solution)/shard_map/substeps/pallas_call | solution.py:621
  (7 shorter events, 0.1 us)
Async XLA Ops:
  0.0 0.9 %copy-start = (f32[6,3,4,6,24]{4,2,3,1,0:T(4,128)S(1)}, f32[6,3,4,6,24]{4,2,3,1,0:T(4,128)}, u32[]{:S(2)}) copy-start(f32[6,3,4,6,24]{4,2,3,1,0:T(4,128)} %param.4) | copy-start | bytes 124420
  0.9 0.7 %copy-start.1 = (f32[6,6,24]{2,1,0:T(8,128)S(1)}, f32[6,6,24]{2,1,0:T(8,128)}, u32[]{:S(2)}) copy-start(f32[6,6,24]{2,1,0:T(8,128)} %coriolis_ref.1) | copy-start | bytes 10372
  1.9 1.4 %collective-permute-start = (f32[216,128]{1,0:T(8,128)S(1)}, f32[216,128]{1,0:T(8,128)S(1)}, u32[]{:S(2)}, u32[]{:S(2)}) collective-permute-start(f32[216,128]{1,0:T(8,128)S(1)} %get-tuple-element.20.swap_ref.own_ref), channel_id=1, source_target_pairs={{0,1},{1,0},{2,3},{3,2},{4,5},{5,4},{6,7},{7,6},{8,9},{9,8},{10,11... | collective-permute-start | bytes 331784 | tf_op jit(solution)/shard_map/ppermute | solution.py:575
  3.3 3.0 %copy-start.2 = (s32[6,4,3]{0,1,2:T(4,128)S(1)}, s32[6,4,3]{0,1,2:T(4,128)}, u32[]{:S(2)}) copy-start(s32[6,4,3]{0,1,2:T(4,128)} %param.7) | copy-start | bytes 868
  3.3 11.7 %collective-permute-start.5 = (f32[240,128]{1,0:T(8,128)S(1)}, f32[240,128]{1,0:T(8,128)S(1)}, u32[]{:S(2)}, u32[]{:S(2)}) collective-permute-start(f32[240,128]{1,0:T(8,128)S(1)} %get-tuple-element.27), channel_id=1, source_target_pairs={{0,2},{1,15},{2,4},{3,1},{4,6},{5,3},{6,8},{7,5},{8,10},{9,7},{10,... | collective-permute-start | bytes 368648 | tf_op jit(solution)/shard_map/ppermute | solution.py:572
  6.5 4.2 %copy-start.3 = (f32[4]{0:T(128)S(1)}, f32[4]{0:T(128)}, u32[]{:S(2)}) copy-start(f32[4]{0:T(128)} %param.6) | copy-start | bytes 52
  6.5 6.9 %collective-permute-start.1 = (f32[96,128]{1,0:T(8,128)S(1)}, f32[96,128]{1,0:T(8,128)S(1)}, u32[]{:S(2)}, u32[]{:S(2)}) collective-permute-start(f32[96,128]{1,0:T(8,128)S(1)} %get-tuple-element.24), channel_id=1, source_target_pairs={{0,6},{1,11},{2,8},{3,13},{4,10},{5,15},{6,12},{7,1},{8,14},{9,3},... | collective-permute-start | bytes 147464 | tf_op jit(solution)/shard_map/ppermute | solution.py:572
  9.1 6.0 %collective-permute-start.3 = (f32[96,128]{1,0:T(8,128)S(1)}, f32[96,128]{1,0:T(8,128)S(1)}, u32[]{:S(2)}, u32[]{:S(2)}) collective-permute-start(f32[96,128]{1,0:T(8,128)S(1)} %get-tuple-element.25), channel_id=1, source_target_pairs={{0,4},{1,13},{2,6},{3,15},{4,8},{5,1},{6,10},{7,3},{8,12},{9,5},{1... | collective-permute-start | bytes 147464 | tf_op jit(solution)/shard_map/ppermute | solution.py:572
  10.7 5.0 %collective-permute-start.6 = (f32[48,128]{1,0:T(8,128)S(1)}, f32[48,128]{1,0:T(8,128)S(1)}, u32[]{:S(2)}, u32[]{:S(2)}) collective-permute-start(f32[48,128]{1,0:T(8,128)S(1)} %get-tuple-element.28), channel_id=1, source_target_pairs={{0,8},{1,9},{2,10},{3,11},{4,12},{5,13},{6,14},{7,15},{8,0},{9,1},... | collective-permute-start | bytes 73736 | tf_op jit(solution)/shard_map/ppermute | solution.py:572
  13.4 2.3 %collective-permute-start.2 = (f32[96,128]{1,0:T(8,128)S(1)}, f32[96,128]{1,0:T(8,128)S(1)}, u32[]{:S(2)}, u32[]{:S(2)}) collective-permute-start(f32[96,128]{1,0:T(8,128)S(1)} %collective-permute-done.1), channel_id=1, source_target_pairs={{0,1},{1,0},{2,3},{3,2},{4,5},{5,4},{6,7},{7,6},{8,9},{9,8},{10,11... | collective-permute-start | bytes 147464 | tf_op jit(solution)/shard_map/ppermute | solution.py:575
  15.0 1.2 %collective-permute-start.4 = (f32[96,128]{1,0:T(8,128)S(1)}, f32[96,128]{1,0:T(8,128)S(1)}, u32[]{:S(2)}, u32[]{:S(2)}) collective-permute-start(f32[96,128]{1,0:T(8,128)S(1)} %collective-permute-done.3), channel_id=1, source_target_pairs={{0,1},{1,0},{2,3},{3,2},{4,5},{5,4},{6,7},{7,6},{8,9},{9,8},{10,11... | collective-permute-start | bytes 147464 | tf_op jit(solution)/shard_map/ppermute | solution.py:575
  15.7 1.4 %collective-permute-start.7 = (f32[288,128]{1,0:T(8,128)S(1)}, f32[288,128]{1,0:T(8,128)S(1)}, u32[]{:S(2)}, u32[]{:S(2)}) collective-permute-start(f32[288,128]{1,0:T(8,128)S(1)} %constant_dynamic-update-slice_fusion.near_ref), channel_id=1, source_target_pairs={{0,1},{1,0},{2,3},{3,2},{4,5},{5,4},{6,7},{7,6},{8,9},{9,8},{10,11... | collective-permute-start | bytes 442376 | tf_op jit(solution)/shard_map/ppermute | solution.py:575
